TPU v7x, 32 devices: a whole 2x2x4 slice. The times are simulated.
32 devices in a mesh: req: 8 (over z, core), tensor: 4 (over y, x).
Axes of the slice: x: 2, y: 2, z: 4, core: 2. Of those that a mesh axis runs over, the one named last changes fastest.
Arguments:
- text: bfloat16 [3072, 4096], P('req', 'tensor'), may hold values from -6 to 6
- patches: bfloat16 [64, 6, 6, 4096], P('req', None, None, 'tensor'), may hold values from -6 to 6
- grids: int32 [64, 2], replicated, may hold values from 2 to 6, as said below
- image_request: int32 [64], replicated, may hold values from 0 to 7, as said below
- slot_start: int32 [64], replicated, may hold values from 1 to 375, as said below
- vis_gain: bfloat16 [4096], P('tensor'), may hold values from 0.099609375 to 1.8984375
- dec_gain: bfloat16 [4096], replicated, may hold values from 0.099609375 to 1.8984375
- w_qkv: bfloat16 [4096, 3, 2048], P(None, None, 'tensor'), may hold values from -0.09375 to 0.09375
- w_out: bfloat16 [2048, 4096], P('tensor'), may hold values from -0.125 to 0.125
Outputs:
- layer_out: bfloat16 [3072, 4096], P('req', 'tensor')
Inputs may be any that keep to these rules, and one draw needn't show every extreme that they name: `grids`: heights and widths are even; some image has a 6 x 6 grid and some a 2 x 2 grid. `image_request`: the images of one index of req go to distinct requests, one to each. `slot_start`: the regions of 9 positions of the images of one request don't intersect and lie within the prompt; position 0 of every prompt lies outside them.
All inputs are finite; a program needn't handle non-finite values.
Results may differ from a plain program's by a relative error of at most 0.011.
Values may be sent and summed in bfloat16 or wider, within the bound.
No kernel may reach another device: no remote copies, remote signals or barrier semaphores. Data moves between devices by JAX's collectives and lax.ppermute only.
A program may use at most 64 MiB of HBM per device.

v0:
```python
import functools

import jax
import jax.numpy as jnp
from jax import lax
from jax.experimental import pallas as pl
from jax.experimental.pallas import tpu as pltpu
from jax.sharding import PartitionSpec as P

D = 4096
HD = 128
EPS = 1e-05
LOG2E = 1.4426950408889634
TINY = pl.CostEstimate(flops=0, bytes_accessed=0, transcendentals=0)


def round_up(n, m):
    return -(-n // m) * m


def swap(x, s, axis="tensor"):
    n = lax.axis_size(axis)
    return lax.ppermute(x, axis, [(i, i ^ s) for i in range(n)])


def in_hbm(x):
    return pltpu.with_memory_space_constraint(x, pltpu.HBM)


def low_bit(s):
    return s & -s


def high_bit(s):
    return 1 << (s.bit_length() - 1)


def by_bits(n, reverse=False):
    return sorted(range(1, n), key=lambda s: (bin(s).count("1"), s), reverse=reverse)


def halves(block):
    if isinstance(block, tuple):
        return block
    half = block.shape[0] // 2
    return block[:half], block[half:]


def near_blocks(x, n):
    return {s: swap(x, s) for s in by_bits(n) if s & (s - 1) == 0}


def far_blocks(blocks, n):
    blocks = dict(blocks)
    for s in by_bits(n):
        if s not in blocks:
            low, high = low_bit(s), high_bit(s)
            blocks[s] = (swap(halves(blocks[s ^ low])[0], low), swap(halves(blocks[s ^ high])[1], high))
    return blocks


def vmem_specs(n):
    return [pl.BlockSpec(memory_space=pltpu.VMEM)] * n


def params(mib):
    return pltpu.CompilerParams(vmem_limit_bytes=mib * 1024 * 1024)


def fetch(pairs, sem_ref):
    copies = [pltpu.make_async_copy(src, dst, sem_ref.at[i]) for i, (src, dst) in enumerate(pairs)]
    for copy in copies:
        copy.start()
    return copies


NOWHERE = 1 << 20


def prep_kernel(n_req, me_ref, req_hbm, start_hbm, grid_hbm, text_hbm, x_hbm, dec_hbm, vis_hbm, *refs):
    outs, refs = refs[:n_req], refs[n_req:]
    (ctext_out, rtext_out, sel_out, table_out, key_out, dec_out, vis_out, req_ref, start_ref, grid_ref, text_ref, x_ref,
     dec_ref, vis_ref, tmp_ref, sem_ref) = refs
    pairs = (
        (req_hbm, req_ref),
        (start_hbm, start_ref),
        (grid_hbm, grid_ref),
        (text_hbm, text_ref),
        (x_hbm, x_ref),
        (dec_hbm, dec_ref),
        (vis_hbm, vis_ref),
    )
    copies = fetch(pairs, sem_ref)
    side, img_dev = x_ref.shape[0], x_ref.shape[2]
    half = side // 2
    region = half * half
    n_img, n_text, length = sel_out.shape[0], ctext_out.shape[0], text_ref.shape[0]
    me = me_ref[0]
    for copy in copies[:3]:
        copy.wait()

    found = []
    for s in range(n_req):
        source = (me ^ s) * img_dev

        def one_image(k, found, source=source):
            hit = req_ref[source + k] == me
            values = (start_ref[source + k], grid_ref[0, source + k] // 2, grid_ref[1, source + k] // 2)
            return tuple(jnp.where(hit, new, old) for new, old in zip(values, found))

        none = (jnp.int32(NOWHERE), jnp.int32(0), jnp.int32(1))
        found.append(lax.fori_loop(0, img_dev, one_image, none, unroll=img_dev <= 8))

    spot = lax.broadcasted_iota(jnp.int32, (8, length), 1)
    before = jnp.zeros((8, length), jnp.int32)
    closed = jnp.zeros((8, length), jnp.int32)
    inside = jnp.zeros((8, length), jnp.int32)
    row = lax.broadcasted_iota(jnp.int32, (n_img, 128), 0)
    pos = jnp.full((n_img, 128), -1, jnp.int32)
    target = jnp.full((n_img, 128), -1, jnp.int32)
    line = lax.broadcasted_iota(jnp.int32, (n_req, 128), 0)
    table = jnp.zeros((n_req, 128), jnp.int32)
    for s, (start, high, wide) in enumerate(found):
        count = high * wide
        c = spot - start
        here = (c >= 0) & (c < region)
        before += jnp.clip(c, 0, region)
        inside = jnp.where(here, 1, inside)
        closed = jnp.where(here & (c >= count), 1, closed)
        c = row - s * region
        here = (c >= 0) & (c < region)
        pos = jnp.where(here, start + c, pos)
        cell = c
        for w in range(1, half):
            cell = jnp.where(wide == w, c // w * half + c % w, cell)
        target = jnp.where(here & (c < count), s * region + cell, target)
        table = jnp.where(line == s, start, table)
    table_out[...] = table
    key_out[...] = 1.0 - closed.astype(jnp.float32)
    rank = jnp.where(inside == 1, -1, spot - before)[0:1]
    gather = (lax.broadcasted_iota(jnp.int32, (n_text, length), 0) == rank).astype(jnp.bfloat16)
    stays = jnp.where(target >= 0, -1, pos)[:, :1]
    keep = (lax.broadcasted_iota(jnp.int32, (n_img, length), 1) == stays).astype(jnp.bfloat16)
    sel = lax.broadcasted_iota(jnp.int32, (n_img, n_img), 1) == target[:, :1]
    sel_out[...] = sel.astype(jnp.bfloat16)
    copies[3].wait()
    text = text_ref[...]
    ctext_out[...] = jnp.dot(gather, text, preferred_element_type=jnp.float32).astype(jnp.bfloat16)
    rtext_out[...] = jnp.dot(keep, text, preferred_element_type=jnp.float32).astype(jnp.bfloat16)

    for copy in copies[4:]:
        copy.wait()
    rows = lax.broadcasted_iota(jnp.int32, (n_req, img_dev), 0)
    cols = lax.broadcasted_iota(jnp.int32, (n_req, img_dev), 1)
    goal = jnp.full((n_req, img_dev), -1, jnp.int32)
    for k in range(img_dev):
        goal = jnp.where(cols == k, req_ref[me * img_dev + k] ^ me, goal)
    onehot = (rows == goal).astype(jnp.bfloat16)
    tmp_ref[...] = jnp.zeros_like(tmp_ref)
    for i in range(half):
        for j in range(half):
            total = x_ref[2 * i, 2 * j].astype(jnp.float32)
            for a, b in ((0, 1), (1, 0), (1, 1)):
                total += x_ref[2 * i + a, 2 * j + b].astype(jnp.float32)
            pooled = (total * 0.25).astype(jnp.bfloat16)
            tmp_ref[:, i * half + j, :] = jnp.dot(onehot, pooled, preferred_element_type=jnp.float32)
    for s in range(n_req):
        outs[s][...] = tmp_ref[s].astype(jnp.bfloat16)
    per = vis_ref.shape[0]
    for i in range(per):
        lanes = pl.ds(i * 128, 128)
        vis_out[:, lanes] = vis_ref[i : i + 1, :].astype(jnp.float32)
        for t in range(dec_out.shape[0]):
            at = t * per + i
            dec_out[t, :, lanes] = dec_ref[at : at + 1, :].astype(jnp.float32)


def prepare(me, image_request, slot_start, grids, text, patches, dec_gain, vis_gain, n_req, n_text, n_img):
    side, _, img_dev, width = patches.shape
    padded = round_up((side // 2) ** 2, 16)
    inputs = (
        image_request,
        slot_start,
        grids.T,
        text,
        patches,
        dec_gain.reshape(-1, 128),
        vis_gain.reshape(-1, 128),
    )
    bf16, f32 = jnp.bfloat16, jnp.float32
    outputs = [((padded, width), bf16)] * n_req + [
        ((n_text, width), bf16),
        ((n_img, width), bf16),
        ((n_img, n_img), bf16),
        ((n_req, 128), jnp.int32),
        ((8, text.shape[0]), f32),
        ((dec_gain.size // width, 1, width), f32),
        ((1, width), f32),
    ]
    return pl.pallas_call(
        functools.partial(prep_kernel, n_req),
        out_shape=tuple(jax.ShapeDtypeStruct(shape, kind) for shape, kind in outputs),
        in_specs=[pl.BlockSpec(memory_space=pltpu.SMEM)] + [pl.BlockSpec(memory_space=pltpu.HBM)] * len(inputs),
        out_specs=tuple(vmem_specs(len(outputs))),
        scratch_shapes=[pltpu.SMEM(x.shape, jnp.int32) for x in inputs[:3]]
        + [pltpu.VMEM(x.shape, x.dtype) for x in inputs[3:]]
        + [pltpu.VMEM((n_req, padded, width), f32), pltpu.SemaphoreType.DMA((len(inputs),))],
        compiler_params=params(12),
        cost_estimate=TINY,
    )(me, *[in_hbm(x) for x in inputs])


def pack_kernel(region, gain_ref, rtext_ref, sel_ref, *refs):
    recs, (out_ref, tmp_ref) = refs[:-2], refs[-2:]
    for r, rec_ref in enumerate(recs):
        tmp_ref[region * r : region * (r + 1)] = rec_ref[...].astype(jnp.float32)[:region]
    done = region * len(recs)
    rest = tmp_ref.shape[0] - done
    tmp_ref[done:] = jnp.zeros((rest, tmp_ref.shape[1]), jnp.float32)
    picked = jnp.dot(sel_ref[...], tmp_ref[...].astype(jnp.bfloat16), preferred_element_type=jnp.float32)
    tmp_ref[...] = picked + rtext_ref[...].astype(jnp.float32)
    tmp_ref[done:] = jnp.broadcast_to(gain_ref[0:1, :], (rest, gain_ref.shape[1]))
    out_ref[...] = tmp_ref[...].astype(jnp.bfloat16)


def pack_images(received, gain, rtext, sel, region):
    n_img, width = rtext.shape
    return pl.pallas_call(
        functools.partial(pack_kernel, region),
        out_shape=jax.ShapeDtypeStruct((n_img, width), jnp.bfloat16),
        in_specs=vmem_specs(3 + len(received)),
        out_specs=pl.BlockSpec(memory_space=pltpu.VMEM),
        scratch_shapes=[pltpu.VMEM((n_img, width), jnp.float32)],
        compiler_params=params(4),
        cost_estimate=TINY,
    )(gain, rtext, sel, *received)


def place_kernel(region, n_text, table_ref, place_ref, text_row_ref):
    length, n_all = place_ref.shape
    spot = lax.broadcasted_iota(jnp.int32, (length, 128), 0)
    before = jnp.zeros((length, 128), jnp.int32)
    at = jnp.full((length, 128), -1, jnp.int32)
    for s in range(table_ref.shape[0]):
        c = spot - table_ref[s : s + 1, :]
        before += jnp.clip(c, 0, region)
        at = jnp.where((c >= 0) & (c < region), n_text + s * region + c, at)
    text_row_ref[...] = jnp.where(at < 0, 1.0, 0.0)
    at = jnp.where(at < 0, spot - before, at)[:, :1]
    place_ref[...] = (lax.broadcasted_iota(jnp.int32, (length, n_all), 1) == at).astype(jnp.bfloat16)


def placement(table, region, length, n_text, n_img):
    return pl.pallas_call(
        functools.partial(place_kernel, region, n_text),
        out_shape=(
            jax.ShapeDtypeStruct((length, n_text + n_img), jnp.bfloat16),
            jax.ShapeDtypeStruct((length, 128), jnp.float32),
        ),
        in_specs=vmem_specs(1),
        out_specs=tuple(vmem_specs(2)),
        compiler_params=params(8),
        cost_estimate=TINY,
    )(table)


def cols_of(ref, owner, width):
    return ref[:, pl.ds(pl.multiple_of(owner * width, width), width)]


def scale_rows(x, gain):
    xf = x.astype(jnp.float32)
    return (xf * gain).astype(jnp.bfloat16), jnp.sum(xf * xf, axis=1, keepdims=True)


def own_kernel(me_ref, x_ref, gain_ref, w_ref, acc_ref, ss_ref, held_ref, sem_ref):
    n_ten, _, width, _ = held_ref.shape
    half = x_ref.shape[0] // 2
    copies = []
    for s in range(n_ten):
        rows = pl.ds(pl.multiple_of((me_ref[0] ^ s) * width, width), width)
        copies += [pltpu.make_async_copy(w_ref.at[j, rows], held_ref.at[s, j], sem_ref.at[s, j]) for j in range(3)]
    for copy in copies:
        copy.start()
    scaled = []
    for side in range(2):
        rows = pl.ds(side * half, half)
        x, total = scale_rows(x_ref[rows], gain_ref[me_ref[0]])
        scaled.append(x)
        ss_ref[rows] = jnp.broadcast_to(total, (half, 128))
    for j in range(3):
        copies[j].wait()
        for side in range(2):
            acc_ref[j, pl.ds(side * half, half)] = jnp.dot(
                scaled[side], held_ref[0, j], preferred_element_type=jnp.float32
            )
    for copy in copies[3:]:
        copy.wait()


def own_part(me, x, gain, w):
    rows, width = x.shape
    n_ten, cols = gain.shape[0], w.shape[2]
    return pl.pallas_call(
        own_kernel,
        out_shape=(
            jax.ShapeDtypeStruct((3, rows, cols), jnp.float32),
            jax.ShapeDtypeStruct((rows, 128), jnp.float32),
            pltpu.VMEM((n_ten, 3, width, cols), w.dtype),
        ),
        in_specs=[pl.BlockSpec(memory_space=pltpu.SMEM)] + vmem_specs(2) + [pl.BlockSpec(memory_space=pltpu.HBM)],
        out_specs=tuple(vmem_specs(3)),
        scratch_shapes=[pltpu.SemaphoreType.DMA((n_ten, 3))],
        compiler_params=params(12),
        cost_estimate=TINY,
    )(me, x, gain, in_hbm(w))


def near_kernel(near, pieces, me_ref, *refs):
    n_x = sum(pieces)
    x_refs, refs = list(refs[:n_x]), refs[n_x:]
    gain_ref, held_ref, acc_in, ss_in, acc_ref, ss_ref = refs
    half = acc_ref.shape[1] // 2
    views = []
    for n in pieces:
        mine, x_refs = x_refs[:n], x_refs[n:]
        views.append([mine[0].at[pl.ds(side * half, half)] if n == 1 else mine[side] for side in range(2)])
    scaled = {}
    for side in range(2):
        rows = pl.ds(side * half, half)
        total = ss_in[rows]
        for b, s in enumerate(near):
            scaled[side, b], part = scale_rows(views[b][side][...], gain_ref[me_ref[0] ^ s])
            total += part
        ss_ref[rows] = total
    for j in range(3):
        for side in range(2):
            rows = pl.ds(side * half, half)
            acc = acc_in[j, rows]
            for b, s in enumerate(near):
                acc += jnp.dot(scaled[side, b], held_ref[s, j], preferred_element_type=jnp.float32)
            acc_ref[j, rows] = acc


def near_part(near, me, blocks, gain, held, acc, ss):
    blocks = [b if isinstance(b, tuple) else (b,) for b in blocks]
    pieces = [len(b) for b in blocks]
    return pl.pallas_call(
        functools.partial(near_kernel, near, pieces),
        out_shape=(
            jax.ShapeDtypeStruct(acc.shape, jnp.float32),
            jax.ShapeDtypeStruct(ss.shape, jnp.float32),
        ),
        in_specs=[pl.BlockSpec(memory_space=pltpu.SMEM)]
        + vmem_specs(sum(pieces) + 4),
        out_specs=tuple(vmem_specs(2)),
        compiler_params=params(12),
        cost_estimate=TINY,
    )(me, *[h for b in blocks for h in b], gain, held, acc, ss)


def image_kernel(n_rows, n_blk, me_ref, *refs):
    x_refs, refs = refs[:n_blk], refs[n_blk:]
    gain_ref, sel_ref, held_ref, w_out_ref, qkv_ref, own_ref, w_out_held, sem_ref = refs
    copy = pltpu.make_async_copy(w_out_ref, w_out_held, sem_ref)
    copy.start()
    is_img = jnp.sum(sel_ref[...].astype(jnp.float32), axis=1, keepdims=True) > 0.5
    total = 0.0
    for s in range(n_blk):
        xf = x_refs[s][...].astype(jnp.float32)
        total += jnp.sum(xf * xf, axis=1, keepdims=True)
    scale = lax.rsqrt(total / D + EPS)
    total = 0.0
    scaled = []
    for s in range(n_blk):
        xf = x_refs[s][...].astype(jnp.float32)
        merged = jnp.where(is_img, xf * scale * xf[n_rows : n_rows + 1], xf).astype(jnp.bfloat16)
        if s == 0:
            own_ref[...] = merged
        mf = merged.astype(jnp.float32)
        total += jnp.sum(mf * mf, axis=1, keepdims=True)
        scaled.append((mf * gain_ref[me_ref[0] ^ s]).astype(jnp.bfloat16))
    scale = lax.rsqrt(total / D + EPS)
    for j in range(3):
        acc = 0.0
        for s in range(n_blk):
            acc += jnp.dot(scaled[s], held_ref[s, j], preferred_element_type=jnp.float32)
        qkv_ref[j] = (acc * scale).astype(jnp.bfloat16)
    copy.wait()


def image_part(me, blocks, gain, sel, held, w_out, n_rows):
    n_img, width = blocks[0].shape
    return pl.pallas_call(
        functools.partial(image_kernel, n_rows, len(blocks)),
        out_shape=(
            jax.ShapeDtypeStruct((3, n_img, held.shape[3]), jnp.bfloat16),
            jax.ShapeDtypeStruct((n_img, width), jnp.bfloat16),
            pltpu.VMEM(w_out.shape, w_out.dtype),
        ),
        in_specs=[pl.BlockSpec(memory_space=pltpu.SMEM)]
        + vmem_specs(len(blocks) + 3)
        + [pl.BlockSpec(memory_space=pltpu.HBM)],
        out_specs=tuple(vmem_specs(3)),
        scratch_shapes=[pltpu.SemaphoreType.DMA],
        compiler_params=params(12),
        cost_estimate=TINY,
    )(me, *blocks, gain, sel, held, in_hbm(w_out))


def final_kernel(far, me_ref, top_ref, bottom_ref, gain_ref, held_ref, acc_ref, ss_ref, img_ref, place_ref, key_ref,
                 w_out_ref, ctx_ref, far_top_ref, far_bottom_ref, all_ref, qkv_ref):
    half, width = top_ref.shape
    n_text = 2 * half
    rows, cols = ctx_ref.shape
    owner = me_ref[0] ^ far
    scaled, scales = [], []
    for side, x_ref in enumerate((top_ref, bottom_ref)):
        part = pl.ds(side * half, half)
        x, total = scale_rows(x_ref[...], gain_ref[owner])
        scaled.append(x)
        total = ss_ref[part] + total
        scales.append(lax.rsqrt(total / D + EPS)[:, :1])
    for j in range(3):
        weight = held_ref[far, j]
        for side in range(2):
            part = pl.ds(side * half, half)
            prod = jnp.dot(scaled[side], weight, preferred_element_type=jnp.float32)
            all_ref[part] = ((prod + acc_ref[j, part]) * scales[side]).astype(jnp.bfloat16)
        all_ref[n_text:] = img_ref[j]
        qkv_ref[j] = jnp.dot(place_ref[...], all_ref[...], preferred_element_type=jnp.float32).astype(jnp.bfloat16)
    step = 128
    heads = [pl.ds(h * HD, HD) for h in range(cols // HD)]
    for r in range(rows // step):
        here, last = pl.ds(r * step, step), (r + 1) * step
        row = lax.broadcasted_iota(jnp.int32, (step, last), 0) + r * step
        col = lax.broadcasted_iota(jnp.int32, (step, last), 1)
        bias = jnp.where((row >= col) & (key_ref[0:1, pl.ds(0, last)] > 0.5), 0.0, -1e30)
        scores = [
            lax.dot_general(
                qkv_ref[0, here, lanes],
                qkv_ref[1, pl.ds(0, last), lanes],
                (((1,), (1,)), ((), ())),
                preferred_element_type=jnp.float32,
            )
            for lanes in heads
        ]
        scores = [x * (LOG2E / HD**0.5) + bias for x in scores]
        tops = [jnp.max(x, axis=1, keepdims=True) for x in scores]
        expo = [jnp.exp2(x - top) for x, top in zip(scores, tops)]
        sums = [jnp.sum(x, axis=1, keepdims=True) for x in expo]
        outs = [
            jnp.dot(x.astype(jnp.bfloat16), qkv_ref[2, pl.ds(0, last), lanes], preferred_element_type=jnp.float32)
            for x, lanes in zip(expo, heads)
        ]
        for lanes, out, total in zip(heads, outs, sums):
            ctx_ref[here, lanes] = (out / total).astype(jnp.bfloat16)
    weight = cols_of(w_out_ref, owner, width)
    half = rows // 2
    for side, out_ref in enumerate((far_top_ref, far_bottom_ref)):
        out_ref[...] = jnp.dot(
            ctx_ref[pl.ds(side * half, half)], weight, preferred_element_type=jnp.float32
        ).astype(jnp.bfloat16)


def final_part(far, me, block, gain, held, acc, ss, img, place, key_ok, w_out):
    width, cols = held.shape[2:]
    rows, n_all = place.shape
    half = rows // 2
    return pl.pallas_call(
        functools.partial(final_kernel, far),
        out_shape=(
            jax.ShapeDtypeStruct((rows, cols), jnp.bfloat16),
            jax.ShapeDtypeStruct((half, width), jnp.bfloat16),
            jax.ShapeDtypeStruct((half, width), jnp.bfloat16),
        ),
        in_specs=[pl.BlockSpec(memory_space=pltpu.SMEM)]
        + vmem_specs(10),
        out_specs=tuple(vmem_specs(3)),
        scratch_shapes=[pltpu.VMEM((n_all, cols), jnp.bfloat16), pltpu.VMEM((3, rows, cols), jnp.bfloat16)],
        compiler_params=params(12),
        cost_estimate=TINY,
    )(me, *block, gain, held, acc, ss, img, place, key_ok, w_out)


def out_kernel(away, me_ref, ctx_ref, w_ref, top_ref, bottom_ref):
    half, width = top_ref.shape
    weight = cols_of(w_ref, me_ref[0] ^ away, width)
    for side, out_ref in enumerate((top_ref, bottom_ref)):
        out_ref[...] = jnp.dot(
            ctx_ref[pl.ds(side * half, half)], weight, preferred_element_type=jnp.float32
        ).astype(out_ref.dtype)


def out_part(away, me, ctx, w, width, dtype=jnp.bfloat16):
    rows, depth = ctx.shape
    return pl.pallas_call(
        functools.partial(out_kernel, away),
        out_shape=(
            jax.ShapeDtypeStruct((rows // 2, width), dtype),
            jax.ShapeDtypeStruct((rows // 2, width), dtype),
        ),
        in_specs=[pl.BlockSpec(memory_space=pltpu.SMEM)] + vmem_specs(2),
        out_specs=tuple(vmem_specs(2)),
        compiler_params=params(12),
        cost_estimate=TINY,
    )(me, ctx, w)


def sum_of(refs, part=slice(None)):
    return functools.reduce(lambda a, b: a + b, [ref[part].astype(jnp.float32) for ref in refs])


def first_kernel(n_top, base_ref, *refs):
    out_ref = refs[-1]
    half = base_ref.shape[0] // 2
    for side, terms in enumerate((refs[:n_top], refs[n_top:-1])):
        part = pl.ds(side * half, half)
        out_ref[part] = base_ref[part].astype(jnp.float32) + sum_of(terms)


def add_first(base, top, bottom):
    return pl.pallas_call(
        functools.partial(first_kernel, len(top)),
        out_shape=jax.ShapeDtypeStruct(base.shape, jnp.float32),
        in_specs=vmem_specs(1 + len(top) + len(bottom)),
        out_specs=pl.BlockSpec(memory_space=pltpu.VMEM),
        compiler_params=params(12),
        cost_estimate=TINY,
    )(base, *top, *bottom)


def last_kernel(n_top, base_ref, *refs):
    refs, (out_ref, tmp_ref, sem_ref) = refs[:-3], refs[-3:]
    half = base_ref.shape[0] // 2
    step = half // 2
    copies = []
    for side, terms in enumerate((refs[:n_top], refs[n_top:])):
        for i in range(2):
            part = pl.ds(side * half + i * step, step)
            total = base_ref[part] + sum_of(terms, pl.ds(i * step, step))
            tmp_ref[part] = total.astype(tmp_ref.dtype)
            copy = pltpu.make_async_copy(tmp_ref.at[part], out_ref.at[part], sem_ref.at[side, i])
            copy.start()
            copies.append(copy)
    for copy in copies:
        copy.wait()


def add_last(base, top, bottom):
    return pl.pallas_call(
        functools.partial(last_kernel, len(top)),
        out_shape=jax.ShapeDtypeStruct(base.shape, jnp.bfloat16),
        in_specs=vmem_specs(1 + len(top) + len(bottom)),
        out_specs=pl.BlockSpec(memory_space=pl.ANY),
        scratch_shapes=[pltpu.VMEM(base.shape, jnp.bfloat16), pltpu.SemaphoreType.DMA((2, 2))],
        compiler_params=params(12),
        cost_estimate=TINY,
    )(base, *top, *bottom)


def scatter_terms(parts, n):
    acc = {s: [[parts[s][0]], [parts[s][1]]] for s in range(n)}
    early, late = [[], []], [[], []]
    for s in by_bits(n, reverse=True):
        for side, bit in ((0, low_bit(s)), (1, high_bit(s))):
            terms = [t.astype(jnp.float32) for t in acc[s][side]]
            out = swap(functools.reduce(lambda a, b: a + b, terms).astype(jnp.bfloat16), bit)
            if s == bit:
                (early if len(terms) == 1 else late)[side].append(out)
            else:
                acc[s ^ bit][side].append(out)
    return early, late


def body(text, patches, grids, image_request, slot_start, vis_gain, dec_gain, w_qkv, w_out):
    n_req = lax.axis_size("req")
    n_ten = lax.axis_size("tensor")
    me_req = lax.axis_index("req")
    me_ten = lax.axis_index("tensor")
    img_dev, side, _, width = patches.shape
    half = side // 2
    region = half * half
    length = text.shape[0]
    w3 = jnp.transpose(w_qkv, (1, 0, 2))
    req_at = me_req.astype(jnp.int32)[None]
    ten_at = me_ten.astype(jnp.int32)[None]
    order = by_bits(n_ten)
    near_at, far = order[:-1], order[-1]

    n_rows = n_req * region
    n_img = round_up(n_rows + 1, 16)
    n_text = round_up(length - (n_rows if img_dev == n_req else 0), 32)
    *outgoing, ctext, rtext, sel, table, key_ok, gains, vis_row = prepare(
        req_at, image_request, slot_start, grids, text, jnp.transpose(patches, (1, 2, 0, 3)), dec_gain, vis_gain, n_req,
        n_text, n_img
    )
    blocks = near_blocks(ctext, n_ten)

    received = [outgoing[0]] + [swap(outgoing[s], s, "req") for s in range(1, n_req)]
    img_own = pack_images(received, vis_row, rtext, sel, region)
    img_blocks = [img_own] + [swap(img_own, s) for s in range(1, n_ten)]
    own, img_own = lax.optimization_barrier((ctext, img_own))
    acc, ss, held = own_part(ten_at, own, gains, w3)
    handed, img_blocks, acc = lax.optimization_barrier((blocks, img_blocks, acc))
    blocks = {**far_blocks(handed, n_ten), **blocks}

    near = [blocks[s] for s in near_at]
    acc, ss = near_part(near_at, ten_at, near, gains, held, acc, ss)
    table, acc = lax.optimization_barrier((table, acc))
    place, text_row = placement(table, region, length, n_text, n_img)
    img_qkv, merged, w_out = image_part(ten_at, img_blocks, gains, sel, held, w_out, n_rows)
    context, far_top, far_bottom = final_part(
        far, ten_at, blocks[far], gains, held, acc, ss, img_qkv, place, key_ok, w_out
    )
    img_here = jnp.dot(place[:, n_text:], merged, preferred_element_type=jnp.float32)
    x_in = (text.astype(jnp.float32) * text_row[:, :1] + img_here).astype(jnp.bfloat16)

    parts = {far: (far_top, far_bottom)}
    for s in reversed([0] + near_at):
        parts[s] = out_part(s, ten_at, context, w_out, width, jnp.float32 if s == 0 else jnp.bfloat16)
    early, late = scatter_terms(parts, n_ten)
    base = add_first(x_in, [parts[0][0]] + early[0], [parts[0][1]] + early[1])
    return add_last(base, late[0], late[1])


def solution(mesh):
    in_specs = (
        P("req", "tensor"),
        P("req", None, None, "tensor"),
        P(),
        P(),
        P(),
        P("tensor"),
        P(),
        P(None, None, "tensor"),
        P("tensor", None),
    )
    out_specs = P("req", "tensor")
    return jax.shard_map(body, mesh=mesh, in_specs=in_specs, out_specs=out_specs, check_vma=False)
```

profile of v0, /device:TPU:0, one launch (start us, length us, event | category | flops | bytes accessed | tf_op | source)
XLA Modules:
  0.0 73.3 jit_solution(13347554618168042614)
XLA Ops:
  0.0 2.7 %shard_map.91 = (bf16[16,1024]{1,0:T(8,128)(2,1)S(1)}, bf16[16,1024]{1,0:T(8,128)(2,1)S(1)}, bf16[16,1024]{1,0:T(8,128)(2,1)S(1)}, bf16[16,1024]{1,0:T(8,128)(2,...) custom-call(s32[1]{0:T(128)} %bitcast.me_ref, ...), custom_call_target="tpu_custom_call" | custom-call | tf_op jit(solution)/shard_map/pallas_call | solution.py:200
  2.7 3.0 %collective-permute-start.1 = (bf16[320,1024]{1,0:T(8,128)(2,1)S(1)}, bf16[320,1024]{1,0:T(8,128)(2,1)S(1)}, u32[]{:S(2)}, u32[]{:S(2)}) collective-permute-start(bf16[320,1024]{1,0:T(8,128)(2,1)S(1)} %get-tuple-element.63.x_ref), channel_id=1, source_target_pairs={{0,2},{1,3},{2,0},{3,1},{4,6},{5,7},{6,4},{7,5},{8,10},{9,11},{10,... | collective-permute-start | bytes 1966088 | tf_op jit(solution)/shard_map/ppermute | solution.py:23
  5.8 1.5 %collective-permute-start = (bf16[320,1024]{1,0:T(8,128)(2,1)S(1)}, bf16[320,1024]{1,0:T(8,128)(2,1)S(1)}, u32[]{:S(2)}, u32[]{:S(2)}) collective-permute-start(bf16[320,1024]{1,0:T(8,128)(2,1)S(1)} %get-tuple-element.63.x_ref), channel_id=1, source_target_pairs={{0,1},{1,0},{2,3},{3,2},{4,5},{5,4},{6,7},{7,6},{8,9},{9,8},{10,11... | collective-permute-start | bytes 1966088 | tf_op jit(solution)/shard_map/ppermute | solution.py:23
  7.3 0.0 collective-permute-start.2
  7.3 1.6 %collective-permute-start.3 = (bf16[16,1024]{1,0:T(8,128)(2,1)S(1)}, bf16[16,1024]{1,0:T(8,128)(2,1)S(1)}, u32[]{:S(2)}, u32[]{:S(2)}) collective-permute-start(bf16[16,1024]{1,0:T(8,128)(2,1)S(1)} %get-tuple-element.57), channel_id=1, source_target_pairs={{0,8},{4,12},{8,0},{12,4},{16,24},{20,28},{24,16},{28,20},{1,9},{5... | collective-permute-start | bytes 98312 | tf_op jit(solution)/shard_map/ppermute | solution.py:23
  8.8 0.3 collective-permute-start.4
  9.1 0.0 collective-permute-done.2.refs_1_
  9.1 2.6 %collective-permute-start.5 = (bf16[16,1024]{1,0:T(8,128)(2,1)S(1)}, bf16[16,1024]{1,0:T(8,128)(2,1)S(1)}, u32[]{:S(2)}, u32[]{:S(2)}) collective-permute-start(bf16[16,1024]{1,0:T(8,128)(2,1)S(1)} %get-tuple-element.59), channel_id=1, source_target_pairs={{0,16},{4,20},{8,24},{12,28},{16,0},{20,4},{24,8},{28,12},{1,17},{... | collective-permute-start | bytes 98312 | tf_op jit(solution)/shard_map/ppermute | solution.py:23
  11.7 0.0 collective-permute-done.3.refs_2_
  11.7 1.3 %collective-permute-start.6 = (bf16[16,1024]{1,0:T(8,128)(2,1)S(1)}, bf16[16,1024]{1,0:T(8,128)(2,1)S(1)}, u32[]{:S(2)}, u32[]{:S(2)}) collective-permute-start(bf16[16,1024]{1,0:T(8,128)(2,1)S(1)} %get-tuple-element.60), channel_id=1, source_target_pairs={{0,20},{4,16},{8,28},{12,24},{16,4},{20,0},{24,12},{28,8},{1,21},{... | collective-permute-start | bytes 98312 | tf_op jit(solution)/shard_map/ppermute | solution.py:23
  13.0 0.0 collective-permute-done.4.refs_3_
  13.0 2.2 %collective-permute-start.7 = (bf16[16,1024]{1,0:T(8,128)(2,1)S(1)}, bf16[16,1024]{1,0:T(8,128)(2,1)S(1)}, u32[]{:S(2)}, u32[]{:S(2)}) collective-permute-start(bf16[16,1024]{1,0:T(8,128)(2,1)S(1)} %get-tuple-element.61), channel_id=1, source_target_pairs={{0,24},{4,28},{8,16},{12,20},{16,8},{20,12},{24,0},{28,4},{1,25},{... | collective-permute-start | bytes 98312 | tf_op jit(solution)/shard_map/ppermute | solution.py:23
  15.3 0.0 collective-permute-done.5.refs_4_
  15.3 1.9 %collective-permute-start.8 = (bf16[16,1024]{1,0:T(8,128)(2,1)S(1)}, bf16[16,1024]{1,0:T(8,128)(2,1)S(1)}, u32[]{:S(2)}, u32[]{:S(2)}) collective-permute-start(bf16[16,1024]{1,0:T(8,128)(2,1)S(1)} %get-tuple-element.62), channel_id=1, source_target_pairs={{0,28},{4,24},{8,20},{12,16},{16,12},{20,8},{24,4},{28,0},{1,29},{... | collective-permute-start | bytes 98312 | tf_op jit(solution)/shard_map/ppermute | solution.py:23
  17.2 0.0 collective-permute-done.6.refs_5_
  17.2 1.9 %collective-permute-done.7.refs_6_ = bf16[16,1024]{1,0:T(8,128)(2,1)S(1)} collective-permute-done((bf16[16,1024]{1,0:T(8,128)(2,1)S(1)}, bf16[16,1024]{1,0:T(8,128)(2,1)S(1)}, u32[]{:S(2)}, u32[]{:S(2)}) %collective-permute-start.7) | collective-permute-done | bytes 32800 | tf_op jit(solution)/shard_map/ppermute | solution.py:23
  19.1 1.3 %collective-permute-done.8.refs_7_ = bf16[16,1024]{1,0:T(8,128)(2,1)S(1)} collective-permute-done((bf16[16,1024]{1,0:T(8,128)(2,1)S(1)}, bf16[16,1024]{1,0:T(8,128)(2,1)S(1)}, u32[]{:S(2)}, u32[]{:S(2)}) %collective-permute-start.8) | collective-permute-done | bytes 32800 | tf_op jit(solution)/shard_map/ppermute | solution.py:23
  20.4 0.2 shard_map.92.refs_0_
  20.6 0.5 collective-permute-start.11
  21.2 1.5 %collective-permute-start.10 = (bf16[80,1024]{1,0:T(8,128)(2,1)S(1)}, bf16[80,1024]{1,0:T(8,128)(2,1)S(1)}, u32[]{:S(2)}, u32[]{:S(2)}) collective-permute-start(bf16[80,1024]{1,0:T(8,128)(2,1)S(1)} %shard_map.92.refs_0_), channel_id=1, source_target_pairs={{0,2},{1,3},{2,0},{3,1},{4,6},{5,7},{6,4},{7,5},{8,10},{9,11},{10,... | collective-permute-start | bytes 491528 | tf_op jit(solution)/shard_map/ppermute | solution.py:23
  22.7 1.5 %collective-permute-start.9 = (bf16[80,1024]{1,0:T(8,128)(2,1)S(1)}, bf16[80,1024]{1,0:T(8,128)(2,1)S(1)}, u32[]{:S(2)}, u32[]{:S(2)}) collective-permute-start(bf16[80,1024]{1,0:T(8,128)(2,1)S(1)} %shard_map.92.refs_0_), channel_id=1, source_target_pairs={{0,1},{1,0},{2,3},{3,2},{4,5},{5,4},{6,7},{7,6},{8,9},{9,8},{10,11... | collective-permute-start | bytes 491528 | tf_op jit(solution)/shard_map/ppermute | solution.py:23
  24.2 4.9 %shard_map.93 = (f32[3,320,512]{2,1,0:T(8,128)S(1)}, f32[320,128]{1,0:T(8,128)S(1)}, bf16[4,3,1024,512]{3,2,1,0:T(8,128)(2,1)S(1)}) custom-call(s32[1]{0:T(128)} %bitcast.5.me_ref, bf16[320,1024]{1,0:T(8,128)(2,1)S(1)} %get-tuple-element.63.x_ref, f32[4,1,1024]{2,1,0:T(1,128)S(1)} %get-tuple-element.51.gain_ref.refs_2_.refs_4_, bf16[3,4096,512]{2,1,0:T(8,128)(2,1)} %bitcast.8), custom_call_target="tpu_custom_call" | custom-call | tf_op jit(solution)/shard_map/pallas_call | solution.py:304
  29.0 0.0 collective-permute-done.11.refs_3_
  29.1 1.7 %collective-permute-done.10.refs_2_ = bf16[80,1024]{1,0:T(8,128)(2,1)S(1)} collective-permute-done((bf16[80,1024]{1,0:T(8,128)(2,1)S(1)}, bf16[80,1024]{1,0:T(8,128)(2,1)S(1)}, u32[]{:S(2)}, u32[]{:S(2)}) %collective-permute-start.10) | collective-permute-done | bytes 163872 | tf_op jit(solution)/shard_map/ppermute | solution.py:23
  30.7 0.0 collective-permute-done.9.refs_1_
  30.7 0.0 collective-permute-done.1.refs_1_
  30.7 0.0 collective-permute-done.refs_0_
  30.8 1.4 %collective-permute-start.13 = (bf16[160,1024]{1,0:T(8,128)(2,1)S(1)}, bf16[160,1024]{1,0:T(8,128)(2,1)S(1)}, u32[]{:S(2)}, u32[]{:S(2)}) collective-permute-start(bf16[160,1024]{1,0:T(8,128)(2,1)S(1)} %slice.15), channel_id=1, source_target_pairs={{0,2},{1,3},{2,0},{3,1},{4,6},{5,7},{6,4},{7,5},{8,10},{9,11},{10,... | collective-permute-start | bytes 983048 | tf_op jit(solution)/shard_map/ppermute | solution.py:23
  32.2 0.5 collective-permute-start.12
  32.7 2.3 %shard_map.94 = (f32[3,320,512]{2,1,0:T(8,128)S(1)}, f32[320,128]{1,0:T(8,128)S(1)}) custom-call(s32[1]{0:T(128)} %bitcast.5.me_ref, bf16[320,1024]{1,0:T(8,128)(2,1)S(1)} %collective-permute-done.refs_0_, bf16[320,1024]{1,0:T(8,128)(2,1)S(1)} %collective-permute-done.1.refs_1_, f32[4,1,1024]{2,1,0:T(1,128)S(1)} %get-tuple-element.51.gain_ref.refs_2_.refs_4_, ...), custom_call_target="tpu_custom_call" | custom-call | tf_op jit(solution)/shard_map/pallas_call | solution.py:348
  35.0 0.7 shard_map.95
  35.6 2.6 %shard_map.96 = (bf16[3,80,512]{2,1,0:T(8,128)(2,1)S(1)}, bf16[80,1024]{1,0:T(8,128)(2,1)S(1)}, bf16[512,4096]{1,0:T(8,128)(2,1)S(1)}) custom-call(s32[1]{0:T(128)} %bitcast.5.me_ref, bf16[80,1024]{1,0:T(8,128)(2,1)S(1)} %shard_map.92.refs_0_, bf16[80,1024]{1,0:T(8,128)(2,1)S(1)} %collective-permute-done.9.refs_1_, ...), custom_call_target="tpu_custom_call" | custom-call | tf_op jit(solution)/shard_map/pallas_call | solution.py:394
  38.3 1.7 %collective-permute-done.13.bottom_ref = bf16[160,1024]{1,0:T(8,128)(2,1)S(1)} collective-permute-done((bf16[160,1024]{1,0:T(8,128)(2,1)S(1)}, bf16[160,1024]{1,0:T(8,128)(2,1)S(1)}, u32[]{:S(2)}, u32[]{:S(2)}) %collective-permute-start.13) | collective-permute-done | bytes 327712 | tf_op jit(solution)/shard_map/ppermute | solution.py:23
  40.0 1.5 %collective-permute-done.12.top_ref = bf16[160,1024]{1,0:T(8,128)(2,1)S(1)} collective-permute-done((bf16[160,1024]{1,0:T(8,128)(2,1)S(1)}, bf16[160,1024]{1,0:T(8,128)(2,1)S(1)}, u32[]{:S(2)}, u32[]{:S(2)}) %collective-permute-start.12) | collective-permute-done | bytes 327712 | tf_op jit(solution)/shard_map/ppermute | solution.py:23
  41.4 3.8 %shard_map.97 = (bf16[384,512]{1,0:T(8,128)(2,1)S(1)}, bf16[192,1024]{1,0:T(8,128)(2,1)S(1)}, bf16[192,1024]{1,0:T(8,128)(2,1)S(1)}) custom-call(s32[1]{0:T(128)} %bitcast.5.me_ref, bf16[160,1024]{1,0:T(8,128)(2,1)S(1)} %collective-permute-done.12.top_ref, bf16[160,1024]{1,0:T(8,128)(2,1)S(1)} %collective-permute-done.13.bottom_ref, ...), custom_call_target="tpu_custom_call" | custom-call | tf_op jit(solution)/shard_map/pallas_call | solution.py:470
  45.2 0.6 collective-permute-start.16
  45.8 1.5 %collective-permute-start.18 = (bf16[192,1024]{1,0:T(8,128)(2,1)S(1)}, bf16[192,1024]{1,0:T(8,128)(2,1)S(1)}, u32[]{:S(2)}, u32[]{:S(2)}) collective-permute-start(bf16[192,1024]{1,0:T(8,128)(2,1)S(1)} %get-tuple-element.92), channel_id=1, source_target_pairs={{0,2},{1,3},{2,0},{3,1},{4,6},{5,7},{6,4},{7,5},{8,10},{9,11},{10,... | collective-permute-start | bytes 1179656 | tf_op jit(solution)/shard_map/ppermute | solution.py:23
  47.3 0.6 shard_map.100
  47.9 0.6 shard_map.99
  48.5 0.0 copy-start
  48.6 0.6 collective-permute-start.15
  49.1 1.5 %collective-permute-start.14 = (bf16[192,1024]{1,0:T(8,128)(2,1)S(1)}, bf16[192,1024]{1,0:T(8,128)(2,1)S(1)}, u32[]{:S(2)}, u32[]{:S(2)}) collective-permute-start(bf16[192,1024]{1,0:T(8,128)(2,1)S(1)} %get-tuple-element.86), channel_id=1, source_target_pairs={{0,1},{1,0},{2,3},{3,2},{4,5},{5,4},{6,7},{7,6},{8,9},{9,8},{10,11... | collective-permute-start | bytes 1179656 | tf_op jit(solution)/shard_map/ppermute | solution.py:23
  50.6 6.7 %collective-permute-done.16 = bf16[192,1024]{1,0:T(8,128)(2,1)S(1)} collective-permute-done((bf16[192,1024]{1,0:T(8,128)(2,1)S(1)}, bf16[192,1024]{1,0:T(8,128)(2,1)S(1)}, u32[]{:S(2)}, u32[]{:S(2)}) %collective-permute-start.16) | collective-permute-done | bytes 393248 | tf_op jit(solution)/shard_map/ppermute | solution.py:23
  57.3 0.1 add_convert_fusion.2
  57.5 0.4 collective-permute-start.17
  57.9 0.0 collective-permute-done.18
  57.9 0.1 add_convert_fusion.1
  58.0 1.8 %collective-permute-start.19 = (bf16[192,1024]{1,0:T(8,128)(2,1)S(1)}, bf16[192,1024]{1,0:T(8,128)(2,1)S(1)}, u32[]{:S(2)}, u32[]{:S(2)}) collective-permute-start(bf16[192,1024]{1,0:T(8,128)(2,1)S(1)} %add_convert_fusion.1), channel_id=1, source_target_pairs={{0,1},{1,0},{2,3},{3,2},{4,5},{5,4},{6,7},{7,6},{8,9},{9,8},{10,11... | collective-permute-start | bytes 1179656 | tf_op jit(solution)/shard_map/ppermute | solution.py:23
  59.8 0.1 slice_reduce_fusion
  59.9 0.0 copy-done
  59.9 0.4 add_convert_fusion.base_ref
  60.4 0.6 shard_map.98
  61.0 5.3 %collective-permute-done.15.refs_3_ = bf16[192,1024]{1,0:T(8,128)(2,1)S(1)} collective-permute-done((bf16[192,1024]{1,0:T(8,128)(2,1)S(1)}, bf16[192,1024]{1,0:T(8,128)(2,1)S(1)}, u32[]{:S(2)}, u32[]{:S(2)}) %collective-permute-start.15) | collective-permute-done | bytes 393248 | tf_op jit(solution)/shard_map/ppermute | solution.py:23
  66.3 0.0 collective-permute-done.14.refs_1_
  66.3 0.2 shard_map.101.base_ref
  66.5 5.8 %collective-permute-done.17.refs_0_ = bf16[192,1024]{1,0:T(8,128)(2,1)S(1)} collective-permute-done((bf16[192,1024]{1,0:T(8,128)(2,1)S(1)}, bf16[192,1024]{1,0:T(8,128)(2,1)S(1)}, u32[]{:S(2)}, u32[]{:S(2)}) %collective-permute-start.17) | collective-permute-done | bytes 393248 | tf_op jit(solution)/shard_map/ppermute | solution.py:23
  72.3 0.0 collective-permute-done.19.refs_1_
  72.4 0.9 %shard_map.102 = bf16[384,1024]{1,0:T(8,128)(2,1)} custom-call(f32[384,1024]{1,0:T(8,128)S(1)} %shard_map.101.base_ref, bf16[192,1024]{1,0:T(8,128)(2,1)S(1)} %collective-permute-done.17.refs_0_, bf16[192,1024]{1,0:T(8,128)(2,1)S(1)} %collective-permute-done.19.refs_1_), custom_call_target="tpu_custom_call" | custom-call | tf_op jit(solution)/shard_map/pallas_call | solution.py:551
  (2 shorter events, 0.0 us)
Async XLA Ops:
  2.7 28.0 %collective-permute-start.1 = (bf16[320,1024]{1,0:T(8,128)(2,1)S(1)}, bf16[320,1024]{1,0:T(8,128)(2,1)S(1)}, u32[]{:S(2)}, u32[]{:S(2)}) collective-permute-start(bf16[320,1024]{1,0:T(8,128)(2,1)S(1)} %get-tuple-element.63.x_ref), channel_id=1, source_target_pairs={{0,2},{1,3},{2,0},{3,1},{4,6},{5,7},{6,4},{7,5},{8,10},{9,11},{10,... | collective-permute-start | bytes 1966088 | tf_op jit(solution)/shard_map/ppermute | solution.py:23
  5.8 25.0 %collective-permute-start = (bf16[320,1024]{1,0:T(8,128)(2,1)S(1)}, bf16[320,1024]{1,0:T(8,128)(2,1)S(1)}, u32[]{:S(2)}, u32[]{:S(2)}) collective-permute-start(bf16[320,1024]{1,0:T(8,128)(2,1)S(1)} %get-tuple-element.63.x_ref), channel_id=1, source_target_pairs={{0,1},{1,0},{2,3},{3,2},{4,5},{5,4},{6,7},{7,6},{8,9},{9,8},{10,11... | collective-permute-start | bytes 1966088 | tf_op jit(solution)/shard_map/ppermute | solution.py:23
  7.3 1.9 %collective-permute-start.2 = (bf16[16,1024]{1,0:T(8,128)(2,1)S(1)}, bf16[16,1024]{1,0:T(8,128)(2,1)S(1)}, u32[]{:S(2)}, u32[]{:S(2)}) collective-permute-start(bf16[16,1024]{1,0:T(8,128)(2,1)S(1)} %get-tuple-element.56), channel_id=1, source_target_pairs={{0,4},{4,0},{8,12},{12,8},{16,20},{20,16},{24,28},{28,24},{1,5},{5... | collective-permute-start | bytes 98312 | tf_op jit(solution)/shard_map/ppermute | solution.py:23
  7.3 4.5 %collective-permute-start.3 = (bf16[16,1024]{1,0:T(8,128)(2,1)S(1)}, bf16[16,1024]{1,0:T(8,128)(2,1)S(1)}, u32[]{:S(2)}, u32[]{:S(2)}) collective-permute-start(bf16[16,1024]{1,0:T(8,128)(2,1)S(1)} %get-tuple-element.57), channel_id=1, source_target_pairs={{0,8},{4,12},{8,0},{12,4},{16,24},{20,28},{24,16},{28,20},{1,9},{5... | collective-permute-start | bytes 98312 | tf_op jit(solution)/shard_map/ppermute | solution.py:23
  8.8 4.2 %collective-permute-start.4 = (bf16[16,1024]{1,0:T(8,128)(2,1)S(1)}, bf16[16,1024]{1,0:T(8,128)(2,1)S(1)}, u32[]{:S(2)}, u32[]{:S(2)}) collective-permute-start(bf16[16,1024]{1,0:T(8,128)(2,1)S(1)} %get-tuple-element.58), channel_id=1, source_target_pairs={{0,12},{4,8},{8,4},{12,0},{16,28},{20,24},{24,20},{28,16},{1,13},{... | collective-permute-start | bytes 98312 | tf_op jit(solution)/shard_map/ppermute | solution.py:23
  9.1 6.1 %collective-permute-start.5 = (bf16[16,1024]{1,0:T(8,128)(2,1)S(1)}, bf16[16,1024]{1,0:T(8,128)(2,1)S(1)}, u32[]{:S(2)}, u32[]{:S(2)}) collective-permute-start(bf16[16,1024]{1,0:T(8,128)(2,1)S(1)} %get-tuple-element.59), channel_id=1, source_target_pairs={{0,16},{4,20},{8,24},{12,28},{16,0},{20,4},{24,8},{28,12},{1,17},{... | collective-permute-start | bytes 98312 | tf_op jit(solution)/shard_map/ppermute | solution.py:23
  11.7 5.5 %collective-permute-start.6 = (bf16[16,1024]{1,0:T(8,128)(2,1)S(1)}, bf16[16,1024]{1,0:T(8,128)(2,1)S(1)}, u32[]{:S(2)}, u32[]{:S(2)}) collective-permute-start(bf16[16,1024]{1,0:T(8,128)(2,1)S(1)} %get-tuple-element.60), channel_id=1, source_target_pairs={{0,20},{4,16},{8,28},{12,24},{16,4},{20,0},{24,12},{28,8},{1,21},{... | collective-permute-start | bytes 98312 | tf_op jit(solution)/shard_map/ppermute | solution.py:23
  13.0 6.1 %collective-permute-start.7 = (bf16[16,1024]{1,0:T(8,128)(2,1)S(1)}, bf16[16,1024]{1,0:T(8,128)(2,1)S(1)}, u32[]{:S(2)}, u32[]{:S(2)}) collective-permute-start(bf16[16,1024]{1,0:T(8,128)(2,1)S(1)} %get-tuple-element.61), channel_id=1, source_target_pairs={{0,24},{4,28},{8,16},{12,20},{16,8},{20,12},{24,0},{28,4},{1,25},{... | collective-permute-start | bytes 98312 | tf_op jit(solution)/shard_map/ppermute | solution.py:23
  15.3 5.1 %collective-permute-start.8 = (bf16[16,1024]{1,0:T(8,128)(2,1)S(1)}, bf16[16,1024]{1,0:T(8,128)(2,1)S(1)}, u32[]{:S(2)}, u32[]{:S(2)}) collective-permute-start(bf16[16,1024]{1,0:T(8,128)(2,1)S(1)} %get-tuple-element.62), channel_id=1, source_target_pairs={{0,28},{4,24},{8,20},{12,16},{16,12},{20,8},{24,4},{28,0},{1,29},{... | collective-permute-start | bytes 98312 | tf_op jit(solution)/shard_map/ppermute | solution.py:23
  20.6 8.4 %collective-permute-start.11 = (bf16[80,1024]{1,0:T(8,128)(2,1)S(1)}, bf16[80,1024]{1,0:T(8,128)(2,1)S(1)}, u32[]{:S(2)}, u32[]{:S(2)}) collective-permute-start(bf16[80,1024]{1,0:T(8,128)(2,1)S(1)} %shard_map.92.refs_0_), channel_id=1, source_target_pairs={{0,3},{1,2},{2,1},{3,0},{4,7},{5,6},{6,5},{7,4},{8,11},{9,10},{10,... | collective-permute-start | bytes 491528 | tf_op jit(solution)/shard_map/ppermute | solution.py:23
  21.2 9.6 %collective-permute-start.10 = (bf16[80,1024]{1,0:T(8,128)(2,1)S(1)}, bf16[80,1024]{1,0:T(8,128)(2,1)S(1)}, u32[]{:S(2)}, u32[]{:S(2)}) collective-permute-start(bf16[80,1024]{1,0:T(8,128)(2,1)S(1)} %shard_map.92.refs_0_), channel_id=1, source_target_pairs={{0,2},{1,3},{2,0},{3,1},{4,6},{5,7},{6,4},{7,5},{8,10},{9,11},{10,... | collective-permute-start | bytes 491528 | tf_op jit(solution)/shard_map/ppermute | solution.py:23
  22.7 8.0 %collective-permute-start.9 = (bf16[80,1024]{1,0:T(8,128)(2,1)S(1)}, bf16[80,1024]{1,0:T(8,128)(2,1)S(1)}, u32[]{:S(2)}, u32[]{:S(2)}) collective-permute-start(bf16[80,1024]{1,0:T(8,128)(2,1)S(1)} %shard_map.92.refs_0_), channel_id=1, source_target_pairs={{0,1},{1,0},{2,3},{3,2},{4,5},{5,4},{6,7},{7,6},{8,9},{9,8},{10,11... | collective-permute-start | bytes 491528 | tf_op jit(solution)/shard_map/ppermute | solution.py:23
  30.8 9.2 %collective-permute-start.13 = (bf16[160,1024]{1,0:T(8,128)(2,1)S(1)}, bf16[160,1024]{1,0:T(8,128)(2,1)S(1)}, u32[]{:S(2)}, u32[]{:S(2)}) collective-permute-start(bf16[160,1024]{1,0:T(8,128)(2,1)S(1)} %slice.15), channel_id=1, source_target_pairs={{0,2},{1,3},{2,0},{3,1},{4,6},{5,7},{6,4},{7,5},{8,10},{9,11},{10,... | collective-permute-start | bytes 983048 | tf_op jit(solution)/shard_map/ppermute | solution.py:23
  32.2 9.3 %collective-permute-start.12 = (bf16[160,1024]{1,0:T(8,128)(2,1)S(1)}, bf16[160,1024]{1,0:T(8,128)(2,1)S(1)}, u32[]{:S(2)}, u32[]{:S(2)}) collective-permute-start(bf16[160,1024]{1,0:T(8,128)(2,1)S(1)} %slice.14), channel_id=1, source_target_pairs={{0,1},{1,0},{2,3},{3,2},{4,5},{5,4},{6,7},{7,6},{8,9},{9,8},{10,11... | collective-permute-start | bytes 983048 | tf_op jit(solution)/shard_map/ppermute | solution.py:23
  45.2 12.1 %collective-permute-start.16 = (bf16[192,1024]{1,0:T(8,128)(2,1)S(1)}, bf16[192,1024]{1,0:T(8,128)(2,1)S(1)}, u32[]{:S(2)}, u32[]{:S(2)}) collective-permute-start(bf16[192,1024]{1,0:T(8,128)(2,1)S(1)} %get-tuple-element.90), channel_id=1, source_target_pairs={{0,1},{1,0},{2,3},{3,2},{4,5},{5,4},{6,7},{7,6},{8,9},{9,8},{10,11... | collective-permute-start | bytes 1179656 | tf_op jit(solution)/shard_map/ppermute | solution.py:23
  45.8 12.1 %collective-permute-start.18 = (bf16[192,1024]{1,0:T(8,128)(2,1)S(1)}, bf16[192,1024]{1,0:T(8,128)(2,1)S(1)}, u32[]{:S(2)}, u32[]{:S(2)}) collective-permute-start(bf16[192,1024]{1,0:T(8,128)(2,1)S(1)} %get-tuple-element.92), channel_id=1, source_target_pairs={{0,2},{1,3},{2,0},{3,1},{4,6},{5,7},{6,4},{7,5},{8,10},{9,11},{10,... | collective-permute-start | bytes 1179656 | tf_op jit(solution)/shard_map/ppermute | solution.py:23
  48.5 11.4 %copy-start = (bf16[384,1024]{1,0:T(8,128)(2,1)S(1)}, bf16[384,1024]{1,0:T(8,128)(2,1)}, u32[]{:S(2)}) copy-start(bf16[384,1024]{1,0:T(8,128)(2,1)} %text_hbm.1) | copy-start | bytes 2359300
  48.6 17.7 %collective-permute-start.15 = (bf16[192,1024]{1,0:T(8,128)(2,1)S(1)}, bf16[192,1024]{1,0:T(8,128)(2,1)S(1)}, u32[]{:S(2)}, u32[]{:S(2)}) collective-permute-start(bf16[192,1024]{1,0:T(8,128)(2,1)S(1)} %get-tuple-element.88), channel_id=1, source_target_pairs={{0,2},{1,3},{2,0},{3,1},{4,6},{5,7},{6,4},{7,5},{8,10},{9,11},{10,... | collective-permute-start | bytes 1179656 | tf_op jit(solution)/shard_map/ppermute | solution.py:23
  49.1 17.2 %collective-permute-start.14 = (bf16[192,1024]{1,0:T(8,128)(2,1)S(1)}, bf16[192,1024]{1,0:T(8,128)(2,1)S(1)}, u32[]{:S(2)}, u32[]{:S(2)}) collective-permute-start(bf16[192,1024]{1,0:T(8,128)(2,1)S(1)} %get-tuple-element.86), channel_id=1, source_target_pairs={{0,1},{1,0},{2,3},{3,2},{4,5},{5,4},{6,7},{7,6},{8,9},{9,8},{10,11... | collective-permute-start | bytes 1179656 | tf_op jit(solution)/shard_map/ppermute | solution.py:23
  57.5 14.9 %collective-permute-start.17 = (bf16[192,1024]{1,0:T(8,128)(2,1)S(1)}, bf16[192,1024]{1,0:T(8,128)(2,1)S(1)}, u32[]{:S(2)}, u32[]{:S(2)}) collective-permute-start(bf16[192,1024]{1,0:T(8,128)(2,1)S(1)} %add_convert_fusion.2), channel_id=1, source_target_pairs={{0,2},{1,3},{2,0},{3,1},{4,6},{5,7},{6,4},{7,5},{8,10},{9,11},{10,... | collective-permute-start | bytes 1179656 | tf_op jit(solution)/shard_map/ppermute | solution.py:23
  58.0 14.3 %collective-permute-start.19 = (bf16[192,1024]{1,0:T(8,128)(2,1)S(1)}, bf16[192,1024]{1,0:T(8,128)(2,1)S(1)}, u32[]{:S(2)}, u32[]{:S(2)}) collective-permute-start(bf16[192,1024]{1,0:T(8,128)(2,1)S(1)} %add_convert_fusion.1), channel_id=1, source_target_pairs={{0,1},{1,0},{2,3},{3,2},{4,5},{5,4},{6,7},{7,6},{8,9},{9,8},{10,11... | collective-permute-start | bytes 1179656 | tf_op jit(solution)/shard_map/ppermute | solution.py:23
where the time goes:
time: 73.4 us; the launch traced here: 73.3 us
  starting transfers between devices  26.2 us (36%)
  waiting for transfers between devices  25.9 us (35%)
  Pallas kernels  20.1 us (27%)
    ppermute x20, starting transfers between devices, swap(): return lax.ppermute(x, axis, [(i, i ^ s) for i in range(n)])  26.2 us
    ppermute x20, waiting for transfers between devices, swap(): return lax.ppermute(x, axis, [(i, i ^ s) for i in range(n)])  25.9 us
    pallas_call x1, Pallas kernels, own_part(): pl.pallas_call(own_kernel, out_shape=(jax.ShapeDtypeStruct((3, rows, cols...  4.86 us
    pallas_call x1, Pallas kernels, final_part(): pl.pallas_call(functools.partial(final_kernel, far), out_shape=(jax.Shape...  3.77 us
    pallas_call x1, Pallas kernels, prepare(): pl.pallas_call(functools.partial(prep_kernel, n_req), out_shape=tuple((ja...  2.72 us
    pallas_call x1, Pallas kernels, image_part(): pl.pallas_call(functools.partial(image_kernel, n_rows, len(blocks)), out_...  2.64 us
    pallas_call x1, Pallas kernels, near_part(): pl.pallas_call(functools.partial(near_kernel, near, pieces), out_shape=(j...  2.27 us
    pallas_call x3, Pallas kernels, out_part(): pl.pallas_call(functools.partial(out_kernel, away), out_shape=(jax.ShapeD...  1.81 us
  transfers between devices with their start and end apart: 20, of which 8 were waited for; matrix products, arithmetic and copies ran while one was open for 1% of the time, Pallas kernels for 17%

commit v1 on v0

--- a/solution.py
+++ b/solution.py
@@ -404,7 +404,7 @@
         out_specs=tuple(vmem_specs(3)),
         scratch_shapes=[pltpu.SemaphoreType.DMA],
         compiler_params=params(12),
-        cost_estimate=TINY,
+        cost_estimate=pl.CostEstimate(flops=10**11, bytes_accessed=0, transcendentals=0),
     )(me, *blocks, gain, sel, held, in_hbm(w_out))
 
 
@@ -602,7 +602,7 @@
     img_blocks = [img_own] + [swap(img_own, s) for s in range(1, n_ten)]
     own, img_own = lax.optimization_barrier((ctext, img_own))
     acc, ss, held = own_part(ten_at, own, gains, w3)
-    handed, img_blocks, acc = lax.optimization_barrier((blocks, img_blocks, acc))
+    handed, img_own = lax.optimization_barrier((blocks, img_own))
     blocks = {**far_blocks(handed, n_ten), **blocks}
 
     near = [blocks[s] for s in near_at]

time: 73.4 us -> 70.2 us (0.956)
  waiting for transfers between devices: 25.9 us -> 23.5 us
    ppermute x20, waiting for transfers between devices: 25.9 us -> 23.5 us  [swap(): return lax.ppermute(x, axis, [(i, i ^ s) for i in range(n)])]
    ppermute x20, starting transfers between devices: 26.2 us -> 25.5 us  [swap(): return lax.ppermute(x, axis, [(i, i ^ s) for i in range(n)])]
  transfers between devices with their start and end apart: 20 -> 20, of which waited for: 8 -> 8; matrix products, arithmetic and copies ran while one was open for 1% -> 1% of each run, Pallas kernels for 17% -> 18%
where the time goes in v1:
time: 70.2 us; the launch traced here: 70 us
  starting transfers between devices  25.5 us (36%)
  waiting for transfers between devices  23.5 us (33%)
  Pallas kernels  20 us (28%)
    ppermute x20, starting transfers between devices, swap(): return lax.ppermute(x, axis, [(i, i ^ s) for i in range(n)])  25.5 us
    ppermute x20, waiting for transfers between devices, swap(): return lax.ppermute(x, axis, [(i, i ^ s) for i in range(n)])  23.5 us
    pallas_call x1, Pallas kernels, own_part(): pl.pallas_call(own_kernel, out_shape=(jax.ShapeDtypeStruct((3, rows, cols...  4.86 us
    pallas_call x1, Pallas kernels, final_part(): pl.pallas_call(functools.partial(final_kernel, far), out_shape=(jax.Shape...  3.73 us
    pallas_call x1, Pallas kernels, prepare(): pl.pallas_call(functools.partial(prep_kernel, n_req), out_shape=tuple((ja...  2.72 us
    pallas_call x1, Pallas kernels, image_part(): pl.pallas_call(functools.partial(image_kernel, n_rows, len(blocks)), out_...  2.65 us
    pallas_call x1, Pallas kernels, near_part(): pl.pallas_call(functools.partial(near_kernel, near, pieces), out_shape=(j...  2.28 us
    pallas_call x3, Pallas kernels, out_part(): pl.pallas_call(functools.partial(out_kernel, away), out_shape=(jax.ShapeD...  1.77 us
  transfers between devices with their start and end apart: 20, of which 8 were waited for; matrix products, arithmetic and copies ran while one was open for 1% of the time, Pallas kernels for 18%

profile of v1, /device:TPU:0, one launch (start us, length us, event | category | flops | bytes accessed | tf_op | source)
XLA Modules:
  0.0 70.0 jit_solution(10738522460148565147)
XLA Ops:
  0.0 2.7 %shard_map.91 = (bf16[16,1024]{1,0:T(8,128)(2,1)S(1)}, bf16[16,1024]{1,0:T(8,128)(2,1)S(1)}, bf16[16,1024]{1,0:T(8,128)(2,1)S(1)}, bf16[16,1024]{1,0:T(8,128)(2,...) custom-call(s32[1]{0:T(128)} %bitcast.me_ref, ...), custom_call_target="tpu_custom_call" | custom-call | tf_op jit(solution)/shard_map/pallas_call | solution.py:200
  2.7 3.0 %collective-permute-start.1 = (bf16[320,1024]{1,0:T(8,128)(2,1)S(1)}, bf16[320,1024]{1,0:T(8,128)(2,1)S(1)}, u32[]{:S(2)}, u32[]{:S(2)}) collective-permute-start(bf16[320,1024]{1,0:T(8,128)(2,1)S(1)} %get-tuple-element.58.x_ref), channel_id=1, source_target_pairs={{0,2},{1,3},{2,0},{3,1},{4,6},{5,7},{6,4},{7,5},{8,10},{9,11},{10,... | collective-permute-start | bytes 1966088 | tf_op jit(solution)/shard_map/ppermute | solution.py:23
  5.8 1.5 %collective-permute-start = (bf16[320,1024]{1,0:T(8,128)(2,1)S(1)}, bf16[320,1024]{1,0:T(8,128)(2,1)S(1)}, u32[]{:S(2)}, u32[]{:S(2)}) collective-permute-start(bf16[320,1024]{1,0:T(8,128)(2,1)S(1)} %get-tuple-element.58.x_ref), channel_id=1, source_target_pairs={{0,1},{1,0},{2,3},{3,2},{4,5},{5,4},{6,7},{7,6},{8,9},{9,8},{10,11... | collective-permute-start | bytes 1966088 | tf_op jit(solution)/shard_map/ppermute | solution.py:23
  7.3 0.0 collective-permute-start.2
  7.3 1.6 %collective-permute-start.3 = (bf16[16,1024]{1,0:T(8,128)(2,1)S(1)}, bf16[16,1024]{1,0:T(8,128)(2,1)S(1)}, u32[]{:S(2)}, u32[]{:S(2)}) collective-permute-start(bf16[16,1024]{1,0:T(8,128)(2,1)S(1)} %get-tuple-element.52), channel_id=1, source_target_pairs={{0,8},{4,12},{8,0},{12,4},{16,24},{20,28},{24,16},{28,20},{1,9},{5... | collective-permute-start | bytes 98312 | tf_op jit(solution)/shard_map/ppermute | solution.py:23
  8.8 0.3 collective-permute-start.4
  9.1 0.0 collective-permute-done.2.refs_1_
  9.1 2.6 %collective-permute-start.5 = (bf16[16,1024]{1,0:T(8,128)(2,1)S(1)}, bf16[16,1024]{1,0:T(8,128)(2,1)S(1)}, u32[]{:S(2)}, u32[]{:S(2)}) collective-permute-start(bf16[16,1024]{1,0:T(8,128)(2,1)S(1)} %get-tuple-element.54), channel_id=1, source_target_pairs={{0,16},{4,20},{8,24},{12,28},{16,0},{20,4},{24,8},{28,12},{1,17},{... | collective-permute-start | bytes 98312 | tf_op jit(solution)/shard_map/ppermute | solution.py:23
  11.7 0.0 collective-permute-done.3.refs_2_
  11.7 1.3 %collective-permute-start.6 = (bf16[16,1024]{1,0:T(8,128)(2,1)S(1)}, bf16[16,1024]{1,0:T(8,128)(2,1)S(1)}, u32[]{:S(2)}, u32[]{:S(2)}) collective-permute-start(bf16[16,1024]{1,0:T(8,128)(2,1)S(1)} %get-tuple-element.55), channel_id=1, source_target_pairs={{0,20},{4,16},{8,28},{12,24},{16,4},{20,0},{24,12},{28,8},{1,21},{... | collective-permute-start | bytes 98312 | tf_op jit(solution)/shard_map/ppermute | solution.py:23
  13.0 0.0 collective-permute-done.4.refs_3_
  13.0 2.2 %collective-permute-start.7 = (bf16[16,1024]{1,0:T(8,128)(2,1)S(1)}, bf16[16,1024]{1,0:T(8,128)(2,1)S(1)}, u32[]{:S(2)}, u32[]{:S(2)}) collective-permute-start(bf16[16,1024]{1,0:T(8,128)(2,1)S(1)} %get-tuple-element.56), channel_id=1, source_target_pairs={{0,24},{4,28},{8,16},{12,20},{16,8},{20,12},{24,0},{28,4},{1,25},{... | collective-permute-start | bytes 98312 | tf_op jit(solution)/shard_map/ppermute | solution.py:23
  15.3 0.0 collective-permute-done.5.refs_4_
  15.3 1.9 %collective-permute-start.8 = (bf16[16,1024]{1,0:T(8,128)(2,1)S(1)}, bf16[16,1024]{1,0:T(8,128)(2,1)S(1)}, u32[]{:S(2)}, u32[]{:S(2)}) collective-permute-start(bf16[16,1024]{1,0:T(8,128)(2,1)S(1)} %get-tuple-element.57), channel_id=1, source_target_pairs={{0,28},{4,24},{8,20},{12,16},{16,12},{20,8},{24,4},{28,0},{1,29},{... | collective-permute-start | bytes 98312 | tf_op jit(solution)/shard_map/ppermute | solution.py:23
  17.2 0.0 collective-permute-done.6.refs_5_
  17.2 1.9 %collective-permute-done.7.refs_6_ = bf16[16,1024]{1,0:T(8,128)(2,1)S(1)} collective-permute-done((bf16[16,1024]{1,0:T(8,128)(2,1)S(1)}, bf16[16,1024]{1,0:T(8,128)(2,1)S(1)}, u32[]{:S(2)}, u32[]{:S(2)}) %collective-permute-start.7) | collective-permute-done | bytes 32800 | tf_op jit(solution)/shard_map/ppermute | solution.py:23
  19.1 1.3 %collective-permute-done.8.refs_7_ = bf16[16,1024]{1,0:T(8,128)(2,1)S(1)} collective-permute-done((bf16[16,1024]{1,0:T(8,128)(2,1)S(1)}, bf16[16,1024]{1,0:T(8,128)(2,1)S(1)}, u32[]{:S(2)}, u32[]{:S(2)}) %collective-permute-start.8) | collective-permute-done | bytes 32800 | tf_op jit(solution)/shard_map/ppermute | solution.py:23
  20.4 0.2 shard_map.92.refs_0_
  20.6 0.5 collective-permute-start.11
  21.2 1.5 %collective-permute-start.10 = (bf16[80,1024]{1,0:T(8,128)(2,1)S(1)}, bf16[80,1024]{1,0:T(8,128)(2,1)S(1)}, u32[]{:S(2)}, u32[]{:S(2)}) collective-permute-start(bf16[80,1024]{1,0:T(8,128)(2,1)S(1)} %shard_map.92.refs_0_), channel_id=1, source_target_pairs={{0,2},{1,3},{2,0},{3,1},{4,6},{5,7},{6,4},{7,5},{8,10},{9,11},{10,... | collective-permute-start | bytes 491528 | tf_op jit(solution)/shard_map/ppermute | solution.py:23
  22.7 1.5 %collective-permute-start.9 = (bf16[80,1024]{1,0:T(8,128)(2,1)S(1)}, bf16[80,1024]{1,0:T(8,128)(2,1)S(1)}, u32[]{:S(2)}, u32[]{:S(2)}) collective-permute-start(bf16[80,1024]{1,0:T(8,128)(2,1)S(1)} %shard_map.92.refs_0_), channel_id=1, source_target_pairs={{0,1},{1,0},{2,3},{3,2},{4,5},{5,4},{6,7},{7,6},{8,9},{9,8},{10,11... | collective-permute-start | bytes 491528 | tf_op jit(solution)/shard_map/ppermute | solution.py:23
  24.2 4.9 %shard_map.93 = (f32[3,320,512]{2,1,0:T(8,128)S(1)}, f32[320,128]{1,0:T(8,128)S(1)}, bf16[4,3,1024,512]{3,2,1,0:T(8,128)(2,1)S(1)}) custom-call(s32[1]{0:T(128)} %bitcast.5.me_ref, bf16[320,1024]{1,0:T(8,128)(2,1)S(1)} %get-tuple-element.58.x_ref, f32[4,1,1024]{2,1,0:T(1,128)S(1)} %get-tuple-element.46.gain_ref.refs_2_.refs_4_, bf16[3,4096,512]{2,1,0:T(8,128)(2,1)} %bitcast.8), custom_call_target="tpu_custom_call" | custom-call | tf_op jit(solution)/shard_map/pallas_call | solution.py:304
  29.0 0.0 collective-permute-done.1.refs_1_
  29.1 0.0 collective-permute-done.refs_0_
  29.1 0.6 collective-permute-start.13
  29.7 0.5 collective-permute-start.12
  30.2 0.0 collective-permute-done.11.refs_3_
  30.2 0.5 collective-permute-done.10.refs_2_
  30.7 0.0 collective-permute-done.9.refs_1_
  30.7 2.7 %shard_map.96 = (bf16[3,80,512]{2,1,0:T(8,128)(2,1)S(1)}, bf16[80,1024]{1,0:T(8,128)(2,1)S(1)}, bf16[512,4096]{1,0:T(8,128)(2,1)S(1)}) custom-call(s32[1]{0:T(128)} %bitcast.5.me_ref, bf16[80,1024]{1,0:T(8,128)(2,1)S(1)} %shard_map.92.refs_0_, bf16[80,1024]{1,0:T(8,128)(2,1)S(1)} %collective-permute-done.9.refs_1_, ...), custom_call_target="tpu_custom_call" | custom-call | flops 99999997952 | tf_op jit(solution)/shard_map/pallas_call | solution.py:394
  33.4 2.3 %shard_map.94 = (f32[3,320,512]{2,1,0:T(8,128)S(1)}, f32[320,128]{1,0:T(8,128)S(1)}) custom-call(s32[1]{0:T(128)} %bitcast.5.me_ref, bf16[320,1024]{1,0:T(8,128)(2,1)S(1)} %collective-permute-done.refs_0_, bf16[320,1024]{1,0:T(8,128)(2,1)S(1)} %collective-permute-done.1.refs_1_, f32[4,1,1024]{2,1,0:T(1,128)S(1)} %get-tuple-element.46.gain_ref.refs_2_.refs_4_, ...), custom_call_target="tpu_custom_call" | custom-call | tf_op jit(solution)/shard_map/pallas_call | solution.py:348
  35.7 0.7 shard_map.95
  36.3 1.9 %collective-permute-done.13.bottom_ref = bf16[160,1024]{1,0:T(8,128)(2,1)S(1)} collective-permute-done((bf16[160,1024]{1,0:T(8,128)(2,1)S(1)}, bf16[160,1024]{1,0:T(8,128)(2,1)S(1)}, u32[]{:S(2)}, u32[]{:S(2)}) %collective-permute-start.13) | collective-permute-done | bytes 327712 | tf_op jit(solution)/shard_map/ppermute | solution.py:23
  38.2 0.2 collective-permute-done.12.top_ref
  38.4 3.7 %shard_map.97 = (bf16[384,512]{1,0:T(8,128)(2,1)S(1)}, bf16[192,1024]{1,0:T(8,128)(2,1)S(1)}, bf16[192,1024]{1,0:T(8,128)(2,1)S(1)}) custom-call(s32[1]{0:T(128)} %bitcast.5.me_ref, bf16[160,1024]{1,0:T(8,128)(2,1)S(1)} %collective-permute-done.12.top_ref, bf16[160,1024]{1,0:T(8,128)(2,1)S(1)} %collective-permute-done.13.bottom_ref, ...), custom_call_target="tpu_custom_call" | custom-call | tf_op jit(solution)/shard_map/pallas_call | solution.py:470
  42.2 0.6 collective-permute-start.16
  42.8 1.5 %collective-permute-start.18 = (bf16[192,1024]{1,0:T(8,128)(2,1)S(1)}, bf16[192,1024]{1,0:T(8,128)(2,1)S(1)}, u32[]{:S(2)}, u32[]{:S(2)}) collective-permute-start(bf16[192,1024]{1,0:T(8,128)(2,1)S(1)} %get-tuple-element.82), channel_id=1, source_target_pairs={{0,2},{1,3},{2,0},{3,1},{4,6},{5,7},{6,4},{7,5},{8,10},{9,11},{10,... | collective-permute-start | bytes 1179656 | tf_op jit(solution)/shard_map/ppermute | solution.py:23
  44.3 0.6 shard_map.100
  44.9 0.6 shard_map.99
  45.5 0.0 copy-start
  45.5 0.6 collective-permute-start.15
  46.1 1.4 %collective-permute-start.14 = (bf16[192,1024]{1,0:T(8,128)(2,1)S(1)}, bf16[192,1024]{1,0:T(8,128)(2,1)S(1)}, u32[]{:S(2)}, u32[]{:S(2)}) collective-permute-start(bf16[192,1024]{1,0:T(8,128)(2,1)S(1)} %get-tuple-element.76), channel_id=1, source_target_pairs={{0,1},{1,0},{2,3},{3,2},{4,5},{5,4},{6,7},{7,6},{8,9},{9,8},{10,11... | collective-permute-start | bytes 1179656 | tf_op jit(solution)/shard_map/ppermute | solution.py:23
  47.5 6.7 %collective-permute-done.16 = bf16[192,1024]{1,0:T(8,128)(2,1)S(1)} collective-permute-done((bf16[192,1024]{1,0:T(8,128)(2,1)S(1)}, bf16[192,1024]{1,0:T(8,128)(2,1)S(1)}, u32[]{:S(2)}, u32[]{:S(2)}) %collective-permute-start.16) | collective-permute-done | bytes 393248 | tf_op jit(solution)/shard_map/ppermute | solution.py:23
  54.3 0.1 add_convert_fusion.2
  54.4 1.6 %collective-permute-start.17 = (bf16[192,1024]{1,0:T(8,128)(2,1)S(1)}, bf16[192,1024]{1,0:T(8,128)(2,1)S(1)}, u32[]{:S(2)}, u32[]{:S(2)}) collective-permute-start(bf16[192,1024]{1,0:T(8,128)(2,1)S(1)} %add_convert_fusion.2), channel_id=1, source_target_pairs={{0,2},{1,3},{2,0},{3,1},{4,6},{5,7},{6,4},{7,5},{8,10},{9,11},{10,... | collective-permute-start | bytes 1179656 | tf_op jit(solution)/shard_map/ppermute | solution.py:23
  56.0 0.0 collective-permute-done.18
  56.0 0.1 add_convert_fusion.1
  56.1 0.6 collective-permute-start.19
  56.7 0.1 slice_reduce_fusion
  56.9 0.0 copy-done
  56.9 0.4 add_convert_fusion.base_ref
  57.3 0.6 shard_map.98
  57.9 5.4 %collective-permute-done.15.refs_3_ = bf16[192,1024]{1,0:T(8,128)(2,1)S(1)} collective-permute-done((bf16[192,1024]{1,0:T(8,128)(2,1)S(1)}, bf16[192,1024]{1,0:T(8,128)(2,1)S(1)}, u32[]{:S(2)}, u32[]{:S(2)}) %collective-permute-start.15) | collective-permute-done | bytes 393248 | tf_op jit(solution)/shard_map/ppermute | solution.py:23
  63.3 0.0 collective-permute-done.14.refs_1_
  63.3 0.2 shard_map.101.base_ref
  63.5 5.6 %collective-permute-done.17.refs_0_ = bf16[192,1024]{1,0:T(8,128)(2,1)S(1)} collective-permute-done((bf16[192,1024]{1,0:T(8,128)(2,1)S(1)}, bf16[192,1024]{1,0:T(8,128)(2,1)S(1)}, u32[]{:S(2)}, u32[]{:S(2)}) %collective-permute-start.17) | collective-permute-done | bytes 393248 | tf_op jit(solution)/shard_map/ppermute | solution.py:23
  69.1 0.0 collective-permute-done.19.refs_1_
  69.1 0.9 %shard_map.102 = bf16[384,1024]{1,0:T(8,128)(2,1)} custom-call(f32[384,1024]{1,0:T(8,128)S(1)} %shard_map.101.base_ref, bf16[192,1024]{1,0:T(8,128)(2,1)S(1)} %collective-permute-done.17.refs_0_, bf16[192,1024]{1,0:T(8,128)(2,1)S(1)} %collective-permute-done.19.refs_1_), custom_call_target="tpu_custom_call" | custom-call | tf_op jit(solution)/shard_map/pallas_call | solution.py:551
  (2 shorter events, 0.0 us)
Async XLA Ops:
  2.7 26.3 %collective-permute-start.1 = (bf16[320,1024]{1,0:T(8,128)(2,1)S(1)}, bf16[320,1024]{1,0:T(8,128)(2,1)S(1)}, u32[]{:S(2)}, u32[]{:S(2)}) collective-permute-start(bf16[320,1024]{1,0:T(8,128)(2,1)S(1)} %get-tuple-element.58.x_ref), channel_id=1, source_target_pairs={{0,2},{1,3},{2,0},{3,1},{4,6},{5,7},{6,4},{7,5},{8,10},{9,11},{10,... | collective-permute-start | bytes 1966088 | tf_op jit(solution)/shard_map/ppermute | solution.py:23
  5.8 23.3 %collective-permute-start = (bf16[320,1024]{1,0:T(8,128)(2,1)S(1)}, bf16[320,1024]{1,0:T(8,128)(2,1)S(1)}, u32[]{:S(2)}, u32[]{:S(2)}) collective-permute-start(bf16[320,1024]{1,0:T(8,128)(2,1)S(1)} %get-tuple-element.58.x_ref), channel_id=1, source_target_pairs={{0,1},{1,0},{2,3},{3,2},{4,5},{5,4},{6,7},{7,6},{8,9},{9,8},{10,11... | collective-permute-start | bytes 1966088 | tf_op jit(solution)/shard_map/ppermute | solution.py:23
  7.3 1.9 %collective-permute-start.2 = (bf16[16,1024]{1,0:T(8,128)(2,1)S(1)}, bf16[16,1024]{1,0:T(8,128)(2,1)S(1)}, u32[]{:S(2)}, u32[]{:S(2)}) collective-permute-start(bf16[16,1024]{1,0:T(8,128)(2,1)S(1)} %get-tuple-element.51), channel_id=1, source_target_pairs={{0,4},{4,0},{8,12},{12,8},{16,20},{20,16},{24,28},{28,24},{1,5},{5... | collective-permute-start | bytes 98312 | tf_op jit(solution)/shard_map/ppermute | solution.py:23
  7.3 4.5 %collective-permute-start.3 = (bf16[16,1024]{1,0:T(8,128)(2,1)S(1)}, bf16[16,1024]{1,0:T(8,128)(2,1)S(1)}, u32[]{:S(2)}, u32[]{:S(2)}) collective-permute-start(bf16[16,1024]{1,0:T(8,128)(2,1)S(1)} %get-tuple-element.52), channel_id=1, source_target_pairs={{0,8},{4,12},{8,0},{12,4},{16,24},{20,28},{24,16},{28,20},{1,9},{5... | collective-permute-start | bytes 98312 | tf_op jit(solution)/shard_map/ppermute | solution.py:23
  8.8 4.2 %collective-permute-start.4 = (bf16[16,1024]{1,0:T(8,128)(2,1)S(1)}, bf16[16,1024]{1,0:T(8,128)(2,1)S(1)}, u32[]{:S(2)}, u32[]{:S(2)}) collective-permute-start(bf16[16,1024]{1,0:T(8,128)(2,1)S(1)} %get-tuple-element.53), channel_id=1, source_target_pairs={{0,12},{4,8},{8,4},{12,0},{16,28},{20,24},{24,20},{28,16},{1,13},{... | collective-permute-start | bytes 98312 | tf_op jit(solution)/shard_map/ppermute | solution.py:23
  9.1 6.1 %collective-permute-start.5 = (bf16[16,1024]{1,0:T(8,128)(2,1)S(1)}, bf16[16,1024]{1,0:T(8,128)(2,1)S(1)}, u32[]{:S(2)}, u32[]{:S(2)}) collective-permute-start(bf16[16,1024]{1,0:T(8,128)(2,1)S(1)} %get-tuple-element.54), channel_id=1, source_target_pairs={{0,16},{4,20},{8,24},{12,28},{16,0},{20,4},{24,8},{28,12},{1,17},{... | collective-permute-start | bytes 98312 | tf_op jit(solution)/shard_map/ppermute | solution.py:23
  11.7 5.5 %collective-permute-start.6 = (bf16[16,1024]{1,0:T(8,128)(2,1)S(1)}, bf16[16,1024]{1,0:T(8,128)(2,1)S(1)}, u32[]{:S(2)}, u32[]{:S(2)}) collective-permute-start(bf16[16,1024]{1,0:T(8,128)(2,1)S(1)} %get-tuple-element.55), channel_id=1, source_target_pairs={{0,20},{4,16},{8,28},{12,24},{16,4},{20,0},{24,12},{28,8},{1,21},{... | collective-permute-start | bytes 98312 | tf_op jit(solution)/shard_map/ppermute | solution.py:23
  13.0 6.1 %collective-permute-start.7 = (bf16[16,1024]{1,0:T(8,128)(2,1)S(1)}, bf16[16,1024]{1,0:T(8,128)(2,1)S(1)}, u32[]{:S(2)}, u32[]{:S(2)}) collective-permute-start(bf16[16,1024]{1,0:T(8,128)(2,1)S(1)} %get-tuple-element.56), channel_id=1, source_target_pairs={{0,24},{4,28},{8,16},{12,20},{16,8},{20,12},{24,0},{28,4},{1,25},{... | collective-permute-start | bytes 98312 | tf_op jit(solution)/shard_map/ppermute | solution.py:23
  15.3 5.1 %collective-permute-start.8 = (bf16[16,1024]{1,0:T(8,128)(2,1)S(1)}, bf16[16,1024]{1,0:T(8,128)(2,1)S(1)}, u32[]{:S(2)}, u32[]{:S(2)}) collective-permute-start(bf16[16,1024]{1,0:T(8,128)(2,1)S(1)} %get-tuple-element.57), channel_id=1, source_target_pairs={{0,28},{4,24},{8,20},{12,16},{16,12},{20,8},{24,4},{28,0},{1,29},{... | collective-permute-start | bytes 98312 | tf_op jit(solution)/shard_map/ppermute | solution.py:23
  20.6 9.6 %collective-permute-start.11 = (bf16[80,1024]{1,0:T(8,128)(2,1)S(1)}, bf16[80,1024]{1,0:T(8,128)(2,1)S(1)}, u32[]{:S(2)}, u32[]{:S(2)}) collective-permute-start(bf16[80,1024]{1,0:T(8,128)(2,1)S(1)} %shard_map.92.refs_0_), channel_id=1, source_target_pairs={{0,3},{1,2},{2,1},{3,0},{4,7},{5,6},{6,5},{7,4},{8,11},{9,10},{10,... | collective-permute-start | bytes 491528 | tf_op jit(solution)/shard_map/ppermute | solution.py:23
  21.2 9.6 %collective-permute-start.10 = (bf16[80,1024]{1,0:T(8,128)(2,1)S(1)}, bf16[80,1024]{1,0:T(8,128)(2,1)S(1)}, u32[]{:S(2)}, u32[]{:S(2)}) collective-permute-start(bf16[80,1024]{1,0:T(8,128)(2,1)S(1)} %shard_map.92.refs_0_), channel_id=1, source_target_pairs={{0,2},{1,3},{2,0},{3,1},{4,6},{5,7},{6,4},{7,5},{8,10},{9,11},{10,... | collective-permute-start | bytes 491528 | tf_op jit(solution)/shard_map/ppermute | solution.py:23
  22.7 8.0 %collective-permute-start.9 = (bf16[80,1024]{1,0:T(8,128)(2,1)S(1)}, bf16[80,1024]{1,0:T(8,128)(2,1)S(1)}, u32[]{:S(2)}, u32[]{:S(2)}) collective-permute-start(bf16[80,1024]{1,0:T(8,128)(2,1)S(1)} %shard_map.92.refs_0_), channel_id=1, source_target_pairs={{0,1},{1,0},{2,3},{3,2},{4,5},{5,4},{6,7},{7,6},{8,9},{9,8},{10,11... | collective-permute-start | bytes 491528 | tf_op jit(solution)/shard_map/ppermute | solution.py:23
  29.1 9.1 %collective-permute-start.13 = (bf16[160,1024]{1,0:T(8,128)(2,1)S(1)}, bf16[160,1024]{1,0:T(8,128)(2,1)S(1)}, u32[]{:S(2)}, u32[]{:S(2)}) collective-permute-start(bf16[160,1024]{1,0:T(8,128)(2,1)S(1)} %slice.15), channel_id=1, source_target_pairs={{0,2},{1,3},{2,0},{3,1},{4,6},{5,7},{6,4},{7,5},{8,10},{9,11},{10,... | collective-permute-start | bytes 983048 | tf_op jit(solution)/shard_map/ppermute | solution.py:23
  29.7 8.7 %collective-permute-start.12 = (bf16[160,1024]{1,0:T(8,128)(2,1)S(1)}, bf16[160,1024]{1,0:T(8,128)(2,1)S(1)}, u32[]{:S(2)}, u32[]{:S(2)}) collective-permute-start(bf16[160,1024]{1,0:T(8,128)(2,1)S(1)} %slice.14), channel_id=1, source_target_pairs={{0,1},{1,0},{2,3},{3,2},{4,5},{5,4},{6,7},{7,6},{8,9},{9,8},{10,11... | collective-permute-start | bytes 983048 | tf_op jit(solution)/shard_map/ppermute | solution.py:23
  42.2 12.1 %collective-permute-start.16 = (bf16[192,1024]{1,0:T(8,128)(2,1)S(1)}, bf16[192,1024]{1,0:T(8,128)(2,1)S(1)}, u32[]{:S(2)}, u32[]{:S(2)}) collective-permute-start(bf16[192,1024]{1,0:T(8,128)(2,1)S(1)} %get-tuple-element.80), channel_id=1, source_target_pairs={{0,1},{1,0},{2,3},{3,2},{4,5},{5,4},{6,7},{7,6},{8,9},{9,8},{10,11... | collective-permute-start | bytes 1179656 | tf_op jit(solution)/shard_map/ppermute | solution.py:23
  42.8 13.2 %collective-permute-start.18 = (bf16[192,1024]{1,0:T(8,128)(2,1)S(1)}, bf16[192,1024]{1,0:T(8,128)(2,1)S(1)}, u32[]{:S(2)}, u32[]{:S(2)}) collective-permute-start(bf16[192,1024]{1,0:T(8,128)(2,1)S(1)} %get-tuple-element.82), channel_id=1, source_target_pairs={{0,2},{1,3},{2,0},{3,1},{4,6},{5,7},{6,4},{7,5},{8,10},{9,11},{10,... | collective-permute-start | bytes 1179656 | tf_op jit(solution)/shard_map/ppermute | solution.py:23
  45.5 11.4 %copy-start = (bf16[384,1024]{1,0:T(8,128)(2,1)S(1)}, bf16[384,1024]{1,0:T(8,128)(2,1)}, u32[]{:S(2)}) copy-start(bf16[384,1024]{1,0:T(8,128)(2,1)} %text_hbm.1) | copy-start | bytes 2359300
  45.5 17.8 %collective-permute-start.15 = (bf16[192,1024]{1,0:T(8,128)(2,1)S(1)}, bf16[192,1024]{1,0:T(8,128)(2,1)S(1)}, u32[]{:S(2)}, u32[]{:S(2)}) collective-permute-start(bf16[192,1024]{1,0:T(8,128)(2,1)S(1)} %get-tuple-element.78), channel_id=1, source_target_pairs={{0,2},{1,3},{2,0},{3,1},{4,6},{5,7},{6,4},{7,5},{8,10},{9,11},{10,... | collective-permute-start | bytes 1179656 | tf_op jit(solution)/shard_map/ppermute | solution.py:23
  46.1 17.2 %collective-permute-start.14 = (bf16[192,1024]{1,0:T(8,128)(2,1)S(1)}, bf16[192,1024]{1,0:T(8,128)(2,1)S(1)}, u32[]{:S(2)}, u32[]{:S(2)}) collective-permute-start(bf16[192,1024]{1,0:T(8,128)(2,1)S(1)} %get-tuple-element.76), channel_id=1, source_target_pairs={{0,1},{1,0},{2,3},{3,2},{4,5},{5,4},{6,7},{7,6},{8,9},{9,8},{10,11... | collective-permute-start | bytes 1179656 | tf_op jit(solution)/shard_map/ppermute | solution.py:23
  54.4 14.7 %collective-permute-start.17 = (bf16[192,1024]{1,0:T(8,128)(2,1)S(1)}, bf16[192,1024]{1,0:T(8,128)(2,1)S(1)}, u32[]{:S(2)}, u32[]{:S(2)}) collective-permute-start(bf16[192,1024]{1,0:T(8,128)(2,1)S(1)} %add_convert_fusion.2), channel_id=1, source_target_pairs={{0,2},{1,3},{2,0},{3,1},{4,6},{5,7},{6,4},{7,5},{8,10},{9,11},{10,... | collective-permute-start | bytes 1179656 | tf_op jit(solution)/shard_map/ppermute | solution.py:23
  56.1 13.0 %collective-permute-start.19 = (bf16[192,1024]{1,0:T(8,128)(2,1)S(1)}, bf16[192,1024]{1,0:T(8,128)(2,1)S(1)}, u32[]{:S(2)}, u32[]{:S(2)}) collective-permute-start(bf16[192,1024]{1,0:T(8,128)(2,1)S(1)} %add_convert_fusion.1), channel_id=1, source_target_pairs={{0,1},{1,0},{2,3},{3,2},{4,5},{5,4},{6,7},{7,6},{8,9},{9,8},{10,11... | collective-permute-start | bytes 1179656 | tf_op jit(solution)/shard_map/ppermute | solution.py:23

commit v2 on v1

--- a/solution.py
+++ b/solution.py
@@ -78,9 +78,8 @@
 
 
 def prep_kernel(n_req, me_ref, req_hbm, start_hbm, grid_hbm, text_hbm, x_hbm, dec_hbm, vis_hbm, *refs):
-    outs, refs = refs[:n_req], refs[n_req:]
-    (ctext_out, rtext_out, sel_out, table_out, key_out, dec_out, vis_out, req_ref, start_ref, grid_ref, text_ref, x_ref,
-     dec_ref, vis_ref, tmp_ref, sem_ref) = refs
+    (even_out, odd_out, ctext_out, rtext_out, sel_out, table_out, key_out, dec_out, vis_out, req_ref, start_ref, grid_ref,
+     text_ref, x_ref, dec_ref, vis_ref, tmp_ref, sem_ref) = refs
     pairs = (
         (req_hbm, req_ref),
         (start_hbm, start_ref),
@@ -165,7 +164,7 @@
             pooled = (total * 0.25).astype(jnp.bfloat16)
             tmp_ref[:, i * half + j, :] = jnp.dot(onehot, pooled, preferred_element_type=jnp.float32)
     for s in range(n_req):
-        outs[s][...] = tmp_ref[s].astype(jnp.bfloat16)
+        (even_out, odd_out)[s % 2][s // 2] = tmp_ref[s].astype(jnp.bfloat16)
     per = vis_ref.shape[0]
     for i in range(per):
         lanes = pl.ds(i * 128, 128)
@@ -188,7 +187,7 @@
         vis_gain.reshape(-1, 128),
     )
     bf16, f32 = jnp.bfloat16, jnp.float32
-    outputs = [((padded, width), bf16)] * n_req + [
+    outputs = [((n_req // 2, padded, width), bf16)] * 2 + [
         ((n_text, width), bf16),
         ((n_img, width), bf16),
         ((n_img, n_img), bf16),
@@ -210,11 +209,34 @@
     )(me, *[in_hbm(x) for x in inputs])
 
 
+def mix_kernel(even_ref, odd_ref, *outs):
+    rows = even_ref.shape[1]
+    for i, out_ref in enumerate(outs):
+        out_ref[:rows] = even_ref[i]
+        out_ref[rows:] = odd_ref[i]
+
+
+def mix_pairs(even, odd):
+    n, rows, width = even.shape
+    return pl.pallas_call(
+        mix_kernel,
+        out_shape=(jax.ShapeDtypeStruct((2 * rows, width), jnp.bfloat16),) * n,
+        in_specs=vmem_specs(2),
+        out_specs=tuple(vmem_specs(n)),
+        compiler_params=params(4),
+        cost_estimate=TINY,
+    )(even, odd)
+
+
 def pack_kernel(region, gain_ref, rtext_ref, sel_ref, *refs):
     recs, (out_ref, tmp_ref) = refs[:-2], refs[-2:]
-    for r, rec_ref in enumerate(recs):
-        tmp_ref[region * r : region * (r + 1)] = rec_ref[...].astype(jnp.float32)[:region]
-    done = region * len(recs)
+    done = 0
+    for rec_ref in recs:
+        rows = rec_ref.shape[0] // 2
+        pair = rec_ref[...].astype(jnp.float32)
+        for first in (0, rows):
+            tmp_ref[done : done + region] = pair[first : first + region]
+            done += region
     rest = tmp_ref.shape[0] - done
     tmp_ref[done:] = jnp.zeros((rest, tmp_ref.shape[1]), jnp.float32)
     picked = jnp.dot(sel_ref[...], tmp_ref[...].astype(jnp.bfloat16), preferred_element_type=jnp.float32)
@@ -591,13 +613,14 @@
     n_rows = n_req * region
     n_img = round_up(n_rows + 1, 16)
     n_text = round_up(length - (n_rows if img_dev == n_req else 0), 32)
-    *outgoing, ctext, rtext, sel, table, key_ok, gains, vis_row = prepare(
+    even, odd, ctext, rtext, sel, table, key_ok, gains, vis_row = prepare(
         req_at, image_request, slot_start, grids, text, jnp.transpose(patches, (1, 2, 0, 3)), dec_gain, vis_gain, n_req,
         n_text, n_img
     )
     blocks = near_blocks(ctext, n_ten)
 
-    received = [outgoing[0]] + [swap(outgoing[s], s, "req") for s in range(1, n_req)]
+    pairs = mix_pairs(even, swap(odd, 1, "req"))
+    received = [pairs[0]] + [swap(pairs[i], 2 * i, "req") for i in range(1, n_req // 2)]
     img_own = pack_images(received, vis_row, rtext, sel, region)
     img_blocks = [img_own] + [swap(img_own, s) for s in range(1, n_ten)]
     own, img_own = lax.optimization_barrier((ctext, img_own))

time: 70.2 us -> 68.1 us (0.970)
  starting transfers between devices: 25.5 us -> 19.5 us
  waiting for transfers between devices: 23.5 us -> 27.3 us
    ppermute x20 -> x17, starting transfers between devices: 25.5 us -> 19.5 us  [swap(): return lax.ppermute(x, axis, [(i, i ^ s) for i in range(n)])]
    ppermute x20 -> x17, waiting for transfers between devices: 23.5 us -> 27.3 us  [swap(): return lax.ppermute(x, axis, [(i, i ^ s) for i in range(n)])]
  transfers between devices with their start and end apart: 20 -> 17, of which waited for: 8 -> 9; matrix products, arithmetic and copies ran while one was open for 1% -> 1% of each run, Pallas kernels for 18% -> 19%
where the time goes in v2:
time: 68.1 us; the launch traced here: 67.9 us
  waiting for transfers between devices  27.3 us (40%)
  Pallas kernels  20.1 us (30%)
  starting transfers between devices  19.5 us (29%)
    ppermute x17, waiting for transfers between devices, swap(): return lax.ppermute(x, axis, [(i, i ^ s) for i in range(n)])  27.3 us
    ppermute x17, starting transfers between devices, swap(): return lax.ppermute(x, axis, [(i, i ^ s) for i in range(n)])  19.5 us
    pallas_call x1, Pallas kernels, own_part(): pl.pallas_call(own_kernel, out_shape=(jax.ShapeDtypeStruct((3, rows, cols...  4.86 us
    pallas_call x1, Pallas kernels, final_part(): pl.pallas_call(functools.partial(final_kernel, far), out_shape=(jax.Shape...  3.73 us
    pallas_call x1, Pallas kernels, prepare(): pl.pallas_call(functools.partial(prep_kernel, n_req), out_shape=tuple((ja...  2.72 us
    pallas_call x1, Pallas kernels, image_part(): pl.pallas_call(functools.partial(image_kernel, n_rows, len(blocks)), out_...  2.65 us
    pallas_call x1, Pallas kernels, near_part(): pl.pallas_call(functools.partial(near_kernel, near, pieces), out_shape=(j...  2.28 us
    pallas_call x3, Pallas kernels, out_part(): pl.pallas_call(functools.partial(out_kernel, away), out_shape=(jax.ShapeD...  1.77 us
  transfers between devices with their start and end apart: 17, of which 9 were waited for; matrix products, arithmetic and copies ran while one was open for 1% of the time, Pallas kernels for 19%

profile of v2, /device:TPU:0, one launch (start us, length us, event | category | flops | bytes accessed | tf_op | source)
XLA Modules:
  0.0 67.9 jit_solution(10634220326555392574)
XLA Ops:
  0.0 2.7 %shard_map.91 = (bf16[4,16,1024]{2,1,0:T(8,128)(2,1)S(1)}, bf16[4,16,1024]{2,1,0:T(8,128)(2,1)S(1)}, bf16[320,1024]{1,0:T(8,128)(2,1)S(1)}, bf16[80,1024]{1,0:T(...) custom-call(s32[1]{0:T(128)} %bitcast.me_ref, ...), custom_call_target="tpu_custom_call" | custom-call | tf_op jit(solution)/shard_map/pallas_call | solution.py:199
  2.7 3.0 %collective-permute-start.1 = (bf16[320,1024]{1,0:T(8,128)(2,1)S(1)}, bf16[320,1024]{1,0:T(8,128)(2,1)S(1)}, u32[]{:S(2)}, u32[]{:S(2)}) collective-permute-start(bf16[320,1024]{1,0:T(8,128)(2,1)S(1)} %get-tuple-element.54.x_ref), channel_id=1, source_target_pairs={{0,2},{1,3},{2,0},{3,1},{4,6},{5,7},{6,4},{7,5},{8,10},{9,11},{10,... | collective-permute-start | bytes 1966088 | tf_op jit(solution)/shard_map/ppermute | solution.py:23
  5.8 1.5 %collective-permute-start = (bf16[320,1024]{1,0:T(8,128)(2,1)S(1)}, bf16[320,1024]{1,0:T(8,128)(2,1)S(1)}, u32[]{:S(2)}, u32[]{:S(2)}) collective-permute-start(bf16[320,1024]{1,0:T(8,128)(2,1)S(1)} %get-tuple-element.54.x_ref), channel_id=1, source_target_pairs={{0,1},{1,0},{2,3},{3,2},{4,5},{5,4},{6,7},{7,6},{8,9},{9,8},{10,11... | collective-permute-start | bytes 1966088 | tf_op jit(solution)/shard_map/ppermute | solution.py:23
  7.3 0.0 collective-permute-start.2
  7.3 1.3 %collective-permute-done.2.odd_ref = bf16[4,16,1024]{2,1,0:T(8,128)(2,1)S(1)} collective-permute-done((bf16[4,16,1024]{2,1,0:T(8,128)(2,1)S(1)}, bf16[4,16,1024]{2,1,0:T(8,128)(2,1)S(1)}, u32[]{:S(2)}, u32[]{:S(2)}) %collective-permute-start.2) | collective-permute-done | bytes 131104 | tf_op jit(solution)/shard_map/ppermute | solution.py:23
  8.6 1.6 %collective-permute-start.3 = (bf16[32,1024]{1,0:T(8,128)(2,1)S(1)}, bf16[32,1024]{1,0:T(8,128)(2,1)S(1)}, u32[]{:S(2)}, u32[]{:S(2)}) collective-permute-start(bf16[32,1024]{1,0:T(8,128)(2,1)S(1)} %get-tuple-element.51), channel_id=1, source_target_pairs={{0,8},{4,12},{8,0},{12,4},{16,24},{20,28},{24,16},{28,20},{1,9},{5... | collective-permute-start | bytes 196616 | tf_op jit(solution)/shard_map/ppermute | solution.py:23
  10.3 2.6 %collective-permute-start.4 = (bf16[32,1024]{1,0:T(8,128)(2,1)S(1)}, bf16[32,1024]{1,0:T(8,128)(2,1)S(1)}, u32[]{:S(2)}, u32[]{:S(2)}) collective-permute-start(bf16[32,1024]{1,0:T(8,128)(2,1)S(1)} %get-tuple-element.52), channel_id=1, source_target_pairs={{0,16},{4,20},{8,24},{12,28},{16,0},{20,4},{24,8},{28,12},{1,17},{... | collective-permute-start | bytes 196616 | tf_op jit(solution)/shard_map/ppermute | solution.py:23
  12.9 0.2 collective-permute-start.5
  13.1 0.0 collective-permute-done.3.refs_1_
  13.1 4.7 %collective-permute-done.4.refs_2_ = bf16[32,1024]{1,0:T(8,128)(2,1)S(1)} collective-permute-done((bf16[32,1024]{1,0:T(8,128)(2,1)S(1)}, bf16[32,1024]{1,0:T(8,128)(2,1)S(1)}, u32[]{:S(2)}, u32[]{:S(2)}) %collective-permute-start.4) | collective-permute-done | bytes 65568 | tf_op jit(solution)/shard_map/ppermute | solution.py:23
  17.8 1.2 %collective-permute-done.5.refs_3_ = bf16[32,1024]{1,0:T(8,128)(2,1)S(1)} collective-permute-done((bf16[32,1024]{1,0:T(8,128)(2,1)S(1)}, bf16[32,1024]{1,0:T(8,128)(2,1)S(1)}, u32[]{:S(2)}, u32[]{:S(2)}) %collective-permute-start.5) | collective-permute-done | bytes 65568 | tf_op jit(solution)/shard_map/ppermute | solution.py:23
  19.0 0.2 shard_map.93.refs_0_
  19.2 0.5 collective-permute-start.8
  19.8 1.5 %collective-permute-start.7 = (bf16[80,1024]{1,0:T(8,128)(2,1)S(1)}, bf16[80,1024]{1,0:T(8,128)(2,1)S(1)}, u32[]{:S(2)}, u32[]{:S(2)}) collective-permute-start(bf16[80,1024]{1,0:T(8,128)(2,1)S(1)} %shard_map.93.refs_0_), channel_id=1, source_target_pairs={{0,2},{1,3},{2,0},{3,1},{4,6},{5,7},{6,4},{7,5},{8,10},{9,11},{10,... | collective-permute-start | bytes 491528 | tf_op jit(solution)/shard_map/ppermute | solution.py:23
  21.3 1.5 %collective-permute-start.6 = (bf16[80,1024]{1,0:T(8,128)(2,1)S(1)}, bf16[80,1024]{1,0:T(8,128)(2,1)S(1)}, u32[]{:S(2)}, u32[]{:S(2)}) collective-permute-start(bf16[80,1024]{1,0:T(8,128)(2,1)S(1)} %shard_map.93.refs_0_), channel_id=1, source_target_pairs={{0,1},{1,0},{2,3},{3,2},{4,5},{5,4},{6,7},{7,6},{8,9},{9,8},{10,11... | collective-permute-start | bytes 491528 | tf_op jit(solution)/shard_map/ppermute | solution.py:23
  22.8 4.9 %shard_map.94 = (f32[3,320,512]{2,1,0:T(8,128)S(1)}, f32[320,128]{1,0:T(8,128)S(1)}, bf16[4,3,1024,512]{3,2,1,0:T(8,128)(2,1)S(1)}) custom-call(s32[1]{0:T(128)} %bitcast.5.me_ref, bf16[320,1024]{1,0:T(8,128)(2,1)S(1)} %get-tuple-element.54.x_ref, f32[4,1,1024]{2,1,0:T(1,128)S(1)} %get-tuple-element.44.gain_ref.refs_2_.refs_4_, bf16[3,4096,512]{2,1,0:T(8,128)(2,1)} %bitcast.8), custom_call_target="tpu_custom_call" | custom-call | tf_op jit(solution)/shard_map/pallas_call | solution.py:326
  27.7 0.0 collective-permute-done.1.refs_1_
  27.7 0.0 collective-permute-done.refs_0_
  27.8 0.6 collective-permute-start.10
  28.3 0.5 collective-permute-start.9
  28.9 0.0 collective-permute-done.8.refs_3_
  28.9 0.0 collective-permute-done.7.refs_2_
  28.9 0.8 %collective-permute-done.6.refs_1_ = bf16[80,1024]{1,0:T(8,128)(2,1)S(1)} collective-permute-done((bf16[80,1024]{1,0:T(8,128)(2,1)S(1)}, bf16[80,1024]{1,0:T(8,128)(2,1)S(1)}, u32[]{:S(2)}, u32[]{:S(2)}) %collective-permute-start.6) | collective-permute-done | bytes 163872 | tf_op jit(solution)/shard_map/ppermute | solution.py:23
  29.6 2.7 %shard_map.97 = (bf16[3,80,512]{2,1,0:T(8,128)(2,1)S(1)}, bf16[80,1024]{1,0:T(8,128)(2,1)S(1)}, bf16[512,4096]{1,0:T(8,128)(2,1)S(1)}) custom-call(s32[1]{0:T(128)} %bitcast.5.me_ref, bf16[80,1024]{1,0:T(8,128)(2,1)S(1)} %shard_map.93.refs_0_, bf16[80,1024]{1,0:T(8,128)(2,1)S(1)} %collective-permute-done.6.refs_1_, ...), custom_call_target="tpu_custom_call" | custom-call | flops 99999997952 | tf_op jit(solution)/shard_map/pallas_call | solution.py:416
  32.3 2.3 %shard_map.95 = (f32[3,320,512]{2,1,0:T(8,128)S(1)}, f32[320,128]{1,0:T(8,128)S(1)}) custom-call(s32[1]{0:T(128)} %bitcast.5.me_ref, bf16[320,1024]{1,0:T(8,128)(2,1)S(1)} %collective-permute-done.refs_0_, bf16[320,1024]{1,0:T(8,128)(2,1)S(1)} %collective-permute-done.1.refs_1_, f32[4,1,1024]{2,1,0:T(1,128)S(1)} %get-tuple-element.44.gain_ref.refs_2_.refs_4_, ...), custom_call_target="tpu_custom_call" | custom-call | tf_op jit(solution)/shard_map/pallas_call | solution.py:370
  34.6 0.7 shard_map.96
  35.3 0.0 collective-permute-done.10.bottom_ref
  35.3 0.7 %collective-permute-done.9.top_ref = bf16[160,1024]{1,0:T(8,128)(2,1)S(1)} collective-permute-done((bf16[160,1024]{1,0:T(8,128)(2,1)S(1)}, bf16[160,1024]{1,0:T(8,128)(2,1)S(1)}, u32[]{:S(2)}, u32[]{:S(2)}) %collective-permute-start.9) | collective-permute-done | bytes 327712 | tf_op jit(solution)/shard_map/ppermute | solution.py:23
  36.0 3.7 %shard_map.98 = (bf16[384,512]{1,0:T(8,128)(2,1)S(1)}, bf16[192,1024]{1,0:T(8,128)(2,1)S(1)}, bf16[192,1024]{1,0:T(8,128)(2,1)S(1)}) custom-call(s32[1]{0:T(128)} %bitcast.5.me_ref, bf16[160,1024]{1,0:T(8,128)(2,1)S(1)} %collective-permute-done.9.top_ref, bf16[160,1024]{1,0:T(8,128)(2,1)S(1)} %collective-permute-done.10.bottom_ref, ...), custom_call_target="tpu_custom_call" | custom-call | tf_op jit(solution)/shard_map/pallas_call | solution.py:492
  39.7 1.6 %collective-permute-start.13 = (bf16[192,1024]{1,0:T(8,128)(2,1)S(1)}, bf16[192,1024]{1,0:T(8,128)(2,1)S(1)}, u32[]{:S(2)}, u32[]{:S(2)}) collective-permute-start(bf16[192,1024]{1,0:T(8,128)(2,1)S(1)} %get-tuple-element.76), channel_id=1, source_target_pairs={{0,1},{1,0},{2,3},{3,2},{4,5},{5,4},{6,7},{7,6},{8,9},{9,8},{10,11... | collective-permute-start | bytes 1179656 | tf_op jit(solution)/shard_map/ppermute | solution.py:23
  41.4 0.4 collective-permute-start.15
  41.8 0.6 shard_map.101
  42.4 0.6 shard_map.100
  43.0 0.0 copy-start
  43.0 1.7 %collective-permute-start.12 = (bf16[192,1024]{1,0:T(8,128)(2,1)S(1)}, bf16[192,1024]{1,0:T(8,128)(2,1)S(1)}, u32[]{:S(2)}, u32[]{:S(2)}) collective-permute-start(bf16[192,1024]{1,0:T(8,128)(2,1)S(1)} %get-tuple-element.74), channel_id=1, source_target_pairs={{0,2},{1,3},{2,0},{3,1},{4,6},{5,7},{6,4},{7,5},{8,10},{9,11},{10,... | collective-permute-start | bytes 1179656 | tf_op jit(solution)/shard_map/ppermute | solution.py:23
  44.7 0.5 collective-permute-start.11
  45.1 6.7 %collective-permute-done.13 = bf16[192,1024]{1,0:T(8,128)(2,1)S(1)} collective-permute-done((bf16[192,1024]{1,0:T(8,128)(2,1)S(1)}, bf16[192,1024]{1,0:T(8,128)(2,1)S(1)}, u32[]{:S(2)}, u32[]{:S(2)}) %collective-permute-start.13) | collective-permute-done | bytes 393248 | tf_op jit(solution)/shard_map/ppermute | solution.py:23
  51.9 0.1 add_convert_fusion.2
  52.0 1.0 %collective-permute-start.14 = (bf16[192,1024]{1,0:T(8,128)(2,1)S(1)}, bf16[192,1024]{1,0:T(8,128)(2,1)S(1)}, u32[]{:S(2)}, u32[]{:S(2)}) collective-permute-start(bf16[192,1024]{1,0:T(8,128)(2,1)S(1)} %add_convert_fusion.2), channel_id=1, source_target_pairs={{0,2},{1,3},{2,0},{3,1},{4,6},{5,7},{6,4},{7,5},{8,10},{9,11},{10,... | collective-permute-start | bytes 1179656 | tf_op jit(solution)/shard_map/ppermute | solution.py:23
  53.0 0.4 collective-permute-done.15
  53.4 0.1 add_convert_fusion.1
  53.6 0.7 %collective-permute-start.16 = (bf16[192,1024]{1,0:T(8,128)(2,1)S(1)}, bf16[192,1024]{1,0:T(8,128)(2,1)S(1)}, u32[]{:S(2)}, u32[]{:S(2)}) collective-permute-start(bf16[192,1024]{1,0:T(8,128)(2,1)S(1)} %add_convert_fusion.1), channel_id=1, source_target_pairs={{0,1},{1,0},{2,3},{3,2},{4,5},{5,4},{6,7},{7,6},{8,9},{9,8},{10,11... | collective-permute-start | bytes 1179656 | tf_op jit(solution)/shard_map/ppermute | solution.py:23
  54.3 0.1 slice_reduce_fusion
  54.4 0.0 copy-done
  54.4 0.4 add_convert_fusion.base_ref
  54.8 0.6 shard_map.99
  55.4 6.4 %collective-permute-done.12.refs_3_ = bf16[192,1024]{1,0:T(8,128)(2,1)S(1)} collective-permute-done((bf16[192,1024]{1,0:T(8,128)(2,1)S(1)}, bf16[192,1024]{1,0:T(8,128)(2,1)S(1)}, u32[]{:S(2)}, u32[]{:S(2)}) %collective-permute-start.12) | collective-permute-done | bytes 393248 | tf_op jit(solution)/shard_map/ppermute | solution.py:23
  61.8 0.0 collective-permute-done.11.refs_1_
  61.8 0.2 shard_map.102.base_ref
  62.1 4.9 %collective-permute-done.14.refs_0_ = bf16[192,1024]{1,0:T(8,128)(2,1)S(1)} collective-permute-done((bf16[192,1024]{1,0:T(8,128)(2,1)S(1)}, bf16[192,1024]{1,0:T(8,128)(2,1)S(1)}, u32[]{:S(2)}, u32[]{:S(2)}) %collective-permute-start.14) | collective-permute-done | bytes 393248 | tf_op jit(solution)/shard_map/ppermute | solution.py:23
  67.0 0.0 collective-permute-done.16.refs_1_
  67.0 0.9 %shard_map.103 = bf16[384,1024]{1,0:T(8,128)(2,1)} custom-call(f32[384,1024]{1,0:T(8,128)S(1)} %shard_map.102.base_ref, bf16[192,1024]{1,0:T(8,128)(2,1)S(1)} %collective-permute-done.14.refs_0_, bf16[192,1024]{1,0:T(8,128)(2,1)S(1)} %collective-permute-done.16.refs_1_), custom_call_target="tpu_custom_call" | custom-call | tf_op jit(solution)/shard_map/pallas_call | solution.py:573
  (3 shorter events, 0.1 us)
Async XLA Ops:
  2.7 24.9 %collective-permute-start.1 = (bf16[320,1024]{1,0:T(8,128)(2,1)S(1)}, bf16[320,1024]{1,0:T(8,128)(2,1)S(1)}, u32[]{:S(2)}, u32[]{:S(2)}) collective-permute-start(bf16[320,1024]{1,0:T(8,128)(2,1)S(1)} %get-tuple-element.54.x_ref), channel_id=1, source_target_pairs={{0,2},{1,3},{2,0},{3,1},{4,6},{5,7},{6,4},{7,5},{8,10},{9,11},{10,... | collective-permute-start | bytes 1966088 | tf_op jit(solution)/shard_map/ppermute | solution.py:23
  5.8 21.9 %collective-permute-start = (bf16[320,1024]{1,0:T(8,128)(2,1)S(1)}, bf16[320,1024]{1,0:T(8,128)(2,1)S(1)}, u32[]{:S(2)}, u32[]{:S(2)}) collective-permute-start(bf16[320,1024]{1,0:T(8,128)(2,1)S(1)} %get-tuple-element.54.x_ref), channel_id=1, source_target_pairs={{0,1},{1,0},{2,3},{3,2},{4,5},{5,4},{6,7},{7,6},{8,9},{9,8},{10,11... | collective-permute-start | bytes 1966088 | tf_op jit(solution)/shard_map/ppermute | solution.py:23
  7.3 1.3 %collective-permute-start.2 = (bf16[4,16,1024]{2,1,0:T(8,128)(2,1)S(1)}, bf16[4,16,1024]{2,1,0:T(8,128)(2,1)S(1)}, u32[]{:S(2)}, u32[]{:S(2)}) collective-permute-start(bf16[4,16,1024]{2,1,0:T(8,128)(2,1)S(1)} %get-tuple-element.49), channel_id=1, source_target_pairs={{0,4},{4,0},{8,12},{12,8},{16,20},{20,16},{24,28},{28,24},{1,5},{5... | collective-permute-start | bytes 393224 | tf_op jit(solution)/shard_map/ppermute | solution.py:23
  8.6 4.5 %collective-permute-start.3 = (bf16[32,1024]{1,0:T(8,128)(2,1)S(1)}, bf16[32,1024]{1,0:T(8,128)(2,1)S(1)}, u32[]{:S(2)}, u32[]{:S(2)}) collective-permute-start(bf16[32,1024]{1,0:T(8,128)(2,1)S(1)} %get-tuple-element.51), channel_id=1, source_target_pairs={{0,8},{4,12},{8,0},{12,4},{16,24},{20,28},{24,16},{28,20},{1,9},{5... | collective-permute-start | bytes 196616 | tf_op jit(solution)/shard_map/ppermute | solution.py:23
  10.3 7.5 %collective-permute-start.4 = (bf16[32,1024]{1,0:T(8,128)(2,1)S(1)}, bf16[32,1024]{1,0:T(8,128)(2,1)S(1)}, u32[]{:S(2)}, u32[]{:S(2)}) collective-permute-start(bf16[32,1024]{1,0:T(8,128)(2,1)S(1)} %get-tuple-element.52), channel_id=1, source_target_pairs={{0,16},{4,20},{8,24},{12,28},{16,0},{20,4},{24,8},{28,12},{1,17},{... | collective-permute-start | bytes 196616 | tf_op jit(solution)/shard_map/ppermute | solution.py:23
  12.9 6.2 %collective-permute-start.5 = (bf16[32,1024]{1,0:T(8,128)(2,1)S(1)}, bf16[32,1024]{1,0:T(8,128)(2,1)S(1)}, u32[]{:S(2)}, u32[]{:S(2)}) collective-permute-start(bf16[32,1024]{1,0:T(8,128)(2,1)S(1)} %get-tuple-element.53), channel_id=1, source_target_pairs={{0,24},{4,28},{8,16},{12,20},{16,8},{20,12},{24,0},{28,4},{1,25},{... | collective-permute-start | bytes 196616 | tf_op jit(solution)/shard_map/ppermute | solution.py:23
  19.2 9.6 %collective-permute-start.8 = (bf16[80,1024]{1,0:T(8,128)(2,1)S(1)}, bf16[80,1024]{1,0:T(8,128)(2,1)S(1)}, u32[]{:S(2)}, u32[]{:S(2)}) collective-permute-start(bf16[80,1024]{1,0:T(8,128)(2,1)S(1)} %shard_map.93.refs_0_), channel_id=1, source_target_pairs={{0,3},{1,2},{2,1},{3,0},{4,7},{5,6},{6,5},{7,4},{8,11},{9,10},{10,... | collective-permute-start | bytes 491528 | tf_op jit(solution)/shard_map/ppermute | solution.py:23
  19.8 9.1 %collective-permute-start.7 = (bf16[80,1024]{1,0:T(8,128)(2,1)S(1)}, bf16[80,1024]{1,0:T(8,128)(2,1)S(1)}, u32[]{:S(2)}, u32[]{:S(2)}) collective-permute-start(bf16[80,1024]{1,0:T(8,128)(2,1)S(1)} %shard_map.93.refs_0_), channel_id=1, source_target_pairs={{0,2},{1,3},{2,0},{3,1},{4,6},{5,7},{6,4},{7,5},{8,10},{9,11},{10,... | collective-permute-start | bytes 491528 | tf_op jit(solution)/shard_map/ppermute | solution.py:23
  21.3 8.3 %collective-permute-start.6 = (bf16[80,1024]{1,0:T(8,128)(2,1)S(1)}, bf16[80,1024]{1,0:T(8,128)(2,1)S(1)}, u32[]{:S(2)}, u32[]{:S(2)}) collective-permute-start(bf16[80,1024]{1,0:T(8,128)(2,1)S(1)} %shard_map.93.refs_0_), channel_id=1, source_target_pairs={{0,1},{1,0},{2,3},{3,2},{4,5},{5,4},{6,7},{7,6},{8,9},{9,8},{10,11... | collective-permute-start | bytes 491528 | tf_op jit(solution)/shard_map/ppermute | solution.py:23
  27.8 7.5 %collective-permute-start.10 = (bf16[160,1024]{1,0:T(8,128)(2,1)S(1)}, bf16[160,1024]{1,0:T(8,128)(2,1)S(1)}, u32[]{:S(2)}, u32[]{:S(2)}) collective-permute-start(bf16[160,1024]{1,0:T(8,128)(2,1)S(1)} %slice.15), channel_id=1, source_target_pairs={{0,2},{1,3},{2,0},{3,1},{4,6},{5,7},{6,4},{7,5},{8,10},{9,11},{10,... | collective-permute-start | bytes 983048 | tf_op jit(solution)/shard_map/ppermute | solution.py:23
  28.3 7.7 %collective-permute-start.9 = (bf16[160,1024]{1,0:T(8,128)(2,1)S(1)}, bf16[160,1024]{1,0:T(8,128)(2,1)S(1)}, u32[]{:S(2)}, u32[]{:S(2)}) collective-permute-start(bf16[160,1024]{1,0:T(8,128)(2,1)S(1)} %slice.14), channel_id=1, source_target_pairs={{0,1},{1,0},{2,3},{3,2},{4,5},{5,4},{6,7},{7,6},{8,9},{9,8},{10,11... | collective-permute-start | bytes 983048 | tf_op jit(solution)/shard_map/ppermute | solution.py:23
  39.7 12.1 %collective-permute-start.13 = (bf16[192,1024]{1,0:T(8,128)(2,1)S(1)}, bf16[192,1024]{1,0:T(8,128)(2,1)S(1)}, u32[]{:S(2)}, u32[]{:S(2)}) collective-permute-start(bf16[192,1024]{1,0:T(8,128)(2,1)S(1)} %get-tuple-element.76), channel_id=1, source_target_pairs={{0,1},{1,0},{2,3},{3,2},{4,5},{5,4},{6,7},{7,6},{8,9},{9,8},{10,11... | collective-permute-start | bytes 1179656 | tf_op jit(solution)/shard_map/ppermute | solution.py:23
  41.4 12.1 %collective-permute-start.15 = (bf16[192,1024]{1,0:T(8,128)(2,1)S(1)}, bf16[192,1024]{1,0:T(8,128)(2,1)S(1)}, u32[]{:S(2)}, u32[]{:S(2)}) collective-permute-start(bf16[192,1024]{1,0:T(8,128)(2,1)S(1)} %get-tuple-element.78), channel_id=1, source_target_pairs={{0,2},{1,3},{2,0},{3,1},{4,6},{5,7},{6,4},{7,5},{8,10},{9,11},{10,... | collective-permute-start | bytes 1179656 | tf_op jit(solution)/shard_map/ppermute | solution.py:23
  43.0 11.4 %copy-start = (bf16[384,1024]{1,0:T(8,128)(2,1)S(1)}, bf16[384,1024]{1,0:T(8,128)(2,1)}, u32[]{:S(2)}) copy-start(bf16[384,1024]{1,0:T(8,128)(2,1)} %text_hbm.1) | copy-start | bytes 2359300
  43.0 18.8 %collective-permute-start.12 = (bf16[192,1024]{1,0:T(8,128)(2,1)S(1)}, bf16[192,1024]{1,0:T(8,128)(2,1)S(1)}, u32[]{:S(2)}, u32[]{:S(2)}) collective-permute-start(bf16[192,1024]{1,0:T(8,128)(2,1)S(1)} %get-tuple-element.74), channel_id=1, source_target_pairs={{0,2},{1,3},{2,0},{3,1},{4,6},{5,7},{6,4},{7,5},{8,10},{9,11},{10,... | collective-permute-start | bytes 1179656 | tf_op jit(solution)/shard_map/ppermute | solution.py:23
  44.7 17.2 %collective-permute-start.11 = (bf16[192,1024]{1,0:T(8,128)(2,1)S(1)}, bf16[192,1024]{1,0:T(8,128)(2,1)S(1)}, u32[]{:S(2)}, u32[]{:S(2)}) collective-permute-start(bf16[192,1024]{1,0:T(8,128)(2,1)S(1)} %get-tuple-element.72), channel_id=1, source_target_pairs={{0,1},{1,0},{2,3},{3,2},{4,5},{5,4},{6,7},{7,6},{8,9},{9,8},{10,11... | collective-permute-start | bytes 1179656 | tf_op jit(solution)/shard_map/ppermute | solution.py:23
  52.0 15.0 %collective-permute-start.14 = (bf16[192,1024]{1,0:T(8,128)(2,1)S(1)}, bf16[192,1024]{1,0:T(8,128)(2,1)S(1)}, u32[]{:S(2)}, u32[]{:S(2)}) collective-permute-start(bf16[192,1024]{1,0:T(8,128)(2,1)S(1)} %add_convert_fusion.2), channel_id=1, source_target_pairs={{0,2},{1,3},{2,0},{3,1},{4,6},{5,7},{6,4},{7,5},{8,10},{9,11},{10,... | collective-permute-start | bytes 1179656 | tf_op jit(solution)/shard_map/ppermute | solution.py:23
  53.6 13.4 %collective-permute-start.16 = (bf16[192,1024]{1,0:T(8,128)(2,1)S(1)}, bf16[192,1024]{1,0:T(8,128)(2,1)S(1)}, u32[]{:S(2)}, u32[]{:S(2)}) collective-permute-start(bf16[192,1024]{1,0:T(8,128)(2,1)S(1)} %add_convert_fusion.1), channel_id=1, source_target_pairs={{0,1},{1,0},{2,3},{3,2},{4,5},{5,4},{6,7},{7,6},{8,9},{9,8},{10,11... | collective-permute-start | bytes 1179656 | tf_op jit(solution)/shard_map/ppermute | solution.py:23

commit v3 on v2

--- a/solution.py
+++ b/solution.py
@@ -258,29 +258,32 @@
     )(gain, rtext, sel, *received)
 
 
-def place_kernel(region, n_text, table_ref, place_ref, text_row_ref):
-    length, n_all = place_ref.shape
+def place_kernel(region, table_ref, text_at_ref, img_at_ref, text_row_ref):
+    length, n_text = text_at_ref.shape
     spot = lax.broadcasted_iota(jnp.int32, (length, 128), 0)
     before = jnp.zeros((length, 128), jnp.int32)
     at = jnp.full((length, 128), -1, jnp.int32)
     for s in range(table_ref.shape[0]):
         c = spot - table_ref[s : s + 1, :]
         before += jnp.clip(c, 0, region)
-        at = jnp.where((c >= 0) & (c < region), n_text + s * region + c, at)
+        at = jnp.where((c >= 0) & (c < region), s * region + c, at)
     text_row_ref[...] = jnp.where(at < 0, 1.0, 0.0)
-    at = jnp.where(at < 0, spot - before, at)[:, :1]
-    place_ref[...] = (lax.broadcasted_iota(jnp.int32, (length, n_all), 1) == at).astype(jnp.bfloat16)
+    rank = jnp.where(at < 0, spot - before, -1)[:, :1]
+    text_at_ref[...] = (lax.broadcasted_iota(jnp.int32, (length, n_text), 1) == rank).astype(jnp.bfloat16)
+    lane = lax.broadcasted_iota(jnp.int32, img_at_ref.shape, 1)
+    img_at_ref[...] = (lane == at[:, :1]).astype(jnp.bfloat16)
 
 
 def placement(table, region, length, n_text, n_img):
     return pl.pallas_call(
-        functools.partial(place_kernel, region, n_text),
+        functools.partial(place_kernel, region),
         out_shape=(
-            jax.ShapeDtypeStruct((length, n_text + n_img), jnp.bfloat16),
+            jax.ShapeDtypeStruct((length, n_text), jnp.bfloat16),
+            jax.ShapeDtypeStruct((length, n_img), jnp.bfloat16),
             jax.ShapeDtypeStruct((length, 128), jnp.float32),
         ),
         in_specs=vmem_specs(1),
-        out_specs=tuple(vmem_specs(2)),
+        out_specs=tuple(vmem_specs(3)),
         compiler_params=params(8),
         cost_estimate=TINY,
     )(table)
@@ -430,32 +433,21 @@
     )(me, *blocks, gain, sel, held, in_hbm(w_out))
 
 
-def final_kernel(far, me_ref, top_ref, bottom_ref, gain_ref, held_ref, acc_ref, ss_ref, img_ref, place_ref, key_ref,
-                 w_out_ref, ctx_ref, far_top_ref, far_bottom_ref, all_ref, qkv_ref):
-    half, width = top_ref.shape
-    n_text = 2 * half
-    rows, cols = ctx_ref.shape
-    owner = me_ref[0] ^ far
-    scaled, scales = [], []
-    for side, x_ref in enumerate((top_ref, bottom_ref)):
-        part = pl.ds(side * half, half)
-        x, total = scale_rows(x_ref[...], gain_ref[owner])
-        scaled.append(x)
-        total = ss_ref[part] + total
-        scales.append(lax.rsqrt(total / D + EPS)[:, :1])
+def project_side(side, far, me_ref, x_ref, gain_ref, held_ref, acc_ref, ss_ref, out_ref):
+    half = x_ref.shape[0]
+    part = pl.ds(side * half, half)
+    x, total = scale_rows(x_ref[...], gain_ref[me_ref[0] ^ far])
+    scale = lax.rsqrt((ss_ref[part] + total) / D + EPS)[:, :1]
     for j in range(3):
-        weight = held_ref[far, j]
-        for side in range(2):
-            part = pl.ds(side * half, half)
-            prod = jnp.dot(scaled[side], weight, preferred_element_type=jnp.float32)
-            all_ref[part] = ((prod + acc_ref[j, part]) * scales[side]).astype(jnp.bfloat16)
-        all_ref[n_text:] = img_ref[j]
-        qkv_ref[j] = jnp.dot(place_ref[...], all_ref[...], preferred_element_type=jnp.float32).astype(jnp.bfloat16)
-    step = 128
-    heads = [pl.ds(h * HD, HD) for h in range(cols // HD)]
-    for r in range(rows // step):
-        here, last = pl.ds(r * step, step), (r + 1) * step
-        row = lax.broadcasted_iota(jnp.int32, (step, last), 0) + r * step
+        prod = jnp.dot(x, held_ref[far, j], preferred_element_type=jnp.float32)
+        out_ref[j, part] = ((prod + acc_ref[j, part]) * scale).astype(jnp.bfloat16)
+
+
+def attend(edges, first, qkv_ref, key_ref, ctx_ref):
+    heads = [pl.ds(h * HD, HD) for h in range(ctx_ref.shape[1] // HD)]
+    for low, last in zip(edges, edges[1:]):
+        here, step = pl.ds(low, last - low), last - low
+        row = lax.broadcasted_iota(jnp.int32, (step, last), 0) + low
         col = lax.broadcasted_iota(jnp.int32, (step, last), 1)
         bias = jnp.where((row >= col) & (key_ref[0:1, pl.ds(0, last)] > 0.5), 0.0, -1e30)
         scores = [
@@ -476,115 +468,163 @@
             for x, lanes in zip(expo, heads)
         ]
         for lanes, out, total in zip(heads, outs, sums):
-            ctx_ref[here, lanes] = (out / total).astype(jnp.bfloat16)
-    weight = cols_of(w_out_ref, owner, width)
-    half = rows // 2
-    for side, out_ref in enumerate((far_top_ref, far_bottom_ref)):
-        out_ref[...] = jnp.dot(
-            ctx_ref[pl.ds(side * half, half)], weight, preferred_element_type=jnp.float32
-        ).astype(jnp.bfloat16)
-
-
-def final_part(far, me, block, gain, held, acc, ss, img, place, key_ok, w_out):
+            ctx_ref[pl.ds(low - first, step), lanes] = (out / total).astype(jnp.bfloat16)
+
+
+def put_columns(product, outs):
+    half = outs[0].shape[1]
+    for i, out_ref in enumerate(outs):
+        out_ref[...] = product[:, i * half : (i + 1) * half].astype(out_ref.dtype)
+
+
+def head_kernel(far, me_ref, top_ref, gain_ref, held_ref, acc_ref, ss_ref, img_ref, text_at_ref, img_at_ref, key_ref,
+                w_out_ref, text_qkv_ref, qkv_ref, ctx_ref, left_ref, right_ref):
+    rows = ctx_ref.shape[0]
+    width = 2 * left_ref.shape[1]
+    project_side(0, far, me_ref, top_ref, gain_ref, held_ref, acc_ref, ss_ref, text_qkv_ref)
+    for j in range(3):
+        qkv = jnp.dot(text_at_ref[:rows, :rows], text_qkv_ref[j], preferred_element_type=jnp.float32)
+        qkv += jnp.dot(img_at_ref[:rows], img_ref[j], preferred_element_type=jnp.float32)
+        qkv_ref[j] = qkv.astype(jnp.bfloat16)
+    attend([0, rows], 0, qkv_ref, key_ref, ctx_ref)
+    weight = cols_of(w_out_ref, me_ref[0] ^ far, width)
+    put_columns(jnp.dot(ctx_ref[...], weight, preferred_element_type=jnp.float32), (left_ref, right_ref))
+
+
+def head_part(far, me, top, gain, held, acc, ss, img, text_at, img_at, key_ok, w_out):
     width, cols = held.shape[2:]
-    rows, n_all = place.shape
-    half = rows // 2
-    return pl.pallas_call(
-        functools.partial(final_kernel, far),
+    rows = top.shape[0]
+    bf16 = jnp.bfloat16
+    return pl.pallas_call(
+        functools.partial(head_kernel, far),
         out_shape=(
-            jax.ShapeDtypeStruct((rows, cols), jnp.bfloat16),
-            jax.ShapeDtypeStruct((half, width), jnp.bfloat16),
-            jax.ShapeDtypeStruct((half, width), jnp.bfloat16),
+            jax.ShapeDtypeStruct((3, rows, cols), bf16),
+            jax.ShapeDtypeStruct((3, rows, cols), bf16),
+            jax.ShapeDtypeStruct((rows, cols), bf16),
+            jax.ShapeDtypeStruct((rows, width // 2), bf16),
+            jax.ShapeDtypeStruct((rows, width // 2), bf16),
         ),
-        in_specs=[pl.BlockSpec(memory_space=pltpu.SMEM)]
-        + vmem_specs(10),
+        in_specs=[pl.BlockSpec(memory_space=pltpu.SMEM)] + vmem_specs(10),
+        out_specs=tuple(vmem_specs(5)),
+        compiler_params=params(12),
+        cost_estimate=TINY,
+    )(me, top, gain, held, acc, ss, img, text_at, img_at, key_ok, w_out)
+
+
+def tail_kernel(far, me_ref, bottom_ref, gain_ref, held_ref, acc_ref, ss_ref, img_ref, text_at_ref, img_at_ref,
+                key_ref, w_out_ref, top_qkv_ref, head_qkv_ref, ctx_ref, left_ref, right_ref, text_qkv_ref, qkv_ref):
+    first = top_qkv_ref.shape[1]
+    length = text_at_ref.shape[0]
+    width = 2 * left_ref.shape[1]
+    project_side(1, far, me_ref, bottom_ref, gain_ref, held_ref, acc_ref, ss_ref, text_qkv_ref)
+    for j in range(3):
+        text_qkv_ref[j, :first] = top_qkv_ref[j]
+        qkv_ref[j, :first] = head_qkv_ref[j]
+        qkv = jnp.dot(text_at_ref[first:], text_qkv_ref[j], preferred_element_type=jnp.float32)
+        qkv += jnp.dot(img_at_ref[first:], img_ref[j], preferred_element_type=jnp.float32)
+        qkv_ref[j, first:] = qkv.astype(jnp.bfloat16)
+    edges = [first] + [at for at in range(128, length, 128) if at > first] + [length]
+    attend(edges, first, qkv_ref, key_ref, ctx_ref)
+    weight = cols_of(w_out_ref, me_ref[0] ^ far, width)
+    put_columns(jnp.dot(ctx_ref[...], weight, preferred_element_type=jnp.float32), (left_ref, right_ref))
+
+
+def tail_part(far, me, bottom, gain, held, acc, ss, img, text_at, img_at, key_ok, w_out, top_qkv, head_qkv):
+    width, cols = held.shape[2:]
+    length, n_text = text_at.shape
+    rows = length - top_qkv.shape[1]
+    bf16 = jnp.bfloat16
+    return pl.pallas_call(
+        functools.partial(tail_kernel, far),
+        out_shape=(
+            jax.ShapeDtypeStruct((rows, cols), bf16),
+            jax.ShapeDtypeStruct((rows, width // 2), bf16),
+            jax.ShapeDtypeStruct((rows, width // 2), bf16),
+        ),
+        in_specs=[pl.BlockSpec(memory_space=pltpu.SMEM)] + vmem_specs(12),
         out_specs=tuple(vmem_specs(3)),
-        scratch_shapes=[pltpu.VMEM((n_all, cols), jnp.bfloat16), pltpu.VMEM((3, rows, cols), jnp.bfloat16)],
-        compiler_params=params(12),
-        cost_estimate=TINY,
-    )(me, *block, gain, held, acc, ss, img, place, key_ok, w_out)
-
-
-def out_kernel(away, me_ref, ctx_ref, w_ref, top_ref, bottom_ref):
-    half, width = top_ref.shape
-    weight = cols_of(w_ref, me_ref[0] ^ away, width)
-    for side, out_ref in enumerate((top_ref, bottom_ref)):
-        out_ref[...] = jnp.dot(
-            ctx_ref[pl.ds(side * half, half)], weight, preferred_element_type=jnp.float32
-        ).astype(out_ref.dtype)
-
-
-def out_part(away, me, ctx, w, width, dtype=jnp.bfloat16):
-    rows, depth = ctx.shape
+        scratch_shapes=[pltpu.VMEM((3, n_text, cols), bf16), pltpu.VMEM((3, length, cols), bf16)],
+        compiler_params=params(12),
+        cost_estimate=pl.CostEstimate(flops=10**10, bytes_accessed=0, transcendentals=0),
+    )(me, bottom, gain, held, acc, ss, img, text_at, img_at, key_ok, w_out, top_qkv, head_qkv)
+
+
+def out_kernel(away, me_ref, head_ref, tail_ref, w_ref, left_ref, right_ref):
+    first = head_ref.shape[0]
+    weight = cols_of(w_ref, me_ref[0] ^ away, 2 * left_ref.shape[1])
+    for ctx_ref, rows in ((head_ref, slice(None, first)), (tail_ref, slice(first, None))):
+        product = jnp.dot(ctx_ref[...], weight, preferred_element_type=jnp.float32)
+        put_columns(product, (left_ref.at[rows], right_ref.at[rows]))
+
+
+def out_part(away, me, head, tail, w, width, dtype=jnp.bfloat16):
+    rows = head.shape[0] + tail.shape[0]
     return pl.pallas_call(
         functools.partial(out_kernel, away),
-        out_shape=(
-            jax.ShapeDtypeStruct((rows // 2, width), dtype),
-            jax.ShapeDtypeStruct((rows // 2, width), dtype),
-        ),
-        in_specs=[pl.BlockSpec(memory_space=pltpu.SMEM)] + vmem_specs(2),
+        out_shape=(jax.ShapeDtypeStruct((rows, width // 2), dtype),) * 2,
+        in_specs=[pl.BlockSpec(memory_space=pltpu.SMEM)] + vmem_specs(3),
         out_specs=tuple(vmem_specs(2)),
         compiler_params=params(12),
-        cost_estimate=TINY,
-    )(me, ctx, w)
-
-
-def sum_of(refs, part=slice(None)):
-    return functools.reduce(lambda a, b: a + b, [ref[part].astype(jnp.float32) for ref in refs])
-
-
-def first_kernel(n_top, base_ref, *refs):
+        cost_estimate=pl.CostEstimate(flops=10**9, bytes_accessed=0, transcendentals=0),
+    )(me, head, tail, w)
+
+
+def sum_of(refs):
+    return functools.reduce(lambda a, b: a + b, [ref[...].astype(jnp.float32) for ref in refs])
+
+
+def first_kernel(n_left, base_ref, *refs):
     out_ref = refs[-1]
-    half = base_ref.shape[0] // 2
-    for side, terms in enumerate((refs[:n_top], refs[n_top:-1])):
+    half = base_ref.shape[1] // 2
+    for side, terms in enumerate((refs[:n_left], refs[n_left:-1])):
         part = pl.ds(side * half, half)
-        out_ref[part] = base_ref[part].astype(jnp.float32) + sum_of(terms)
-
-
-def add_first(base, top, bottom):
-    return pl.pallas_call(
-        functools.partial(first_kernel, len(top)),
+        out_ref[:, part] = base_ref[:, part].astype(jnp.float32) + sum_of(terms)
+
+
+def add_first(base, left, right):
+    return pl.pallas_call(
+        functools.partial(first_kernel, len(left)),
         out_shape=jax.ShapeDtypeStruct(base.shape, jnp.float32),
-        in_specs=vmem_specs(1 + len(top) + len(bottom)),
+        in_specs=vmem_specs(1 + len(left) + len(right)),
         out_specs=pl.BlockSpec(memory_space=pltpu.VMEM),
         compiler_params=params(12),
         cost_estimate=TINY,
-    )(base, *top, *bottom)
-
-
-def last_kernel(n_top, base_ref, *refs):
+    )(base, *left, *right)
+
+
+def last_kernel(n_left, base_ref, *refs):
     refs, (out_ref, tmp_ref, sem_ref) = refs[:-3], refs[-3:]
-    half = base_ref.shape[0] // 2
-    step = half // 2
+    half = base_ref.shape[1] // 2
     copies = []
-    for side, terms in enumerate((refs[:n_top], refs[n_top:])):
-        for i in range(2):
-            part = pl.ds(side * half + i * step, step)
-            total = base_ref[part] + sum_of(terms, pl.ds(i * step, step))
-            tmp_ref[part] = total.astype(tmp_ref.dtype)
-            copy = pltpu.make_async_copy(tmp_ref.at[part], out_ref.at[part], sem_ref.at[side, i])
-            copy.start()
-            copies.append(copy)
+    for side, terms in enumerate((refs[:n_left], refs[n_left:])):
+        part = pl.ds(side * half, half)
+        tmp_ref[:, part] = (base_ref[:, part] + sum_of(terms)).astype(tmp_ref.dtype)
+        copy = pltpu.make_async_copy(tmp_ref.at[:, part], out_ref.at[:, part], sem_ref.at[side])
+        copy.start()
+        copies.append(copy)
     for copy in copies:
         copy.wait()
 
 
-def add_last(base, top, bottom):
-    return pl.pallas_call(
-        functools.partial(last_kernel, len(top)),
+def add_last(base, left, right):
+    return pl.pallas_call(
+        functools.partial(last_kernel, len(left)),
         out_shape=jax.ShapeDtypeStruct(base.shape, jnp.bfloat16),
-        in_specs=vmem_specs(1 + len(top) + len(bottom)),
+        in_specs=vmem_specs(1 + len(left) + len(right)),
         out_specs=pl.BlockSpec(memory_space=pl.ANY),
-        scratch_shapes=[pltpu.VMEM(base.shape, jnp.bfloat16), pltpu.SemaphoreType.DMA((2, 2))],
-        compiler_params=params(12),
-        cost_estimate=TINY,
-    )(base, *top, *bottom)
-
-
-def scatter_terms(parts, n):
-    acc = {s: [[parts[s][0]], [parts[s][1]]] for s in range(n)}
+        scratch_shapes=[pltpu.VMEM(base.shape, jnp.bfloat16), pltpu.SemaphoreType.DMA((2,))],
+        compiler_params=params(12),
+        cost_estimate=TINY,
+    )(base, *left, *right)
+
+
+def scatter_terms(parts, got, n):
+    acc = {s: [[parts[s][0]], [parts[s][1]]] for s in parts}
+    far = n - 1
+    acc[far ^ low_bit(far)][0].append(got[0])
+    acc[far ^ high_bit(far)][1].append(got[1])
     early, late = [[], []], [[], []]
-    for s in by_bits(n, reverse=True):
+    for s in by_bits(n, reverse=True)[1:]:
         for side, bit in ((0, low_bit(s)), (1, high_bit(s))):
             terms = [t.astype(jnp.float32) for t in acc[s][side]]
             out = swap(functools.reduce(lambda a, b: a + b, terms).astype(jnp.bfloat16), bit)
@@ -631,18 +671,26 @@
     near = [blocks[s] for s in near_at]
     acc, ss = near_part(near_at, ten_at, near, gains, held, acc, ss)
     table, acc = lax.optimization_barrier((table, acc))
-    place, text_row = placement(table, region, length, n_text, n_img)
+    text_at, img_at, text_row = placement(table, region, length, n_text, n_img)
+    img_blocks, text_at = lax.optimization_barrier((img_blocks, text_at))
     img_qkv, merged, w_out = image_part(ten_at, img_blocks, gains, sel, held, w_out, n_rows)
-    context, far_top, far_bottom = final_part(
-        far, ten_at, blocks[far], gains, held, acc, ss, img_qkv, place, key_ok, w_out
-    )
-    img_here = jnp.dot(place[:, n_text:], merged, preferred_element_type=jnp.float32)
+
+    shared = (gains, held, acc, ss, img_qkv, text_at, img_at, key_ok, w_out)
+    top_qkv, head_qkv, head_ctx, *head_far = head_part(far, ten_at, blocks[far][0], *shared)
+    tail_ctx, *tail_far = tail_part(far, ten_at, blocks[far][1], *shared, top_qkv, head_qkv)
+
+    img_here = jnp.dot(img_at, merged, preferred_element_type=jnp.float32)
     x_in = (text.astype(jnp.float32) * text_row[:, :1] + img_here).astype(jnp.bfloat16)
 
-    parts = {far: (far_top, far_bottom)}
+    bits = (low_bit(far), high_bit(far))
+    head_got = [swap(t, bit) for t, bit in zip(head_far, bits)]
+    tail_got = [swap(t, bit) for t, bit in zip(tail_far, bits)]
+    head_got, head_ctx, tail_ctx = lax.optimization_barrier((head_got, head_ctx, tail_ctx))
+    parts = {}
     for s in reversed([0] + near_at):
-        parts[s] = out_part(s, ten_at, context, w_out, width, jnp.float32 if s == 0 else jnp.bfloat16)
-    early, late = scatter_terms(parts, n_ten)
+        parts[s] = out_part(s, ten_at, head_ctx, tail_ctx, w_out, width, jnp.float32 if s == 0 else jnp.bfloat16)
+    got = [jnp.concatenate(pair, axis=0) for pair in zip(head_got, tail_got)]
+    early, late = scatter_terms(parts, got, n_ten)
     base = add_first(x_in, [parts[0][0]] + early[0], [parts[0][1]] + early[1])
     return add_last(base, late[0], late[1])
 

time: 68.1 us -> 68 us (level)
  waiting for transfers between devices: 27.3 us -> 24.6 us
  starting transfers between devices: 19.5 us -> 21.9 us
    ppermute x17 -> x19, waiting for transfers between devices: 27.3 us -> 24.6 us  [swap(): return lax.ppermute(x, axis, [(i, i ^ s) for i in range(n)])]
    ppermute x17 -> x19, starting transfers between devices: 19.5 us -> 21.9 us  [swap(): return lax.ppermute(x, axis, [(i, i ^ s) for i in range(n)])]
    pallas_call x4 -> x5, Pallas kernels: 5.55 us -> 5.88 us  [the longest x1 2.25 us: tail_part(): pl.pallas_call(functools.partial(tail_kernel, far), out_shape=(jax.ShapeD...]
  transfers between devices with their start and end apart: 17 -> 19, of which waited for: 9 -> 10; matrix products, arithmetic and copies ran while one was open for 1% -> 1% of each run, Pallas kernels for 19% -> 25%
where the time goes in v3:
time: 68 us; the launch traced here: 67.8 us
  waiting for transfers between devices  24.6 us (36%)
  starting transfers between devices  21.9 us (32%)
  Pallas kernels  20.4 us (30%)
    ppermute x19, waiting for transfers between devices, swap(): return lax.ppermute(x, axis, [(i, i ^ s) for i in range(n)])  24.6 us
    ppermute x19, starting transfers between devices, swap(): return lax.ppermute(x, axis, [(i, i ^ s) for i in range(n)])  21.9 us
    pallas_call x1, Pallas kernels, own_part(): pl.pallas_call(own_kernel, out_shape=(jax.ShapeDtypeStruct((3, rows, cols...  4.86 us
    pallas_call x1, Pallas kernels, prepare(): pl.pallas_call(functools.partial(prep_kernel, n_req), out_shape=tuple((ja...  2.72 us
    pallas_call x1, Pallas kernels, image_part(): pl.pallas_call(functools.partial(image_kernel, n_rows, len(blocks)), out_...  2.65 us
    pallas_call x1, Pallas kernels, near_part(): pl.pallas_call(functools.partial(near_kernel, near, pieces), out_shape=(j...  2.28 us
    pallas_call x1, Pallas kernels, tail_part(): pl.pallas_call(functools.partial(tail_kernel, far), out_shape=(jax.ShapeD...  2.25 us
    pallas_call x3, Pallas kernels, out_part(): pl.pallas_call(functools.partial(out_kernel, away), out_shape=(jax.ShapeD...  1.8 us
  transfers between devices with their start and end apart: 19, of which 10 were waited for; matrix products, arithmetic and copies ran while one was open for 1% of the time, Pallas kernels for 25%

profile of v3, /device:TPU:0, one launch (start us, length us, event | category | flops | bytes accessed | tf_op | source)
XLA Modules:
  0.0 67.8 jit_solution(3867621272750931694)
XLA Ops:
  0.0 2.7 %shard_map.91 = (bf16[4,16,1024]{2,1,0:T(8,128)(2,1)S(1)}, bf16[4,16,1024]{2,1,0:T(8,128)(2,1)S(1)}, bf16[320,1024]{1,0:T(8,128)(2,1)S(1)}, bf16[80,1024]{1,0:T(...) custom-call(s32[1]{0:T(128)} %bitcast.me_ref, ...), custom_call_target="tpu_custom_call" | custom-call | tf_op jit(solution)/shard_map/pallas_call | solution.py:199
  2.7 3.0 %collective-permute-start = (bf16[320,1024]{1,0:T(8,128)(2,1)S(1)}, bf16[320,1024]{1,0:T(8,128)(2,1)S(1)}, u32[]{:S(2)}, u32[]{:S(2)}) collective-permute-start(bf16[320,1024]{1,0:T(8,128)(2,1)S(1)} %get-tuple-element.69.x_ref), channel_id=1, source_target_pairs={{0,1},{1,0},{2,3},{3,2},{4,5},{5,4},{6,7},{7,6},{8,9},{9,8},{10,11... | collective-permute-start | bytes 1966088 | tf_op jit(solution)/shard_map/ppermute | solution.py:23
  5.7 1.5 %collective-permute-start.1 = (bf16[320,1024]{1,0:T(8,128)(2,1)S(1)}, bf16[320,1024]{1,0:T(8,128)(2,1)S(1)}, u32[]{:S(2)}, u32[]{:S(2)}) collective-permute-start(bf16[320,1024]{1,0:T(8,128)(2,1)S(1)} %get-tuple-element.69.x_ref), channel_id=1, source_target_pairs={{0,2},{1,3},{2,0},{3,1},{4,6},{5,7},{6,4},{7,5},{8,10},{9,11},{10,... | collective-permute-start | bytes 1966088 | tf_op jit(solution)/shard_map/ppermute | solution.py:23
  7.3 0.0 collective-permute-start.2
  7.3 1.3 %collective-permute-done.2.odd_ref = bf16[4,16,1024]{2,1,0:T(8,128)(2,1)S(1)} collective-permute-done((bf16[4,16,1024]{2,1,0:T(8,128)(2,1)S(1)}, bf16[4,16,1024]{2,1,0:T(8,128)(2,1)S(1)}, u32[]{:S(2)}, u32[]{:S(2)}) %collective-permute-start.2) | collective-permute-done | bytes 131104 | tf_op jit(solution)/shard_map/ppermute | solution.py:23
  8.6 1.6 %collective-permute-start.3 = (bf16[32,1024]{1,0:T(8,128)(2,1)S(1)}, bf16[32,1024]{1,0:T(8,128)(2,1)S(1)}, u32[]{:S(2)}, u32[]{:S(2)}) collective-permute-start(bf16[32,1024]{1,0:T(8,128)(2,1)S(1)} %get-tuple-element.66), channel_id=1, source_target_pairs={{0,8},{4,12},{8,0},{12,4},{16,24},{20,28},{24,16},{28,20},{1,9},{5... | collective-permute-start | bytes 196616 | tf_op jit(solution)/shard_map/ppermute | solution.py:23
  10.3 2.6 %collective-permute-start.4 = (bf16[32,1024]{1,0:T(8,128)(2,1)S(1)}, bf16[32,1024]{1,0:T(8,128)(2,1)S(1)}, u32[]{:S(2)}, u32[]{:S(2)}) collective-permute-start(bf16[32,1024]{1,0:T(8,128)(2,1)S(1)} %get-tuple-element.67), channel_id=1, source_target_pairs={{0,16},{4,20},{8,24},{12,28},{16,0},{20,4},{24,8},{28,12},{1,17},{... | collective-permute-start | bytes 196616 | tf_op jit(solution)/shard_map/ppermute | solution.py:23
  12.9 0.2 collective-permute-start.5
  13.1 0.0 collective-permute-done.3.refs_1_
  13.1 4.7 %collective-permute-done.4.refs_2_ = bf16[32,1024]{1,0:T(8,128)(2,1)S(1)} collective-permute-done((bf16[32,1024]{1,0:T(8,128)(2,1)S(1)}, bf16[32,1024]{1,0:T(8,128)(2,1)S(1)}, u32[]{:S(2)}, u32[]{:S(2)}) %collective-permute-start.4) | collective-permute-done | bytes 65568 | tf_op jit(solution)/shard_map/ppermute | solution.py:23
  17.8 1.2 %collective-permute-done.5.refs_3_ = bf16[32,1024]{1,0:T(8,128)(2,1)S(1)} collective-permute-done((bf16[32,1024]{1,0:T(8,128)(2,1)S(1)}, bf16[32,1024]{1,0:T(8,128)(2,1)S(1)}, u32[]{:S(2)}, u32[]{:S(2)}) %collective-permute-start.5) | collective-permute-done | bytes 65568 | tf_op jit(solution)/shard_map/ppermute | solution.py:23
  19.0 0.2 shard_map.93.refs_0_
  19.2 0.6 collective-permute-start.6
  19.8 0.5 collective-permute-start.7
  20.4 2.4 %collective-permute-start.8 = (bf16[80,1024]{1,0:T(8,128)(2,1)S(1)}, bf16[80,1024]{1,0:T(8,128)(2,1)S(1)}, u32[]{:S(2)}, u32[]{:S(2)}) collective-permute-start(bf16[80,1024]{1,0:T(8,128)(2,1)S(1)} %shard_map.93.refs_0_), channel_id=1, source_target_pairs={{0,3},{1,2},{2,1},{3,0},{4,7},{5,6},{6,5},{7,4},{8,11},{9,10},{10,... | collective-permute-start | bytes 491528 | tf_op jit(solution)/shard_map/ppermute | solution.py:23
  22.8 4.9 %shard_map.94 = (f32[3,320,512]{2,1,0:T(8,128)S(1)}, f32[320,128]{1,0:T(8,128)S(1)}, bf16[4,3,1024,512]{3,2,1,0:T(8,128)(2,1)S(1)}) custom-call(s32[1]{0:T(128)} %bitcast.5.me_ref, bf16[320,1024]{1,0:T(8,128)(2,1)S(1)} %get-tuple-element.69.x_ref, f32[4,1,1024]{2,1,0:T(1,128)S(1)} %get-tuple-element.59.gain_ref.refs_2_.refs_4_, bf16[3,4096,512]{2,1,0:T(8,128)(2,1)} %bitcast.9), custom_call_target="tpu_custom_call" | custom-call | tf_op jit(solution)/shard_map/pallas_call | solution.py:329
  27.7 0.0 collective-permute-done.refs_0_
  27.7 0.0 collective-permute-done.1.refs_1_
  27.7 2.3 %shard_map.95 = (f32[3,320,512]{2,1,0:T(8,128)S(1)}, f32[320,128]{1,0:T(8,128)S(1)}) custom-call(s32[1]{0:T(128)} %bitcast.5.me_ref, bf16[320,1024]{1,0:T(8,128)(2,1)S(1)} %collective-permute-done.refs_0_, bf16[320,1024]{1,0:T(8,128)(2,1)S(1)} %collective-permute-done.1.refs_1_, f32[4,1,1024]{2,1,0:T(1,128)S(1)} %get-tuple-element.59.gain_ref.refs_2_.refs_4_, ...), custom_call_target="tpu_custom_call" | custom-call | tf_op jit(solution)/shard_map/pallas_call | solution.py:373
  30.0 0.7 %shard_map.96 = (bf16[384,320]{1,0:T(8,128)(2,1)S(1)}, bf16[384,80]{1,0:T(8,128)(2,1)S(1)}, f32[384,128]{1,0:T(8,128)S(1)}) custom-call(s32[8,128]{1,0:T(8,128)S(1)} %get-tuple-element.74.table_ref), custom_call_target="tpu_custom_call" | custom-call | tf_op jit(solution)/shard_map/pallas_call | solution.py:278
  30.7 0.0 collective-permute-done.6.refs_1_
  30.7 0.0 collective-permute-done.7.refs_2_
  30.7 0.0 collective-permute-done.8.refs_3_
  30.8 0.6 collective-permute-start.9
  31.4 0.6 collective-permute-start.12
  32.0 2.7 %shard_map.97 = (bf16[3,80,512]{2,1,0:T(8,128)(2,1)S(1)}, bf16[80,1024]{1,0:T(8,128)(2,1)S(1)}, bf16[512,4096]{1,0:T(8,128)(2,1)S(1)}) custom-call(s32[1]{0:T(128)} %bitcast.5.me_ref, bf16[80,1024]{1,0:T(8,128)(2,1)S(1)} %shard_map.93.refs_0_, bf16[80,1024]{1,0:T(8,128)(2,1)S(1)} %collective-permute-done.6.refs_1_, ...), custom_call_target="tpu_custom_call" | custom-call | flops 99999997952 | tf_op jit(solution)/shard_map/pallas_call | solution.py:419
  34.6 3.4 %collective-permute-done.9.top_ref = bf16[160,1024]{1,0:T(8,128)(2,1)S(1)} collective-permute-done((bf16[160,1024]{1,0:T(8,128)(2,1)S(1)}, bf16[160,1024]{1,0:T(8,128)(2,1)S(1)}, u32[]{:S(2)}, u32[]{:S(2)}) %collective-permute-start.9) | collective-permute-done | bytes 327712 | tf_op jit(solution)/shard_map/ppermute | solution.py:23
  38.0 1.7 %shard_map.98 = (bf16[3,160,512]{2,1,0:T(8,128)(2,1)S(1)}, bf16[3,160,512]{2,1,0:T(8,128)(2,1)S(1)}, bf16[160,512]{1,0:T(8,128)(2,1)S(1)}, bf16[160,512]{1,0:T(8,128)(2,1)S(1)}, bf16[160,512]{1,0:T(8,128)(2,1)S(1)}) custom-call(s32[1]{0:T(128)} %bitcast.5.me_ref, bf16[160,1024]{1,0:T(8,128)(2,1)S(1)} %collective-permute-done.9.top_ref, ...), custom_call_target="tpu_custom_call" | custom-call | tf_op jit(solution)/shard_map/pallas_call | solution.py:498
  39.7 0.9 %collective-permute-start.10 = (bf16[160,512]{1,0:T(8,128)(2,1)S(1)}, bf16[160,512]{1,0:T(8,128)(2,1)S(1)}, u32[]{:S(2)}, u32[]{:S(2)}) collective-permute-start(bf16[160,512]{1,0:T(8,128)(2,1)S(1)} %get-tuple-element.90), channel_id=1, source_target_pairs={{0,1},{1,0},{2,3},{3,2},{4,5},{5,4},{6,7},{7,6},{8,9},{9,8},{10,11... | collective-permute-start | bytes 491528 | tf_op jit(solution)/shard_map/ppermute | solution.py:23
  40.6 0.4 collective-permute-start.11
  41.0 0.0 collective-permute-done.12.bottom_ref
  41.1 2.3 %shard_map.99 = (bf16[224,512]{1,0:T(8,128)(2,1)S(1)}, bf16[224,512]{1,0:T(8,128)(2,1)S(1)}, bf16[224,512]{1,0:T(8,128)(2,1)S(1)}) custom-call(s32[1]{0:T(128)} %bitcast.5.me_ref, bf16[160,1024]{1,0:T(8,128)(2,1)S(1)} %collective-permute-done.12.bottom_ref, f32[4,1,1024]{2,1,0:T(1,128)S(1)} %get-tuple-element.59.gain_ref.refs_2_.refs_4_, ...), custom_call_target="tpu_custom_call" | custom-call | flops 10000000000 | tf_op jit(solution)/shard_map/pallas_call | solution.py:537
  43.3 1.7 %collective-permute-start.17 = (bf16[224,512]{1,0:T(8,128)(2,1)S(1)}, bf16[224,512]{1,0:T(8,128)(2,1)S(1)}, u32[]{:S(2)}, u32[]{:S(2)}) collective-permute-start(bf16[224,512]{1,0:T(8,128)(2,1)S(1)} %get-tuple-element.108), channel_id=1, source_target_pairs={{0,2},{1,3},{2,0},{3,1},{4,6},{5,7},{6,4},{7,5},{8,10},{9,11},{10,... | collective-permute-start | bytes 688136 | tf_op jit(solution)/shard_map/ppermute | solution.py:23
  45.0 1.2 %collective-permute-start.15 = (bf16[224,512]{1,0:T(8,128)(2,1)S(1)}, bf16[224,512]{1,0:T(8,128)(2,1)S(1)}, u32[]{:S(2)}, u32[]{:S(2)}) collective-permute-start(bf16[224,512]{1,0:T(8,128)(2,1)S(1)} %get-tuple-element.105), channel_id=1, source_target_pairs={{0,1},{1,0},{2,3},{3,2},{4,5},{5,4},{6,7},{7,6},{8,9},{9,8},{10,11... | collective-permute-start | bytes 688136 | tf_op jit(solution)/shard_map/ppermute | solution.py:23
  46.2 0.4 collective-permute-done.10
  46.6 1.1 %collective-permute-done.11 = bf16[160,512]{1,0:T(8,128)(2,1)S(1)} collective-permute-done((bf16[160,512]{1,0:T(8,128)(2,1)S(1)}, bf16[160,512]{1,0:T(8,128)(2,1)S(1)}, u32[]{:S(2)}, u32[]{:S(2)}) %collective-permute-start.11) | collective-permute-done | bytes 163872 | tf_op jit(solution)/shard_map/ppermute | solution.py:23
  47.8 0.6 shard_map.102
  48.4 0.4 collective-permute-start.14
  48.7 0.6 shard_map.101
  49.3 0.0 copy-start
  49.3 1.4 %collective-permute-start.13 = (bf16[384,512]{1,0:T(8,128)(2,1)S(1)}, bf16[384,512]{1,0:T(8,128)(2,1)S(1)}, u32[]{:S(2)}, u32[]{:S(2)}) collective-permute-start(bf16[384,512]{1,0:T(8,128)(2,1)S(1)} %get-tuple-element.100), channel_id=1, source_target_pairs={{0,1},{1,0},{2,3},{3,2},{4,5},{5,4},{6,7},{7,6},{8,9},{9,8},{10,11... | collective-permute-start | bytes 1179656 | tf_op jit(solution)/shard_map/ppermute | solution.py:23
  50.7 1.9 %collective-permute-done.17 = bf16[224,512]{1,0:T(8,128)(2,1)S(1)} collective-permute-done((bf16[224,512]{1,0:T(8,128)(2,1)S(1)}, bf16[224,512]{1,0:T(8,128)(2,1)S(1)}, u32[]{:S(2)}, u32[]{:S(2)}) %collective-permute-start.17) | collective-permute-done | bytes 229408 | tf_op jit(solution)/shard_map/ppermute | solution.py:23
  52.7 0.1 add_convert_fusion.1
  52.8 1.3 %collective-permute-start.18 = (bf16[384,512]{1,0:T(8,128)(2,1)S(1)}, bf16[384,512]{1,0:T(8,128)(2,1)S(1)}, u32[]{:S(2)}, u32[]{:S(2)}) collective-permute-start(bf16[384,512]{1,0:T(8,128)(2,1)S(1)} %add_convert_fusion.1), channel_id=1, source_target_pairs={{0,1},{1,0},{2,3},{3,2},{4,5},{5,4},{6,7},{7,6},{8,9},{9,8},{10,11... | collective-permute-start | bytes 1179656 | tf_op jit(solution)/shard_map/ppermute | solution.py:23
  54.0 0.0 collective-permute-done.15
  54.0 0.1 add_convert_fusion.2
  54.1 0.9 %collective-permute-start.16 = (bf16[384,512]{1,0:T(8,128)(2,1)S(1)}, bf16[384,512]{1,0:T(8,128)(2,1)S(1)}, u32[]{:S(2)}, u32[]{:S(2)}) collective-permute-start(bf16[384,512]{1,0:T(8,128)(2,1)S(1)} %add_convert_fusion.2), channel_id=1, source_target_pairs={{0,2},{1,3},{2,0},{3,1},{4,6},{5,7},{6,4},{7,5},{8,10},{9,11},{10,... | collective-permute-start | bytes 1179656 | tf_op jit(solution)/shard_map/ppermute | solution.py:23
  55.1 0.1 slice_reduce_fusion
  55.2 0.0 copy-done
  55.2 0.4 add_convert_fusion.base_ref
  55.6 0.6 shard_map.100
  56.2 4.9 %collective-permute-done.14.refs_3_ = bf16[384,512]{1,0:T(8,128)(2,1)S(1)} collective-permute-done((bf16[384,512]{1,0:T(8,128)(2,1)S(1)}, bf16[384,512]{1,0:T(8,128)(2,1)S(1)}, u32[]{:S(2)}, u32[]{:S(2)}) %collective-permute-start.14) | collective-permute-done | bytes 393248 | tf_op jit(solution)/shard_map/ppermute | solution.py:23
  61.1 0.8 %collective-permute-done.13.refs_1_ = bf16[384,512]{1,0:T(8,128)(2,1)S(1)} collective-permute-done((bf16[384,512]{1,0:T(8,128)(2,1)S(1)}, bf16[384,512]{1,0:T(8,128)(2,1)S(1)}, u32[]{:S(2)}, u32[]{:S(2)}) %collective-permute-start.13) | collective-permute-done | bytes 393248 | tf_op jit(solution)/shard_map/ppermute | solution.py:23
  61.9 0.3 shard_map.103.base_ref
  62.2 4.7 %collective-permute-done.18.refs_1_ = bf16[384,512]{1,0:T(8,128)(2,1)S(1)} collective-permute-done((bf16[384,512]{1,0:T(8,128)(2,1)S(1)}, bf16[384,512]{1,0:T(8,128)(2,1)S(1)}, u32[]{:S(2)}, u32[]{:S(2)}) %collective-permute-start.18) | collective-permute-done | bytes 393248 | tf_op jit(solution)/shard_map/ppermute | solution.py:23
  66.9 0.0 collective-permute-done.16.refs_0_
  66.9 1.0 %shard_map.104 = bf16[384,1024]{1,0:T(8,128)(2,1)} custom-call(f32[384,1024]{1,0:T(8,128)S(1)} %shard_map.103.base_ref, bf16[384,512]{1,0:T(8,128)(2,1)S(1)} %collective-permute-done.16.refs_0_, bf16[384,512]{1,0:T(8,128)(2,1)S(1)} %collective-permute-done.18.refs_1_), custom_call_target="tpu_custom_call" | custom-call | tf_op jit(solution)/shard_map/pallas_call | solution.py:610
  (3 shorter events, 0.1 us)
Async XLA Ops:
  2.7 24.9 %collective-permute-start = (bf16[320,1024]{1,0:T(8,128)(2,1)S(1)}, bf16[320,1024]{1,0:T(8,128)(2,1)S(1)}, u32[]{:S(2)}, u32[]{:S(2)}) collective-permute-start(bf16[320,1024]{1,0:T(8,128)(2,1)S(1)} %get-tuple-element.69.x_ref), channel_id=1, source_target_pairs={{0,1},{1,0},{2,3},{3,2},{4,5},{5,4},{6,7},{7,6},{8,9},{9,8},{10,11... | collective-permute-start | bytes 1966088 | tf_op jit(solution)/shard_map/ppermute | solution.py:23
  5.7 22.0 %collective-permute-start.1 = (bf16[320,1024]{1,0:T(8,128)(2,1)S(1)}, bf16[320,1024]{1,0:T(8,128)(2,1)S(1)}, u32[]{:S(2)}, u32[]{:S(2)}) collective-permute-start(bf16[320,1024]{1,0:T(8,128)(2,1)S(1)} %get-tuple-element.69.x_ref), channel_id=1, source_target_pairs={{0,2},{1,3},{2,0},{3,1},{4,6},{5,7},{6,4},{7,5},{8,10},{9,11},{10,... | collective-permute-start | bytes 1966088 | tf_op jit(solution)/shard_map/ppermute | solution.py:23
  7.3 1.3 %collective-permute-start.2 = (bf16[4,16,1024]{2,1,0:T(8,128)(2,1)S(1)}, bf16[4,16,1024]{2,1,0:T(8,128)(2,1)S(1)}, u32[]{:S(2)}, u32[]{:S(2)}) collective-permute-start(bf16[4,16,1024]{2,1,0:T(8,128)(2,1)S(1)} %get-tuple-element.64), channel_id=1, source_target_pairs={{0,4},{4,0},{8,12},{12,8},{16,20},{20,16},{24,28},{28,24},{1,5},{5... | collective-permute-start | bytes 393224 | tf_op jit(solution)/shard_map/ppermute | solution.py:23
  8.6 4.5 %collective-permute-start.3 = (bf16[32,1024]{1,0:T(8,128)(2,1)S(1)}, bf16[32,1024]{1,0:T(8,128)(2,1)S(1)}, u32[]{:S(2)}, u32[]{:S(2)}) collective-permute-start(bf16[32,1024]{1,0:T(8,128)(2,1)S(1)} %get-tuple-element.66), channel_id=1, source_target_pairs={{0,8},{4,12},{8,0},{12,4},{16,24},{20,28},{24,16},{28,20},{1,9},{5... | collective-permute-start | bytes 196616 | tf_op jit(solution)/shard_map/ppermute | solution.py:23
  10.3 7.5 %collective-permute-start.4 = (bf16[32,1024]{1,0:T(8,128)(2,1)S(1)}, bf16[32,1024]{1,0:T(8,128)(2,1)S(1)}, u32[]{:S(2)}, u32[]{:S(2)}) collective-permute-start(bf16[32,1024]{1,0:T(8,128)(2,1)S(1)} %get-tuple-element.67), channel_id=1, source_target_pairs={{0,16},{4,20},{8,24},{12,28},{16,0},{20,4},{24,8},{28,12},{1,17},{... | collective-permute-start | bytes 196616 | tf_op jit(solution)/shard_map/ppermute | solution.py:23
  12.9 6.2 %collective-permute-start.5 = (bf16[32,1024]{1,0:T(8,128)(2,1)S(1)}, bf16[32,1024]{1,0:T(8,128)(2,1)S(1)}, u32[]{:S(2)}, u32[]{:S(2)}) collective-permute-start(bf16[32,1024]{1,0:T(8,128)(2,1)S(1)} %get-tuple-element.68), channel_id=1, source_target_pairs={{0,24},{4,28},{8,16},{12,20},{16,8},{20,12},{24,0},{28,4},{1,25},{... | collective-permute-start | bytes 196616 | tf_op jit(solution)/shard_map/ppermute | solution.py:23
  19.2 11.4 %collective-permute-start.6 = (bf16[80,1024]{1,0:T(8,128)(2,1)S(1)}, bf16[80,1024]{1,0:T(8,128)(2,1)S(1)}, u32[]{:S(2)}, u32[]{:S(2)}) collective-permute-start(bf16[80,1024]{1,0:T(8,128)(2,1)S(1)} %shard_map.93.refs_0_), channel_id=1, source_target_pairs={{0,1},{1,0},{2,3},{3,2},{4,5},{5,4},{6,7},{7,6},{8,9},{9,8},{10,11... | collective-permute-start | bytes 491528 | tf_op jit(solution)/shard_map/ppermute | solution.py:23
  19.8 10.9 %collective-permute-start.7 = (bf16[80,1024]{1,0:T(8,128)(2,1)S(1)}, bf16[80,1024]{1,0:T(8,128)(2,1)S(1)}, u32[]{:S(2)}, u32[]{:S(2)}) collective-permute-start(bf16[80,1024]{1,0:T(8,128)(2,1)S(1)} %shard_map.93.refs_0_), channel_id=1, source_target_pairs={{0,2},{1,3},{2,0},{3,1},{4,6},{5,7},{6,4},{7,5},{8,10},{9,11},{10,... | collective-permute-start | bytes 491528 | tf_op jit(solution)/shard_map/ppermute | solution.py:23
  20.4 10.4 %collective-permute-start.8 = (bf16[80,1024]{1,0:T(8,128)(2,1)S(1)}, bf16[80,1024]{1,0:T(8,128)(2,1)S(1)}, u32[]{:S(2)}, u32[]{:S(2)}) collective-permute-start(bf16[80,1024]{1,0:T(8,128)(2,1)S(1)} %shard_map.93.refs_0_), channel_id=1, source_target_pairs={{0,3},{1,2},{2,1},{3,0},{4,7},{5,6},{6,5},{7,4},{8,11},{9,10},{10,... | collective-permute-start | bytes 491528 | tf_op jit(solution)/shard_map/ppermute | solution.py:23
  30.8 7.3 %collective-permute-start.9 = (bf16[160,1024]{1,0:T(8,128)(2,1)S(1)}, bf16[160,1024]{1,0:T(8,128)(2,1)S(1)}, u32[]{:S(2)}, u32[]{:S(2)}) collective-permute-start(bf16[160,1024]{1,0:T(8,128)(2,1)S(1)} %slice.10), channel_id=1, source_target_pairs={{0,1},{1,0},{2,3},{3,2},{4,5},{5,4},{6,7},{7,6},{8,9},{9,8},{10,11... | collective-permute-start | bytes 983048 | tf_op jit(solution)/shard_map/ppermute | solution.py:23
  31.4 9.7 %collective-permute-start.12 = (bf16[160,1024]{1,0:T(8,128)(2,1)S(1)}, bf16[160,1024]{1,0:T(8,128)(2,1)S(1)}, u32[]{:S(2)}, u32[]{:S(2)}) collective-permute-start(bf16[160,1024]{1,0:T(8,128)(2,1)S(1)} %slice.11), channel_id=1, source_target_pairs={{0,2},{1,3},{2,0},{3,1},{4,6},{5,7},{6,4},{7,5},{8,10},{9,11},{10,... | collective-permute-start | bytes 983048 | tf_op jit(solution)/shard_map/ppermute | solution.py:23
  39.7 6.9 %collective-permute-start.10 = (bf16[160,512]{1,0:T(8,128)(2,1)S(1)}, bf16[160,512]{1,0:T(8,128)(2,1)S(1)}, u32[]{:S(2)}, u32[]{:S(2)}) collective-permute-start(bf16[160,512]{1,0:T(8,128)(2,1)S(1)} %get-tuple-element.90), channel_id=1, source_target_pairs={{0,1},{1,0},{2,3},{3,2},{4,5},{5,4},{6,7},{7,6},{8,9},{9,8},{10,11... | collective-permute-start | bytes 491528 | tf_op jit(solution)/shard_map/ppermute | solution.py:23
  40.6 7.1 %collective-permute-start.11 = (bf16[160,512]{1,0:T(8,128)(2,1)S(1)}, bf16[160,512]{1,0:T(8,128)(2,1)S(1)}, u32[]{:S(2)}, u32[]{:S(2)}) collective-permute-start(bf16[160,512]{1,0:T(8,128)(2,1)S(1)} %get-tuple-element.91), channel_id=1, source_target_pairs={{0,2},{1,3},{2,0},{3,1},{4,6},{5,7},{6,4},{7,5},{8,10},{9,11},{10,... | collective-permute-start | bytes 491528 | tf_op jit(solution)/shard_map/ppermute | solution.py:23
  43.3 9.4 %collective-permute-start.17 = (bf16[224,512]{1,0:T(8,128)(2,1)S(1)}, bf16[224,512]{1,0:T(8,128)(2,1)S(1)}, u32[]{:S(2)}, u32[]{:S(2)}) collective-permute-start(bf16[224,512]{1,0:T(8,128)(2,1)S(1)} %get-tuple-element.108), channel_id=1, source_target_pairs={{0,2},{1,3},{2,0},{3,1},{4,6},{5,7},{6,4},{7,5},{8,10},{9,11},{10,... | collective-permute-start | bytes 688136 | tf_op jit(solution)/shard_map/ppermute | solution.py:23
  45.0 9.1 %collective-permute-start.15 = (bf16[224,512]{1,0:T(8,128)(2,1)S(1)}, bf16[224,512]{1,0:T(8,128)(2,1)S(1)}, u32[]{:S(2)}, u32[]{:S(2)}) collective-permute-start(bf16[224,512]{1,0:T(8,128)(2,1)S(1)} %get-tuple-element.105), channel_id=1, source_target_pairs={{0,1},{1,0},{2,3},{3,2},{4,5},{5,4},{6,7},{7,6},{8,9},{9,8},{10,11... | collective-permute-start | bytes 688136 | tf_op jit(solution)/shard_map/ppermute | solution.py:23
  48.4 12.7 %collective-permute-start.14 = (bf16[384,512]{1,0:T(8,128)(2,1)S(1)}, bf16[384,512]{1,0:T(8,128)(2,1)S(1)}, u32[]{:S(2)}, u32[]{:S(2)}) collective-permute-start(bf16[384,512]{1,0:T(8,128)(2,1)S(1)} %get-tuple-element.102), channel_id=1, source_target_pairs={{0,2},{1,3},{2,0},{3,1},{4,6},{5,7},{6,4},{7,5},{8,10},{9,11},{10,... | collective-permute-start | bytes 1179656 | tf_op jit(solution)/shard_map/ppermute | solution.py:23
  49.3 5.9 %copy-start = (bf16[384,1024]{1,0:T(8,128)(2,1)S(1)}, bf16[384,1024]{1,0:T(8,128)(2,1)}, u32[]{:S(2)}) copy-start(bf16[384,1024]{1,0:T(8,128)(2,1)} %text_hbm.1) | copy-start | bytes 2359300
  49.3 12.6 %collective-permute-start.13 = (bf16[384,512]{1,0:T(8,128)(2,1)S(1)}, bf16[384,512]{1,0:T(8,128)(2,1)S(1)}, u32[]{:S(2)}, u32[]{:S(2)}) collective-permute-start(bf16[384,512]{1,0:T(8,128)(2,1)S(1)} %get-tuple-element.100), channel_id=1, source_target_pairs={{0,1},{1,0},{2,3},{3,2},{4,5},{5,4},{6,7},{7,6},{8,9},{9,8},{10,11... | collective-permute-start | bytes 1179656 | tf_op jit(solution)/shard_map/ppermute | solution.py:23
  52.8 14.1 %collective-permute-start.18 = (bf16[384,512]{1,0:T(8,128)(2,1)S(1)}, bf16[384,512]{1,0:T(8,128)(2,1)S(1)}, u32[]{:S(2)}, u32[]{:S(2)}) collective-permute-start(bf16[384,512]{1,0:T(8,128)(2,1)S(1)} %add_convert_fusion.1), channel_id=1, source_target_pairs={{0,1},{1,0},{2,3},{3,2},{4,5},{5,4},{6,7},{7,6},{8,9},{9,8},{10,11... | collective-permute-start | bytes 1179656 | tf_op jit(solution)/shard_map/ppermute | solution.py:23
  54.1 12.7 %collective-permute-start.16 = (bf16[384,512]{1,0:T(8,128)(2,1)S(1)}, bf16[384,512]{1,0:T(8,128)(2,1)S(1)}, u32[]{:S(2)}, u32[]{:S(2)}) collective-permute-start(bf16[384,512]{1,0:T(8,128)(2,1)S(1)} %add_convert_fusion.2), channel_id=1, source_target_pairs={{0,2},{1,3},{2,0},{3,1},{4,6},{5,7},{6,4},{7,5},{8,10},{9,11},{10,... | collective-permute-start | bytes 1179656 | tf_op jit(solution)/shard_map/ppermute | solution.py:23

commit v4 on v3

--- a/solution.py
+++ b/solution.py
@@ -380,7 +380,7 @@
         + vmem_specs(sum(pieces) + 4),
         out_specs=tuple(vmem_specs(2)),
         compiler_params=params(12),
-        cost_estimate=TINY,
+        cost_estimate=pl.CostEstimate(flops=10**11, bytes_accessed=0, transcendentals=0),
     )(me, *[h for b in blocks for h in b], gain, held, acc, ss)
 
 
@@ -429,7 +429,7 @@
         out_specs=tuple(vmem_specs(3)),
         scratch_shapes=[pltpu.SemaphoreType.DMA],
         compiler_params=params(12),
-        cost_estimate=pl.CostEstimate(flops=10**11, bytes_accessed=0, transcendentals=0),
+        cost_estimate=pl.CostEstimate(flops=0, bytes_accessed=0, transcendentals=0),
     )(me, *blocks, gain, sel, held, in_hbm(w_out))
 
 

time: 68 us -> 66.2 us (0.974)
  waiting for transfers between devices: 24.6 us -> 22.1 us
  starting transfers between devices: 21.9 us -> 22.7 us
    ppermute x19, waiting for transfers between devices: 24.6 us -> 22.1 us  [swap(): return lax.ppermute(x, axis, [(i, i ^ s) for i in range(n)])]
    ppermute x19, starting transfers between devices: 21.9 us -> 22.7 us  [swap(): return lax.ppermute(x, axis, [(i, i ^ s) for i in range(n)])]
where the time goes in v4:
time: 66.2 us; the launch traced here: 66.1 us
  starting transfers between devices  22.7 us (34%)
  waiting for transfers between devices  22.1 us (33%)
  Pallas kernels  20.4 us (31%)
    ppermute x19, starting transfers between devices, swap(): return lax.ppermute(x, axis, [(i, i ^ s) for i in range(n)])  22.7 us
    ppermute x19, waiting for transfers between devices, swap(): return lax.ppermute(x, axis, [(i, i ^ s) for i in range(n)])  22.1 us
    pallas_call x1, Pallas kernels, own_part(): pl.pallas_call(own_kernel, out_shape=(jax.ShapeDtypeStruct((3, rows, cols...  4.86 us
    pallas_call x1, Pallas kernels, prepare(): pl.pallas_call(functools.partial(prep_kernel, n_req), out_shape=tuple((ja...  2.72 us
    pallas_call x1, Pallas kernels, image_part(): pl.pallas_call(functools.partial(image_kernel, n_rows, len(blocks)), out_...  2.65 us
    pallas_call x1, Pallas kernels, near_part(): pl.pallas_call(functools.partial(near_kernel, near, pieces), out_shape=(j...  2.27 us
    pallas_call x1, Pallas kernels, tail_part(): pl.pallas_call(functools.partial(tail_kernel, far), out_shape=(jax.ShapeD...  2.25 us
    pallas_call x3, Pallas kernels, out_part(): pl.pallas_call(functools.partial(out_kernel, away), out_shape=(jax.ShapeD...  1.77 us
  transfers between devices with their start and end apart: 19, of which 10 were waited for; matrix products, arithmetic and copies ran while one was open for 1% of the time, Pallas kernels for 25%

profile of v4, /device:TPU:0, one launch (start us, length us, event | category | flops | bytes accessed | tf_op | source)
XLA Modules:
  0.0 66.1 jit_solution(2097886698088819745)
XLA Ops:
  0.0 2.7 %shard_map.91 = (bf16[4,16,1024]{2,1,0:T(8,128)(2,1)S(1)}, bf16[4,16,1024]{2,1,0:T(8,128)(2,1)S(1)}, bf16[320,1024]{1,0:T(8,128)(2,1)S(1)}, bf16[80,1024]{1,0:T(...) custom-call(s32[1]{0:T(128)} %bitcast.me_ref, ...), custom_call_target="tpu_custom_call" | custom-call | tf_op jit(solution)/shard_map/pallas_call | solution.py:199
  2.7 3.0 %collective-permute-start = (bf16[320,1024]{1,0:T(8,128)(2,1)S(1)}, bf16[320,1024]{1,0:T(8,128)(2,1)S(1)}, u32[]{:S(2)}, u32[]{:S(2)}) collective-permute-start(bf16[320,1024]{1,0:T(8,128)(2,1)S(1)} %get-tuple-element.69.x_ref), channel_id=1, source_target_pairs={{0,1},{1,0},{2,3},{3,2},{4,5},{5,4},{6,7},{7,6},{8,9},{9,8},{10,11... | collective-permute-start | bytes 1966088 | tf_op jit(solution)/shard_map/ppermute | solution.py:23
  5.7 1.5 %collective-permute-start.1 = (bf16[320,1024]{1,0:T(8,128)(2,1)S(1)}, bf16[320,1024]{1,0:T(8,128)(2,1)S(1)}, u32[]{:S(2)}, u32[]{:S(2)}) collective-permute-start(bf16[320,1024]{1,0:T(8,128)(2,1)S(1)} %get-tuple-element.69.x_ref), channel_id=1, source_target_pairs={{0,2},{1,3},{2,0},{3,1},{4,6},{5,7},{6,4},{7,5},{8,10},{9,11},{10,... | collective-permute-start | bytes 1966088 | tf_op jit(solution)/shard_map/ppermute | solution.py:23
  7.3 0.0 collective-permute-start.2
  7.3 1.3 %collective-permute-done.2.odd_ref = bf16[4,16,1024]{2,1,0:T(8,128)(2,1)S(1)} collective-permute-done((bf16[4,16,1024]{2,1,0:T(8,128)(2,1)S(1)}, bf16[4,16,1024]{2,1,0:T(8,128)(2,1)S(1)}, u32[]{:S(2)}, u32[]{:S(2)}) %collective-permute-start.2) | collective-permute-done | bytes 131104 | tf_op jit(solution)/shard_map/ppermute | solution.py:23
  8.6 1.6 %collective-permute-start.3 = (bf16[32,1024]{1,0:T(8,128)(2,1)S(1)}, bf16[32,1024]{1,0:T(8,128)(2,1)S(1)}, u32[]{:S(2)}, u32[]{:S(2)}) collective-permute-start(bf16[32,1024]{1,0:T(8,128)(2,1)S(1)} %get-tuple-element.66), channel_id=1, source_target_pairs={{0,8},{4,12},{8,0},{12,4},{16,24},{20,28},{24,16},{28,20},{1,9},{5... | collective-permute-start | bytes 196616 | tf_op jit(solution)/shard_map/ppermute | solution.py:23
  10.3 2.6 %collective-permute-start.4 = (bf16[32,1024]{1,0:T(8,128)(2,1)S(1)}, bf16[32,1024]{1,0:T(8,128)(2,1)S(1)}, u32[]{:S(2)}, u32[]{:S(2)}) collective-permute-start(bf16[32,1024]{1,0:T(8,128)(2,1)S(1)} %get-tuple-element.67), channel_id=1, source_target_pairs={{0,16},{4,20},{8,24},{12,28},{16,0},{20,4},{24,8},{28,12},{1,17},{... | collective-permute-start | bytes 196616 | tf_op jit(solution)/shard_map/ppermute | solution.py:23
  12.9 0.2 collective-permute-start.5
  13.1 0.0 collective-permute-done.3.refs_1_
  13.1 4.7 %collective-permute-done.4.refs_2_ = bf16[32,1024]{1,0:T(8,128)(2,1)S(1)} collective-permute-done((bf16[32,1024]{1,0:T(8,128)(2,1)S(1)}, bf16[32,1024]{1,0:T(8,128)(2,1)S(1)}, u32[]{:S(2)}, u32[]{:S(2)}) %collective-permute-start.4) | collective-permute-done | bytes 65568 | tf_op jit(solution)/shard_map/ppermute | solution.py:23
  17.8 1.2 %collective-permute-done.5.refs_3_ = bf16[32,1024]{1,0:T(8,128)(2,1)S(1)} collective-permute-done((bf16[32,1024]{1,0:T(8,128)(2,1)S(1)}, bf16[32,1024]{1,0:T(8,128)(2,1)S(1)}, u32[]{:S(2)}, u32[]{:S(2)}) %collective-permute-start.5) | collective-permute-done | bytes 65568 | tf_op jit(solution)/shard_map/ppermute | solution.py:23
  19.0 0.2 shard_map.93.refs_0_
  19.2 0.6 collective-permute-start.6
  19.8 0.5 collective-permute-start.7
  20.4 2.4 %collective-permute-start.8 = (bf16[80,1024]{1,0:T(8,128)(2,1)S(1)}, bf16[80,1024]{1,0:T(8,128)(2,1)S(1)}, u32[]{:S(2)}, u32[]{:S(2)}) collective-permute-start(bf16[80,1024]{1,0:T(8,128)(2,1)S(1)} %shard_map.93.refs_0_), channel_id=1, source_target_pairs={{0,3},{1,2},{2,1},{3,0},{4,7},{5,6},{6,5},{7,4},{8,11},{9,10},{10,... | collective-permute-start | bytes 491528 | tf_op jit(solution)/shard_map/ppermute | solution.py:23
  22.8 4.9 %shard_map.94 = (f32[3,320,512]{2,1,0:T(8,128)S(1)}, f32[320,128]{1,0:T(8,128)S(1)}, bf16[4,3,1024,512]{3,2,1,0:T(8,128)(2,1)S(1)}) custom-call(s32[1]{0:T(128)} %bitcast.5.me_ref, bf16[320,1024]{1,0:T(8,128)(2,1)S(1)} %get-tuple-element.69.x_ref, f32[4,1,1024]{2,1,0:T(1,128)S(1)} %get-tuple-element.59.gain_ref.refs_2_.refs_4_, bf16[3,4096,512]{2,1,0:T(8,128)(2,1)} %bitcast.9), custom_call_target="tpu_custom_call" | custom-call | tf_op jit(solution)/shard_map/pallas_call | solution.py:329
  27.7 0.0 collective-permute-done.refs_0_
  27.7 0.0 collective-permute-done.1.refs_1_
  27.7 0.6 collective-permute-start.9
  28.3 0.6 collective-permute-start.12
  28.9 2.3 %shard_map.95 = (f32[3,320,512]{2,1,0:T(8,128)S(1)}, f32[320,128]{1,0:T(8,128)S(1)}) custom-call(s32[1]{0:T(128)} %bitcast.5.me_ref, bf16[320,1024]{1,0:T(8,128)(2,1)S(1)} %collective-permute-done.refs_0_, bf16[320,1024]{1,0:T(8,128)(2,1)S(1)} %collective-permute-done.1.refs_1_, f32[4,1,1024]{2,1,0:T(1,128)S(1)} %get-tuple-element.59.gain_ref.refs_2_.refs_4_, ...), custom_call_target="tpu_custom_call" | custom-call | flops 99999997952 | tf_op jit(solution)/shard_map/pallas_call | solution.py:373
  31.2 0.7 %shard_map.96 = (bf16[384,320]{1,0:T(8,128)(2,1)S(1)}, bf16[384,80]{1,0:T(8,128)(2,1)S(1)}, f32[384,128]{1,0:T(8,128)S(1)}) custom-call(s32[8,128]{1,0:T(8,128)S(1)} %get-tuple-element.74.table_ref), custom_call_target="tpu_custom_call" | custom-call | tf_op jit(solution)/shard_map/pallas_call | solution.py:278
  31.9 0.0 collective-permute-done.6.refs_1_
  31.9 0.0 collective-permute-done.7.refs_2_
  31.9 0.0 collective-permute-done.8.refs_3_
  31.9 2.7 %shard_map.97 = (bf16[3,80,512]{2,1,0:T(8,128)(2,1)S(1)}, bf16[80,1024]{1,0:T(8,128)(2,1)S(1)}, bf16[512,4096]{1,0:T(8,128)(2,1)S(1)}) custom-call(s32[1]{0:T(128)} %bitcast.5.me_ref, bf16[80,1024]{1,0:T(8,128)(2,1)S(1)} %shard_map.93.refs_0_, bf16[80,1024]{1,0:T(8,128)(2,1)S(1)} %collective-permute-done.6.refs_1_, ...), custom_call_target="tpu_custom_call" | custom-call | tf_op jit(solution)/shard_map/pallas_call | solution.py:419
  34.6 0.4 collective-permute-done.9.top_ref
  35.0 1.7 %shard_map.98 = (bf16[3,160,512]{2,1,0:T(8,128)(2,1)S(1)}, bf16[3,160,512]{2,1,0:T(8,128)(2,1)S(1)}, bf16[160,512]{1,0:T(8,128)(2,1)S(1)}, bf16[160,512]{1,0:T(8,128)(2,1)S(1)}, bf16[160,512]{1,0:T(8,128)(2,1)S(1)}) custom-call(s32[1]{0:T(128)} %bitcast.5.me_ref, bf16[160,1024]{1,0:T(8,128)(2,1)S(1)} %collective-permute-done.9.top_ref, ...), custom_call_target="tpu_custom_call" | custom-call | tf_op jit(solution)/shard_map/pallas_call | solution.py:498
  36.7 1.4 %collective-permute-start.10 = (bf16[160,512]{1,0:T(8,128)(2,1)S(1)}, bf16[160,512]{1,0:T(8,128)(2,1)S(1)}, u32[]{:S(2)}, u32[]{:S(2)}) collective-permute-start(bf16[160,512]{1,0:T(8,128)(2,1)S(1)} %get-tuple-element.90), channel_id=1, source_target_pairs={{0,1},{1,0},{2,3},{3,2},{4,5},{5,4},{6,7},{7,6},{8,9},{9,8},{10,11... | collective-permute-start | bytes 491528 | tf_op jit(solution)/shard_map/ppermute | solution.py:23
  38.1 1.5 %collective-permute-start.11 = (bf16[160,512]{1,0:T(8,128)(2,1)S(1)}, bf16[160,512]{1,0:T(8,128)(2,1)S(1)}, u32[]{:S(2)}, u32[]{:S(2)}) collective-permute-start(bf16[160,512]{1,0:T(8,128)(2,1)S(1)} %get-tuple-element.91), channel_id=1, source_target_pairs={{0,2},{1,3},{2,0},{3,1},{4,6},{5,7},{6,4},{7,5},{8,10},{9,11},{10,... | collective-permute-start | bytes 491528 | tf_op jit(solution)/shard_map/ppermute | solution.py:23
  39.5 0.0 collective-permute-done.12.bottom_ref
  39.5 2.3 %shard_map.99 = (bf16[224,512]{1,0:T(8,128)(2,1)S(1)}, bf16[224,512]{1,0:T(8,128)(2,1)S(1)}, bf16[224,512]{1,0:T(8,128)(2,1)S(1)}) custom-call(s32[1]{0:T(128)} %bitcast.5.me_ref, bf16[160,1024]{1,0:T(8,128)(2,1)S(1)} %collective-permute-done.12.bottom_ref, f32[4,1,1024]{2,1,0:T(1,128)S(1)} %get-tuple-element.59.gain_ref.refs_2_.refs_4_, ...), custom_call_target="tpu_custom_call" | custom-call | flops 10000000000 | tf_op jit(solution)/shard_map/pallas_call | solution.py:537
  41.8 0.6 collective-permute-start.17
  42.4 0.7 %collective-permute-start.15 = (bf16[224,512]{1,0:T(8,128)(2,1)S(1)}, bf16[224,512]{1,0:T(8,128)(2,1)S(1)}, u32[]{:S(2)}, u32[]{:S(2)}) collective-permute-start(bf16[224,512]{1,0:T(8,128)(2,1)S(1)} %get-tuple-element.105), channel_id=1, source_target_pairs={{0,1},{1,0},{2,3},{3,2},{4,5},{5,4},{6,7},{7,6},{8,9},{9,8},{10,11... | collective-permute-start | bytes 688136 | tf_op jit(solution)/shard_map/ppermute | solution.py:23
  43.1 0.0 collective-permute-done.10
  43.1 1.4 %collective-permute-done.11 = bf16[160,512]{1,0:T(8,128)(2,1)S(1)} collective-permute-done((bf16[160,512]{1,0:T(8,128)(2,1)S(1)}, bf16[160,512]{1,0:T(8,128)(2,1)S(1)}, u32[]{:S(2)}, u32[]{:S(2)}) %collective-permute-start.11) | collective-permute-done | bytes 163872 | tf_op jit(solution)/shard_map/ppermute | solution.py:23
  44.5 0.6 shard_map.102
  45.1 2.1 %collective-permute-start.14 = (bf16[384,512]{1,0:T(8,128)(2,1)S(1)}, bf16[384,512]{1,0:T(8,128)(2,1)S(1)}, u32[]{:S(2)}, u32[]{:S(2)}) collective-permute-start(bf16[384,512]{1,0:T(8,128)(2,1)S(1)} %get-tuple-element.102), channel_id=1, source_target_pairs={{0,2},{1,3},{2,0},{3,1},{4,6},{5,7},{6,4},{7,5},{8,10},{9,11},{10,... | collective-permute-start | bytes 1179656 | tf_op jit(solution)/shard_map/ppermute | solution.py:23
  47.2 0.6 shard_map.101
  47.8 0.0 copy-start
  47.8 0.7 %collective-permute-start.13 = (bf16[384,512]{1,0:T(8,128)(2,1)S(1)}, bf16[384,512]{1,0:T(8,128)(2,1)S(1)}, u32[]{:S(2)}, u32[]{:S(2)}) collective-permute-start(bf16[384,512]{1,0:T(8,128)(2,1)S(1)} %get-tuple-element.100), channel_id=1, source_target_pairs={{0,1},{1,0},{2,3},{3,2},{4,5},{5,4},{6,7},{7,6},{8,9},{9,8},{10,11... | collective-permute-start | bytes 1179656 | tf_op jit(solution)/shard_map/ppermute | solution.py:23
  48.5 1.9 %collective-permute-done.17 = bf16[224,512]{1,0:T(8,128)(2,1)S(1)} collective-permute-done((bf16[224,512]{1,0:T(8,128)(2,1)S(1)}, bf16[224,512]{1,0:T(8,128)(2,1)S(1)}, u32[]{:S(2)}, u32[]{:S(2)}) %collective-permute-start.17) | collective-permute-done | bytes 229408 | tf_op jit(solution)/shard_map/ppermute | solution.py:23
  50.4 0.1 add_convert_fusion.1
  50.5 0.7 collective-permute-start.18
  51.2 0.0 collective-permute-done.15
  51.2 0.1 add_convert_fusion.2
  51.3 1.3 %collective-permute-start.16 = (bf16[384,512]{1,0:T(8,128)(2,1)S(1)}, bf16[384,512]{1,0:T(8,128)(2,1)S(1)}, u32[]{:S(2)}, u32[]{:S(2)}) collective-permute-start(bf16[384,512]{1,0:T(8,128)(2,1)S(1)} %add_convert_fusion.2), channel_id=1, source_target_pairs={{0,2},{1,3},{2,0},{3,1},{4,6},{5,7},{6,4},{7,5},{8,10},{9,11},{10,... | collective-permute-start | bytes 1179656 | tf_op jit(solution)/shard_map/ppermute | solution.py:23
  52.6 0.1 slice_reduce_fusion
  52.7 0.0 copy-done
  52.7 0.4 add_convert_fusion.base_ref
  53.1 0.6 shard_map.100
  53.7 5.1 %collective-permute-done.14.refs_3_ = bf16[384,512]{1,0:T(8,128)(2,1)S(1)} collective-permute-done((bf16[384,512]{1,0:T(8,128)(2,1)S(1)}, bf16[384,512]{1,0:T(8,128)(2,1)S(1)}, u32[]{:S(2)}, u32[]{:S(2)}) %collective-permute-start.14) | collective-permute-done | bytes 393248 | tf_op jit(solution)/shard_map/ppermute | solution.py:23
  58.8 1.1 %collective-permute-done.13.refs_1_ = bf16[384,512]{1,0:T(8,128)(2,1)S(1)} collective-permute-done((bf16[384,512]{1,0:T(8,128)(2,1)S(1)}, bf16[384,512]{1,0:T(8,128)(2,1)S(1)}, u32[]{:S(2)}, u32[]{:S(2)}) %collective-permute-start.13) | collective-permute-done | bytes 393248 | tf_op jit(solution)/shard_map/ppermute | solution.py:23
  59.9 0.3 shard_map.103.base_ref
  60.2 4.9 %collective-permute-done.18.refs_1_ = bf16[384,512]{1,0:T(8,128)(2,1)S(1)} collective-permute-done((bf16[384,512]{1,0:T(8,128)(2,1)S(1)}, bf16[384,512]{1,0:T(8,128)(2,1)S(1)}, u32[]{:S(2)}, u32[]{:S(2)}) %collective-permute-start.18) | collective-permute-done | bytes 393248 | tf_op jit(solution)/shard_map/ppermute | solution.py:23
  65.1 0.1 collective-permute-done.16.refs_0_
  65.1 1.0 %shard_map.104 = bf16[384,1024]{1,0:T(8,128)(2,1)} custom-call(f32[384,1024]{1,0:T(8,128)S(1)} %shard_map.103.base_ref, bf16[384,512]{1,0:T(8,128)(2,1)S(1)} %collective-permute-done.16.refs_0_, bf16[384,512]{1,0:T(8,128)(2,1)S(1)} %collective-permute-done.18.refs_1_), custom_call_target="tpu_custom_call" | custom-call | tf_op jit(solution)/shard_map/pallas_call | solution.py:610
  (3 shorter events, 0.1 us)
Async XLA Ops:
  2.7 24.9 %collective-permute-start = (bf16[320,1024]{1,0:T(8,128)(2,1)S(1)}, bf16[320,1024]{1,0:T(8,128)(2,1)S(1)}, u32[]{:S(2)}, u32[]{:S(2)}) collective-permute-start(bf16[320,1024]{1,0:T(8,128)(2,1)S(1)} %get-tuple-element.69.x_ref), channel_id=1, source_target_pairs={{0,1},{1,0},{2,3},{3,2},{4,5},{5,4},{6,7},{7,6},{8,9},{9,8},{10,11... | collective-permute-start | bytes 1966088 | tf_op jit(solution)/shard_map/ppermute | solution.py:23
  5.7 21.9 %collective-permute-start.1 = (bf16[320,1024]{1,0:T(8,128)(2,1)S(1)}, bf16[320,1024]{1,0:T(8,128)(2,1)S(1)}, u32[]{:S(2)}, u32[]{:S(2)}) collective-permute-start(bf16[320,1024]{1,0:T(8,128)(2,1)S(1)} %get-tuple-element.69.x_ref), channel_id=1, source_target_pairs={{0,2},{1,3},{2,0},{3,1},{4,6},{5,7},{6,4},{7,5},{8,10},{9,11},{10,... | collective-permute-start | bytes 1966088 | tf_op jit(solution)/shard_map/ppermute | solution.py:23
  7.3 1.3 %collective-permute-start.2 = (bf16[4,16,1024]{2,1,0:T(8,128)(2,1)S(1)}, bf16[4,16,1024]{2,1,0:T(8,128)(2,1)S(1)}, u32[]{:S(2)}, u32[]{:S(2)}) collective-permute-start(bf16[4,16,1024]{2,1,0:T(8,128)(2,1)S(1)} %get-tuple-element.64), channel_id=1, source_target_pairs={{0,4},{4,0},{8,12},{12,8},{16,20},{20,16},{24,28},{28,24},{1,5},{5... | collective-permute-start | bytes 393224 | tf_op jit(solution)/shard_map/ppermute | solution.py:23
  8.6 4.5 %collective-permute-start.3 = (bf16[32,1024]{1,0:T(8,128)(2,1)S(1)}, bf16[32,1024]{1,0:T(8,128)(2,1)S(1)}, u32[]{:S(2)}, u32[]{:S(2)}) collective-permute-start(bf16[32,1024]{1,0:T(8,128)(2,1)S(1)} %get-tuple-element.66), channel_id=1, source_target_pairs={{0,8},{4,12},{8,0},{12,4},{16,24},{20,28},{24,16},{28,20},{1,9},{5... | collective-permute-start | bytes 196616 | tf_op jit(solution)/shard_map/ppermute | solution.py:23
  10.3 7.5 %collective-permute-start.4 = (bf16[32,1024]{1,0:T(8,128)(2,1)S(1)}, bf16[32,1024]{1,0:T(8,128)(2,1)S(1)}, u32[]{:S(2)}, u32[]{:S(2)}) collective-permute-start(bf16[32,1024]{1,0:T(8,128)(2,1)S(1)} %get-tuple-element.67), channel_id=1, source_target_pairs={{0,16},{4,20},{8,24},{12,28},{16,0},{20,4},{24,8},{28,12},{1,17},{... | collective-permute-start | bytes 196616 | tf_op jit(solution)/shard_map/ppermute | solution.py:23
  12.9 6.2 %collective-permute-start.5 = (bf16[32,1024]{1,0:T(8,128)(2,1)S(1)}, bf16[32,1024]{1,0:T(8,128)(2,1)S(1)}, u32[]{:S(2)}, u32[]{:S(2)}) collective-permute-start(bf16[32,1024]{1,0:T(8,128)(2,1)S(1)} %get-tuple-element.68), channel_id=1, source_target_pairs={{0,24},{4,28},{8,16},{12,20},{16,8},{20,12},{24,0},{28,4},{1,25},{... | collective-permute-start | bytes 196616 | tf_op jit(solution)/shard_map/ppermute | solution.py:23
  19.2 12.7 %collective-permute-start.6 = (bf16[80,1024]{1,0:T(8,128)(2,1)S(1)}, bf16[80,1024]{1,0:T(8,128)(2,1)S(1)}, u32[]{:S(2)}, u32[]{:S(2)}) collective-permute-start(bf16[80,1024]{1,0:T(8,128)(2,1)S(1)} %shard_map.93.refs_0_), channel_id=1, source_target_pairs={{0,1},{1,0},{2,3},{3,2},{4,5},{5,4},{6,7},{7,6},{8,9},{9,8},{10,11... | collective-permute-start | bytes 491528 | tf_op jit(solution)/shard_map/ppermute | solution.py:23
  19.8 12.1 %collective-permute-start.7 = (bf16[80,1024]{1,0:T(8,128)(2,1)S(1)}, bf16[80,1024]{1,0:T(8,128)(2,1)S(1)}, u32[]{:S(2)}, u32[]{:S(2)}) collective-permute-start(bf16[80,1024]{1,0:T(8,128)(2,1)S(1)} %shard_map.93.refs_0_), channel_id=1, source_target_pairs={{0,2},{1,3},{2,0},{3,1},{4,6},{5,7},{6,4},{7,5},{8,10},{9,11},{10,... | collective-permute-start | bytes 491528 | tf_op jit(solution)/shard_map/ppermute | solution.py:23
  20.4 11.6 %collective-permute-start.8 = (bf16[80,1024]{1,0:T(8,128)(2,1)S(1)}, bf16[80,1024]{1,0:T(8,128)(2,1)S(1)}, u32[]{:S(2)}, u32[]{:S(2)}) collective-permute-start(bf16[80,1024]{1,0:T(8,128)(2,1)S(1)} %shard_map.93.refs_0_), channel_id=1, source_target_pairs={{0,3},{1,2},{2,1},{3,0},{4,7},{5,6},{6,5},{7,4},{8,11},{9,10},{10,... | collective-permute-start | bytes 491528 | tf_op jit(solution)/shard_map/ppermute | solution.py:23
  27.7 7.3 %collective-permute-start.9 = (bf16[160,1024]{1,0:T(8,128)(2,1)S(1)}, bf16[160,1024]{1,0:T(8,128)(2,1)S(1)}, u32[]{:S(2)}, u32[]{:S(2)}) collective-permute-start(bf16[160,1024]{1,0:T(8,128)(2,1)S(1)} %slice.10), channel_id=1, source_target_pairs={{0,1},{1,0},{2,3},{3,2},{4,5},{5,4},{6,7},{7,6},{8,9},{9,8},{10,11... | collective-permute-start | bytes 983048 | tf_op jit(solution)/shard_map/ppermute | solution.py:23
  28.3 11.2 %collective-permute-start.12 = (bf16[160,1024]{1,0:T(8,128)(2,1)S(1)}, bf16[160,1024]{1,0:T(8,128)(2,1)S(1)}, u32[]{:S(2)}, u32[]{:S(2)}) collective-permute-start(bf16[160,1024]{1,0:T(8,128)(2,1)S(1)} %slice.11), channel_id=1, source_target_pairs={{0,2},{1,3},{2,0},{3,1},{4,6},{5,7},{6,4},{7,5},{8,10},{9,11},{10,... | collective-permute-start | bytes 983048 | tf_op jit(solution)/shard_map/ppermute | solution.py:23
  36.7 6.5 %collective-permute-start.10 = (bf16[160,512]{1,0:T(8,128)(2,1)S(1)}, bf16[160,512]{1,0:T(8,128)(2,1)S(1)}, u32[]{:S(2)}, u32[]{:S(2)}) collective-permute-start(bf16[160,512]{1,0:T(8,128)(2,1)S(1)} %get-tuple-element.90), channel_id=1, source_target_pairs={{0,1},{1,0},{2,3},{3,2},{4,5},{5,4},{6,7},{7,6},{8,9},{9,8},{10,11... | collective-permute-start | bytes 491528 | tf_op jit(solution)/shard_map/ppermute | solution.py:23
  38.1 6.4 %collective-permute-start.11 = (bf16[160,512]{1,0:T(8,128)(2,1)S(1)}, bf16[160,512]{1,0:T(8,128)(2,1)S(1)}, u32[]{:S(2)}, u32[]{:S(2)}) collective-permute-start(bf16[160,512]{1,0:T(8,128)(2,1)S(1)} %get-tuple-element.91), channel_id=1, source_target_pairs={{0,2},{1,3},{2,0},{3,1},{4,6},{5,7},{6,4},{7,5},{8,10},{9,11},{10,... | collective-permute-start | bytes 491528 | tf_op jit(solution)/shard_map/ppermute | solution.py:23
  41.8 8.6 %collective-permute-start.17 = (bf16[224,512]{1,0:T(8,128)(2,1)S(1)}, bf16[224,512]{1,0:T(8,128)(2,1)S(1)}, u32[]{:S(2)}, u32[]{:S(2)}) collective-permute-start(bf16[224,512]{1,0:T(8,128)(2,1)S(1)} %get-tuple-element.108), channel_id=1, source_target_pairs={{0,2},{1,3},{2,0},{3,1},{4,6},{5,7},{6,4},{7,5},{8,10},{9,11},{10,... | collective-permute-start | bytes 688136 | tf_op jit(solution)/shard_map/ppermute | solution.py:23
  42.4 8.7 %collective-permute-start.15 = (bf16[224,512]{1,0:T(8,128)(2,1)S(1)}, bf16[224,512]{1,0:T(8,128)(2,1)S(1)}, u32[]{:S(2)}, u32[]{:S(2)}) collective-permute-start(bf16[224,512]{1,0:T(8,128)(2,1)S(1)} %get-tuple-element.105), channel_id=1, source_target_pairs={{0,1},{1,0},{2,3},{3,2},{4,5},{5,4},{6,7},{7,6},{8,9},{9,8},{10,11... | collective-permute-start | bytes 688136 | tf_op jit(solution)/shard_map/ppermute | solution.py:23
  45.1 13.7 %collective-permute-start.14 = (bf16[384,512]{1,0:T(8,128)(2,1)S(1)}, bf16[384,512]{1,0:T(8,128)(2,1)S(1)}, u32[]{:S(2)}, u32[]{:S(2)}) collective-permute-start(bf16[384,512]{1,0:T(8,128)(2,1)S(1)} %get-tuple-element.102), channel_id=1, source_target_pairs={{0,2},{1,3},{2,0},{3,1},{4,6},{5,7},{6,4},{7,5},{8,10},{9,11},{10,... | collective-permute-start | bytes 1179656 | tf_op jit(solution)/shard_map/ppermute | solution.py:23
  47.8 4.9 %copy-start = (bf16[384,1024]{1,0:T(8,128)(2,1)S(1)}, bf16[384,1024]{1,0:T(8,128)(2,1)}, u32[]{:S(2)}) copy-start(bf16[384,1024]{1,0:T(8,128)(2,1)} %text_hbm.1) | copy-start | bytes 2359300
  47.8 12.1 %collective-permute-start.13 = (bf16[384,512]{1,0:T(8,128)(2,1)S(1)}, bf16[384,512]{1,0:T(8,128)(2,1)S(1)}, u32[]{:S(2)}, u32[]{:S(2)}) collective-permute-start(bf16[384,512]{1,0:T(8,128)(2,1)S(1)} %get-tuple-element.100), channel_id=1, source_target_pairs={{0,1},{1,0},{2,3},{3,2},{4,5},{5,4},{6,7},{7,6},{8,9},{9,8},{10,11... | collective-permute-start | bytes 1179656 | tf_op jit(solution)/shard_map/ppermute | solution.py:23
  50.5 14.6 %collective-permute-start.18 = (bf16[384,512]{1,0:T(8,128)(2,1)S(1)}, bf16[384,512]{1,0:T(8,128)(2,1)S(1)}, u32[]{:S(2)}, u32[]{:S(2)}) collective-permute-start(bf16[384,512]{1,0:T(8,128)(2,1)S(1)} %add_convert_fusion.1), channel_id=1, source_target_pairs={{0,1},{1,0},{2,3},{3,2},{4,5},{5,4},{6,7},{7,6},{8,9},{9,8},{10,11... | collective-permute-start | bytes 1179656 | tf_op jit(solution)/shard_map/ppermute | solution.py:23
  51.3 13.9 %collective-permute-start.16 = (bf16[384,512]{1,0:T(8,128)(2,1)S(1)}, bf16[384,512]{1,0:T(8,128)(2,1)S(1)}, u32[]{:S(2)}, u32[]{:S(2)}) collective-permute-start(bf16[384,512]{1,0:T(8,128)(2,1)S(1)} %add_convert_fusion.2), channel_id=1, source_target_pairs={{0,2},{1,3},{2,0},{3,1},{4,6},{5,7},{6,4},{7,5},{8,10},{9,11},{10,... | collective-permute-start | bytes 1179656 | tf_op jit(solution)/shard_map/ppermute | solution.py:23

commit v5 on v4

--- a/solution.py
+++ b/solution.py
@@ -77,15 +77,64 @@
 NOWHERE = 1 << 20
 
 
+def find_images(n_req, img_dev, me, req_ref, start_ref, grid_ref=None):
+    found = []
+    for s in range(n_req):
+        source = (me ^ s) * img_dev
+
+        def one_image(k, found, source=source):
+            hit = req_ref[source + k] == me
+            values = (start_ref[source + k],)
+            if grid_ref is not None:
+                values += (grid_ref[0, source + k] // 2, grid_ref[1, source + k] // 2)
+            return tuple(jnp.where(hit, new, old) for new, old in zip(values, found))
+
+        none = (jnp.int32(NOWHERE), jnp.int32(0), jnp.int32(1))[: 1 if grid_ref is None else 3]
+        found.append(lax.fori_loop(0, img_dev, one_image, none, unroll=img_dev <= 8))
+    return found
+
+
+def text_kernel(n_req, region, me_ref, req_hbm, start_hbm, text_hbm, ctext_out, req_ref, start_ref, text_ref, sem_ref):
+    copies = fetch(((req_hbm, req_ref), (start_hbm, start_ref), (text_hbm, text_ref)), sem_ref)
+    n_text, length = ctext_out.shape[0], text_ref.shape[0]
+    spot = lax.broadcasted_iota(jnp.int32, (8, length), 1)
+    before = jnp.zeros((8, length), jnp.int32)
+    inside = jnp.zeros((8, length), jnp.int32)
+    copies[0].wait()
+    copies[1].wait()
+    for (start,) in find_images(n_req, req_ref.shape[0] // n_req, me_ref[0], req_ref, start_ref):
+        c = spot - start
+        before += jnp.clip(c, 0, region)
+        inside = jnp.where((c >= 0) & (c < region), 1, inside)
+    rank = jnp.where(inside == 1, -1, spot - before)[0:1]
+    gather = (lax.broadcasted_iota(jnp.int32, (n_text, length), 0) == rank).astype(jnp.bfloat16)
+    copies[2].wait()
+    ctext_out[...] = jnp.dot(gather, text_ref[...], preferred_element_type=jnp.float32).astype(jnp.bfloat16)
+
+
+def gather_text(me, image_request, slot_start, text, n_req, region, n_text):
+    inputs = (image_request, slot_start, text)
+    return pl.pallas_call(
+        functools.partial(text_kernel, n_req, region),
+        out_shape=jax.ShapeDtypeStruct((n_text, text.shape[1]), text.dtype),
+        in_specs=[pl.BlockSpec(memory_space=pltpu.SMEM)] + [pl.BlockSpec(memory_space=pltpu.HBM)] * 3,
+        out_specs=pl.BlockSpec(memory_space=pltpu.VMEM),
+        scratch_shapes=[pltpu.SMEM(x.shape, jnp.int32) for x in inputs[:2]]
+        + [pltpu.VMEM(text.shape, text.dtype), pltpu.SemaphoreType.DMA((3,))],
+        compiler_params=params(8),
+        cost_estimate=TINY,
+    )(me, *[in_hbm(x) for x in inputs])
+
+
 def prep_kernel(n_req, me_ref, req_hbm, start_hbm, grid_hbm, text_hbm, x_hbm, dec_hbm, vis_hbm, *refs):
-    (even_out, odd_out, ctext_out, rtext_out, sel_out, table_out, key_out, dec_out, vis_out, req_ref, start_ref, grid_ref,
+    (even_out, odd_out, rtext_out, sel_out, table_out, key_out, dec_out, vis_out, req_ref, start_ref, grid_ref,
      text_ref, x_ref, dec_ref, vis_ref, tmp_ref, sem_ref) = refs
     pairs = (
         (req_hbm, req_ref),
         (start_hbm, start_ref),
         (grid_hbm, grid_ref),
+        (x_hbm, x_ref),
         (text_hbm, text_ref),
-        (x_hbm, x_ref),
         (dec_hbm, dec_ref),
         (vis_hbm, vis_ref),
     )
@@ -93,39 +142,23 @@
     side, img_dev = x_ref.shape[0], x_ref.shape[2]
     half = side // 2
     region = half * half
-    n_img, n_text, length = sel_out.shape[0], ctext_out.shape[0], text_ref.shape[0]
+    n_img, length = sel_out.shape[0], text_ref.shape[0]
     me = me_ref[0]
+    tmp_ref[...] = jnp.zeros_like(tmp_ref)
     for copy in copies[:3]:
         copy.wait()
 
-    found = []
-    for s in range(n_req):
-        source = (me ^ s) * img_dev
-
-        def one_image(k, found, source=source):
-            hit = req_ref[source + k] == me
-            values = (start_ref[source + k], grid_ref[0, source + k] // 2, grid_ref[1, source + k] // 2)
-            return tuple(jnp.where(hit, new, old) for new, old in zip(values, found))
-
-        none = (jnp.int32(NOWHERE), jnp.int32(0), jnp.int32(1))
-        found.append(lax.fori_loop(0, img_dev, one_image, none, unroll=img_dev <= 8))
-
     spot = lax.broadcasted_iota(jnp.int32, (8, length), 1)
-    before = jnp.zeros((8, length), jnp.int32)
     closed = jnp.zeros((8, length), jnp.int32)
-    inside = jnp.zeros((8, length), jnp.int32)
     row = lax.broadcasted_iota(jnp.int32, (n_img, 128), 0)
     pos = jnp.full((n_img, 128), -1, jnp.int32)
     target = jnp.full((n_img, 128), -1, jnp.int32)
     line = lax.broadcasted_iota(jnp.int32, (n_req, 128), 0)
     table = jnp.zeros((n_req, 128), jnp.int32)
-    for s, (start, high, wide) in enumerate(found):
+    for s, (start, high, wide) in enumerate(find_images(n_req, img_dev, me, req_ref, start_ref, grid_ref)):
         count = high * wide
         c = spot - start
-        here = (c >= 0) & (c < region)
-        before += jnp.clip(c, 0, region)
-        inside = jnp.where(here, 1, inside)
-        closed = jnp.where(here & (c >= count), 1, closed)
+        closed = jnp.where((c >= count) & (c < region) & (c >= 0), 1, closed)
         c = row - s * region
         here = (c >= 0) & (c < region)
         pos = jnp.where(here, start + c, pos)
@@ -136,26 +169,20 @@
         table = jnp.where(line == s, start, table)
     table_out[...] = table
     key_out[...] = 1.0 - closed.astype(jnp.float32)
-    rank = jnp.where(inside == 1, -1, spot - before)[0:1]
-    gather = (lax.broadcasted_iota(jnp.int32, (n_text, length), 0) == rank).astype(jnp.bfloat16)
     stays = jnp.where(target >= 0, -1, pos)[:, :1]
     keep = (lax.broadcasted_iota(jnp.int32, (n_img, length), 1) == stays).astype(jnp.bfloat16)
     sel = lax.broadcasted_iota(jnp.int32, (n_img, n_img), 1) == target[:, :1]
     sel_out[...] = sel.astype(jnp.bfloat16)
-    copies[3].wait()
-    text = text_ref[...]
-    ctext_out[...] = jnp.dot(gather, text, preferred_element_type=jnp.float32).astype(jnp.bfloat16)
-    rtext_out[...] = jnp.dot(keep, text, preferred_element_type=jnp.float32).astype(jnp.bfloat16)
-
-    for copy in copies[4:]:
-        copy.wait()
     rows = lax.broadcasted_iota(jnp.int32, (n_req, img_dev), 0)
     cols = lax.broadcasted_iota(jnp.int32, (n_req, img_dev), 1)
     goal = jnp.full((n_req, img_dev), -1, jnp.int32)
     for k in range(img_dev):
         goal = jnp.where(cols == k, req_ref[me * img_dev + k] ^ me, goal)
     onehot = (rows == goal).astype(jnp.bfloat16)
-    tmp_ref[...] = jnp.zeros_like(tmp_ref)
+
+    for copy in copies[3:]:
+        copy.wait()
+    rtext_out[...] = jnp.dot(keep, text_ref[...], preferred_element_type=jnp.float32).astype(jnp.bfloat16)
     for i in range(half):
         for j in range(half):
             total = x_ref[2 * i, 2 * j].astype(jnp.float32)
@@ -174,7 +201,7 @@
             dec_out[t, :, lanes] = dec_ref[at : at + 1, :].astype(jnp.float32)
 
 
-def prepare(me, image_request, slot_start, grids, text, patches, dec_gain, vis_gain, n_req, n_text, n_img):
+def prepare(me, image_request, slot_start, grids, text, patches, dec_gain, vis_gain, n_req, n_img):
     side, _, img_dev, width = patches.shape
     padded = round_up((side // 2) ** 2, 16)
     inputs = (
@@ -188,7 +215,6 @@
     )
     bf16, f32 = jnp.bfloat16, jnp.float32
     outputs = [((n_req // 2, padded, width), bf16)] * 2 + [
-        ((n_text, width), bf16),
         ((n_img, width), bf16),
         ((n_img, n_img), bf16),
         ((n_req, 128), jnp.int32),
@@ -209,20 +235,24 @@
     )(me, *[in_hbm(x) for x in inputs])
 
 
-def mix_kernel(even_ref, odd_ref, *outs):
-    rows = even_ref.shape[1]
+def mix_kernel(region, even_ref, odd_ref, *refs):
+    outs, tmp_ref = refs[:-1], refs[-1]
     for i, out_ref in enumerate(outs):
-        out_ref[:rows] = even_ref[i]
-        out_ref[rows:] = odd_ref[i]
-
-
-def mix_pairs(even, odd):
-    n, rows, width = even.shape
-    return pl.pallas_call(
-        mix_kernel,
-        out_shape=(jax.ShapeDtypeStruct((2 * rows, width), jnp.bfloat16),) * n,
+        tmp_ref[:region] = even_ref[i].astype(jnp.float32)[:region]
+        tmp_ref[region : 2 * region] = odd_ref[i].astype(jnp.float32)[:region]
+        tmp_ref[2 * region :] = jnp.zeros((tmp_ref.shape[0] - 2 * region, tmp_ref.shape[1]), jnp.float32)
+        out_ref[...] = tmp_ref[...].astype(jnp.bfloat16)
+
+
+def mix_pairs(even, odd, region):
+    n, _, width = even.shape
+    rows = round_up(2 * region, 8)
+    return pl.pallas_call(
+        functools.partial(mix_kernel, region),
+        out_shape=(jax.ShapeDtypeStruct((rows, width), jnp.bfloat16),) * n,
         in_specs=vmem_specs(2),
         out_specs=tuple(vmem_specs(n)),
+        scratch_shapes=[pltpu.VMEM((rows, width), jnp.float32)],
         compiler_params=params(4),
         cost_estimate=TINY,
     )(even, odd)
@@ -232,11 +262,8 @@
     recs, (out_ref, tmp_ref) = refs[:-2], refs[-2:]
     done = 0
     for rec_ref in recs:
-        rows = rec_ref.shape[0] // 2
-        pair = rec_ref[...].astype(jnp.float32)
-        for first in (0, rows):
-            tmp_ref[done : done + region] = pair[first : first + region]
-            done += region
+        tmp_ref[done : done + 2 * region] = rec_ref[...].astype(jnp.float32)[: 2 * region]
+        done += 2 * region
     rest = tmp_ref.shape[0] - done
     tmp_ref[done:] = jnp.zeros((rest, tmp_ref.shape[1]), jnp.float32)
     picked = jnp.dot(sel_ref[...], tmp_ref[...].astype(jnp.bfloat16), preferred_element_type=jnp.float32)
@@ -653,13 +680,15 @@
     n_rows = n_req * region
     n_img = round_up(n_rows + 1, 16)
     n_text = round_up(length - (n_rows if img_dev == n_req else 0), 32)
-    even, odd, ctext, rtext, sel, table, key_ok, gains, vis_row = prepare(
-        req_at, image_request, slot_start, grids, text, jnp.transpose(patches, (1, 2, 0, 3)), dec_gain, vis_gain, n_req,
-        n_text, n_img
+    ctext = gather_text(req_at, image_request, slot_start, text, n_req, region, n_text)
+    blocks = near_blocks(ctext, n_ten)
+
+    late_text, ctext = lax.optimization_barrier((text, ctext))
+    even, odd, rtext, sel, table, key_ok, gains, vis_row = prepare(
+        req_at, image_request, slot_start, grids, late_text, jnp.transpose(patches, (1, 2, 0, 3)), dec_gain, vis_gain,
+        n_req, n_img
     )
-    blocks = near_blocks(ctext, n_ten)
-
-    pairs = mix_pairs(even, swap(odd, 1, "req"))
+    pairs = mix_pairs(even, swap(odd, 1, "req"), region)
     received = [pairs[0]] + [swap(pairs[i], 2 * i, "req") for i in range(1, n_req // 2)]
     img_own = pack_images(received, vis_row, rtext, sel, region)
     img_blocks = [img_own] + [swap(img_own, s) for s in range(1, n_ten)]

time: 66.2 us -> 66.6 us (level)
  Pallas kernels: 20.4 us -> 21.8 us
  waiting for transfers between devices: 22.1 us -> 21.4 us
    pallas_call x1 -> x2, Pallas kernels: 0.02 us -> 1.73 us  [the longest x1 1.67 us: gather_text(): pl.pallas_call(functools.partial(text_kernel, n_req, region), out_shape=j...]
    ppermute x19, waiting for transfers between devices: 22.1 us -> 21.4 us  [swap(): return lax.ppermute(x, axis, [(i, i ^ s) for i in range(n)])]
  transfers between devices with their start and end apart: 19 -> 19, of which waited for: 10 -> 10; matrix products, arithmetic and copies ran while one was open for 1% -> 1% of each run, Pallas kernels for 25% -> 29%
where the time goes in v5:
time: 66.6 us; the launch traced here: 66.4 us
  starting transfers between devices  22.2 us (33%)
  Pallas kernels  21.8 us (33%)
  waiting for transfers between devices  21.4 us (32%)
    ppermute x19, starting transfers between devices, swap(): return lax.ppermute(x, axis, [(i, i ^ s) for i in range(n)])  22.2 us
    ppermute x19, waiting for transfers between devices, swap(): return lax.ppermute(x, axis, [(i, i ^ s) for i in range(n)])  21.4 us
    pallas_call x1, Pallas kernels, own_part(): pl.pallas_call(own_kernel, out_shape=(jax.ShapeDtypeStruct((3, rows, cols...  4.86 us
    pallas_call x1, Pallas kernels, image_part(): pl.pallas_call(functools.partial(image_kernel, n_rows, len(blocks)), out_...  2.65 us
    pallas_call x1, Pallas kernels, near_part(): pl.pallas_call(functools.partial(near_kernel, near, pieces), out_shape=(j...  2.28 us
    pallas_call x1, Pallas kernels, tail_part(): pl.pallas_call(functools.partial(tail_kernel, far), out_shape=(jax.ShapeD...  2.25 us
    pallas_call x1, Pallas kernels, prepare(): pl.pallas_call(functools.partial(prep_kernel, n_req), out_shape=tuple((ja...  2.2 us
    pallas_call x3, Pallas kernels, out_part(): pl.pallas_call(functools.partial(out_kernel, away), out_shape=(jax.ShapeD...  1.96 us
  transfers between devices with their start and end apart: 19, of which 10 were waited for; matrix products, arithmetic and copies ran while one was open for 1% of the time, Pallas kernels for 29%

profile of v5, /device:TPU:0, one launch (start us, length us, event | category | flops | bytes accessed | tf_op | source)
XLA Modules:
  0.0 66.4 jit_solution(13234642569287790591)
XLA Ops:
  0.0 1.7 %shard_map.91.x_ref = bf16[320,1024]{1,0:T(8,128)(2,1)S(1)} custom-call(s32[1]{0:T(128)} %bitcast.me_ref, s32[64]{0:T(128)} %req_hbm.3, s32[64]{0:T(128)} %start_hbm.3, bf16[384,1024]{1,0:T(8,128)(2,1)} %text_hbm.2), custom_call_target="tpu_custom_call" | custom-call | tf_op jit(solution)/shard_map/pallas_call | solution.py:117
  1.7 3.0 %collective-permute-start = (bf16[320,1024]{1,0:T(8,128)(2,1)S(1)}, bf16[320,1024]{1,0:T(8,128)(2,1)S(1)}, u32[]{:S(2)}, u32[]{:S(2)}) collective-permute-start(bf16[320,1024]{1,0:T(8,128)(2,1)S(1)} %shard_map.91.x_ref), channel_id=1, source_target_pairs={{0,1},{1,0},{2,3},{3,2},{4,5},{5,4},{6,7},{7,6},{8,9},{9,8},{10,11... | collective-permute-start | bytes 1966088 | tf_op jit(solution)/shard_map/ppermute | solution.py:23
  4.7 1.5 %collective-permute-start.1 = (bf16[320,1024]{1,0:T(8,128)(2,1)S(1)}, bf16[320,1024]{1,0:T(8,128)(2,1)S(1)}, u32[]{:S(2)}, u32[]{:S(2)}) collective-permute-start(bf16[320,1024]{1,0:T(8,128)(2,1)S(1)} %shard_map.91.x_ref), channel_id=1, source_target_pairs={{0,2},{1,3},{2,0},{3,1},{4,6},{5,7},{6,4},{7,5},{8,10},{9,11},{10,... | collective-permute-start | bytes 1966088 | tf_op jit(solution)/shard_map/ppermute | solution.py:23
  6.2 2.2 %shard_map.92 = (bf16[4,16,1024]{2,1,0:T(8,128)(2,1)S(1)}, bf16[4,16,1024]{2,1,0:T(8,128)(2,1)S(1)}, bf16[80,1024]{1,0:T(8,128)(2,1)S(1)}, bf16[80,80]{1,0:T(8,1...) custom-call(s32[1]{0:T(128)} %bitcast.me_ref, ...), custom_call_target="tpu_custom_call" | custom-call | tf_op jit(solution)/shard_map/pallas_call | solution.py:225
  8.4 0.1 collective-permute-start.2
  8.5 1.3 %collective-permute-done.2.odd_ref = bf16[4,16,1024]{2,1,0:T(8,128)(2,1)S(1)} collective-permute-done((bf16[4,16,1024]{2,1,0:T(8,128)(2,1)S(1)}, bf16[4,16,1024]{2,1,0:T(8,128)(2,1)S(1)}, u32[]{:S(2)}, u32[]{:S(2)}) %collective-permute-start.2) | collective-permute-done | bytes 131104 | tf_op jit(solution)/shard_map/ppermute | solution.py:23
  9.8 0.1 shard_map.93
  9.9 1.6 %collective-permute-start.3 = (bf16[24,1024]{1,0:T(8,128)(2,1)S(1)}, bf16[24,1024]{1,0:T(8,128)(2,1)S(1)}, u32[]{:S(2)}, u32[]{:S(2)}) collective-permute-start(bf16[24,1024]{1,0:T(8,128)(2,1)S(1)} %get-tuple-element.68), channel_id=1, source_target_pairs={{0,8},{4,12},{8,0},{12,4},{16,24},{20,28},{24,16},{28,20},{1,9},{5... | collective-permute-start | bytes 147464 | tf_op jit(solution)/shard_map/ppermute | solution.py:23
  11.5 2.6 %collective-permute-start.4 = (bf16[24,1024]{1,0:T(8,128)(2,1)S(1)}, bf16[24,1024]{1,0:T(8,128)(2,1)S(1)}, u32[]{:S(2)}, u32[]{:S(2)}) collective-permute-start(bf16[24,1024]{1,0:T(8,128)(2,1)S(1)} %get-tuple-element.69), channel_id=1, source_target_pairs={{0,16},{4,20},{8,24},{12,28},{16,0},{20,4},{24,8},{28,12},{1,17},{... | collective-permute-start | bytes 147464 | tf_op jit(solution)/shard_map/ppermute | solution.py:23
  14.1 0.2 collective-permute-start.5
  14.3 0.0 collective-permute-done.3.refs_1_
  14.3 3.1 %collective-permute-done.4.refs_2_ = bf16[24,1024]{1,0:T(8,128)(2,1)S(1)} collective-permute-done((bf16[24,1024]{1,0:T(8,128)(2,1)S(1)}, bf16[24,1024]{1,0:T(8,128)(2,1)S(1)}, u32[]{:S(2)}, u32[]{:S(2)}) %collective-permute-start.4) | collective-permute-done | bytes 49184 | tf_op jit(solution)/shard_map/ppermute | solution.py:23
  17.4 2.6 %collective-permute-done.5.refs_3_ = bf16[24,1024]{1,0:T(8,128)(2,1)S(1)} collective-permute-done((bf16[24,1024]{1,0:T(8,128)(2,1)S(1)}, bf16[24,1024]{1,0:T(8,128)(2,1)S(1)}, u32[]{:S(2)}, u32[]{:S(2)}) %collective-permute-start.5) | collective-permute-done | bytes 49184 | tf_op jit(solution)/shard_map/ppermute | solution.py:23
  20.0 0.2 shard_map.94.refs_0_
  20.2 0.6 collective-permute-start.6
  20.8 0.5 collective-permute-start.7
  21.3 2.4 %collective-permute-start.8 = (bf16[80,1024]{1,0:T(8,128)(2,1)S(1)}, bf16[80,1024]{1,0:T(8,128)(2,1)S(1)}, u32[]{:S(2)}, u32[]{:S(2)}) collective-permute-start(bf16[80,1024]{1,0:T(8,128)(2,1)S(1)} %shard_map.94.refs_0_), channel_id=1, source_target_pairs={{0,3},{1,2},{2,1},{3,0},{4,7},{5,6},{6,5},{7,4},{8,11},{9,10},{10,... | collective-permute-start | bytes 491528 | tf_op jit(solution)/shard_map/ppermute | solution.py:23
  23.8 4.9 %shard_map.95 = (f32[3,320,512]{2,1,0:T(8,128)S(1)}, f32[320,128]{1,0:T(8,128)S(1)}, bf16[4,3,1024,512]{3,2,1,0:T(8,128)(2,1)S(1)}) custom-call(s32[1]{0:T(128)} %bitcast.5.me_ref, bf16[320,1024]{1,0:T(8,128)(2,1)S(1)} %shard_map.91.x_ref, f32[4,1,1024]{2,1,0:T(1,128)S(1)} %get-tuple-element.60.gain_ref.refs_2_.refs_4_, bf16[3,4096,512]{2,1,0:T(8,128)(2,1)} %bitcast.9), custom_call_target="tpu_custom_call" | custom-call | tf_op jit(solution)/shard_map/pallas_call | solution.py:356
  28.6 0.0 collective-permute-done.refs_0_
  28.6 0.0 collective-permute-done.1.refs_1_
  28.7 0.6 collective-permute-start.9
  29.3 0.6 collective-permute-start.12
  29.9 2.3 %shard_map.96 = (f32[3,320,512]{2,1,0:T(8,128)S(1)}, f32[320,128]{1,0:T(8,128)S(1)}) custom-call(s32[1]{0:T(128)} %bitcast.5.me_ref, bf16[320,1024]{1,0:T(8,128)(2,1)S(1)} %collective-permute-done.refs_0_, bf16[320,1024]{1,0:T(8,128)(2,1)S(1)} %collective-permute-done.1.refs_1_, f32[4,1,1024]{2,1,0:T(1,128)S(1)} %get-tuple-element.60.gain_ref.refs_2_.refs_4_, ...), custom_call_target="tpu_custom_call" | custom-call | flops 99999997952 | tf_op jit(solution)/shard_map/pallas_call | solution.py:400
  32.2 0.7 %shard_map.97 = (bf16[384,320]{1,0:T(8,128)(2,1)S(1)}, bf16[384,80]{1,0:T(8,128)(2,1)S(1)}, f32[384,128]{1,0:T(8,128)S(1)}) custom-call(s32[8,128]{1,0:T(8,128)S(1)} %get-tuple-element.76.table_ref), custom_call_target="tpu_custom_call" | custom-call | tf_op jit(solution)/shard_map/pallas_call | solution.py:305
  32.9 0.0 collective-permute-done.6.refs_1_
  32.9 0.0 collective-permute-done.7.refs_2_
  32.9 0.0 collective-permute-done.8.refs_3_
  32.9 2.7 %shard_map.98 = (bf16[3,80,512]{2,1,0:T(8,128)(2,1)S(1)}, bf16[80,1024]{1,0:T(8,128)(2,1)S(1)}, bf16[512,4096]{1,0:T(8,128)(2,1)S(1)}) custom-call(s32[1]{0:T(128)} %bitcast.5.me_ref, bf16[80,1024]{1,0:T(8,128)(2,1)S(1)} %shard_map.94.refs_0_, bf16[80,1024]{1,0:T(8,128)(2,1)S(1)} %collective-permute-done.6.refs_1_, ...), custom_call_target="tpu_custom_call" | custom-call | tf_op jit(solution)/shard_map/pallas_call | solution.py:446
  35.6 0.4 collective-permute-done.9.top_ref
  36.0 1.7 %shard_map.99 = (bf16[3,160,512]{2,1,0:T(8,128)(2,1)S(1)}, bf16[3,160,512]{2,1,0:T(8,128)(2,1)S(1)}, bf16[160,512]{1,0:T(8,128)(2,1)S(1)}, bf16[160,512]{1,0:T(8,128)(2,1)S(1)}, bf16[160,512]{1,0:T(8,128)(2,1)S(1)}) custom-call(s32[1]{0:T(128)} %bitcast.5.me_ref, bf16[160,1024]{1,0:T(8,128)(2,1)S(1)} %collective-permute-done.9.top_ref, ...), custom_call_target="tpu_custom_call" | custom-call | tf_op jit(solution)/shard_map/pallas_call | solution.py:525
  37.7 1.2 %collective-permute-start.10 = (bf16[160,512]{1,0:T(8,128)(2,1)S(1)}, bf16[160,512]{1,0:T(8,128)(2,1)S(1)}, u32[]{:S(2)}, u32[]{:S(2)}) collective-permute-start(bf16[160,512]{1,0:T(8,128)(2,1)S(1)} %get-tuple-element.92), channel_id=1, source_target_pairs={{0,1},{1,0},{2,3},{3,2},{4,5},{5,4},{6,7},{7,6},{8,9},{9,8},{10,11... | collective-permute-start | bytes 491528 | tf_op jit(solution)/shard_map/ppermute | solution.py:23
  38.8 1.5 %collective-permute-start.11 = (bf16[160,512]{1,0:T(8,128)(2,1)S(1)}, bf16[160,512]{1,0:T(8,128)(2,1)S(1)}, u32[]{:S(2)}, u32[]{:S(2)}) collective-permute-start(bf16[160,512]{1,0:T(8,128)(2,1)S(1)} %get-tuple-element.93), channel_id=1, source_target_pairs={{0,2},{1,3},{2,0},{3,1},{4,6},{5,7},{6,4},{7,5},{8,10},{9,11},{10,... | collective-permute-start | bytes 491528 | tf_op jit(solution)/shard_map/ppermute | solution.py:23
  40.4 0.0 collective-permute-done.12.bottom_ref
  40.4 2.3 %shard_map.100 = (bf16[224,512]{1,0:T(8,128)(2,1)S(1)}, bf16[224,512]{1,0:T(8,128)(2,1)S(1)}, bf16[224,512]{1,0:T(8,128)(2,1)S(1)}) custom-call(s32[1]{0:T(128)} %bitcast.5.me_ref, bf16[160,1024]{1,0:T(8,128)(2,1)S(1)} %collective-permute-done.12.bottom_ref, f32[4,1,1024]{2,1,0:T(1,128)S(1)} %get-tuple-element.60.gain_ref.refs_2_.refs_4_, ...), custom_call_target="tpu_custom_call" | custom-call | flops 10000000000 | tf_op jit(solution)/shard_map/pallas_call | solution.py:564
  42.6 0.6 collective-permute-start.17
  43.2 0.9 %collective-permute-start.15 = (bf16[224,512]{1,0:T(8,128)(2,1)S(1)}, bf16[224,512]{1,0:T(8,128)(2,1)S(1)}, u32[]{:S(2)}, u32[]{:S(2)}) collective-permute-start(bf16[224,512]{1,0:T(8,128)(2,1)S(1)} %get-tuple-element.107), channel_id=1, source_target_pairs={{0,1},{1,0},{2,3},{3,2},{4,5},{5,4},{6,7},{7,6},{8,9},{9,8},{10,11... | collective-permute-start | bytes 688136 | tf_op jit(solution)/shard_map/ppermute | solution.py:23
  44.1 0.0 collective-permute-done.10
  44.2 1.7 %collective-permute-done.11 = bf16[160,512]{1,0:T(8,128)(2,1)S(1)} collective-permute-done((bf16[160,512]{1,0:T(8,128)(2,1)S(1)}, bf16[160,512]{1,0:T(8,128)(2,1)S(1)}, u32[]{:S(2)}, u32[]{:S(2)}) %collective-permute-start.11) | collective-permute-done | bytes 163872 | tf_op jit(solution)/shard_map/ppermute | solution.py:23
  45.9 0.8 %shard_map.103 = (bf16[384,512]{1,0:T(8,128)(2,1)S(1)}, bf16[384,512]{1,0:T(8,128)(2,1)S(1)}) custom-call(s32[1]{0:T(128)} %bitcast.5.me_ref, bf16[160,512]{1,0:T(8,128)(2,1)S(1)} %get-tuple-element.99.head_ref, bf16[224,512]{1,0:T(8,128)(2,1)S(1)} %get-tuple-element.100.tail_ref, bf16[512,4096]{1,0:T(8,128)(2,1)S(1)} %get-tuple-element.91.w_out_ref.w_ref), custom_call_target="tpu_custom_call" | custom-call | flops 1000000000 | tf_op jit(solution)/shard_map/pallas_call | solution.py:589
  46.6 1.7 %collective-permute-start.14 = (bf16[384,512]{1,0:T(8,128)(2,1)S(1)}, bf16[384,512]{1,0:T(8,128)(2,1)S(1)}, u32[]{:S(2)}, u32[]{:S(2)}) collective-permute-start(bf16[384,512]{1,0:T(8,128)(2,1)S(1)} %get-tuple-element.104), channel_id=1, source_target_pairs={{0,2},{1,3},{2,0},{3,1},{4,6},{5,7},{6,4},{7,5},{8,10},{9,11},{10,... | collective-permute-start | bytes 1179656 | tf_op jit(solution)/shard_map/ppermute | solution.py:23
  48.3 0.6 shard_map.102
  48.9 0.0 copy-start
  49.0 0.5 collective-permute-start.13
  49.5 1.7 %collective-permute-done.17 = bf16[224,512]{1,0:T(8,128)(2,1)S(1)} collective-permute-done((bf16[224,512]{1,0:T(8,128)(2,1)S(1)}, bf16[224,512]{1,0:T(8,128)(2,1)S(1)}, u32[]{:S(2)}, u32[]{:S(2)}) %collective-permute-start.17) | collective-permute-done | bytes 229408 | tf_op jit(solution)/shard_map/ppermute | solution.py:23
  51.2 0.1 add_convert_fusion.1
  51.3 0.6 collective-permute-start.18
  51.9 0.0 collective-permute-done.15
  51.9 0.1 add_convert_fusion.2
  52.0 1.4 %collective-permute-start.16 = (bf16[384,512]{1,0:T(8,128)(2,1)S(1)}, bf16[384,512]{1,0:T(8,128)(2,1)S(1)}, u32[]{:S(2)}, u32[]{:S(2)}) collective-permute-start(bf16[384,512]{1,0:T(8,128)(2,1)S(1)} %add_convert_fusion.2), channel_id=1, source_target_pairs={{0,2},{1,3},{2,0},{3,1},{4,6},{5,7},{6,4},{7,5},{8,10},{9,11},{10,... | collective-permute-start | bytes 1179656 | tf_op jit(solution)/shard_map/ppermute | solution.py:23
  53.4 0.1 slice_reduce_fusion
  53.6 0.0 copy-done
  53.6 0.4 add_convert_fusion.base_ref
  53.9 0.6 shard_map.101
  54.5 5.1 %collective-permute-done.14.refs_3_ = bf16[384,512]{1,0:T(8,128)(2,1)S(1)} collective-permute-done((bf16[384,512]{1,0:T(8,128)(2,1)S(1)}, bf16[384,512]{1,0:T(8,128)(2,1)S(1)}, u32[]{:S(2)}, u32[]{:S(2)}) %collective-permute-start.14) | collective-permute-done | bytes 393248 | tf_op jit(solution)/shard_map/ppermute | solution.py:23
  59.7 1.0 %collective-permute-done.13.refs_1_ = bf16[384,512]{1,0:T(8,128)(2,1)S(1)} collective-permute-done((bf16[384,512]{1,0:T(8,128)(2,1)S(1)}, bf16[384,512]{1,0:T(8,128)(2,1)S(1)}, u32[]{:S(2)}, u32[]{:S(2)}) %collective-permute-start.13) | collective-permute-done | bytes 393248 | tf_op jit(solution)/shard_map/ppermute | solution.py:23
  60.6 0.3 shard_map.104.base_ref
  60.9 3.9 %collective-permute-done.18.refs_1_ = bf16[384,512]{1,0:T(8,128)(2,1)S(1)} collective-permute-done((bf16[384,512]{1,0:T(8,128)(2,1)S(1)}, bf16[384,512]{1,0:T(8,128)(2,1)S(1)}, u32[]{:S(2)}, u32[]{:S(2)}) %collective-permute-start.18) | collective-permute-done | bytes 393248 | tf_op jit(solution)/shard_map/ppermute | solution.py:23
  64.8 0.5 collective-permute-done.16.refs_0_
  65.3 1.0 %shard_map.105 = bf16[384,1024]{1,0:T(8,128)(2,1)} custom-call(f32[384,1024]{1,0:T(8,128)S(1)} %shard_map.104.base_ref, bf16[384,512]{1,0:T(8,128)(2,1)S(1)} %collective-permute-done.16.refs_0_, bf16[384,512]{1,0:T(8,128)(2,1)S(1)} %collective-permute-done.18.refs_1_), custom_call_target="tpu_custom_call" | custom-call | tf_op jit(solution)/shard_map/pallas_call | solution.py:637
  (2 shorter events, 0.0 us)
Async XLA Ops:
  1.7 27.0 %collective-permute-start = (bf16[320,1024]{1,0:T(8,128)(2,1)S(1)}, bf16[320,1024]{1,0:T(8,128)(2,1)S(1)}, u32[]{:S(2)}, u32[]{:S(2)}) collective-permute-start(bf16[320,1024]{1,0:T(8,128)(2,1)S(1)} %shard_map.91.x_ref), channel_id=1, source_target_pairs={{0,1},{1,0},{2,3},{3,2},{4,5},{5,4},{6,7},{7,6},{8,9},{9,8},{10,11... | collective-permute-start | bytes 1966088 | tf_op jit(solution)/shard_map/ppermute | solution.py:23
  4.7 24.0 %collective-permute-start.1 = (bf16[320,1024]{1,0:T(8,128)(2,1)S(1)}, bf16[320,1024]{1,0:T(8,128)(2,1)S(1)}, u32[]{:S(2)}, u32[]{:S(2)}) collective-permute-start(bf16[320,1024]{1,0:T(8,128)(2,1)S(1)} %shard_map.91.x_ref), channel_id=1, source_target_pairs={{0,2},{1,3},{2,0},{3,1},{4,6},{5,7},{6,4},{7,5},{8,10},{9,11},{10,... | collective-permute-start | bytes 1966088 | tf_op jit(solution)/shard_map/ppermute | solution.py:23
  8.4 1.4 %collective-permute-start.2 = (bf16[4,16,1024]{2,1,0:T(8,128)(2,1)S(1)}, bf16[4,16,1024]{2,1,0:T(8,128)(2,1)S(1)}, u32[]{:S(2)}, u32[]{:S(2)}) collective-permute-start(bf16[4,16,1024]{2,1,0:T(8,128)(2,1)S(1)} %get-tuple-element.66), channel_id=1, source_target_pairs={{0,4},{4,0},{8,12},{12,8},{16,20},{20,16},{24,28},{28,24},{1,5},{5... | collective-permute-start | bytes 393224 | tf_op jit(solution)/shard_map/ppermute | solution.py:23
  9.9 4.5 %collective-permute-start.3 = (bf16[24,1024]{1,0:T(8,128)(2,1)S(1)}, bf16[24,1024]{1,0:T(8,128)(2,1)S(1)}, u32[]{:S(2)}, u32[]{:S(2)}) collective-permute-start(bf16[24,1024]{1,0:T(8,128)(2,1)S(1)} %get-tuple-element.68), channel_id=1, source_target_pairs={{0,8},{4,12},{8,0},{12,4},{16,24},{20,28},{24,16},{28,20},{1,9},{5... | collective-permute-start | bytes 147464 | tf_op jit(solution)/shard_map/ppermute | solution.py:23
  11.5 5.9 %collective-permute-start.4 = (bf16[24,1024]{1,0:T(8,128)(2,1)S(1)}, bf16[24,1024]{1,0:T(8,128)(2,1)S(1)}, u32[]{:S(2)}, u32[]{:S(2)}) collective-permute-start(bf16[24,1024]{1,0:T(8,128)(2,1)S(1)} %get-tuple-element.69), channel_id=1, source_target_pairs={{0,16},{4,20},{8,24},{12,28},{16,0},{20,4},{24,8},{28,12},{1,17},{... | collective-permute-start | bytes 147464 | tf_op jit(solution)/shard_map/ppermute | solution.py:23
  14.1 5.9 %collective-permute-start.5 = (bf16[24,1024]{1,0:T(8,128)(2,1)S(1)}, bf16[24,1024]{1,0:T(8,128)(2,1)S(1)}, u32[]{:S(2)}, u32[]{:S(2)}) collective-permute-start(bf16[24,1024]{1,0:T(8,128)(2,1)S(1)} %get-tuple-element.70), channel_id=1, source_target_pairs={{0,24},{4,28},{8,16},{12,20},{16,8},{20,12},{24,0},{28,4},{1,25},{... | collective-permute-start | bytes 147464 | tf_op jit(solution)/shard_map/ppermute | solution.py:23
  20.2 12.7 %collective-permute-start.6 = (bf16[80,1024]{1,0:T(8,128)(2,1)S(1)}, bf16[80,1024]{1,0:T(8,128)(2,1)S(1)}, u32[]{:S(2)}, u32[]{:S(2)}) collective-permute-start(bf16[80,1024]{1,0:T(8,128)(2,1)S(1)} %shard_map.94.refs_0_), channel_id=1, source_target_pairs={{0,1},{1,0},{2,3},{3,2},{4,5},{5,4},{6,7},{7,6},{8,9},{9,8},{10,11... | collective-permute-start | bytes 491528 | tf_op jit(solution)/shard_map/ppermute | solution.py:23
  20.8 12.1 %collective-permute-start.7 = (bf16[80,1024]{1,0:T(8,128)(2,1)S(1)}, bf16[80,1024]{1,0:T(8,128)(2,1)S(1)}, u32[]{:S(2)}, u32[]{:S(2)}) collective-permute-start(bf16[80,1024]{1,0:T(8,128)(2,1)S(1)} %shard_map.94.refs_0_), channel_id=1, source_target_pairs={{0,2},{1,3},{2,0},{3,1},{4,6},{5,7},{6,4},{7,5},{8,10},{9,11},{10,... | collective-permute-start | bytes 491528 | tf_op jit(solution)/shard_map/ppermute | solution.py:23
  21.3 11.6 %collective-permute-start.8 = (bf16[80,1024]{1,0:T(8,128)(2,1)S(1)}, bf16[80,1024]{1,0:T(8,128)(2,1)S(1)}, u32[]{:S(2)}, u32[]{:S(2)}) collective-permute-start(bf16[80,1024]{1,0:T(8,128)(2,1)S(1)} %shard_map.94.refs_0_), channel_id=1, source_target_pairs={{0,3},{1,2},{2,1},{3,0},{4,7},{5,6},{6,5},{7,4},{8,11},{9,10},{10,... | collective-permute-start | bytes 491528 | tf_op jit(solution)/shard_map/ppermute | solution.py:23
  28.7 7.3 %collective-permute-start.9 = (bf16[160,1024]{1,0:T(8,128)(2,1)S(1)}, bf16[160,1024]{1,0:T(8,128)(2,1)S(1)}, u32[]{:S(2)}, u32[]{:S(2)}) collective-permute-start(bf16[160,1024]{1,0:T(8,128)(2,1)S(1)} %slice.10), channel_id=1, source_target_pairs={{0,1},{1,0},{2,3},{3,2},{4,5},{5,4},{6,7},{7,6},{8,9},{9,8},{10,11... | collective-permute-start | bytes 983048 | tf_op jit(solution)/shard_map/ppermute | solution.py:23
  29.3 11.1 %collective-permute-start.12 = (bf16[160,1024]{1,0:T(8,128)(2,1)S(1)}, bf16[160,1024]{1,0:T(8,128)(2,1)S(1)}, u32[]{:S(2)}, u32[]{:S(2)}) collective-permute-start(bf16[160,1024]{1,0:T(8,128)(2,1)S(1)} %slice.11), channel_id=1, source_target_pairs={{0,2},{1,3},{2,0},{3,1},{4,6},{5,7},{6,4},{7,5},{8,10},{9,11},{10,... | collective-permute-start | bytes 983048 | tf_op jit(solution)/shard_map/ppermute | solution.py:23
  37.7 6.5 %collective-permute-start.10 = (bf16[160,512]{1,0:T(8,128)(2,1)S(1)}, bf16[160,512]{1,0:T(8,128)(2,1)S(1)}, u32[]{:S(2)}, u32[]{:S(2)}) collective-permute-start(bf16[160,512]{1,0:T(8,128)(2,1)S(1)} %get-tuple-element.92), channel_id=1, source_target_pairs={{0,1},{1,0},{2,3},{3,2},{4,5},{5,4},{6,7},{7,6},{8,9},{9,8},{10,11... | collective-permute-start | bytes 491528 | tf_op jit(solution)/shard_map/ppermute | solution.py:23
  38.8 7.0 %collective-permute-start.11 = (bf16[160,512]{1,0:T(8,128)(2,1)S(1)}, bf16[160,512]{1,0:T(8,128)(2,1)S(1)}, u32[]{:S(2)}, u32[]{:S(2)}) collective-permute-start(bf16[160,512]{1,0:T(8,128)(2,1)S(1)} %get-tuple-element.93), channel_id=1, source_target_pairs={{0,2},{1,3},{2,0},{3,1},{4,6},{5,7},{6,4},{7,5},{8,10},{9,11},{10,... | collective-permute-start | bytes 491528 | tf_op jit(solution)/shard_map/ppermute | solution.py:23
  42.6 8.6 %collective-permute-start.17 = (bf16[224,512]{1,0:T(8,128)(2,1)S(1)}, bf16[224,512]{1,0:T(8,128)(2,1)S(1)}, u32[]{:S(2)}, u32[]{:S(2)}) collective-permute-start(bf16[224,512]{1,0:T(8,128)(2,1)S(1)} %get-tuple-element.110), channel_id=1, source_target_pairs={{0,2},{1,3},{2,0},{3,1},{4,6},{5,7},{6,4},{7,5},{8,10},{9,11},{10,... | collective-permute-start | bytes 688136 | tf_op jit(solution)/shard_map/ppermute | solution.py:23
  43.2 8.7 %collective-permute-start.15 = (bf16[224,512]{1,0:T(8,128)(2,1)S(1)}, bf16[224,512]{1,0:T(8,128)(2,1)S(1)}, u32[]{:S(2)}, u32[]{:S(2)}) collective-permute-start(bf16[224,512]{1,0:T(8,128)(2,1)S(1)} %get-tuple-element.107), channel_id=1, source_target_pairs={{0,1},{1,0},{2,3},{3,2},{4,5},{5,4},{6,7},{7,6},{8,9},{9,8},{10,11... | collective-permute-start | bytes 688136 | tf_op jit(solution)/shard_map/ppermute | solution.py:23
  46.6 13.0 %collective-permute-start.14 = (bf16[384,512]{1,0:T(8,128)(2,1)S(1)}, bf16[384,512]{1,0:T(8,128)(2,1)S(1)}, u32[]{:S(2)}, u32[]{:S(2)}) collective-permute-start(bf16[384,512]{1,0:T(8,128)(2,1)S(1)} %get-tuple-element.104), channel_id=1, source_target_pairs={{0,2},{1,3},{2,0},{3,1},{4,6},{5,7},{6,4},{7,5},{8,10},{9,11},{10,... | collective-permute-start | bytes 1179656 | tf_op jit(solution)/shard_map/ppermute | solution.py:23
  48.9 4.6 %copy-start = (bf16[384,1024]{1,0:T(8,128)(2,1)S(1)}, bf16[384,1024]{1,0:T(8,128)(2,1)}, u32[]{:S(2)}) copy-start(bf16[384,1024]{1,0:T(8,128)(2,1)} %text_hbm.2) | copy-start | bytes 2359300
  49.0 11.7 %collective-permute-start.13 = (bf16[384,512]{1,0:T(8,128)(2,1)S(1)}, bf16[384,512]{1,0:T(8,128)(2,1)S(1)}, u32[]{:S(2)}, u32[]{:S(2)}) collective-permute-start(bf16[384,512]{1,0:T(8,128)(2,1)S(1)} %get-tuple-element.102), channel_id=1, source_target_pairs={{0,1},{1,0},{2,3},{3,2},{4,5},{5,4},{6,7},{7,6},{8,9},{9,8},{10,11... | collective-permute-start | bytes 1179656 | tf_op jit(solution)/shard_map/ppermute | solution.py:23
  51.3 13.5 %collective-permute-start.18 = (bf16[384,512]{1,0:T(8,128)(2,1)S(1)}, bf16[384,512]{1,0:T(8,128)(2,1)S(1)}, u32[]{:S(2)}, u32[]{:S(2)}) collective-permute-start(bf16[384,512]{1,0:T(8,128)(2,1)S(1)} %add_convert_fusion.1), channel_id=1, source_target_pairs={{0,1},{1,0},{2,3},{3,2},{4,5},{5,4},{6,7},{7,6},{8,9},{9,8},{10,11... | collective-permute-start | bytes 1179656 | tf_op jit(solution)/shard_map/ppermute | solution.py:23
  52.0 13.3 %collective-permute-start.16 = (bf16[384,512]{1,0:T(8,128)(2,1)S(1)}, bf16[384,512]{1,0:T(8,128)(2,1)S(1)}, u32[]{:S(2)}, u32[]{:S(2)}) collective-permute-start(bf16[384,512]{1,0:T(8,128)(2,1)S(1)} %add_convert_fusion.2), channel_id=1, source_target_pairs={{0,2},{1,3},{2,0},{3,1},{4,6},{5,7},{6,4},{7,5},{8,10},{9,11},{10,... | collective-permute-start | bytes 1179656 | tf_op jit(solution)/shard_map/ppermute | solution.py:23

commit v6 on v5

--- a/solution.py
+++ b/solution.py
@@ -42,7 +42,7 @@
 def halves(block):
     if isinstance(block, tuple):
         return block
-    half = block.shape[0] // 2
+    half = round_up(block.shape[0] // 2, 16)
     return block[:half], block[half:]
 
 
@@ -411,43 +411,49 @@
     )(me, *[h for b in blocks for h in b], gain, held, acc, ss)
 
 
-def image_kernel(n_rows, n_blk, me_ref, *refs):
-    x_refs, refs = refs[:n_blk], refs[n_blk:]
-    gain_ref, sel_ref, held_ref, w_out_ref, qkv_ref, own_ref, w_out_held, sem_ref = refs
+def image_rows(x, vis_row, is_img, gain):
+    xf = x.astype(jnp.float32)
+    y = jnp.where(is_img, xf * vis_row, xf)
+    sums = [jnp.sum(t * t, axis=1, keepdims=True) for t in (xf, y)]
+    return (y * gain).astype(jnp.bfloat16), *sums
+
+
+def image_flags(sel_ref):
+    return jnp.sum(sel_ref[...].astype(jnp.float32), axis=1, keepdims=True) > 0.5
+
+
+def image_kernel(n_rows, away, me_ref, *refs):
+    x_refs, refs = refs[: len(away)], refs[len(away) :]
+    gain_ref, sel_ref, held_ref, w_out_ref, acc_ref, sums_ref, w_out_held, sem_ref = refs
     copy = pltpu.make_async_copy(w_out_ref, w_out_held, sem_ref)
     copy.start()
-    is_img = jnp.sum(sel_ref[...].astype(jnp.float32), axis=1, keepdims=True) > 0.5
-    total = 0.0
-    for s in range(n_blk):
-        xf = x_refs[s][...].astype(jnp.float32)
-        total += jnp.sum(xf * xf, axis=1, keepdims=True)
-    scale = lax.rsqrt(total / D + EPS)
-    total = 0.0
+    is_img = image_flags(sel_ref)
+    before, after = 0.0, 0.0
     scaled = []
-    for s in range(n_blk):
-        xf = x_refs[s][...].astype(jnp.float32)
-        merged = jnp.where(is_img, xf * scale * xf[n_rows : n_rows + 1], xf).astype(jnp.bfloat16)
-        if s == 0:
-            own_ref[...] = merged
-        mf = merged.astype(jnp.float32)
-        total += jnp.sum(mf * mf, axis=1, keepdims=True)
-        scaled.append((mf * gain_ref[me_ref[0] ^ s]).astype(jnp.bfloat16))
-    scale = lax.rsqrt(total / D + EPS)
+    for s, x_ref in zip(away, x_refs):
+        x = x_ref[...]
+        vis_row = x.astype(jnp.float32)[n_rows : n_rows + 1]
+        rows, one, two = image_rows(x, vis_row, is_img, gain_ref[me_ref[0] ^ s])
+        scaled.append(rows)
+        before += one
+        after += two
+    sums_ref[0] = jnp.broadcast_to(before, sums_ref.shape[1:])
+    sums_ref[1] = jnp.broadcast_to(after, sums_ref.shape[1:])
     for j in range(3):
         acc = 0.0
-        for s in range(n_blk):
-            acc += jnp.dot(scaled[s], held_ref[s, j], preferred_element_type=jnp.float32)
-        qkv_ref[j] = (acc * scale).astype(jnp.bfloat16)
+        for s, rows in zip(away, scaled):
+            acc += jnp.dot(rows, held_ref[s, j], preferred_element_type=jnp.float32)
+        acc_ref[j] = acc
     copy.wait()
 
 
-def image_part(me, blocks, gain, sel, held, w_out, n_rows):
-    n_img, width = blocks[0].shape
-    return pl.pallas_call(
-        functools.partial(image_kernel, n_rows, len(blocks)),
+def image_part(away, me, blocks, gain, sel, held, w_out, n_rows):
+    n_img = sel.shape[0]
+    return pl.pallas_call(
+        functools.partial(image_kernel, n_rows, away),
         out_shape=(
-            jax.ShapeDtypeStruct((3, n_img, held.shape[3]), jnp.bfloat16),
-            jax.ShapeDtypeStruct((n_img, width), jnp.bfloat16),
+            jax.ShapeDtypeStruct((3, n_img, held.shape[3]), jnp.float32),
+            jax.ShapeDtypeStruct((2, n_img, 128), jnp.float32),
             pltpu.VMEM(w_out.shape, w_out.dtype),
         ),
         in_specs=[pl.BlockSpec(memory_space=pltpu.SMEM)]
@@ -456,8 +462,58 @@
         out_specs=tuple(vmem_specs(3)),
         scratch_shapes=[pltpu.SemaphoreType.DMA],
         compiler_params=params(12),
-        cost_estimate=pl.CostEstimate(flops=0, bytes_accessed=0, transcendentals=0),
+        cost_estimate=TINY,
     )(me, *blocks, gain, sel, held, in_hbm(w_out))
+
+
+def image_end_kernel(n_rows, away, me_ref, *refs):
+    x_refs, refs = refs[: 2 * len(away)], refs[2 * len(away) :]
+    own_ref, gain_ref, sel_ref, held_ref, acc_ref, sums_ref, qkv_ref, merged_ref = refs
+    is_img = image_flags(sel_ref)
+    half = x_refs[0].shape[0]
+    before, after = sums_ref[0], sums_ref[1]
+    parts = ((0, half), (half, sel_ref.shape[0]))
+    scaled, one, two = [], [[], []], [[], []]
+    for i, s in enumerate(away):
+        vis_row = x_refs[2 * i + 1][...].astype(jnp.float32)[n_rows - half : n_rows - half + 1]
+        for side, (low, high) in enumerate(parts):
+            x = x_refs[2 * i + side][...]
+            rows, a, b = image_rows(x, vis_row, is_img[low:high], gain_ref[me_ref[0] ^ s])
+            scaled.append(rows)
+            one[side].append(a)
+            two[side].append(b)
+    norms, scales = [], []
+    for side, (low, high) in enumerate(parts):
+        merge = lax.rsqrt((before[low:high] + sum(one[side])) / D + EPS)[:, :1]
+        merge = jnp.where(is_img[low:high], merge, 1.0)
+        mean = (after[low:high] + sum(two[side]))[:, :1] * merge * merge / D
+        norms.append(lax.rsqrt(mean + EPS) * merge)
+        scales.append(merge)
+    for j in range(3):
+        for side, (low, high) in enumerate(parts):
+            acc = acc_ref[j, low:high]
+            for i, s in enumerate(away):
+                acc += jnp.dot(scaled[2 * i + side], held_ref[s, j], preferred_element_type=jnp.float32)
+            qkv_ref[j, low:high] = (acc * norms[side]).astype(jnp.bfloat16)
+    own = own_ref[...].astype(jnp.float32)
+    own = jnp.where(is_img, own * own[n_rows : n_rows + 1], own)
+    for side, (low, high) in enumerate(parts):
+        merged_ref[low:high] = (own[low:high] * scales[side]).astype(jnp.bfloat16)
+
+
+def image_end(away, me, blocks, own, gain, sel, held, acc, sums, n_rows):
+    n_img, width = own.shape
+    return pl.pallas_call(
+        functools.partial(image_end_kernel, n_rows, away),
+        out_shape=(
+            jax.ShapeDtypeStruct((3, n_img, held.shape[3]), jnp.bfloat16),
+            jax.ShapeDtypeStruct((n_img, width), jnp.bfloat16),
+        ),
+        in_specs=[pl.BlockSpec(memory_space=pltpu.SMEM)] + vmem_specs(2 * len(blocks) + 6),
+        out_specs=tuple(vmem_specs(2)),
+        compiler_params=params(12),
+        cost_estimate=TINY,
+    )(me, *[h for b in blocks for h in b], own, gain, sel, held, acc, sums)
 
 
 def project_side(side, far, me_ref, x_ref, gain_ref, held_ref, acc_ref, ss_ref, out_ref):
@@ -690,19 +746,28 @@
     )
     pairs = mix_pairs(even, swap(odd, 1, "req"), region)
     received = [pairs[0]] + [swap(pairs[i], 2 * i, "req") for i in range(1, n_req // 2)]
+    ctext, pairs = lax.optimization_barrier((ctext, pairs))
+    acc, ss, held = own_part(ten_at, ctext, gains, w3)
+    received, acc = lax.optimization_barrier((received, acc))
     img_own = pack_images(received, vis_row, rtext, sel, region)
-    img_blocks = [img_own] + [swap(img_own, s) for s in range(1, n_ten)]
-    own, img_own = lax.optimization_barrier((ctext, img_own))
-    acc, ss, held = own_part(ten_at, own, gains, w3)
+    img_near = near_blocks(img_own, n_ten)
     handed, img_own = lax.optimization_barrier((blocks, img_own))
     blocks = {**far_blocks(handed, n_ten), **blocks}
 
     near = [blocks[s] for s in near_at]
     acc, ss = near_part(near_at, ten_at, near, gains, held, acc, ss)
-    table, acc = lax.optimization_barrier((table, acc))
+    table, img_near, acc = lax.optimization_barrier((table, img_near, acc))
     text_at, img_at, text_row = placement(table, region, length, n_text, n_img)
-    img_blocks, text_at = lax.optimization_barrier((img_blocks, text_at))
-    img_qkv, merged, w_out = image_part(ten_at, img_blocks, gains, sel, held, w_out, n_rows)
+    img_blocks = far_blocks(img_near, n_ten)
+    img_near, text_at = lax.optimization_barrier((img_near, text_at))
+    one_bit = [0] + sorted(img_near)
+    img_acc, img_sums, w_out = image_part(
+        one_bit, ten_at, [img_own] + [img_near[s] for s in one_bit[1:]], gains, sel, held, w_out, n_rows
+    )
+    more_bits = [s for s in order if s not in img_near]
+    img_qkv, merged = image_end(
+        more_bits, ten_at, [img_blocks[s] for s in more_bits], img_own, gains, sel, held, img_acc, img_sums, n_rows
+    )
 
     shared = (gains, held, acc, ss, img_qkv, text_at, img_at, key_ok, w_out)
     top_qkv, head_qkv, head_ctx, *head_far = head_part(far, ten_at, blocks[far][0], *shared)

time: 66.6 us -> 66.6 us (level)
  waiting for transfers between devices: 21.4 us -> 18.4 us
  starting transfers between devices: 22.2 us -> 24.1 us
  Pallas kernels: 21.8 us -> 22.9 us
    ppermute x19 -> x20, waiting for transfers between devices: 21.4 us -> 18.4 us  [swap(): return lax.ppermute(x, axis, [(i, i ^ s) for i in range(n)])]
    ppermute x19 -> x20, starting transfers between devices: 22.2 us -> 24.1 us  [swap(): return lax.ppermute(x, axis, [(i, i ^ s) for i in range(n)])]
    pallas_call x1 -> x2, Pallas kernels: 2.65 us -> 3.69 us  [the longest x1 2.42 us: image_part(): pl.pallas_call(functools.partial(image_kernel, n_rows, away), out_shape=(...]
  transfers between devices with their start and end apart: 19 -> 20, of which waited for: 10 -> 12; matrix products, arithmetic and copies ran while one was open for 1% -> 1% of each run, Pallas kernels for 29% -> 30%
where the time goes in v6:
time: 66.6 us; the launch traced here: 66.5 us
  starting transfers between devices  24.1 us (36%)
  Pallas kernels  22.9 us (34%)
  waiting for transfers between devices  18.4 us (28%)
    ppermute x20, starting transfers between devices, swap(): return lax.ppermute(x, axis, [(i, i ^ s) for i in range(n)])  24.1 us
    ppermute x20, waiting for transfers between devices, swap(): return lax.ppermute(x, axis, [(i, i ^ s) for i in range(n)])  18.4 us
    pallas_call x1, Pallas kernels, own_part(): pl.pallas_call(own_kernel, out_shape=(jax.ShapeDtypeStruct((3, rows, cols...  4.86 us
    pallas_call x1, Pallas kernels, tail_part(): pl.pallas_call(functools.partial(tail_kernel, far), out_shape=(jax.ShapeD...  2.49 us
    pallas_call x1, Pallas kernels, image_part(): pl.pallas_call(functools.partial(image_kernel, n_rows, away), out_shape=(...  2.42 us
    pallas_call x1, Pallas kernels, near_part(): pl.pallas_call(functools.partial(near_kernel, near, pieces), out_shape=(j...  2.29 us
    pallas_call x1, Pallas kernels, prepare(): pl.pallas_call(functools.partial(prep_kernel, n_req), out_shape=tuple((ja...  2.2 us
    pallas_call x3, Pallas kernels, out_part(): pl.pallas_call(functools.partial(out_kernel, away), out_shape=(jax.ShapeD...  1.74 us
  transfers between devices with their start and end apart: 20, of which 12 were waited for; matrix products, arithmetic and copies ran while one was open for 1% of the time, Pallas kernels for 30%

profile of v6, /device:TPU:0, one launch (start us, length us, event | category | flops | bytes accessed | tf_op | source)
XLA Modules:
  0.0 66.5 jit_solution(12686990782953280578)
XLA Ops:
  0.0 1.7 %shard_map.91.x_ref = bf16[320,1024]{1,0:T(8,128)(2,1)S(1)} custom-call(s32[1]{0:T(128)} %bitcast.me_ref, s32[64]{0:T(128)} %req_hbm.3, s32[64]{0:T(128)} %start_hbm.3, bf16[384,1024]{1,0:T(8,128)(2,1)} %text_hbm.2), custom_call_target="tpu_custom_call" | custom-call | tf_op jit(solution)/shard_map/pallas_call | solution.py:117
  1.7 3.0 %collective-permute-start.6 = (bf16[320,1024]{1,0:T(8,128)(2,1)S(1)}, bf16[320,1024]{1,0:T(8,128)(2,1)S(1)}, u32[]{:S(2)}, u32[]{:S(2)}) collective-permute-start(bf16[320,1024]{1,0:T(8,128)(2,1)S(1)} %shard_map.91.x_ref), channel_id=1, source_target_pairs={{0,1},{1,0},{2,3},{3,2},{4,5},{5,4},{6,7},{7,6},{8,9},{9,8},{10,11... | collective-permute-start | bytes 1966088 | tf_op jit(solution)/shard_map/ppermute | solution.py:23
  4.7 1.5 %collective-permute-start.7 = (bf16[320,1024]{1,0:T(8,128)(2,1)S(1)}, bf16[320,1024]{1,0:T(8,128)(2,1)S(1)}, u32[]{:S(2)}, u32[]{:S(2)}) collective-permute-start(bf16[320,1024]{1,0:T(8,128)(2,1)S(1)} %shard_map.91.x_ref), channel_id=1, source_target_pairs={{0,2},{1,3},{2,0},{3,1},{4,6},{5,7},{6,4},{7,5},{8,10},{9,11},{10,... | collective-permute-start | bytes 1966088 | tf_op jit(solution)/shard_map/ppermute | solution.py:23
  6.2 2.2 %shard_map.92 = (bf16[4,16,1024]{2,1,0:T(8,128)(2,1)S(1)}, bf16[4,16,1024]{2,1,0:T(8,128)(2,1)S(1)}, bf16[80,1024]{1,0:T(8,128)(2,1)S(1)}, bf16[80,80]{1,0:T(8,1...) custom-call(s32[1]{0:T(128)} %bitcast.me_ref, ...), custom_call_target="tpu_custom_call" | custom-call | tf_op jit(solution)/shard_map/pallas_call | solution.py:225
  8.4 0.1 collective-permute-start
  8.5 1.3 %collective-permute-done.odd_ref = bf16[4,16,1024]{2,1,0:T(8,128)(2,1)S(1)} collective-permute-done((bf16[4,16,1024]{2,1,0:T(8,128)(2,1)S(1)}, bf16[4,16,1024]{2,1,0:T(8,128)(2,1)S(1)}, u32[]{:S(2)}, u32[]{:S(2)}) %collective-permute-start) | collective-permute-done | bytes 131104 | tf_op jit(solution)/shard_map/ppermute | solution.py:23
  9.8 0.1 shard_map.93
  9.9 1.6 %collective-permute-start.1 = (bf16[24,1024]{1,0:T(8,128)(2,1)S(1)}, bf16[24,1024]{1,0:T(8,128)(2,1)S(1)}, u32[]{:S(2)}, u32[]{:S(2)}) collective-permute-start(bf16[24,1024]{1,0:T(8,128)(2,1)S(1)} %get-tuple-element.74), channel_id=1, source_target_pairs={{0,8},{4,12},{8,0},{12,4},{16,24},{20,28},{24,16},{28,20},{1,9},{5... | collective-permute-start | bytes 147464 | tf_op jit(solution)/shard_map/ppermute | solution.py:23
  11.5 2.6 %collective-permute-start.2 = (bf16[24,1024]{1,0:T(8,128)(2,1)S(1)}, bf16[24,1024]{1,0:T(8,128)(2,1)S(1)}, u32[]{:S(2)}, u32[]{:S(2)}) collective-permute-start(bf16[24,1024]{1,0:T(8,128)(2,1)S(1)} %get-tuple-element.75), channel_id=1, source_target_pairs={{0,16},{4,20},{8,24},{12,28},{16,0},{20,4},{24,8},{28,12},{1,17},{... | collective-permute-start | bytes 147464 | tf_op jit(solution)/shard_map/ppermute | solution.py:23
  14.1 0.2 collective-permute-start.3
  14.3 4.9 %shard_map.94 = (f32[3,320,512]{2,1,0:T(8,128)S(1)}, f32[320,128]{1,0:T(8,128)S(1)}, bf16[4,3,1024,512]{3,2,1,0:T(8,128)(2,1)S(1)}) custom-call(s32[1]{0:T(128)} %bitcast.5.me_ref, bf16[320,1024]{1,0:T(8,128)(2,1)S(1)} %shard_map.91.x_ref, f32[4,1,1024]{2,1,0:T(1,128)S(1)} %get-tuple-element.79.gain_ref.refs_2_.refs_3_, bf16[3,4096,512]{2,1,0:T(8,128)(2,1)} %bitcast.9), custom_call_target="tpu_custom_call" | custom-call | tf_op jit(solution)/shard_map/pallas_call | solution.py:356
  19.2 0.0 collective-permute-done.1.refs_1_
  19.2 0.0 collective-permute-done.2.refs_2_
  19.2 0.8 %collective-permute-done.3.refs_3_ = bf16[24,1024]{1,0:T(8,128)(2,1)S(1)} collective-permute-done((bf16[24,1024]{1,0:T(8,128)(2,1)S(1)}, bf16[24,1024]{1,0:T(8,128)(2,1)S(1)}, u32[]{:S(2)}, u32[]{:S(2)}) %collective-permute-start.3) | collective-permute-done | bytes 49184 | tf_op jit(solution)/shard_map/ppermute | solution.py:23
  20.0 0.2 shard_map.95.refs_0_.refs_2_
  20.2 0.6 collective-permute-start.4
  20.8 0.5 collective-permute-start.5
  21.3 0.0 collective-permute-done.6.refs_0_
  21.3 0.0 collective-permute-done.7.refs_1_
  21.3 1.6 %collective-permute-start.10 = (bf16[160,1024]{1,0:T(8,128)(2,1)S(1)}, bf16[160,1024]{1,0:T(8,128)(2,1)S(1)}, u32[]{:S(2)}, u32[]{:S(2)}) collective-permute-start(bf16[160,1024]{1,0:T(8,128)(2,1)S(1)} %slice.18), channel_id=1, source_target_pairs={{0,1},{1,0},{2,3},{3,2},{4,5},{5,4},{6,7},{7,6},{8,9},{9,8},{10,11... | collective-permute-start | bytes 983048 | tf_op jit(solution)/shard_map/ppermute | solution.py:23
  22.9 1.6 %collective-permute-start.13 = (bf16[160,1024]{1,0:T(8,128)(2,1)S(1)}, bf16[160,1024]{1,0:T(8,128)(2,1)S(1)}, u32[]{:S(2)}, u32[]{:S(2)}) collective-permute-start(bf16[160,1024]{1,0:T(8,128)(2,1)S(1)} %slice.19), channel_id=1, source_target_pairs={{0,2},{1,3},{2,0},{3,1},{4,6},{5,7},{6,4},{7,5},{8,10},{9,11},{10,... | collective-permute-start | bytes 983048 | tf_op jit(solution)/shard_map/ppermute | solution.py:23
  24.5 2.3 %shard_map.96 = (f32[3,320,512]{2,1,0:T(8,128)S(1)}, f32[320,128]{1,0:T(8,128)S(1)}) custom-call(s32[1]{0:T(128)} %bitcast.5.me_ref, bf16[320,1024]{1,0:T(8,128)(2,1)S(1)} %collective-permute-done.6.refs_0_, bf16[320,1024]{1,0:T(8,128)(2,1)S(1)} %collective-permute-done.7.refs_1_, f32[4,1,1024]{2,1,0:T(1,128)S(1)} %get-tuple-element.79.gain_ref.refs_2_.refs_3_, ...), custom_call_target="tpu_custom_call" | custom-call | flops 99999997952 | tf_op jit(solution)/shard_map/pallas_call | solution.py:400
  26.8 0.6 collective-permute-done.4.refs_1_
  27.4 0.5 collective-permute-done.5.refs_2_
  28.0 1.6 %collective-permute-start.8 = (bf16[48,1024]{1,0:T(8,128)(2,1)S(1)}, bf16[48,1024]{1,0:T(8,128)(2,1)S(1)}, u32[]{:S(2)}, u32[]{:S(2)}) collective-permute-start(bf16[48,1024]{1,0:T(8,128)(2,1)S(1)} %slice.16), channel_id=1, source_target_pairs={{0,1},{1,0},{2,3},{3,2},{4,5},{5,4},{6,7},{7,6},{8,9},{9,8},{10,11... | collective-permute-start | bytes 294920 | tf_op jit(solution)/shard_map/ppermute | solution.py:23
  29.5 0.4 collective-permute-start.9
  29.9 0.7 %shard_map.97 = (bf16[384,320]{1,0:T(8,128)(2,1)S(1)}, bf16[384,80]{1,0:T(8,128)(2,1)S(1)}, f32[384,128]{1,0:T(8,128)S(1)}) custom-call(s32[8,128]{1,0:T(8,128)S(1)} %get-tuple-element.89.table_ref), custom_call_target="tpu_custom_call" | custom-call | tf_op jit(solution)/shard_map/pallas_call | solution.py:305
  30.7 2.4 %shard_map.98 = (f32[3,80,512]{2,1,0:T(8,128)S(1)}, f32[2,80,128]{2,1,0:T(8,128)S(1)}, bf16[512,4096]{1,0:T(8,128)(2,1)S(1)}) custom-call(s32[1]{0:T(128)} %bitcast.5.me_ref, bf16[80,1024]{1,0:T(8,128)(2,1)S(1)} %shard_map.95.refs_0_.refs_2_, bf16[80,1024]{1,0:T(8,128)(2,1)S(1)} %collective-permute-done.4.refs_1_, ...), custom_call_target="tpu_custom_call" | custom-call | tf_op jit(solution)/shard_map/pallas_call | solution.py:452
  33.1 0.7 %collective-permute-done.9.refs_1_ = bf16[32,1024]{1,0:T(8,128)(2,1)S(1)} collective-permute-done((bf16[32,1024]{1,0:T(8,128)(2,1)S(1)}, bf16[32,1024]{1,0:T(8,128)(2,1)S(1)}, u32[]{:S(2)}, u32[]{:S(2)}) %collective-permute-start.9) | collective-permute-done | bytes 65568 | tf_op jit(solution)/shard_map/ppermute | solution.py:23
  33.8 0.3 collective-permute-done.8.refs_0_
  34.1 1.3 %shard_map.99 = (bf16[3,80,512]{2,1,0:T(8,128)(2,1)S(1)}, bf16[80,1024]{1,0:T(8,128)(2,1)S(1)}) custom-call(s32[1]{0:T(128)} %bitcast.5.me_ref, bf16[48,1024]{1,0:T(8,128)(2,1)S(1)} %collective-permute-done.8.refs_0_, bf16[32,1024]{1,0:T(8,128)(2,1)S(1)} %collective-permute-done.9.refs_1_, bf16[80,1024]{1,0:T(8,128)(2,1)S(1)} %shard_map.95.refs_0_.refs_2_, ...), custom_call_target="tpu_custom_call" | custom-call | tf_op jit(solution)/shard_map/pallas_call | solution.py:506
  35.4 0.0 collective-permute-done.10.top_ref
  35.4 1.7 %shard_map.100 = (bf16[3,160,512]{2,1,0:T(8,128)(2,1)S(1)}, bf16[3,160,512]{2,1,0:T(8,128)(2,1)S(1)}, bf16[160,512]{1,0:T(8,128)(2,1)S(1)}, bf16[160,512]{1,0:T(8,128)(2,1)S(1)}, bf16[160,512]{1,0:T(8,128)(2,1)S(1)}) custom-call(s32[1]{0:T(128)} %bitcast.5.me_ref, bf16[160,1024]{1,0:T(8,128)(2,1)S(1)} %collective-permute-done.10.top_ref, ...), custom_call_target="tpu_custom_call" | custom-call | tf_op jit(solution)/shard_map/pallas_call | solution.py:581
  37.1 1.1 %collective-permute-start.11 = (bf16[160,512]{1,0:T(8,128)(2,1)S(1)}, bf16[160,512]{1,0:T(8,128)(2,1)S(1)}, u32[]{:S(2)}, u32[]{:S(2)}) collective-permute-start(bf16[160,512]{1,0:T(8,128)(2,1)S(1)} %get-tuple-element.108), channel_id=1, source_target_pairs={{0,1},{1,0},{2,3},{3,2},{4,5},{5,4},{6,7},{7,6},{8,9},{9,8},{10,11... | collective-permute-start | bytes 491528 | tf_op jit(solution)/shard_map/ppermute | solution.py:23
  38.2 0.6 collective-permute-start.12
  38.8 0.0 collective-permute-done.13.bottom_ref
  38.8 2.5 %shard_map.101 = (bf16[224,512]{1,0:T(8,128)(2,1)S(1)}, bf16[224,512]{1,0:T(8,128)(2,1)S(1)}, bf16[224,512]{1,0:T(8,128)(2,1)S(1)}) custom-call(s32[1]{0:T(128)} %bitcast.5.me_ref, bf16[160,1024]{1,0:T(8,128)(2,1)S(1)} %collective-permute-done.13.bottom_ref, f32[4,1,1024]{2,1,0:T(1,128)S(1)} %get-tuple-element.79.gain_ref.refs_2_.refs_3_, ...), custom_call_target="tpu_custom_call" | custom-call | flops 10000000000 | tf_op jit(solution)/shard_map/pallas_call | solution.py:620
  41.3 1.5 %collective-permute-start.18 = (bf16[224,512]{1,0:T(8,128)(2,1)S(1)}, bf16[224,512]{1,0:T(8,128)(2,1)S(1)}, u32[]{:S(2)}, u32[]{:S(2)}) collective-permute-start(bf16[224,512]{1,0:T(8,128)(2,1)S(1)} %get-tuple-element.126), channel_id=1, source_target_pairs={{0,2},{1,3},{2,0},{3,1},{4,6},{5,7},{6,4},{7,5},{8,10},{9,11},{10,... | collective-permute-start | bytes 688136 | tf_op jit(solution)/shard_map/ppermute | solution.py:23
  42.8 1.0 %collective-permute-start.16 = (bf16[224,512]{1,0:T(8,128)(2,1)S(1)}, bf16[224,512]{1,0:T(8,128)(2,1)S(1)}, u32[]{:S(2)}, u32[]{:S(2)}) collective-permute-start(bf16[224,512]{1,0:T(8,128)(2,1)S(1)} %get-tuple-element.123), channel_id=1, source_target_pairs={{0,1},{1,0},{2,3},{3,2},{4,5},{5,4},{6,7},{7,6},{8,9},{9,8},{10,11... | collective-permute-start | bytes 688136 | tf_op jit(solution)/shard_map/ppermute | solution.py:23
  43.8 0.0 collective-permute-done.11
  43.8 1.3 %collective-permute-done.12 = bf16[160,512]{1,0:T(8,128)(2,1)S(1)} collective-permute-done((bf16[160,512]{1,0:T(8,128)(2,1)S(1)}, bf16[160,512]{1,0:T(8,128)(2,1)S(1)}, u32[]{:S(2)}, u32[]{:S(2)}) %collective-permute-start.12) | collective-permute-done | bytes 163872 | tf_op jit(solution)/shard_map/ppermute | solution.py:23
  45.1 0.6 shard_map.104
  45.7 0.8 %collective-permute-start.15 = (bf16[384,512]{1,0:T(8,128)(2,1)S(1)}, bf16[384,512]{1,0:T(8,128)(2,1)S(1)}, u32[]{:S(2)}, u32[]{:S(2)}) collective-permute-start(bf16[384,512]{1,0:T(8,128)(2,1)S(1)} %get-tuple-element.120), channel_id=1, source_target_pairs={{0,2},{1,3},{2,0},{3,1},{4,6},{5,7},{6,4},{7,5},{8,10},{9,11},{10,... | collective-permute-start | bytes 1179656 | tf_op jit(solution)/shard_map/ppermute | solution.py:23
  46.5 0.6 shard_map.103
  47.1 0.0 copy-start
  47.1 1.4 %collective-permute-start.14 = (bf16[384,512]{1,0:T(8,128)(2,1)S(1)}, bf16[384,512]{1,0:T(8,128)(2,1)S(1)}, u32[]{:S(2)}, u32[]{:S(2)}) collective-permute-start(bf16[384,512]{1,0:T(8,128)(2,1)S(1)} %get-tuple-element.118), channel_id=1, source_target_pairs={{0,1},{1,0},{2,3},{3,2},{4,5},{5,4},{6,7},{7,6},{8,9},{9,8},{10,11... | collective-permute-start | bytes 1179656 | tf_op jit(solution)/shard_map/ppermute | solution.py:23
  48.5 1.5 %collective-permute-done.18 = bf16[224,512]{1,0:T(8,128)(2,1)S(1)} collective-permute-done((bf16[224,512]{1,0:T(8,128)(2,1)S(1)}, bf16[224,512]{1,0:T(8,128)(2,1)S(1)}, u32[]{:S(2)}, u32[]{:S(2)}) %collective-permute-start.18) | collective-permute-done | bytes 229408 | tf_op jit(solution)/shard_map/ppermute | solution.py:23
  50.0 0.1 add_convert_fusion.1
  50.1 1.3 %collective-permute-start.19 = (bf16[384,512]{1,0:T(8,128)(2,1)S(1)}, bf16[384,512]{1,0:T(8,128)(2,1)S(1)}, u32[]{:S(2)}, u32[]{:S(2)}) collective-permute-start(bf16[384,512]{1,0:T(8,128)(2,1)S(1)} %add_convert_fusion.1), channel_id=1, source_target_pairs={{0,1},{1,0},{2,3},{3,2},{4,5},{5,4},{6,7},{7,6},{8,9},{9,8},{10,11... | collective-permute-start | bytes 1179656 | tf_op jit(solution)/shard_map/ppermute | solution.py:23
  51.4 0.0 collective-permute-done.16
  51.4 0.1 add_convert_fusion.2
  51.5 1.1 %collective-permute-start.17 = (bf16[384,512]{1,0:T(8,128)(2,1)S(1)}, bf16[384,512]{1,0:T(8,128)(2,1)S(1)}, u32[]{:S(2)}, u32[]{:S(2)}) collective-permute-start(bf16[384,512]{1,0:T(8,128)(2,1)S(1)} %add_convert_fusion.2), channel_id=1, source_target_pairs={{0,2},{1,3},{2,0},{3,1},{4,6},{5,7},{6,4},{7,5},{8,10},{9,11},{10,... | collective-permute-start | bytes 1179656 | tf_op jit(solution)/shard_map/ppermute | solution.py:23
  52.7 0.1 slice_reduce_fusion
  52.8 0.0 copy-done
  52.8 0.4 add_convert_fusion.base_ref
  53.2 0.6 shard_map.102
  53.8 4.7 %collective-permute-done.15.refs_3_ = bf16[384,512]{1,0:T(8,128)(2,1)S(1)} collective-permute-done((bf16[384,512]{1,0:T(8,128)(2,1)S(1)}, bf16[384,512]{1,0:T(8,128)(2,1)S(1)}, u32[]{:S(2)}, u32[]{:S(2)}) %collective-permute-start.15) | collective-permute-done | bytes 393248 | tf_op jit(solution)/shard_map/ppermute | solution.py:23
  58.5 1.2 %collective-permute-done.14.refs_1_ = bf16[384,512]{1,0:T(8,128)(2,1)S(1)} collective-permute-done((bf16[384,512]{1,0:T(8,128)(2,1)S(1)}, bf16[384,512]{1,0:T(8,128)(2,1)S(1)}, u32[]{:S(2)}, u32[]{:S(2)}) %collective-permute-start.14) | collective-permute-done | bytes 393248 | tf_op jit(solution)/shard_map/ppermute | solution.py:23
  59.7 0.3 shard_map.105.base_ref
  59.9 5.0 %collective-permute-done.19.refs_1_ = bf16[384,512]{1,0:T(8,128)(2,1)S(1)} collective-permute-done((bf16[384,512]{1,0:T(8,128)(2,1)S(1)}, bf16[384,512]{1,0:T(8,128)(2,1)S(1)}, u32[]{:S(2)}, u32[]{:S(2)}) %collective-permute-start.19) | collective-permute-done | bytes 393248 | tf_op jit(solution)/shard_map/ppermute | solution.py:23
  64.9 0.4 collective-permute-done.17.refs_0_
  65.3 1.0 %shard_map.106 = bf16[384,1024]{1,0:T(8,128)(2,1)} custom-call(f32[384,1024]{1,0:T(8,128)S(1)} %shard_map.105.base_ref, bf16[384,512]{1,0:T(8,128)(2,1)S(1)} %collective-permute-done.17.refs_0_, bf16[384,512]{1,0:T(8,128)(2,1)S(1)} %collective-permute-done.19.refs_1_), custom_call_target="tpu_custom_call" | custom-call | tf_op jit(solution)/shard_map/pallas_call | solution.py:693
  (4 shorter events, 0.1 us)
Async XLA Ops:
  1.7 19.6 %collective-permute-start.6 = (bf16[320,1024]{1,0:T(8,128)(2,1)S(1)}, bf16[320,1024]{1,0:T(8,128)(2,1)S(1)}, u32[]{:S(2)}, u32[]{:S(2)}) collective-permute-start(bf16[320,1024]{1,0:T(8,128)(2,1)S(1)} %shard_map.91.x_ref), channel_id=1, source_target_pairs={{0,1},{1,0},{2,3},{3,2},{4,5},{5,4},{6,7},{7,6},{8,9},{9,8},{10,11... | collective-permute-start | bytes 1966088 | tf_op jit(solution)/shard_map/ppermute | solution.py:23
  4.7 16.6 %collective-permute-start.7 = (bf16[320,1024]{1,0:T(8,128)(2,1)S(1)}, bf16[320,1024]{1,0:T(8,128)(2,1)S(1)}, u32[]{:S(2)}, u32[]{:S(2)}) collective-permute-start(bf16[320,1024]{1,0:T(8,128)(2,1)S(1)} %shard_map.91.x_ref), channel_id=1, source_target_pairs={{0,2},{1,3},{2,0},{3,1},{4,6},{5,7},{6,4},{7,5},{8,10},{9,11},{10,... | collective-permute-start | bytes 1966088 | tf_op jit(solution)/shard_map/ppermute | solution.py:23
  8.4 1.4 %collective-permute-start = (bf16[4,16,1024]{2,1,0:T(8,128)(2,1)S(1)}, bf16[4,16,1024]{2,1,0:T(8,128)(2,1)S(1)}, u32[]{:S(2)}, u32[]{:S(2)}) collective-permute-start(bf16[4,16,1024]{2,1,0:T(8,128)(2,1)S(1)} %get-tuple-element.72), channel_id=1, source_target_pairs={{0,4},{4,0},{8,12},{12,8},{16,20},{20,16},{24,28},{28,24},{1,5},{5... | collective-permute-start | bytes 393224 | tf_op jit(solution)/shard_map/ppermute | solution.py:23
  9.9 9.3 %collective-permute-start.1 = (bf16[24,1024]{1,0:T(8,128)(2,1)S(1)}, bf16[24,1024]{1,0:T(8,128)(2,1)S(1)}, u32[]{:S(2)}, u32[]{:S(2)}) collective-permute-start(bf16[24,1024]{1,0:T(8,128)(2,1)S(1)} %get-tuple-element.74), channel_id=1, source_target_pairs={{0,8},{4,12},{8,0},{12,4},{16,24},{20,28},{24,16},{28,20},{1,9},{5... | collective-permute-start | bytes 147464 | tf_op jit(solution)/shard_map/ppermute | solution.py:23
  11.5 7.7 %collective-permute-start.2 = (bf16[24,1024]{1,0:T(8,128)(2,1)S(1)}, bf16[24,1024]{1,0:T(8,128)(2,1)S(1)}, u32[]{:S(2)}, u32[]{:S(2)}) collective-permute-start(bf16[24,1024]{1,0:T(8,128)(2,1)S(1)} %get-tuple-element.75), channel_id=1, source_target_pairs={{0,16},{4,20},{8,24},{12,28},{16,0},{20,4},{24,8},{28,12},{1,17},{... | collective-permute-start | bytes 147464 | tf_op jit(solution)/shard_map/ppermute | solution.py:23
  14.1 5.9 %collective-permute-start.3 = (bf16[24,1024]{1,0:T(8,128)(2,1)S(1)}, bf16[24,1024]{1,0:T(8,128)(2,1)S(1)}, u32[]{:S(2)}, u32[]{:S(2)}) collective-permute-start(bf16[24,1024]{1,0:T(8,128)(2,1)S(1)} %get-tuple-element.76), channel_id=1, source_target_pairs={{0,24},{4,28},{8,16},{12,20},{16,8},{20,12},{24,0},{28,4},{1,25},{... | collective-permute-start | bytes 147464 | tf_op jit(solution)/shard_map/ppermute | solution.py:23
  20.2 7.2 %collective-permute-start.4 = (bf16[80,1024]{1,0:T(8,128)(2,1)S(1)}, bf16[80,1024]{1,0:T(8,128)(2,1)S(1)}, u32[]{:S(2)}, u32[]{:S(2)}) collective-permute-start(bf16[80,1024]{1,0:T(8,128)(2,1)S(1)} %shard_map.95.refs_0_.refs_2_), channel_id=1, source_target_pairs={{0,1},{1,0},{2,3},{3,2},{4,5},{5,4},{6,7},{7,6},{8,9},{9,8},{10,11... | collective-permute-start | bytes 491528 | tf_op jit(solution)/shard_map/ppermute | solution.py:23
  20.8 7.1 %collective-permute-start.5 = (bf16[80,1024]{1,0:T(8,128)(2,1)S(1)}, bf16[80,1024]{1,0:T(8,128)(2,1)S(1)}, u32[]{:S(2)}, u32[]{:S(2)}) collective-permute-start(bf16[80,1024]{1,0:T(8,128)(2,1)S(1)} %shard_map.95.refs_0_.refs_2_), channel_id=1, source_target_pairs={{0,2},{1,3},{2,0},{3,1},{4,6},{5,7},{6,4},{7,5},{8,10},{9,11},{10,... | collective-permute-start | bytes 491528 | tf_op jit(solution)/shard_map/ppermute | solution.py:23
  21.3 14.0 %collective-permute-start.10 = (bf16[160,1024]{1,0:T(8,128)(2,1)S(1)}, bf16[160,1024]{1,0:T(8,128)(2,1)S(1)}, u32[]{:S(2)}, u32[]{:S(2)}) collective-permute-start(bf16[160,1024]{1,0:T(8,128)(2,1)S(1)} %slice.18), channel_id=1, source_target_pairs={{0,1},{1,0},{2,3},{3,2},{4,5},{5,4},{6,7},{7,6},{8,9},{9,8},{10,11... | collective-permute-start | bytes 983048 | tf_op jit(solution)/shard_map/ppermute | solution.py:23
  22.9 15.9 %collective-permute-start.13 = (bf16[160,1024]{1,0:T(8,128)(2,1)S(1)}, bf16[160,1024]{1,0:T(8,128)(2,1)S(1)}, u32[]{:S(2)}, u32[]{:S(2)}) collective-permute-start(bf16[160,1024]{1,0:T(8,128)(2,1)S(1)} %slice.19), channel_id=1, source_target_pairs={{0,2},{1,3},{2,0},{3,1},{4,6},{5,7},{6,4},{7,5},{8,10},{9,11},{10,... | collective-permute-start | bytes 983048 | tf_op jit(solution)/shard_map/ppermute | solution.py:23
  28.0 6.2 %collective-permute-start.8 = (bf16[48,1024]{1,0:T(8,128)(2,1)S(1)}, bf16[48,1024]{1,0:T(8,128)(2,1)S(1)}, u32[]{:S(2)}, u32[]{:S(2)}) collective-permute-start(bf16[48,1024]{1,0:T(8,128)(2,1)S(1)} %slice.16), channel_id=1, source_target_pairs={{0,1},{1,0},{2,3},{3,2},{4,5},{5,4},{6,7},{7,6},{8,9},{9,8},{10,11... | collective-permute-start | bytes 294920 | tf_op jit(solution)/shard_map/ppermute | solution.py:23
  29.5 4.3 %collective-permute-start.9 = (bf16[32,1024]{1,0:T(8,128)(2,1)S(1)}, bf16[32,1024]{1,0:T(8,128)(2,1)S(1)}, u32[]{:S(2)}, u32[]{:S(2)}) collective-permute-start(bf16[32,1024]{1,0:T(8,128)(2,1)S(1)} %slice.17), channel_id=1, source_target_pairs={{0,2},{1,3},{2,0},{3,1},{4,6},{5,7},{6,4},{7,5},{8,10},{9,11},{10,... | collective-permute-start | bytes 196616 | tf_op jit(solution)/shard_map/ppermute | solution.py:23
  37.1 6.7 %collective-permute-start.11 = (bf16[160,512]{1,0:T(8,128)(2,1)S(1)}, bf16[160,512]{1,0:T(8,128)(2,1)S(1)}, u32[]{:S(2)}, u32[]{:S(2)}) collective-permute-start(bf16[160,512]{1,0:T(8,128)(2,1)S(1)} %get-tuple-element.108), channel_id=1, source_target_pairs={{0,1},{1,0},{2,3},{3,2},{4,5},{5,4},{6,7},{7,6},{8,9},{9,8},{10,11... | collective-permute-start | bytes 491528 | tf_op jit(solution)/shard_map/ppermute | solution.py:23
  38.2 6.9 %collective-permute-start.12 = (bf16[160,512]{1,0:T(8,128)(2,1)S(1)}, bf16[160,512]{1,0:T(8,128)(2,1)S(1)}, u32[]{:S(2)}, u32[]{:S(2)}) collective-permute-start(bf16[160,512]{1,0:T(8,128)(2,1)S(1)} %get-tuple-element.109), channel_id=1, source_target_pairs={{0,2},{1,3},{2,0},{3,1},{4,6},{5,7},{6,4},{7,5},{8,10},{9,11},{10,... | collective-permute-start | bytes 491528 | tf_op jit(solution)/shard_map/ppermute | solution.py:23
  41.3 8.7 %collective-permute-start.18 = (bf16[224,512]{1,0:T(8,128)(2,1)S(1)}, bf16[224,512]{1,0:T(8,128)(2,1)S(1)}, u32[]{:S(2)}, u32[]{:S(2)}) collective-permute-start(bf16[224,512]{1,0:T(8,128)(2,1)S(1)} %get-tuple-element.126), channel_id=1, source_target_pairs={{0,2},{1,3},{2,0},{3,1},{4,6},{5,7},{6,4},{7,5},{8,10},{9,11},{10,... | collective-permute-start | bytes 688136 | tf_op jit(solution)/shard_map/ppermute | solution.py:23
  42.8 8.6 %collective-permute-start.16 = (bf16[224,512]{1,0:T(8,128)(2,1)S(1)}, bf16[224,512]{1,0:T(8,128)(2,1)S(1)}, u32[]{:S(2)}, u32[]{:S(2)}) collective-permute-start(bf16[224,512]{1,0:T(8,128)(2,1)S(1)} %get-tuple-element.123), channel_id=1, source_target_pairs={{0,1},{1,0},{2,3},{3,2},{4,5},{5,4},{6,7},{7,6},{8,9},{9,8},{10,11... | collective-permute-start | bytes 688136 | tf_op jit(solution)/shard_map/ppermute | solution.py:23
  45.7 12.8 %collective-permute-start.15 = (bf16[384,512]{1,0:T(8,128)(2,1)S(1)}, bf16[384,512]{1,0:T(8,128)(2,1)S(1)}, u32[]{:S(2)}, u32[]{:S(2)}) collective-permute-start(bf16[384,512]{1,0:T(8,128)(2,1)S(1)} %get-tuple-element.120), channel_id=1, source_target_pairs={{0,2},{1,3},{2,0},{3,1},{4,6},{5,7},{6,4},{7,5},{8,10},{9,11},{10,... | collective-permute-start | bytes 1179656 | tf_op jit(solution)/shard_map/ppermute | solution.py:23
  47.1 5.7 %copy-start = (bf16[384,1024]{1,0:T(8,128)(2,1)S(1)}, bf16[384,1024]{1,0:T(8,128)(2,1)}, u32[]{:S(2)}) copy-start(bf16[384,1024]{1,0:T(8,128)(2,1)} %text_hbm.2) | copy-start | bytes 2359300
  47.1 12.5 %collective-permute-start.14 = (bf16[384,512]{1,0:T(8,128)(2,1)S(1)}, bf16[384,512]{1,0:T(8,128)(2,1)S(1)}, u32[]{:S(2)}, u32[]{:S(2)}) collective-permute-start(bf16[384,512]{1,0:T(8,128)(2,1)S(1)} %get-tuple-element.118), channel_id=1, source_target_pairs={{0,1},{1,0},{2,3},{3,2},{4,5},{5,4},{6,7},{7,6},{8,9},{9,8},{10,11... | collective-permute-start | bytes 1179656 | tf_op jit(solution)/shard_map/ppermute | solution.py:23
  50.1 14.8 %collective-permute-start.19 = (bf16[384,512]{1,0:T(8,128)(2,1)S(1)}, bf16[384,512]{1,0:T(8,128)(2,1)S(1)}, u32[]{:S(2)}, u32[]{:S(2)}) collective-permute-start(bf16[384,512]{1,0:T(8,128)(2,1)S(1)} %add_convert_fusion.1), channel_id=1, source_target_pairs={{0,1},{1,0},{2,3},{3,2},{4,5},{5,4},{6,7},{7,6},{8,9},{9,8},{10,11... | collective-permute-start | bytes 1179656 | tf_op jit(solution)/shard_map/ppermute | solution.py:23
  51.5 13.8 %collective-permute-start.17 = (bf16[384,512]{1,0:T(8,128)(2,1)S(1)}, bf16[384,512]{1,0:T(8,128)(2,1)S(1)}, u32[]{:S(2)}, u32[]{:S(2)}) collective-permute-start(bf16[384,512]{1,0:T(8,128)(2,1)S(1)} %add_convert_fusion.2), channel_id=1, source_target_pairs={{0,2},{1,3},{2,0},{3,1},{4,6},{5,7},{6,4},{7,5},{8,10},{9,11},{10,... | collective-permute-start | bytes 1179656 | tf_op jit(solution)/shard_map/ppermute | solution.py:23

commit v7 on v5

--- a/solution.py
+++ b/solution.py
@@ -690,18 +690,18 @@
     )
     pairs = mix_pairs(even, swap(odd, 1, "req"), region)
     received = [pairs[0]] + [swap(pairs[i], 2 * i, "req") for i in range(1, n_req // 2)]
+    ctext, table, pairs = lax.optimization_barrier((ctext, table, pairs))
+    acc, ss, held = own_part(ten_at, ctext, gains, w3)
+    text_at, img_at, text_row = placement(table, region, length, n_text, n_img)
+    received, acc, text_at = lax.optimization_barrier((received, acc, text_at))
     img_own = pack_images(received, vis_row, rtext, sel, region)
     img_blocks = [img_own] + [swap(img_own, s) for s in range(1, n_ten)]
-    own, img_own = lax.optimization_barrier((ctext, img_own))
-    acc, ss, held = own_part(ten_at, own, gains, w3)
     handed, img_own = lax.optimization_barrier((blocks, img_own))
     blocks = {**far_blocks(handed, n_ten), **blocks}
 
     near = [blocks[s] for s in near_at]
     acc, ss = near_part(near_at, ten_at, near, gains, held, acc, ss)
-    table, acc = lax.optimization_barrier((table, acc))
-    text_at, img_at, text_row = placement(table, region, length, n_text, n_img)
-    img_blocks, text_at = lax.optimization_barrier((img_blocks, text_at))
+    img_blocks, acc = lax.optimization_barrier((img_blocks, acc))
     img_qkv, merged, w_out = image_part(ten_at, img_blocks, gains, sel, held, w_out, n_rows)
 
     shared = (gains, held, acc, ss, img_qkv, text_at, img_at, key_ok, w_out)

time: 66.6 us -> 66.9 us (level)
  transfers between devices with their start and end apart: 19 -> 19, of which waited for: 10 -> 12; matrix products, arithmetic and copies ran while one was open for 1% -> 1% of each run, Pallas kernels for 29% -> 29%
where the time goes in v7:
time: 66.9 us; the launch traced here: 66.7 us
  starting transfers between devices  22.7 us (34%)
  Pallas kernels  21.8 us (33%)
  waiting for transfers between devices  21.2 us (32%)
    ppermute x19, starting transfers between devices, swap(): return lax.ppermute(x, axis, [(i, i ^ s) for i in range(n)])  22.7 us
    ppermute x19, waiting for transfers between devices, swap(): return lax.ppermute(x, axis, [(i, i ^ s) for i in range(n)])  21.2 us
    pallas_call x1, Pallas kernels, own_part(): pl.pallas_call(own_kernel, out_shape=(jax.ShapeDtypeStruct((3, rows, cols...  4.86 us
    pallas_call x1, Pallas kernels, image_part(): pl.pallas_call(functools.partial(image_kernel, n_rows, len(blocks)), out_...  2.65 us
    pallas_call x1, Pallas kernels, near_part(): pl.pallas_call(functools.partial(near_kernel, near, pieces), out_shape=(j...  2.27 us
    pallas_call x1, Pallas kernels, tail_part(): pl.pallas_call(functools.partial(tail_kernel, far), out_shape=(jax.ShapeD...  2.26 us
    pallas_call x1, Pallas kernels, prepare(): pl.pallas_call(functools.partial(prep_kernel, n_req), out_shape=tuple((ja...  2.2 us
    pallas_call x3, Pallas kernels, out_part(): pl.pallas_call(functools.partial(out_kernel, away), out_shape=(jax.ShapeD...  1.98 us
  transfers between devices with their start and end apart: 19, of which 12 were waited for; matrix products, arithmetic and copies ran while one was open for 1% of the time, Pallas kernels for 29%

profile of v7, /device:TPU:0, one launch (start us, length us, event | category | flops | bytes accessed | tf_op | source)
XLA Modules:
  0.0 66.7 jit_solution(8153803896673187721)
XLA Ops:
  0.0 1.7 %shard_map.91.x_ref = bf16[320,1024]{1,0:T(8,128)(2,1)S(1)} custom-call(s32[1]{0:T(128)} %bitcast.me_ref, s32[64]{0:T(128)} %req_hbm.3, s32[64]{0:T(128)} %start_hbm.3, bf16[384,1024]{1,0:T(8,128)(2,1)} %text_hbm.2), custom_call_target="tpu_custom_call" | custom-call | tf_op jit(solution)/shard_map/pallas_call | solution.py:117
  1.7 3.0 %collective-permute-start.7 = (bf16[320,1024]{1,0:T(8,128)(2,1)S(1)}, bf16[320,1024]{1,0:T(8,128)(2,1)S(1)}, u32[]{:S(2)}, u32[]{:S(2)}) collective-permute-start(bf16[320,1024]{1,0:T(8,128)(2,1)S(1)} %shard_map.91.x_ref), channel_id=1, source_target_pairs={{0,1},{1,0},{2,3},{3,2},{4,5},{5,4},{6,7},{7,6},{8,9},{9,8},{10,11... | collective-permute-start | bytes 1966088 | tf_op jit(solution)/shard_map/ppermute | solution.py:23
  4.7 1.5 %collective-permute-start.8 = (bf16[320,1024]{1,0:T(8,128)(2,1)S(1)}, bf16[320,1024]{1,0:T(8,128)(2,1)S(1)}, u32[]{:S(2)}, u32[]{:S(2)}) collective-permute-start(bf16[320,1024]{1,0:T(8,128)(2,1)S(1)} %shard_map.91.x_ref), channel_id=1, source_target_pairs={{0,2},{1,3},{2,0},{3,1},{4,6},{5,7},{6,4},{7,5},{8,10},{9,11},{10,... | collective-permute-start | bytes 1966088 | tf_op jit(solution)/shard_map/ppermute | solution.py:23
  6.2 2.2 %shard_map.92 = (bf16[4,16,1024]{2,1,0:T(8,128)(2,1)S(1)}, bf16[4,16,1024]{2,1,0:T(8,128)(2,1)S(1)}, bf16[80,1024]{1,0:T(8,128)(2,1)S(1)}, bf16[80,80]{1,0:T(8,1...) custom-call(s32[1]{0:T(128)} %bitcast.me_ref, ...), custom_call_target="tpu_custom_call" | custom-call | tf_op jit(solution)/shard_map/pallas_call | solution.py:225
  8.4 0.1 collective-permute-start
  8.5 1.3 %collective-permute-done.odd_ref = bf16[4,16,1024]{2,1,0:T(8,128)(2,1)S(1)} collective-permute-done((bf16[4,16,1024]{2,1,0:T(8,128)(2,1)S(1)}, bf16[4,16,1024]{2,1,0:T(8,128)(2,1)S(1)}, u32[]{:S(2)}, u32[]{:S(2)}) %collective-permute-start) | collective-permute-done | bytes 131104 | tf_op jit(solution)/shard_map/ppermute | solution.py:23
  9.8 0.1 shard_map.93
  9.9 1.6 %collective-permute-start.1 = (bf16[24,1024]{1,0:T(8,128)(2,1)S(1)}, bf16[24,1024]{1,0:T(8,128)(2,1)S(1)}, u32[]{:S(2)}, u32[]{:S(2)}) collective-permute-start(bf16[24,1024]{1,0:T(8,128)(2,1)S(1)} %get-tuple-element.69), channel_id=1, source_target_pairs={{0,8},{4,12},{8,0},{12,4},{16,24},{20,28},{24,16},{28,20},{1,9},{5... | collective-permute-start | bytes 147464 | tf_op jit(solution)/shard_map/ppermute | solution.py:23
  11.5 2.6 %collective-permute-start.2 = (bf16[24,1024]{1,0:T(8,128)(2,1)S(1)}, bf16[24,1024]{1,0:T(8,128)(2,1)S(1)}, u32[]{:S(2)}, u32[]{:S(2)}) collective-permute-start(bf16[24,1024]{1,0:T(8,128)(2,1)S(1)} %get-tuple-element.70), channel_id=1, source_target_pairs={{0,16},{4,20},{8,24},{12,28},{16,0},{20,4},{24,8},{28,12},{1,17},{... | collective-permute-start | bytes 147464 | tf_op jit(solution)/shard_map/ppermute | solution.py:23
  14.1 0.2 collective-permute-start.3
  14.3 0.7 %shard_map.94 = (bf16[384,320]{1,0:T(8,128)(2,1)S(1)}, bf16[384,80]{1,0:T(8,128)(2,1)S(1)}, f32[384,128]{1,0:T(8,128)S(1)}) custom-call(s32[8,128]{1,0:T(8,128)S(1)} %get-tuple-element.72.table_ref), custom_call_target="tpu_custom_call" | custom-call | tf_op jit(solution)/shard_map/pallas_call | solution.py:305
  15.1 4.9 %shard_map.95 = (f32[3,320,512]{2,1,0:T(8,128)S(1)}, f32[320,128]{1,0:T(8,128)S(1)}, bf16[4,3,1024,512]{3,2,1,0:T(8,128)(2,1)S(1)}) custom-call(s32[1]{0:T(128)} %bitcast.5.me_ref, bf16[320,1024]{1,0:T(8,128)(2,1)S(1)} %shard_map.91.x_ref, f32[4,1,1024]{2,1,0:T(1,128)S(1)} %get-tuple-element.79.gain_ref.refs_2_.refs_4_, bf16[3,4096,512]{2,1,0:T(8,128)(2,1)} %bitcast.9), custom_call_target="tpu_custom_call" | custom-call | tf_op jit(solution)/shard_map/pallas_call | solution.py:356
  19.9 0.0 collective-permute-done.1.refs_1_
  19.9 0.0 collective-permute-done.2.refs_2_
  19.9 0.1 collective-permute-done.3.refs_3_
  20.0 0.2 shard_map.96.refs_0_
  20.2 0.6 collective-permute-start.4
  20.8 0.5 collective-permute-start.5
  21.3 2.4 %collective-permute-start.6 = (bf16[80,1024]{1,0:T(8,128)(2,1)S(1)}, bf16[80,1024]{1,0:T(8,128)(2,1)S(1)}, u32[]{:S(2)}, u32[]{:S(2)}) collective-permute-start(bf16[80,1024]{1,0:T(8,128)(2,1)S(1)} %shard_map.96.refs_0_), channel_id=1, source_target_pairs={{0,3},{1,2},{2,1},{3,0},{4,7},{5,6},{6,5},{7,4},{8,11},{9,10},{10,... | collective-permute-start | bytes 491528 | tf_op jit(solution)/shard_map/ppermute | solution.py:23
  23.8 0.0 collective-permute-done.7.refs_0_
  23.8 0.0 collective-permute-done.8.refs_1_
  23.8 0.6 collective-permute-start.9
  24.4 0.6 collective-permute-start.12
  25.0 2.3 %shard_map.97 = (f32[3,320,512]{2,1,0:T(8,128)S(1)}, f32[320,128]{1,0:T(8,128)S(1)}) custom-call(s32[1]{0:T(128)} %bitcast.5.me_ref, bf16[320,1024]{1,0:T(8,128)(2,1)S(1)} %collective-permute-done.7.refs_0_, bf16[320,1024]{1,0:T(8,128)(2,1)S(1)} %collective-permute-done.8.refs_1_, f32[4,1,1024]{2,1,0:T(1,128)S(1)} %get-tuple-element.79.gain_ref.refs_2_.refs_4_, ...), custom_call_target="tpu_custom_call" | custom-call | flops 99999997952 | tf_op jit(solution)/shard_map/pallas_call | solution.py:400
  27.3 0.1 collective-permute-done.4.refs_1_
  27.4 3.4 %collective-permute-done.5.refs_2_ = bf16[80,1024]{1,0:T(8,128)(2,1)S(1)} collective-permute-done((bf16[80,1024]{1,0:T(8,128)(2,1)S(1)}, bf16[80,1024]{1,0:T(8,128)(2,1)S(1)}, u32[]{:S(2)}, u32[]{:S(2)}) %collective-permute-start.5) | collective-permute-done | bytes 163872 | tf_op jit(solution)/shard_map/ppermute | solution.py:23
  30.8 0.1 collective-permute-done.6.refs_3_
  30.9 2.6 %shard_map.98 = (bf16[3,80,512]{2,1,0:T(8,128)(2,1)S(1)}, bf16[80,1024]{1,0:T(8,128)(2,1)S(1)}, bf16[512,4096]{1,0:T(8,128)(2,1)S(1)}) custom-call(s32[1]{0:T(128)} %bitcast.5.me_ref, bf16[80,1024]{1,0:T(8,128)(2,1)S(1)} %shard_map.96.refs_0_, bf16[80,1024]{1,0:T(8,128)(2,1)S(1)} %collective-permute-done.4.refs_1_, ...), custom_call_target="tpu_custom_call" | custom-call | tf_op jit(solution)/shard_map/pallas_call | solution.py:446
  33.5 2.7 %collective-permute-done.9.top_ref = bf16[160,1024]{1,0:T(8,128)(2,1)S(1)} collective-permute-done((bf16[160,1024]{1,0:T(8,128)(2,1)S(1)}, bf16[160,1024]{1,0:T(8,128)(2,1)S(1)}, u32[]{:S(2)}, u32[]{:S(2)}) %collective-permute-start.9) | collective-permute-done | bytes 327712 | tf_op jit(solution)/shard_map/ppermute | solution.py:23
  36.2 1.7 %shard_map.99 = (bf16[3,160,512]{2,1,0:T(8,128)(2,1)S(1)}, bf16[3,160,512]{2,1,0:T(8,128)(2,1)S(1)}, bf16[160,512]{1,0:T(8,128)(2,1)S(1)}, bf16[160,512]{1,0:T(8,128)(2,1)S(1)}, bf16[160,512]{1,0:T(8,128)(2,1)S(1)}) custom-call(s32[1]{0:T(128)} %bitcast.5.me_ref, bf16[160,1024]{1,0:T(8,128)(2,1)S(1)} %collective-permute-done.9.top_ref, ...), custom_call_target="tpu_custom_call" | custom-call | tf_op jit(solution)/shard_map/pallas_call | solution.py:525
  37.9 0.6 collective-permute-start.10
  38.5 0.5 collective-permute-start.11
  39.0 0.0 collective-permute-done.12.bottom_ref
  39.0 2.3 %shard_map.100 = (bf16[224,512]{1,0:T(8,128)(2,1)S(1)}, bf16[224,512]{1,0:T(8,128)(2,1)S(1)}, bf16[224,512]{1,0:T(8,128)(2,1)S(1)}) custom-call(s32[1]{0:T(128)} %bitcast.5.me_ref, bf16[160,1024]{1,0:T(8,128)(2,1)S(1)} %collective-permute-done.12.bottom_ref, f32[4,1,1024]{2,1,0:T(1,128)S(1)} %get-tuple-element.79.gain_ref.refs_2_.refs_4_, ...), custom_call_target="tpu_custom_call" | custom-call | flops 10000000000 | tf_op jit(solution)/shard_map/pallas_call | solution.py:564
  41.3 1.6 %collective-permute-start.17 = (bf16[224,512]{1,0:T(8,128)(2,1)S(1)}, bf16[224,512]{1,0:T(8,128)(2,1)S(1)}, u32[]{:S(2)}, u32[]{:S(2)}) collective-permute-start(bf16[224,512]{1,0:T(8,128)(2,1)S(1)} %get-tuple-element.120), channel_id=1, source_target_pairs={{0,2},{1,3},{2,0},{3,1},{4,6},{5,7},{6,4},{7,5},{8,10},{9,11},{10,... | collective-permute-start | bytes 688136 | tf_op jit(solution)/shard_map/ppermute | solution.py:23
  42.9 1.5 %collective-permute-start.15 = (bf16[224,512]{1,0:T(8,128)(2,1)S(1)}, bf16[224,512]{1,0:T(8,128)(2,1)S(1)}, u32[]{:S(2)}, u32[]{:S(2)}) collective-permute-start(bf16[224,512]{1,0:T(8,128)(2,1)S(1)} %get-tuple-element.117), channel_id=1, source_target_pairs={{0,1},{1,0},{2,3},{3,2},{4,5},{5,4},{6,7},{7,6},{8,9},{9,8},{10,11... | collective-permute-start | bytes 688136 | tf_op jit(solution)/shard_map/ppermute | solution.py:23
  44.4 0.0 collective-permute-done.10
  44.4 0.9 %collective-permute-done.11 = bf16[160,512]{1,0:T(8,128)(2,1)S(1)} collective-permute-done((bf16[160,512]{1,0:T(8,128)(2,1)S(1)}, bf16[160,512]{1,0:T(8,128)(2,1)S(1)}, u32[]{:S(2)}, u32[]{:S(2)}) %collective-permute-start.11) | collective-permute-done | bytes 163872 | tf_op jit(solution)/shard_map/ppermute | solution.py:23
  45.4 0.8 %shard_map.103 = (bf16[384,512]{1,0:T(8,128)(2,1)S(1)}, bf16[384,512]{1,0:T(8,128)(2,1)S(1)}) custom-call(s32[1]{0:T(128)} %bitcast.5.me_ref, bf16[160,512]{1,0:T(8,128)(2,1)S(1)} %get-tuple-element.109.head_ref, bf16[224,512]{1,0:T(8,128)(2,1)S(1)} %get-tuple-element.110.tail_ref, bf16[512,4096]{1,0:T(8,128)(2,1)S(1)} %get-tuple-element.101.w_out_ref.w_ref), custom_call_target="tpu_custom_call" | custom-call | flops 1000000000 | tf_op jit(solution)/shard_map/pallas_call | solution.py:589
  46.1 0.1 collective-permute-start.14
  46.2 0.6 shard_map.102
  46.8 0.0 copy-start
  46.8 1.8 %collective-permute-start.13 = (bf16[384,512]{1,0:T(8,128)(2,1)S(1)}, bf16[384,512]{1,0:T(8,128)(2,1)S(1)}, u32[]{:S(2)}, u32[]{:S(2)}) collective-permute-start(bf16[384,512]{1,0:T(8,128)(2,1)S(1)} %get-tuple-element.112), channel_id=1, source_target_pairs={{0,1},{1,0},{2,3},{3,2},{4,5},{5,4},{6,7},{7,6},{8,9},{9,8},{10,11... | collective-permute-start | bytes 1179656 | tf_op jit(solution)/shard_map/ppermute | solution.py:23
  48.7 1.6 %collective-permute-done.17 = bf16[224,512]{1,0:T(8,128)(2,1)S(1)} collective-permute-done((bf16[224,512]{1,0:T(8,128)(2,1)S(1)}, bf16[224,512]{1,0:T(8,128)(2,1)S(1)}, u32[]{:S(2)}, u32[]{:S(2)}) %collective-permute-start.17) | collective-permute-done | bytes 229408 | tf_op jit(solution)/shard_map/ppermute | solution.py:23
  50.3 0.1 add_convert_fusion.1
  50.4 1.8 %collective-permute-start.18 = (bf16[384,512]{1,0:T(8,128)(2,1)S(1)}, bf16[384,512]{1,0:T(8,128)(2,1)S(1)}, u32[]{:S(2)}, u32[]{:S(2)}) collective-permute-start(bf16[384,512]{1,0:T(8,128)(2,1)S(1)} %add_convert_fusion.1), channel_id=1, source_target_pairs={{0,1},{1,0},{2,3},{3,2},{4,5},{5,4},{6,7},{7,6},{8,9},{9,8},{10,11... | collective-permute-start | bytes 1179656 | tf_op jit(solution)/shard_map/ppermute | solution.py:23
  52.2 0.0 collective-permute-done.15
  52.2 0.1 add_convert_fusion.2
  52.3 1.0 %collective-permute-start.16 = (bf16[384,512]{1,0:T(8,128)(2,1)S(1)}, bf16[384,512]{1,0:T(8,128)(2,1)S(1)}, u32[]{:S(2)}, u32[]{:S(2)}) collective-permute-start(bf16[384,512]{1,0:T(8,128)(2,1)S(1)} %add_convert_fusion.2), channel_id=1, source_target_pairs={{0,2},{1,3},{2,0},{3,1},{4,6},{5,7},{6,4},{7,5},{8,10},{9,11},{10,... | collective-permute-start | bytes 1179656 | tf_op jit(solution)/shard_map/ppermute | solution.py:23
  53.3 0.1 slice_reduce_fusion
  53.4 0.0 copy-done
  53.4 0.4 add_convert_fusion.base_ref
  53.8 0.6 shard_map.101
  54.4 4.3 %collective-permute-done.14.refs_3_ = bf16[384,512]{1,0:T(8,128)(2,1)S(1)} collective-permute-done((bf16[384,512]{1,0:T(8,128)(2,1)S(1)}, bf16[384,512]{1,0:T(8,128)(2,1)S(1)}, u32[]{:S(2)}, u32[]{:S(2)}) %collective-permute-start.14) | collective-permute-done | bytes 393248 | tf_op jit(solution)/shard_map/ppermute | solution.py:23
  58.7 1.2 %collective-permute-done.13.refs_1_ = bf16[384,512]{1,0:T(8,128)(2,1)S(1)} collective-permute-done((bf16[384,512]{1,0:T(8,128)(2,1)S(1)}, bf16[384,512]{1,0:T(8,128)(2,1)S(1)}, u32[]{:S(2)}, u32[]{:S(2)}) %collective-permute-start.13) | collective-permute-done | bytes 393248 | tf_op jit(solution)/shard_map/ppermute | solution.py:23
  59.9 0.3 shard_map.104.base_ref
  60.1 5.3 %collective-permute-done.18.refs_1_ = bf16[384,512]{1,0:T(8,128)(2,1)S(1)} collective-permute-done((bf16[384,512]{1,0:T(8,128)(2,1)S(1)}, bf16[384,512]{1,0:T(8,128)(2,1)S(1)}, u32[]{:S(2)}, u32[]{:S(2)}) %collective-permute-start.18) | collective-permute-done | bytes 393248 | tf_op jit(solution)/shard_map/ppermute | solution.py:23
  65.4 0.2 collective-permute-done.16.refs_0_
  65.6 1.0 %shard_map.105 = bf16[384,1024]{1,0:T(8,128)(2,1)} custom-call(f32[384,1024]{1,0:T(8,128)S(1)} %shard_map.104.base_ref, bf16[384,512]{1,0:T(8,128)(2,1)S(1)} %collective-permute-done.16.refs_0_, bf16[384,512]{1,0:T(8,128)(2,1)S(1)} %collective-permute-done.18.refs_1_), custom_call_target="tpu_custom_call" | custom-call | tf_op jit(solution)/shard_map/pallas_call | solution.py:637
  (2 shorter events, 0.0 us)
Async XLA Ops:
  1.7 22.1 %collective-permute-start.7 = (bf16[320,1024]{1,0:T(8,128)(2,1)S(1)}, bf16[320,1024]{1,0:T(8,128)(2,1)S(1)}, u32[]{:S(2)}, u32[]{:S(2)}) collective-permute-start(bf16[320,1024]{1,0:T(8,128)(2,1)S(1)} %shard_map.91.x_ref), channel_id=1, source_target_pairs={{0,1},{1,0},{2,3},{3,2},{4,5},{5,4},{6,7},{7,6},{8,9},{9,8},{10,11... | collective-permute-start | bytes 1966088 | tf_op jit(solution)/shard_map/ppermute | solution.py:23
  4.7 19.1 %collective-permute-start.8 = (bf16[320,1024]{1,0:T(8,128)(2,1)S(1)}, bf16[320,1024]{1,0:T(8,128)(2,1)S(1)}, u32[]{:S(2)}, u32[]{:S(2)}) collective-permute-start(bf16[320,1024]{1,0:T(8,128)(2,1)S(1)} %shard_map.91.x_ref), channel_id=1, source_target_pairs={{0,2},{1,3},{2,0},{3,1},{4,6},{5,7},{6,4},{7,5},{8,10},{9,11},{10,... | collective-permute-start | bytes 1966088 | tf_op jit(solution)/shard_map/ppermute | solution.py:23
  8.4 1.4 %collective-permute-start = (bf16[4,16,1024]{2,1,0:T(8,128)(2,1)S(1)}, bf16[4,16,1024]{2,1,0:T(8,128)(2,1)S(1)}, u32[]{:S(2)}, u32[]{:S(2)}) collective-permute-start(bf16[4,16,1024]{2,1,0:T(8,128)(2,1)S(1)} %get-tuple-element.67), channel_id=1, source_target_pairs={{0,4},{4,0},{8,12},{12,8},{16,20},{20,16},{24,28},{28,24},{1,5},{5... | collective-permute-start | bytes 393224 | tf_op jit(solution)/shard_map/ppermute | solution.py:23
  9.9 10.0 %collective-permute-start.1 = (bf16[24,1024]{1,0:T(8,128)(2,1)S(1)}, bf16[24,1024]{1,0:T(8,128)(2,1)S(1)}, u32[]{:S(2)}, u32[]{:S(2)}) collective-permute-start(bf16[24,1024]{1,0:T(8,128)(2,1)S(1)} %get-tuple-element.69), channel_id=1, source_target_pairs={{0,8},{4,12},{8,0},{12,4},{16,24},{20,28},{24,16},{28,20},{1,9},{5... | collective-permute-start | bytes 147464 | tf_op jit(solution)/shard_map/ppermute | solution.py:23
  11.5 8.4 %collective-permute-start.2 = (bf16[24,1024]{1,0:T(8,128)(2,1)S(1)}, bf16[24,1024]{1,0:T(8,128)(2,1)S(1)}, u32[]{:S(2)}, u32[]{:S(2)}) collective-permute-start(bf16[24,1024]{1,0:T(8,128)(2,1)S(1)} %get-tuple-element.70), channel_id=1, source_target_pairs={{0,16},{4,20},{8,24},{12,28},{16,0},{20,4},{24,8},{28,12},{1,17},{... | collective-permute-start | bytes 147464 | tf_op jit(solution)/shard_map/ppermute | solution.py:23
  14.1 5.9 %collective-permute-start.3 = (bf16[24,1024]{1,0:T(8,128)(2,1)S(1)}, bf16[24,1024]{1,0:T(8,128)(2,1)S(1)}, u32[]{:S(2)}, u32[]{:S(2)}) collective-permute-start(bf16[24,1024]{1,0:T(8,128)(2,1)S(1)} %get-tuple-element.71), channel_id=1, source_target_pairs={{0,24},{4,28},{8,16},{12,20},{16,8},{20,12},{24,0},{28,4},{1,25},{... | collective-permute-start | bytes 147464 | tf_op jit(solution)/shard_map/ppermute | solution.py:23
  20.2 7.2 %collective-permute-start.4 = (bf16[80,1024]{1,0:T(8,128)(2,1)S(1)}, bf16[80,1024]{1,0:T(8,128)(2,1)S(1)}, u32[]{:S(2)}, u32[]{:S(2)}) collective-permute-start(bf16[80,1024]{1,0:T(8,128)(2,1)S(1)} %shard_map.96.refs_0_), channel_id=1, source_target_pairs={{0,1},{1,0},{2,3},{3,2},{4,5},{5,4},{6,7},{7,6},{8,9},{9,8},{10,11... | collective-permute-start | bytes 491528 | tf_op jit(solution)/shard_map/ppermute | solution.py:23
  20.8 10.0 %collective-permute-start.5 = (bf16[80,1024]{1,0:T(8,128)(2,1)S(1)}, bf16[80,1024]{1,0:T(8,128)(2,1)S(1)}, u32[]{:S(2)}, u32[]{:S(2)}) collective-permute-start(bf16[80,1024]{1,0:T(8,128)(2,1)S(1)} %shard_map.96.refs_0_), channel_id=1, source_target_pairs={{0,2},{1,3},{2,0},{3,1},{4,6},{5,7},{6,4},{7,5},{8,10},{9,11},{10,... | collective-permute-start | bytes 491528 | tf_op jit(solution)/shard_map/ppermute | solution.py:23
  21.3 9.6 %collective-permute-start.6 = (bf16[80,1024]{1,0:T(8,128)(2,1)S(1)}, bf16[80,1024]{1,0:T(8,128)(2,1)S(1)}, u32[]{:S(2)}, u32[]{:S(2)}) collective-permute-start(bf16[80,1024]{1,0:T(8,128)(2,1)S(1)} %shard_map.96.refs_0_), channel_id=1, source_target_pairs={{0,3},{1,2},{2,1},{3,0},{4,7},{5,6},{6,5},{7,4},{8,11},{9,10},{10,... | collective-permute-start | bytes 491528 | tf_op jit(solution)/shard_map/ppermute | solution.py:23
  23.8 12.4 %collective-permute-start.9 = (bf16[160,1024]{1,0:T(8,128)(2,1)S(1)}, bf16[160,1024]{1,0:T(8,128)(2,1)S(1)}, u32[]{:S(2)}, u32[]{:S(2)}) collective-permute-start(bf16[160,1024]{1,0:T(8,128)(2,1)S(1)} %slice.10), channel_id=1, source_target_pairs={{0,1},{1,0},{2,3},{3,2},{4,5},{5,4},{6,7},{7,6},{8,9},{9,8},{10,11... | collective-permute-start | bytes 983048 | tf_op jit(solution)/shard_map/ppermute | solution.py:23
  24.4 14.6 %collective-permute-start.12 = (bf16[160,1024]{1,0:T(8,128)(2,1)S(1)}, bf16[160,1024]{1,0:T(8,128)(2,1)S(1)}, u32[]{:S(2)}, u32[]{:S(2)}) collective-permute-start(bf16[160,1024]{1,0:T(8,128)(2,1)S(1)} %slice.11), channel_id=1, source_target_pairs={{0,2},{1,3},{2,0},{3,1},{4,6},{5,7},{6,4},{7,5},{8,10},{9,11},{10,... | collective-permute-start | bytes 983048 | tf_op jit(solution)/shard_map/ppermute | solution.py:23
  37.9 6.5 %collective-permute-start.10 = (bf16[160,512]{1,0:T(8,128)(2,1)S(1)}, bf16[160,512]{1,0:T(8,128)(2,1)S(1)}, u32[]{:S(2)}, u32[]{:S(2)}) collective-permute-start(bf16[160,512]{1,0:T(8,128)(2,1)S(1)} %get-tuple-element.102), channel_id=1, source_target_pairs={{0,1},{1,0},{2,3},{3,2},{4,5},{5,4},{6,7},{7,6},{8,9},{9,8},{10,11... | collective-permute-start | bytes 491528 | tf_op jit(solution)/shard_map/ppermute | solution.py:23
  38.5 6.8 %collective-permute-start.11 = (bf16[160,512]{1,0:T(8,128)(2,1)S(1)}, bf16[160,512]{1,0:T(8,128)(2,1)S(1)}, u32[]{:S(2)}, u32[]{:S(2)}) collective-permute-start(bf16[160,512]{1,0:T(8,128)(2,1)S(1)} %get-tuple-element.103), channel_id=1, source_target_pairs={{0,2},{1,3},{2,0},{3,1},{4,6},{5,7},{6,4},{7,5},{8,10},{9,11},{10,... | collective-permute-start | bytes 491528 | tf_op jit(solution)/shard_map/ppermute | solution.py:23
  41.3 9.0 %collective-permute-start.17 = (bf16[224,512]{1,0:T(8,128)(2,1)S(1)}, bf16[224,512]{1,0:T(8,128)(2,1)S(1)}, u32[]{:S(2)}, u32[]{:S(2)}) collective-permute-start(bf16[224,512]{1,0:T(8,128)(2,1)S(1)} %get-tuple-element.120), channel_id=1, source_target_pairs={{0,2},{1,3},{2,0},{3,1},{4,6},{5,7},{6,4},{7,5},{8,10},{9,11},{10,... | collective-permute-start | bytes 688136 | tf_op jit(solution)/shard_map/ppermute | solution.py:23
  42.9 9.3 %collective-permute-start.15 = (bf16[224,512]{1,0:T(8,128)(2,1)S(1)}, bf16[224,512]{1,0:T(8,128)(2,1)S(1)}, u32[]{:S(2)}, u32[]{:S(2)}) collective-permute-start(bf16[224,512]{1,0:T(8,128)(2,1)S(1)} %get-tuple-element.117), channel_id=1, source_target_pairs={{0,1},{1,0},{2,3},{3,2},{4,5},{5,4},{6,7},{7,6},{8,9},{9,8},{10,11... | collective-permute-start | bytes 688136 | tf_op jit(solution)/shard_map/ppermute | solution.py:23
  46.1 12.6 %collective-permute-start.14 = (bf16[384,512]{1,0:T(8,128)(2,1)S(1)}, bf16[384,512]{1,0:T(8,128)(2,1)S(1)}, u32[]{:S(2)}, u32[]{:S(2)}) collective-permute-start(bf16[384,512]{1,0:T(8,128)(2,1)S(1)} %get-tuple-element.114), channel_id=1, source_target_pairs={{0,2},{1,3},{2,0},{3,1},{4,6},{5,7},{6,4},{7,5},{8,10},{9,11},{10,... | collective-permute-start | bytes 1179656 | tf_op jit(solution)/shard_map/ppermute | solution.py:23
  46.8 6.6 %copy-start = (bf16[384,1024]{1,0:T(8,128)(2,1)S(1)}, bf16[384,1024]{1,0:T(8,128)(2,1)}, u32[]{:S(2)}) copy-start(bf16[384,1024]{1,0:T(8,128)(2,1)} %text_hbm.2) | copy-start | bytes 2359300
  46.8 13.0 %collective-permute-start.13 = (bf16[384,512]{1,0:T(8,128)(2,1)S(1)}, bf16[384,512]{1,0:T(8,128)(2,1)S(1)}, u32[]{:S(2)}, u32[]{:S(2)}) collective-permute-start(bf16[384,512]{1,0:T(8,128)(2,1)S(1)} %get-tuple-element.112), channel_id=1, source_target_pairs={{0,1},{1,0},{2,3},{3,2},{4,5},{5,4},{6,7},{7,6},{8,9},{9,8},{10,11... | collective-permute-start | bytes 1179656 | tf_op jit(solution)/shard_map/ppermute | solution.py:23
  50.4 15.0 %collective-permute-start.18 = (bf16[384,512]{1,0:T(8,128)(2,1)S(1)}, bf16[384,512]{1,0:T(8,128)(2,1)S(1)}, u32[]{:S(2)}, u32[]{:S(2)}) collective-permute-start(bf16[384,512]{1,0:T(8,128)(2,1)S(1)} %add_convert_fusion.1), channel_id=1, source_target_pairs={{0,1},{1,0},{2,3},{3,2},{4,5},{5,4},{6,7},{7,6},{8,9},{9,8},{10,11... | collective-permute-start | bytes 1179656 | tf_op jit(solution)/shard_map/ppermute | solution.py:23
  52.3 13.3 %collective-permute-start.16 = (bf16[384,512]{1,0:T(8,128)(2,1)S(1)}, bf16[384,512]{1,0:T(8,128)(2,1)S(1)}, u32[]{:S(2)}, u32[]{:S(2)}) collective-permute-start(bf16[384,512]{1,0:T(8,128)(2,1)S(1)} %add_convert_fusion.2), channel_id=1, source_target_pairs={{0,2},{1,3},{2,0},{3,1},{4,6},{5,7},{6,4},{7,5},{8,10},{9,11},{10,... | collective-permute-start | bytes 1179656 | tf_op jit(solution)/shard_map/ppermute | solution.py:23

commit v8 on v6

--- a/solution.py
+++ b/solution.py
@@ -462,7 +462,7 @@
         out_specs=tuple(vmem_specs(3)),
         scratch_shapes=[pltpu.SemaphoreType.DMA],
         compiler_params=params(12),
-        cost_estimate=TINY,
+        cost_estimate=pl.CostEstimate(flops=3*10**9, bytes_accessed=0, transcendentals=0),
     )(me, *blocks, gain, sel, held, in_hbm(w_out))
 
 
@@ -746,25 +746,26 @@
     )
     pairs = mix_pairs(even, swap(odd, 1, "req"), region)
     received = [pairs[0]] + [swap(pairs[i], 2 * i, "req") for i in range(1, n_req // 2)]
-    ctext, pairs = lax.optimization_barrier((ctext, pairs))
+    ctext, table, pairs = lax.optimization_barrier((ctext, table, pairs))
     acc, ss, held = own_part(ten_at, ctext, gains, w3)
-    received, acc = lax.optimization_barrier((received, acc))
+    text_at, img_at, text_row = placement(table, region, length, n_text, n_img)
+    received, acc, text_at = lax.optimization_barrier((received, acc, text_at))
     img_own = pack_images(received, vis_row, rtext, sel, region)
     img_near = near_blocks(img_own, n_ten)
-    handed, img_own = lax.optimization_barrier((blocks, img_own))
-    blocks = {**far_blocks(handed, n_ten), **blocks}
-
-    near = [blocks[s] for s in near_at]
-    acc, ss = near_part(near_at, ten_at, near, gains, held, acc, ss)
-    table, img_near, acc = lax.optimization_barrier((table, img_near, acc))
-    text_at, img_at, text_row = placement(table, region, length, n_text, n_img)
+    one_bit = sorted(img_near)
+    more_bits = [s for s in order if s not in img_near]
+
+    blocks, img_own = lax.optimization_barrier((blocks, img_own))
+    acc, ss = near_part(one_bit, ten_at, [blocks[s] for s in one_bit], gains, held, acc, ss)
+    blocks, acc = lax.optimization_barrier((blocks, acc))
+    blocks = far_blocks(blocks, n_ten)
+    between = more_bits[:-1]
+    if between:
+        acc, ss = near_part(between, ten_at, [blocks[s] for s in between], gains, held, acc, ss)
     img_blocks = far_blocks(img_near, n_ten)
-    img_near, text_at = lax.optimization_barrier((img_near, text_at))
-    one_bit = [0] + sorted(img_near)
     img_acc, img_sums, w_out = image_part(
-        one_bit, ten_at, [img_own] + [img_near[s] for s in one_bit[1:]], gains, sel, held, w_out, n_rows
+        [0] + one_bit, ten_at, [img_own] + [img_near[s] for s in one_bit], gains, sel, held, w_out, n_rows
     )
-    more_bits = [s for s in order if s not in img_near]
     img_qkv, merged = image_end(
         more_bits, ten_at, [img_blocks[s] for s in more_bits], img_own, gains, sel, held, img_acc, img_sums, n_rows
     )

time: 66.6 us -> 67.6 us (1.015)
  starting transfers between devices: 24.1 us -> 25.4 us
    ppermute x20, starting transfers between devices: 24.1 us -> 25.4 us  [swap(): return lax.ppermute(x, axis, [(i, i ^ s) for i in range(n)])]
  transfers between devices with their start and end apart: 20 -> 20, of which waited for: 12 -> 8; matrix products, arithmetic and copies ran while one was open for 1% -> 1% of each run, Pallas kernels for 30% -> 30%
where the time goes in v8:
time: 67.6 us; the launch traced here: 67.4 us
  starting transfers between devices  25.4 us (38%)
  Pallas kernels  22.8 us (34%)
  waiting for transfers between devices  18.1 us (27%)
    ppermute x20, starting transfers between devices, swap(): return lax.ppermute(x, axis, [(i, i ^ s) for i in range(n)])  25.4 us
    ppermute x20, waiting for transfers between devices, swap(): return lax.ppermute(x, axis, [(i, i ^ s) for i in range(n)])  18.1 us
    pallas_call x1, Pallas kernels, own_part(): pl.pallas_call(own_kernel, out_shape=(jax.ShapeDtypeStruct((3, rows, cols...  4.86 us
    pallas_call x1, Pallas kernels, tail_part(): pl.pallas_call(functools.partial(tail_kernel, far), out_shape=(jax.ShapeD...  2.47 us
    pallas_call x1, Pallas kernels, image_part(): pl.pallas_call(functools.partial(image_kernel, n_rows, away), out_shape=(...  2.41 us
    pallas_call x1, Pallas kernels, near_part(): pl.pallas_call(functools.partial(near_kernel, near, pieces), out_shape=(j...  2.28 us
    pallas_call x1, Pallas kernels, prepare(): pl.pallas_call(functools.partial(prep_kernel, n_req), out_shape=tuple((ja...  2.2 us
    pallas_call x3, Pallas kernels, out_part(): pl.pallas_call(functools.partial(out_kernel, away), out_shape=(jax.ShapeD...  1.74 us
  transfers between devices with their start and end apart: 20, of which 8 were waited for; matrix products, arithmetic and copies ran while one was open for 1% of the time, Pallas kernels for 30%

profile of v8, /device:TPU:0, one launch (start us, length us, event | category | flops | bytes accessed | tf_op | source)
XLA Modules:
  0.0 67.4 jit_solution(9060225969828620972)
XLA Ops:
  0.0 1.7 %shard_map.91.x_ref = bf16[320,1024]{1,0:T(8,128)(2,1)S(1)} custom-call(s32[1]{0:T(128)} %bitcast.me_ref, s32[64]{0:T(128)} %req_hbm.3, s32[64]{0:T(128)} %start_hbm.3, bf16[384,1024]{1,0:T(8,128)(2,1)} %text_hbm.2), custom_call_target="tpu_custom_call" | custom-call | tf_op jit(solution)/shard_map/pallas_call | solution.py:117
  1.7 3.0 %collective-permute-start.8 = (bf16[320,1024]{1,0:T(8,128)(2,1)S(1)}, bf16[320,1024]{1,0:T(8,128)(2,1)S(1)}, u32[]{:S(2)}, u32[]{:S(2)}) collective-permute-start(bf16[320,1024]{1,0:T(8,128)(2,1)S(1)} %shard_map.91.x_ref), channel_id=1, source_target_pairs={{0,1},{1,0},{2,3},{3,2},{4,5},{5,4},{6,7},{7,6},{8,9},{9,8},{10,11... | collective-permute-start | bytes 1966088 | tf_op jit(solution)/shard_map/ppermute | solution.py:23
  4.7 1.5 %collective-permute-start.9 = (bf16[320,1024]{1,0:T(8,128)(2,1)S(1)}, bf16[320,1024]{1,0:T(8,128)(2,1)S(1)}, u32[]{:S(2)}, u32[]{:S(2)}) collective-permute-start(bf16[320,1024]{1,0:T(8,128)(2,1)S(1)} %shard_map.91.x_ref), channel_id=1, source_target_pairs={{0,2},{1,3},{2,0},{3,1},{4,6},{5,7},{6,4},{7,5},{8,10},{9,11},{10,... | collective-permute-start | bytes 1966088 | tf_op jit(solution)/shard_map/ppermute | solution.py:23
  6.2 2.2 %shard_map.92 = (bf16[4,16,1024]{2,1,0:T(8,128)(2,1)S(1)}, bf16[4,16,1024]{2,1,0:T(8,128)(2,1)S(1)}, bf16[80,1024]{1,0:T(8,128)(2,1)S(1)}, bf16[80,80]{1,0:T(8,1...) custom-call(s32[1]{0:T(128)} %bitcast.me_ref, ...), custom_call_target="tpu_custom_call" | custom-call | tf_op jit(solution)/shard_map/pallas_call | solution.py:225
  8.4 0.1 collective-permute-start
  8.5 1.3 %collective-permute-done.odd_ref = bf16[4,16,1024]{2,1,0:T(8,128)(2,1)S(1)} collective-permute-done((bf16[4,16,1024]{2,1,0:T(8,128)(2,1)S(1)}, bf16[4,16,1024]{2,1,0:T(8,128)(2,1)S(1)}, u32[]{:S(2)}, u32[]{:S(2)}) %collective-permute-start) | collective-permute-done | bytes 131104 | tf_op jit(solution)/shard_map/ppermute | solution.py:23
  9.8 0.1 shard_map.93
  9.9 1.6 %collective-permute-start.1 = (bf16[24,1024]{1,0:T(8,128)(2,1)S(1)}, bf16[24,1024]{1,0:T(8,128)(2,1)S(1)}, u32[]{:S(2)}, u32[]{:S(2)}) collective-permute-start(bf16[24,1024]{1,0:T(8,128)(2,1)S(1)} %get-tuple-element.70), channel_id=1, source_target_pairs={{0,8},{4,12},{8,0},{12,4},{16,24},{20,28},{24,16},{28,20},{1,9},{5... | collective-permute-start | bytes 147464 | tf_op jit(solution)/shard_map/ppermute | solution.py:23
  11.5 2.6 %collective-permute-start.2 = (bf16[24,1024]{1,0:T(8,128)(2,1)S(1)}, bf16[24,1024]{1,0:T(8,128)(2,1)S(1)}, u32[]{:S(2)}, u32[]{:S(2)}) collective-permute-start(bf16[24,1024]{1,0:T(8,128)(2,1)S(1)} %get-tuple-element.71), channel_id=1, source_target_pairs={{0,16},{4,20},{8,24},{12,28},{16,0},{20,4},{24,8},{28,12},{1,17},{... | collective-permute-start | bytes 147464 | tf_op jit(solution)/shard_map/ppermute | solution.py:23
  14.1 0.2 collective-permute-start.3
  14.3 0.7 %shard_map.94 = (bf16[384,320]{1,0:T(8,128)(2,1)S(1)}, bf16[384,80]{1,0:T(8,128)(2,1)S(1)}, f32[384,128]{1,0:T(8,128)S(1)}) custom-call(s32[8,128]{1,0:T(8,128)S(1)} %get-tuple-element.73.table_ref), custom_call_target="tpu_custom_call" | custom-call | tf_op jit(solution)/shard_map/pallas_call | solution.py:305
  15.1 4.9 %shard_map.95 = (f32[3,320,512]{2,1,0:T(8,128)S(1)}, f32[320,128]{1,0:T(8,128)S(1)}, bf16[4,3,1024,512]{3,2,1,0:T(8,128)(2,1)S(1)}) custom-call(s32[1]{0:T(128)} %bitcast.5.me_ref, bf16[320,1024]{1,0:T(8,128)(2,1)S(1)} %shard_map.91.x_ref, f32[4,1,1024]{2,1,0:T(1,128)S(1)} %get-tuple-element.80.gain_ref.refs_3_.refs_2_, bf16[3,4096,512]{2,1,0:T(8,128)(2,1)} %bitcast.9), custom_call_target="tpu_custom_call" | custom-call | tf_op jit(solution)/shard_map/pallas_call | solution.py:356
  19.9 0.0 collective-permute-done.1.refs_1_
  19.9 0.0 collective-permute-done.2.refs_2_
  19.9 0.1 collective-permute-done.3.refs_3_
  20.0 0.2 shard_map.96.refs_0_.refs_2_
  20.2 0.6 collective-permute-start.4
  20.8 0.5 collective-permute-start.6
  21.3 0.0 collective-permute-done.8.refs_0_
  21.3 0.0 collective-permute-done.9.refs_1_
  21.3 2.3 %shard_map.99 = (f32[3,320,512]{2,1,0:T(8,128)S(1)}, f32[320,128]{1,0:T(8,128)S(1)}) custom-call(s32[1]{0:T(128)} %bitcast.5.me_ref, bf16[320,1024]{1,0:T(8,128)(2,1)S(1)} %collective-permute-done.8.refs_0_, bf16[320,1024]{1,0:T(8,128)(2,1)S(1)} %collective-permute-done.9.refs_1_, f32[4,1,1024]{2,1,0:T(1,128)S(1)} %get-tuple-element.80.gain_ref.refs_3_.refs_2_, ...), custom_call_target="tpu_custom_call" | custom-call | flops 99999997952 | tf_op jit(solution)/shard_map/pallas_call | solution.py:400
  23.6 1.6 %collective-permute-start.10 = (bf16[160,1024]{1,0:T(8,128)(2,1)S(1)}, bf16[160,1024]{1,0:T(8,128)(2,1)S(1)}, u32[]{:S(2)}, u32[]{:S(2)}) collective-permute-start(bf16[160,1024]{1,0:T(8,128)(2,1)S(1)} %slice.18), channel_id=1, source_target_pairs={{0,1},{1,0},{2,3},{3,2},{4,5},{5,4},{6,7},{7,6},{8,9},{9,8},{10,11... | collective-permute-start | bytes 983048 | tf_op jit(solution)/shard_map/ppermute | solution.py:23
  25.2 1.6 %collective-permute-start.13 = (bf16[160,1024]{1,0:T(8,128)(2,1)S(1)}, bf16[160,1024]{1,0:T(8,128)(2,1)S(1)}, u32[]{:S(2)}, u32[]{:S(2)}) collective-permute-start(bf16[160,1024]{1,0:T(8,128)(2,1)S(1)} %slice.19), channel_id=1, source_target_pairs={{0,2},{1,3},{2,0},{3,1},{4,6},{5,7},{6,4},{7,5},{8,10},{9,11},{10,... | collective-permute-start | bytes 983048 | tf_op jit(solution)/shard_map/ppermute | solution.py:23
  26.8 0.0 collective-permute-done.4.refs_2_
  26.8 0.6 collective-permute-start.5
  27.4 0.0 collective-permute-done.6.refs_1_
  27.5 1.3 %collective-permute-start.7 = (bf16[32,1024]{1,0:T(8,128)(2,1)S(1)}, bf16[32,1024]{1,0:T(8,128)(2,1)S(1)}, u32[]{:S(2)}, u32[]{:S(2)}) collective-permute-start(bf16[32,1024]{1,0:T(8,128)(2,1)S(1)} %slice.21), channel_id=1, source_target_pairs={{0,2},{1,3},{2,0},{3,1},{4,6},{5,7},{6,4},{7,5},{8,10},{9,11},{10,... | collective-permute-start | bytes 196616 | tf_op jit(solution)/shard_map/ppermute | solution.py:23
  28.7 2.4 %shard_map.97 = (f32[3,80,512]{2,1,0:T(8,128)S(1)}, f32[2,80,128]{2,1,0:T(8,128)S(1)}, bf16[512,4096]{1,0:T(8,128)(2,1)S(1)}) custom-call(s32[1]{0:T(128)} %bitcast.5.me_ref, bf16[80,1024]{1,0:T(8,128)(2,1)S(1)} %shard_map.96.refs_0_.refs_2_, bf16[80,1024]{1,0:T(8,128)(2,1)S(1)} %collective-permute-done.6.refs_1_, ...), custom_call_target="tpu_custom_call" | custom-call | flops 3000000000 | tf_op jit(solution)/shard_map/pallas_call | solution.py:452
  31.1 3.7 %collective-permute-done.7.refs_1_ = bf16[32,1024]{1,0:T(8,128)(2,1)S(1)} collective-permute-done((bf16[32,1024]{1,0:T(8,128)(2,1)S(1)}, bf16[32,1024]{1,0:T(8,128)(2,1)S(1)}, u32[]{:S(2)}, u32[]{:S(2)}) %collective-permute-start.7) | collective-permute-done | bytes 65568 | tf_op jit(solution)/shard_map/ppermute | solution.py:23
  34.8 0.4 collective-permute-done.5.refs_0_
  35.2 1.3 %shard_map.98 = (bf16[3,80,512]{2,1,0:T(8,128)(2,1)S(1)}, bf16[80,1024]{1,0:T(8,128)(2,1)S(1)}) custom-call(s32[1]{0:T(128)} %bitcast.5.me_ref, bf16[48,1024]{1,0:T(8,128)(2,1)S(1)} %collective-permute-done.5.refs_0_, bf16[32,1024]{1,0:T(8,128)(2,1)S(1)} %collective-permute-done.7.refs_1_, bf16[80,1024]{1,0:T(8,128)(2,1)S(1)} %shard_map.96.refs_0_.refs_2_, ...), custom_call_target="tpu_custom_call" | custom-call | tf_op jit(solution)/shard_map/pallas_call | solution.py:506
  36.5 0.0 collective-permute-done.10.top_ref
  36.5 1.7 %shard_map.100 = (bf16[3,160,512]{2,1,0:T(8,128)(2,1)S(1)}, bf16[3,160,512]{2,1,0:T(8,128)(2,1)S(1)}, bf16[160,512]{1,0:T(8,128)(2,1)S(1)}, bf16[160,512]{1,0:T(8,128)(2,1)S(1)}, bf16[160,512]{1,0:T(8,128)(2,1)S(1)}) custom-call(s32[1]{0:T(128)} %bitcast.5.me_ref, bf16[160,1024]{1,0:T(8,128)(2,1)S(1)} %collective-permute-done.10.top_ref, ...), custom_call_target="tpu_custom_call" | custom-call | tf_op jit(solution)/shard_map/pallas_call | solution.py:581
  38.2 0.6 collective-permute-start.11
  38.8 1.5 %collective-permute-start.12 = (bf16[160,512]{1,0:T(8,128)(2,1)S(1)}, bf16[160,512]{1,0:T(8,128)(2,1)S(1)}, u32[]{:S(2)}, u32[]{:S(2)}) collective-permute-start(bf16[160,512]{1,0:T(8,128)(2,1)S(1)} %get-tuple-element.105), channel_id=1, source_target_pairs={{0,2},{1,3},{2,0},{3,1},{4,6},{5,7},{6,4},{7,5},{8,10},{9,11},{10,... | collective-permute-start | bytes 491528 | tf_op jit(solution)/shard_map/ppermute | solution.py:23
  40.3 0.0 collective-permute-done.13.bottom_ref
  40.3 2.5 %shard_map.101 = (bf16[224,512]{1,0:T(8,128)(2,1)S(1)}, bf16[224,512]{1,0:T(8,128)(2,1)S(1)}, bf16[224,512]{1,0:T(8,128)(2,1)S(1)}) custom-call(s32[1]{0:T(128)} %bitcast.5.me_ref, bf16[160,1024]{1,0:T(8,128)(2,1)S(1)} %collective-permute-done.13.bottom_ref, f32[4,1,1024]{2,1,0:T(1,128)S(1)} %get-tuple-element.80.gain_ref.refs_3_.refs_2_, ...), custom_call_target="tpu_custom_call" | custom-call | flops 10000000000 | tf_op jit(solution)/shard_map/pallas_call | solution.py:620
  42.8 0.6 collective-permute-start.18
  43.4 1.5 %collective-permute-start.16 = (bf16[224,512]{1,0:T(8,128)(2,1)S(1)}, bf16[224,512]{1,0:T(8,128)(2,1)S(1)}, u32[]{:S(2)}, u32[]{:S(2)}) collective-permute-start(bf16[224,512]{1,0:T(8,128)(2,1)S(1)} %get-tuple-element.119), channel_id=1, source_target_pairs={{0,1},{1,0},{2,3},{3,2},{4,5},{5,4},{6,7},{7,6},{8,9},{9,8},{10,11... | collective-permute-start | bytes 688136 | tf_op jit(solution)/shard_map/ppermute | solution.py:23
  44.9 0.0 collective-permute-done.11
  44.9 0.0 collective-permute-done.12
  44.9 0.6 shard_map.104
  45.5 2.3 %collective-permute-start.15 = (bf16[384,512]{1,0:T(8,128)(2,1)S(1)}, bf16[384,512]{1,0:T(8,128)(2,1)S(1)}, u32[]{:S(2)}, u32[]{:S(2)}) collective-permute-start(bf16[384,512]{1,0:T(8,128)(2,1)S(1)} %get-tuple-element.116), channel_id=1, source_target_pairs={{0,2},{1,3},{2,0},{3,1},{4,6},{5,7},{6,4},{7,5},{8,10},{9,11},{10,... | collective-permute-start | bytes 1179656 | tf_op jit(solution)/shard_map/ppermute | solution.py:23
  47.8 0.6 shard_map.103
  48.4 0.0 copy-start
  48.4 1.5 %collective-permute-start.14 = (bf16[384,512]{1,0:T(8,128)(2,1)S(1)}, bf16[384,512]{1,0:T(8,128)(2,1)S(1)}, u32[]{:S(2)}, u32[]{:S(2)}) collective-permute-start(bf16[384,512]{1,0:T(8,128)(2,1)S(1)} %get-tuple-element.114), channel_id=1, source_target_pairs={{0,1},{1,0},{2,3},{3,2},{4,5},{5,4},{6,7},{7,6},{8,9},{9,8},{10,11... | collective-permute-start | bytes 1179656 | tf_op jit(solution)/shard_map/ppermute | solution.py:23
  49.9 1.5 %collective-permute-done.18 = bf16[224,512]{1,0:T(8,128)(2,1)S(1)} collective-permute-done((bf16[224,512]{1,0:T(8,128)(2,1)S(1)}, bf16[224,512]{1,0:T(8,128)(2,1)S(1)}, u32[]{:S(2)}, u32[]{:S(2)}) %collective-permute-start.18) | collective-permute-done | bytes 229408 | tf_op jit(solution)/shard_map/ppermute | solution.py:23
  51.4 0.1 add_convert_fusion.1
  51.5 1.6 %collective-permute-start.19 = (bf16[384,512]{1,0:T(8,128)(2,1)S(1)}, bf16[384,512]{1,0:T(8,128)(2,1)S(1)}, u32[]{:S(2)}, u32[]{:S(2)}) collective-permute-start(bf16[384,512]{1,0:T(8,128)(2,1)S(1)} %add_convert_fusion.1), channel_id=1, source_target_pairs={{0,1},{1,0},{2,3},{3,2},{4,5},{5,4},{6,7},{7,6},{8,9},{9,8},{10,11... | collective-permute-start | bytes 1179656 | tf_op jit(solution)/shard_map/ppermute | solution.py:23
  53.1 0.0 collective-permute-done.16
  53.1 0.1 add_convert_fusion.2
  53.2 0.6 collective-permute-start.17
  53.8 0.1 slice_reduce_fusion
  54.0 0.0 copy-done
  54.0 0.4 add_convert_fusion.base_ref
  54.3 0.6 shard_map.102
  54.9 4.9 %collective-permute-done.15.refs_3_ = bf16[384,512]{1,0:T(8,128)(2,1)S(1)} collective-permute-done((bf16[384,512]{1,0:T(8,128)(2,1)S(1)}, bf16[384,512]{1,0:T(8,128)(2,1)S(1)}, u32[]{:S(2)}, u32[]{:S(2)}) %collective-permute-start.15) | collective-permute-done | bytes 393248 | tf_op jit(solution)/shard_map/ppermute | solution.py:23
  59.9 0.7 %collective-permute-done.14.refs_1_ = bf16[384,512]{1,0:T(8,128)(2,1)S(1)} collective-permute-done((bf16[384,512]{1,0:T(8,128)(2,1)S(1)}, bf16[384,512]{1,0:T(8,128)(2,1)S(1)}, u32[]{:S(2)}, u32[]{:S(2)}) %collective-permute-start.14) | collective-permute-done | bytes 393248 | tf_op jit(solution)/shard_map/ppermute | solution.py:23
  60.5 0.3 shard_map.105.base_ref
  60.8 5.5 %collective-permute-done.19.refs_1_ = bf16[384,512]{1,0:T(8,128)(2,1)S(1)} collective-permute-done((bf16[384,512]{1,0:T(8,128)(2,1)S(1)}, bf16[384,512]{1,0:T(8,128)(2,1)S(1)}, u32[]{:S(2)}, u32[]{:S(2)}) %collective-permute-start.19) | collective-permute-done | bytes 393248 | tf_op jit(solution)/shard_map/ppermute | solution.py:23
  66.3 0.0 collective-permute-done.17.refs_0_
  66.3 1.0 %shard_map.106 = bf16[384,1024]{1,0:T(8,128)(2,1)} custom-call(f32[384,1024]{1,0:T(8,128)S(1)} %shard_map.105.base_ref, bf16[384,512]{1,0:T(8,128)(2,1)S(1)} %collective-permute-done.17.refs_0_, bf16[384,512]{1,0:T(8,128)(2,1)S(1)} %collective-permute-done.19.refs_1_), custom_call_target="tpu_custom_call" | custom-call | tf_op jit(solution)/shard_map/pallas_call | solution.py:693
  (4 shorter events, 0.1 us)
Async XLA Ops:
  1.7 19.6 %collective-permute-start.8 = (bf16[320,1024]{1,0:T(8,128)(2,1)S(1)}, bf16[320,1024]{1,0:T(8,128)(2,1)S(1)}, u32[]{:S(2)}, u32[]{:S(2)}) collective-permute-start(bf16[320,1024]{1,0:T(8,128)(2,1)S(1)} %shard_map.91.x_ref), channel_id=1, source_target_pairs={{0,1},{1,0},{2,3},{3,2},{4,5},{5,4},{6,7},{7,6},{8,9},{9,8},{10,11... | collective-permute-start | bytes 1966088 | tf_op jit(solution)/shard_map/ppermute | solution.py:23
  4.7 16.6 %collective-permute-start.9 = (bf16[320,1024]{1,0:T(8,128)(2,1)S(1)}, bf16[320,1024]{1,0:T(8,128)(2,1)S(1)}, u32[]{:S(2)}, u32[]{:S(2)}) collective-permute-start(bf16[320,1024]{1,0:T(8,128)(2,1)S(1)} %shard_map.91.x_ref), channel_id=1, source_target_pairs={{0,2},{1,3},{2,0},{3,1},{4,6},{5,7},{6,4},{7,5},{8,10},{9,11},{10,... | collective-permute-start | bytes 1966088 | tf_op jit(solution)/shard_map/ppermute | solution.py:23
  8.4 1.4 %collective-permute-start = (bf16[4,16,1024]{2,1,0:T(8,128)(2,1)S(1)}, bf16[4,16,1024]{2,1,0:T(8,128)(2,1)S(1)}, u32[]{:S(2)}, u32[]{:S(2)}) collective-permute-start(bf16[4,16,1024]{2,1,0:T(8,128)(2,1)S(1)} %get-tuple-element.68), channel_id=1, source_target_pairs={{0,4},{4,0},{8,12},{12,8},{16,20},{20,16},{24,28},{28,24},{1,5},{5... | collective-permute-start | bytes 393224 | tf_op jit(solution)/shard_map/ppermute | solution.py:23
  9.9 10.0 %collective-permute-start.1 = (bf16[24,1024]{1,0:T(8,128)(2,1)S(1)}, bf16[24,1024]{1,0:T(8,128)(2,1)S(1)}, u32[]{:S(2)}, u32[]{:S(2)}) collective-permute-start(bf16[24,1024]{1,0:T(8,128)(2,1)S(1)} %get-tuple-element.70), channel_id=1, source_target_pairs={{0,8},{4,12},{8,0},{12,4},{16,24},{20,28},{24,16},{28,20},{1,9},{5... | collective-permute-start | bytes 147464 | tf_op jit(solution)/shard_map/ppermute | solution.py:23
  11.5 8.4 %collective-permute-start.2 = (bf16[24,1024]{1,0:T(8,128)(2,1)S(1)}, bf16[24,1024]{1,0:T(8,128)(2,1)S(1)}, u32[]{:S(2)}, u32[]{:S(2)}) collective-permute-start(bf16[24,1024]{1,0:T(8,128)(2,1)S(1)} %get-tuple-element.71), channel_id=1, source_target_pairs={{0,16},{4,20},{8,24},{12,28},{16,0},{20,4},{24,8},{28,12},{1,17},{... | collective-permute-start | bytes 147464 | tf_op jit(solution)/shard_map/ppermute | solution.py:23
  14.1 5.9 %collective-permute-start.3 = (bf16[24,1024]{1,0:T(8,128)(2,1)S(1)}, bf16[24,1024]{1,0:T(8,128)(2,1)S(1)}, u32[]{:S(2)}, u32[]{:S(2)}) collective-permute-start(bf16[24,1024]{1,0:T(8,128)(2,1)S(1)} %get-tuple-element.72), channel_id=1, source_target_pairs={{0,24},{4,28},{8,16},{12,20},{16,8},{20,12},{24,0},{28,4},{1,25},{... | collective-permute-start | bytes 147464 | tf_op jit(solution)/shard_map/ppermute | solution.py:23
  20.2 6.6 %collective-permute-start.4 = (bf16[80,1024]{1,0:T(8,128)(2,1)S(1)}, bf16[80,1024]{1,0:T(8,128)(2,1)S(1)}, u32[]{:S(2)}, u32[]{:S(2)}) collective-permute-start(bf16[80,1024]{1,0:T(8,128)(2,1)S(1)} %shard_map.96.refs_0_.refs_2_), channel_id=1, source_target_pairs={{0,2},{1,3},{2,0},{3,1},{4,6},{5,7},{6,4},{7,5},{8,10},{9,11},{10,... | collective-permute-start | bytes 491528 | tf_op jit(solution)/shard_map/ppermute | solution.py:23
  20.8 6.7 %collective-permute-start.6 = (bf16[80,1024]{1,0:T(8,128)(2,1)S(1)}, bf16[80,1024]{1,0:T(8,128)(2,1)S(1)}, u32[]{:S(2)}, u32[]{:S(2)}) collective-permute-start(bf16[80,1024]{1,0:T(8,128)(2,1)S(1)} %shard_map.96.refs_0_.refs_2_), channel_id=1, source_target_pairs={{0,1},{1,0},{2,3},{3,2},{4,5},{5,4},{6,7},{7,6},{8,9},{9,8},{10,11... | collective-permute-start | bytes 491528 | tf_op jit(solution)/shard_map/ppermute | solution.py:23
  23.6 12.9 %collective-permute-start.10 = (bf16[160,1024]{1,0:T(8,128)(2,1)S(1)}, bf16[160,1024]{1,0:T(8,128)(2,1)S(1)}, u32[]{:S(2)}, u32[]{:S(2)}) collective-permute-start(bf16[160,1024]{1,0:T(8,128)(2,1)S(1)} %slice.18), channel_id=1, source_target_pairs={{0,1},{1,0},{2,3},{3,2},{4,5},{5,4},{6,7},{7,6},{8,9},{9,8},{10,11... | collective-permute-start | bytes 983048 | tf_op jit(solution)/shard_map/ppermute | solution.py:23
  25.2 15.1 %collective-permute-start.13 = (bf16[160,1024]{1,0:T(8,128)(2,1)S(1)}, bf16[160,1024]{1,0:T(8,128)(2,1)S(1)}, u32[]{:S(2)}, u32[]{:S(2)}) collective-permute-start(bf16[160,1024]{1,0:T(8,128)(2,1)S(1)} %slice.19), channel_id=1, source_target_pairs={{0,2},{1,3},{2,0},{3,1},{4,6},{5,7},{6,4},{7,5},{8,10},{9,11},{10,... | collective-permute-start | bytes 983048 | tf_op jit(solution)/shard_map/ppermute | solution.py:23
  26.8 8.4 %collective-permute-start.5 = (bf16[48,1024]{1,0:T(8,128)(2,1)S(1)}, bf16[48,1024]{1,0:T(8,128)(2,1)S(1)}, u32[]{:S(2)}, u32[]{:S(2)}) collective-permute-start(bf16[48,1024]{1,0:T(8,128)(2,1)S(1)} %slice.20), channel_id=1, source_target_pairs={{0,1},{1,0},{2,3},{3,2},{4,5},{5,4},{6,7},{7,6},{8,9},{9,8},{10,11... | collective-permute-start | bytes 294920 | tf_op jit(solution)/shard_map/ppermute | solution.py:23
  27.5 7.3 %collective-permute-start.7 = (bf16[32,1024]{1,0:T(8,128)(2,1)S(1)}, bf16[32,1024]{1,0:T(8,128)(2,1)S(1)}, u32[]{:S(2)}, u32[]{:S(2)}) collective-permute-start(bf16[32,1024]{1,0:T(8,128)(2,1)S(1)} %slice.21), channel_id=1, source_target_pairs={{0,2},{1,3},{2,0},{3,1},{4,6},{5,7},{6,4},{7,5},{8,10},{9,11},{10,... | collective-permute-start | bytes 196616 | tf_op jit(solution)/shard_map/ppermute | solution.py:23
  38.2 6.7 %collective-permute-start.11 = (bf16[160,512]{1,0:T(8,128)(2,1)S(1)}, bf16[160,512]{1,0:T(8,128)(2,1)S(1)}, u32[]{:S(2)}, u32[]{:S(2)}) collective-permute-start(bf16[160,512]{1,0:T(8,128)(2,1)S(1)} %get-tuple-element.104), channel_id=1, source_target_pairs={{0,1},{1,0},{2,3},{3,2},{4,5},{5,4},{6,7},{7,6},{8,9},{9,8},{10,11... | collective-permute-start | bytes 491528 | tf_op jit(solution)/shard_map/ppermute | solution.py:23
  38.8 6.1 %collective-permute-start.12 = (bf16[160,512]{1,0:T(8,128)(2,1)S(1)}, bf16[160,512]{1,0:T(8,128)(2,1)S(1)}, u32[]{:S(2)}, u32[]{:S(2)}) collective-permute-start(bf16[160,512]{1,0:T(8,128)(2,1)S(1)} %get-tuple-element.105), channel_id=1, source_target_pairs={{0,2},{1,3},{2,0},{3,1},{4,6},{5,7},{6,4},{7,5},{8,10},{9,11},{10,... | collective-permute-start | bytes 491528 | tf_op jit(solution)/shard_map/ppermute | solution.py:23
  42.8 8.6 %collective-permute-start.18 = (bf16[224,512]{1,0:T(8,128)(2,1)S(1)}, bf16[224,512]{1,0:T(8,128)(2,1)S(1)}, u32[]{:S(2)}, u32[]{:S(2)}) collective-permute-start(bf16[224,512]{1,0:T(8,128)(2,1)S(1)} %get-tuple-element.122), channel_id=1, source_target_pairs={{0,2},{1,3},{2,0},{3,1},{4,6},{5,7},{6,4},{7,5},{8,10},{9,11},{10,... | collective-permute-start | bytes 688136 | tf_op jit(solution)/shard_map/ppermute | solution.py:23
  43.4 9.7 %collective-permute-start.16 = (bf16[224,512]{1,0:T(8,128)(2,1)S(1)}, bf16[224,512]{1,0:T(8,128)(2,1)S(1)}, u32[]{:S(2)}, u32[]{:S(2)}) collective-permute-start(bf16[224,512]{1,0:T(8,128)(2,1)S(1)} %get-tuple-element.119), channel_id=1, source_target_pairs={{0,1},{1,0},{2,3},{3,2},{4,5},{5,4},{6,7},{7,6},{8,9},{9,8},{10,11... | collective-permute-start | bytes 688136 | tf_op jit(solution)/shard_map/ppermute | solution.py:23
  45.5 14.4 %collective-permute-start.15 = (bf16[384,512]{1,0:T(8,128)(2,1)S(1)}, bf16[384,512]{1,0:T(8,128)(2,1)S(1)}, u32[]{:S(2)}, u32[]{:S(2)}) collective-permute-start(bf16[384,512]{1,0:T(8,128)(2,1)S(1)} %get-tuple-element.116), channel_id=1, source_target_pairs={{0,2},{1,3},{2,0},{3,1},{4,6},{5,7},{6,4},{7,5},{8,10},{9,11},{10,... | collective-permute-start | bytes 1179656 | tf_op jit(solution)/shard_map/ppermute | solution.py:23
  48.4 5.6 %copy-start = (bf16[384,1024]{1,0:T(8,128)(2,1)S(1)}, bf16[384,1024]{1,0:T(8,128)(2,1)}, u32[]{:S(2)}) copy-start(bf16[384,1024]{1,0:T(8,128)(2,1)} %text_hbm.2) | copy-start | bytes 2359300
  48.4 12.1 %collective-permute-start.14 = (bf16[384,512]{1,0:T(8,128)(2,1)S(1)}, bf16[384,512]{1,0:T(8,128)(2,1)S(1)}, u32[]{:S(2)}, u32[]{:S(2)}) collective-permute-start(bf16[384,512]{1,0:T(8,128)(2,1)S(1)} %get-tuple-element.114), channel_id=1, source_target_pairs={{0,1},{1,0},{2,3},{3,2},{4,5},{5,4},{6,7},{7,6},{8,9},{9,8},{10,11... | collective-permute-start | bytes 1179656 | tf_op jit(solution)/shard_map/ppermute | solution.py:23
  51.5 14.7 %collective-permute-start.19 = (bf16[384,512]{1,0:T(8,128)(2,1)S(1)}, bf16[384,512]{1,0:T(8,128)(2,1)S(1)}, u32[]{:S(2)}, u32[]{:S(2)}) collective-permute-start(bf16[384,512]{1,0:T(8,128)(2,1)S(1)} %add_convert_fusion.1), channel_id=1, source_target_pairs={{0,1},{1,0},{2,3},{3,2},{4,5},{5,4},{6,7},{7,6},{8,9},{9,8},{10,11... | collective-permute-start | bytes 1179656 | tf_op jit(solution)/shard_map/ppermute | solution.py:23
  53.2 13.1 %collective-permute-start.17 = (bf16[384,512]{1,0:T(8,128)(2,1)S(1)}, bf16[384,512]{1,0:T(8,128)(2,1)S(1)}, u32[]{:S(2)}, u32[]{:S(2)}) collective-permute-start(bf16[384,512]{1,0:T(8,128)(2,1)S(1)} %add_convert_fusion.2), channel_id=1, source_target_pairs={{0,2},{1,3},{2,0},{3,1},{4,6},{5,7},{6,4},{7,5},{8,10},{9,11},{10,... | collective-permute-start | bytes 1179656 | tf_op jit(solution)/shard_map/ppermute | solution.py:23

commit v9 on v7

--- a/solution.py
+++ b/solution.py
@@ -94,8 +94,10 @@
     return found
 
 
-def text_kernel(n_req, region, me_ref, req_hbm, start_hbm, text_hbm, ctext_out, req_ref, start_ref, text_ref, sem_ref):
-    copies = fetch(((req_hbm, req_ref), (start_hbm, start_ref), (text_hbm, text_ref)), sem_ref)
+def text_kernel(n_req, region, me_ref, req_hbm, start_hbm, text_hbm, *refs):
+    others, (ctext_out, text_ref, *kept), (req_ref, start_ref, sem_ref) = refs[:3], refs[3:8], refs[8:]
+    pairs = ((req_hbm, req_ref), (start_hbm, start_ref), (text_hbm, text_ref)) + tuple(zip(others, kept))
+    copies = fetch(pairs, sem_ref)
     n_text, length = ctext_out.shape[0], text_ref.shape[0]
     spot = lax.broadcasted_iota(jnp.int32, (8, length), 1)
     before = jnp.zeros((8, length), jnp.int32)
@@ -110,42 +112,41 @@
     gather = (lax.broadcasted_iota(jnp.int32, (n_text, length), 0) == rank).astype(jnp.bfloat16)
     copies[2].wait()
     ctext_out[...] = jnp.dot(gather, text_ref[...], preferred_element_type=jnp.float32).astype(jnp.bfloat16)
-
-
-def gather_text(me, image_request, slot_start, text, n_req, region, n_text):
-    inputs = (image_request, slot_start, text)
+    for copy in copies[3:]:
+        copy.wait()
+
+
+def gather_text(me, image_request, slot_start, text, patches, dec_gain, vis_gain, n_req, region, n_text):
+    inputs = (image_request, slot_start, text, patches, dec_gain.reshape(-1, 128), vis_gain.reshape(-1, 128))
     return pl.pallas_call(
         functools.partial(text_kernel, n_req, region),
-        out_shape=jax.ShapeDtypeStruct((n_text, text.shape[1]), text.dtype),
-        in_specs=[pl.BlockSpec(memory_space=pltpu.SMEM)] + [pl.BlockSpec(memory_space=pltpu.HBM)] * 3,
-        out_specs=pl.BlockSpec(memory_space=pltpu.VMEM),
-        scratch_shapes=[pltpu.SMEM(x.shape, jnp.int32) for x in inputs[:2]]
-        + [pltpu.VMEM(text.shape, text.dtype), pltpu.SemaphoreType.DMA((3,))],
+        out_shape=(jax.ShapeDtypeStruct((n_text, text.shape[1]), text.dtype),)
+        + tuple(pltpu.VMEM(x.shape, x.dtype) for x in inputs[2:]),
+        in_specs=[pl.BlockSpec(memory_space=pltpu.SMEM)] + [pl.BlockSpec(memory_space=pltpu.HBM)] * len(inputs),
+        out_specs=tuple(vmem_specs(len(inputs) - 1)),
+        scratch_shapes=[pltpu.SMEM(x.shape, jnp.int32) for x in inputs[:2]] + [pltpu.SemaphoreType.DMA((len(inputs),))],
         compiler_params=params(8),
         cost_estimate=TINY,
     )(me, *[in_hbm(x) for x in inputs])
 
 
-def prep_kernel(n_req, me_ref, req_hbm, start_hbm, grid_hbm, text_hbm, x_hbm, dec_hbm, vis_hbm, *refs):
+def prep_kernel(n_req, me_ref, req_hbm, start_hbm, grid_hbm, text_ref, x_ref, dec_ref, vis_ref, *refs):
     (even_out, odd_out, rtext_out, sel_out, table_out, key_out, dec_out, vis_out, req_ref, start_ref, grid_ref,
-     text_ref, x_ref, dec_ref, vis_ref, tmp_ref, sem_ref) = refs
-    pairs = (
-        (req_hbm, req_ref),
-        (start_hbm, start_ref),
-        (grid_hbm, grid_ref),
-        (x_hbm, x_ref),
-        (text_hbm, text_ref),
-        (dec_hbm, dec_ref),
-        (vis_hbm, vis_ref),
-    )
-    copies = fetch(pairs, sem_ref)
+     pool_ref, tmp_ref, sem_ref) = refs
+    copies = fetch(((req_hbm, req_ref), (start_hbm, start_ref), (grid_hbm, grid_ref)), sem_ref)
     side, img_dev = x_ref.shape[0], x_ref.shape[2]
     half = side // 2
     region = half * half
     n_img, length = sel_out.shape[0], text_ref.shape[0]
     me = me_ref[0]
+    for i in range(half):
+        for j in range(half):
+            total = x_ref[2 * i, 2 * j].astype(jnp.float32)
+            for a, b in ((0, 1), (1, 0), (1, 1)):
+                total += x_ref[2 * i + a, 2 * j + b].astype(jnp.float32)
+            pool_ref[i * half + j] = total * 0.25
     tmp_ref[...] = jnp.zeros_like(tmp_ref)
-    for copy in copies[:3]:
+    for copy in copies:
         copy.wait()
 
     spot = lax.broadcasted_iota(jnp.int32, (8, length), 1)
@@ -180,16 +181,10 @@
         goal = jnp.where(cols == k, req_ref[me * img_dev + k] ^ me, goal)
     onehot = (rows == goal).astype(jnp.bfloat16)
 
-    for copy in copies[3:]:
-        copy.wait()
     rtext_out[...] = jnp.dot(keep, text_ref[...], preferred_element_type=jnp.float32).astype(jnp.bfloat16)
-    for i in range(half):
-        for j in range(half):
-            total = x_ref[2 * i, 2 * j].astype(jnp.float32)
-            for a, b in ((0, 1), (1, 0), (1, 1)):
-                total += x_ref[2 * i + a, 2 * j + b].astype(jnp.float32)
-            pooled = (total * 0.25).astype(jnp.bfloat16)
-            tmp_ref[:, i * half + j, :] = jnp.dot(onehot, pooled, preferred_element_type=jnp.float32)
+    for cell in range(region):
+        pooled = pool_ref[cell].astype(jnp.bfloat16)
+        tmp_ref[:, cell, :] = jnp.dot(onehot, pooled, preferred_element_type=jnp.float32)
     for s in range(n_req):
         (even_out, odd_out)[s % 2][s // 2] = tmp_ref[s].astype(jnp.bfloat16)
     per = vis_ref.shape[0]
@@ -201,38 +196,35 @@
             dec_out[t, :, lanes] = dec_ref[at : at + 1, :].astype(jnp.float32)
 
 
-def prepare(me, image_request, slot_start, grids, text, patches, dec_gain, vis_gain, n_req, n_img):
+def prepare(me, image_request, slot_start, grids, text, patches, dec_rows, vis_rows, n_req, n_img):
     side, _, img_dev, width = patches.shape
     padded = round_up((side // 2) ** 2, 16)
-    inputs = (
-        image_request,
-        slot_start,
-        grids.T,
-        text,
-        patches,
-        dec_gain.reshape(-1, 128),
-        vis_gain.reshape(-1, 128),
-    )
+    inputs = (image_request, slot_start, grids.T)
     bf16, f32 = jnp.bfloat16, jnp.float32
     outputs = [((n_req // 2, padded, width), bf16)] * 2 + [
         ((n_img, width), bf16),
         ((n_img, n_img), bf16),
         ((n_req, 128), jnp.int32),
         ((8, text.shape[0]), f32),
-        ((dec_gain.size // width, 1, width), f32),
+        ((dec_rows.size // width, 1, width), f32),
         ((1, width), f32),
     ]
     return pl.pallas_call(
         functools.partial(prep_kernel, n_req),
         out_shape=tuple(jax.ShapeDtypeStruct(shape, kind) for shape, kind in outputs),
-        in_specs=[pl.BlockSpec(memory_space=pltpu.SMEM)] + [pl.BlockSpec(memory_space=pltpu.HBM)] * len(inputs),
+        in_specs=[pl.BlockSpec(memory_space=pltpu.SMEM)]
+        + [pl.BlockSpec(memory_space=pltpu.HBM)] * 3
+        + vmem_specs(4),
         out_specs=tuple(vmem_specs(len(outputs))),
-        scratch_shapes=[pltpu.SMEM(x.shape, jnp.int32) for x in inputs[:3]]
-        + [pltpu.VMEM(x.shape, x.dtype) for x in inputs[3:]]
-        + [pltpu.VMEM((n_req, padded, width), f32), pltpu.SemaphoreType.DMA((len(inputs),))],
-        compiler_params=params(12),
-        cost_estimate=TINY,
-    )(me, *[in_hbm(x) for x in inputs])
+        scratch_shapes=[pltpu.SMEM(x.shape, jnp.int32) for x in inputs]
+        + [
+            pltpu.VMEM(((side // 2) ** 2, img_dev, width), f32),
+            pltpu.VMEM((n_req, padded, width), f32),
+            pltpu.SemaphoreType.DMA((3,)),
+        ],
+        compiler_params=params(12),
+        cost_estimate=TINY,
+    )(me, *[in_hbm(x) for x in inputs], text, patches, dec_rows, vis_rows)
 
 
 def mix_kernel(region, even_ref, odd_ref, *refs):
@@ -456,7 +448,7 @@
         out_specs=tuple(vmem_specs(3)),
         scratch_shapes=[pltpu.SemaphoreType.DMA],
         compiler_params=params(12),
-        cost_estimate=pl.CostEstimate(flops=0, bytes_accessed=0, transcendentals=0),
+        cost_estimate=pl.CostEstimate(flops=3*10**9, bytes_accessed=0, transcendentals=0),
     )(me, *blocks, gain, sel, held, in_hbm(w_out))
 
 
@@ -680,13 +672,14 @@
     n_rows = n_req * region
     n_img = round_up(n_rows + 1, 16)
     n_text = round_up(length - (n_rows if img_dev == n_req else 0), 32)
-    ctext = gather_text(req_at, image_request, slot_start, text, n_req, region, n_text)
+    ctext, *kept = gather_text(
+        req_at, image_request, slot_start, text, jnp.transpose(patches, (1, 2, 0, 3)), dec_gain, vis_gain, n_req, region,
+        n_text
+    )
     blocks = near_blocks(ctext, n_ten)
 
-    late_text, ctext = lax.optimization_barrier((text, ctext))
     even, odd, rtext, sel, table, key_ok, gains, vis_row = prepare(
-        req_at, image_request, slot_start, grids, late_text, jnp.transpose(patches, (1, 2, 0, 3)), dec_gain, vis_gain,
-        n_req, n_img
+        req_at, image_request, slot_start, grids, *kept, n_req, n_img
     )
     pairs = mix_pairs(even, swap(odd, 1, "req"), region)
     received = [pairs[0]] + [swap(pairs[i], 2 * i, "req") for i in range(1, n_req // 2)]
@@ -696,12 +689,15 @@
     received, acc, text_at = lax.optimization_barrier((received, acc, text_at))
     img_own = pack_images(received, vis_row, rtext, sel, region)
     img_blocks = [img_own] + [swap(img_own, s) for s in range(1, n_ten)]
-    handed, img_own = lax.optimization_barrier((blocks, img_own))
-    blocks = {**far_blocks(handed, n_ten), **blocks}
-
-    near = [blocks[s] for s in near_at]
-    acc, ss = near_part(near_at, ten_at, near, gains, held, acc, ss)
-    img_blocks, acc = lax.optimization_barrier((img_blocks, acc))
+
+    one_bit = sorted(blocks)
+    between = [s for s in near_at if s not in one_bit]
+    blocks, img_own = lax.optimization_barrier((blocks, img_own))
+    acc, ss = near_part(one_bit, ten_at, [blocks[s] for s in one_bit], gains, held, acc, ss)
+    blocks, acc = lax.optimization_barrier((blocks, acc))
+    blocks = far_blocks(blocks, n_ten)
+    if between:
+        acc, ss = near_part(between, ten_at, [blocks[s] for s in between], gains, held, acc, ss)
     img_qkv, merged, w_out = image_part(ten_at, img_blocks, gains, sel, held, w_out, n_rows)
 
     shared = (gains, held, acc, ss, img_qkv, text_at, img_at, key_ok, w_out)

time: 66.9 us -> 66.5 us (level)
  transfers between devices with their start and end apart: 19 -> 19, of which waited for: 12 -> 12; matrix products, arithmetic and copies ran while one was open for 1% -> 1% of each run, Pallas kernels for 29% -> 28%
where the time goes in v9:
time: 66.5 us; the launch traced here: 66.3 us
  starting transfers between devices  22.7 us (34%)
  Pallas kernels  21.4 us (32%)
  waiting for transfers between devices  21.4 us (32%)
    ppermute x19, starting transfers between devices, swap(): return lax.ppermute(x, axis, [(i, i ^ s) for i in range(n)])  22.7 us
    ppermute x19, waiting for transfers between devices, swap(): return lax.ppermute(x, axis, [(i, i ^ s) for i in range(n)])  21.4 us
    pallas_call x1, Pallas kernels, own_part(): pl.pallas_call(own_kernel, out_shape=(jax.ShapeDtypeStruct((3, rows, cols...  4.86 us
    pallas_call x1, Pallas kernels, image_part(): pl.pallas_call(functools.partial(image_kernel, n_rows, len(blocks)), out_...  2.65 us
    pallas_call x1, Pallas kernels, near_part(): pl.pallas_call(functools.partial(near_kernel, near, pieces), out_shape=(j...  2.27 us
    pallas_call x1, Pallas kernels, tail_part(): pl.pallas_call(functools.partial(tail_kernel, far), out_shape=(jax.ShapeD...  2.26 us
    pallas_call x1, Pallas kernels, prepare(): pl.pallas_call(functools.partial(prep_kernel, n_req), out_shape=tuple((ja...  1.94 us
    pallas_call x3, Pallas kernels, out_part(): pl.pallas_call(functools.partial(out_kernel, away), out_shape=(jax.ShapeD...  1.79 us
  transfers between devices with their start and end apart: 19, of which 12 were waited for; matrix products, arithmetic and copies ran while one was open for 1% of the time, Pallas kernels for 28%

profile of v9, /device:TPU:0, one launch (start us, length us, event | category | flops | bytes accessed | tf_op | source)
XLA Modules:
  0.0 66.3 jit_solution(4630306787658516475)
XLA Ops:
  0.0 1.7 %shard_map.91 = (bf16[320,1024]{1,0:T(8,128)(2,1)S(1)}, bf16[384,1024]{1,0:T(8,128)(2,1)S(1)}, bf16[6,6,8,1024]{3,2,1,0:T(8,128)(2,1)S(1)}, bf16[32,128]{1,0:T(8,128)(2,1)S(1)}, bf16[8,128]{1,0:T(8,128)(2,1)S(1)}) custom-call(s32[1]{0:T(128)} %bitcast.me_ref, s32[64]{0:T(128)} %req_hbm.3, s32[64]{0:T(128)} %start_hbm.3, bf16[384,1024]{1,0:T(8,128)(2,1)} %text_hbm.1, ...), custom_call_target="tpu_custom_call" | custom-call | tf_op jit(solution)/shard_map/pallas_call | solution.py:121
  1.7 3.0 %collective-permute-start.7 = (bf16[320,1024]{1,0:T(8,128)(2,1)S(1)}, bf16[320,1024]{1,0:T(8,128)(2,1)S(1)}, u32[]{:S(2)}, u32[]{:S(2)}) collective-permute-start(bf16[320,1024]{1,0:T(8,128)(2,1)S(1)} %get-tuple-element.82.x_ref), channel_id=1, source_target_pairs={{0,1},{1,0},{2,3},{3,2},{4,5},{5,4},{6,7},{7,6},{8,9},{9,8},{10,11... | collective-permute-start | bytes 1966088 | tf_op jit(solution)/shard_map/ppermute | solution.py:23
  4.7 1.5 %collective-permute-start.8 = (bf16[320,1024]{1,0:T(8,128)(2,1)S(1)}, bf16[320,1024]{1,0:T(8,128)(2,1)S(1)}, u32[]{:S(2)}, u32[]{:S(2)}) collective-permute-start(bf16[320,1024]{1,0:T(8,128)(2,1)S(1)} %get-tuple-element.82.x_ref), channel_id=1, source_target_pairs={{0,2},{1,3},{2,0},{3,1},{4,6},{5,7},{6,4},{7,5},{8,10},{9,11},{10,... | collective-permute-start | bytes 1966088 | tf_op jit(solution)/shard_map/ppermute | solution.py:23
  6.2 1.9 %shard_map.92 = (bf16[4,16,1024]{2,1,0:T(8,128)(2,1)S(1)}, bf16[4,16,1024]{2,1,0:T(8,128)(2,1)S(1)}, bf16[80,1024]{1,0:T(8,128)(2,1)S(1)}, bf16[80,80]{1,0:T(8,1...) custom-call(s32[1]{0:T(128)} %bitcast.me_ref, ...), custom_call_target="tpu_custom_call" | custom-call | tf_op jit(solution)/shard_map/pallas_call | solution.py:212
  8.2 0.1 collective-permute-start
  8.3 1.3 %collective-permute-done.odd_ref = bf16[4,16,1024]{2,1,0:T(8,128)(2,1)S(1)} collective-permute-done((bf16[4,16,1024]{2,1,0:T(8,128)(2,1)S(1)}, bf16[4,16,1024]{2,1,0:T(8,128)(2,1)S(1)}, u32[]{:S(2)}, u32[]{:S(2)}) %collective-permute-start) | collective-permute-done | bytes 131104 | tf_op jit(solution)/shard_map/ppermute | solution.py:23
  9.6 0.1 shard_map.93
  9.7 1.6 %collective-permute-start.1 = (bf16[24,1024]{1,0:T(8,128)(2,1)S(1)}, bf16[24,1024]{1,0:T(8,128)(2,1)S(1)}, u32[]{:S(2)}, u32[]{:S(2)}) collective-permute-start(bf16[24,1024]{1,0:T(8,128)(2,1)S(1)} %get-tuple-element.73), channel_id=1, source_target_pairs={{0,8},{4,12},{8,0},{12,4},{16,24},{20,28},{24,16},{28,20},{1,9},{5... | collective-permute-start | bytes 147464 | tf_op jit(solution)/shard_map/ppermute | solution.py:23
  11.3 2.6 %collective-permute-start.2 = (bf16[24,1024]{1,0:T(8,128)(2,1)S(1)}, bf16[24,1024]{1,0:T(8,128)(2,1)S(1)}, u32[]{:S(2)}, u32[]{:S(2)}) collective-permute-start(bf16[24,1024]{1,0:T(8,128)(2,1)S(1)} %get-tuple-element.74), channel_id=1, source_target_pairs={{0,16},{4,20},{8,24},{12,28},{16,0},{20,4},{24,8},{28,12},{1,17},{... | collective-permute-start | bytes 147464 | tf_op jit(solution)/shard_map/ppermute | solution.py:23
  13.9 0.2 collective-permute-start.3
  14.1 0.7 %shard_map.94 = (bf16[384,320]{1,0:T(8,128)(2,1)S(1)}, bf16[384,80]{1,0:T(8,128)(2,1)S(1)}, f32[384,128]{1,0:T(8,128)S(1)}) custom-call(s32[8,128]{1,0:T(8,128)S(1)} %get-tuple-element.76.table_ref), custom_call_target="tpu_custom_call" | custom-call | tf_op jit(solution)/shard_map/pallas_call | solution.py:297
  14.8 4.9 %shard_map.95 = (f32[3,320,512]{2,1,0:T(8,128)S(1)}, f32[320,128]{1,0:T(8,128)S(1)}, bf16[4,3,1024,512]{3,2,1,0:T(8,128)(2,1)S(1)}) custom-call(s32[1]{0:T(128)} %bitcast.5.me_ref, bf16[320,1024]{1,0:T(8,128)(2,1)S(1)} %get-tuple-element.82.x_ref, f32[4,1,1024]{2,1,0:T(1,128)S(1)} %get-tuple-element.83.gain_ref.refs_4_.refs_2_, bf16[3,4096,512]{2,1,0:T(8,128)(2,1)} %bitcast.9), custom_call_target="tpu_custom_call" | custom-call | tf_op jit(solution)/shard_map/pallas_call | solution.py:348
  19.7 0.0 collective-permute-done.1.refs_1_
  19.7 0.0 collective-permute-done.2.refs_2_
  19.7 0.1 collective-permute-done.3.refs_3_
  19.8 0.2 shard_map.96.refs_0_
  20.0 0.6 collective-permute-start.4
  20.6 0.5 collective-permute-start.5
  21.1 2.5 %collective-permute-start.6 = (bf16[80,1024]{1,0:T(8,128)(2,1)S(1)}, bf16[80,1024]{1,0:T(8,128)(2,1)S(1)}, u32[]{:S(2)}, u32[]{:S(2)}) collective-permute-start(bf16[80,1024]{1,0:T(8,128)(2,1)S(1)} %shard_map.96.refs_0_), channel_id=1, source_target_pairs={{0,3},{1,2},{2,1},{3,0},{4,7},{5,6},{6,5},{7,4},{8,11},{9,10},{10,... | collective-permute-start | bytes 491528 | tf_op jit(solution)/shard_map/ppermute | solution.py:23
  23.5 0.0 collective-permute-done.7.refs_0_
  23.5 0.0 collective-permute-done.8.refs_1_
  23.5 2.3 %shard_map.98 = (f32[3,320,512]{2,1,0:T(8,128)S(1)}, f32[320,128]{1,0:T(8,128)S(1)}) custom-call(s32[1]{0:T(128)} %bitcast.5.me_ref, bf16[320,1024]{1,0:T(8,128)(2,1)S(1)} %collective-permute-done.7.refs_0_, bf16[320,1024]{1,0:T(8,128)(2,1)S(1)} %collective-permute-done.8.refs_1_, f32[4,1,1024]{2,1,0:T(1,128)S(1)} %get-tuple-element.83.gain_ref.refs_4_.refs_2_, ...), custom_call_target="tpu_custom_call" | custom-call | flops 99999997952 | tf_op jit(solution)/shard_map/pallas_call | solution.py:392
  25.9 0.6 collective-permute-start.9
  26.5 0.6 collective-permute-start.12
  27.0 0.1 collective-permute-done.4.refs_1_
  27.2 0.9 %collective-permute-done.5.refs_2_ = bf16[80,1024]{1,0:T(8,128)(2,1)S(1)} collective-permute-done((bf16[80,1024]{1,0:T(8,128)(2,1)S(1)}, bf16[80,1024]{1,0:T(8,128)(2,1)S(1)}, u32[]{:S(2)}, u32[]{:S(2)}) %collective-permute-start.5) | collective-permute-done | bytes 163872 | tf_op jit(solution)/shard_map/ppermute | solution.py:23
  28.1 2.5 %collective-permute-done.6.refs_3_ = bf16[80,1024]{1,0:T(8,128)(2,1)S(1)} collective-permute-done((bf16[80,1024]{1,0:T(8,128)(2,1)S(1)}, bf16[80,1024]{1,0:T(8,128)(2,1)S(1)}, u32[]{:S(2)}, u32[]{:S(2)}) %collective-permute-start.6) | collective-permute-done | bytes 163872 | tf_op jit(solution)/shard_map/ppermute | solution.py:23
  30.6 2.6 %shard_map.97 = (bf16[3,80,512]{2,1,0:T(8,128)(2,1)S(1)}, bf16[80,1024]{1,0:T(8,128)(2,1)S(1)}, bf16[512,4096]{1,0:T(8,128)(2,1)S(1)}) custom-call(s32[1]{0:T(128)} %bitcast.5.me_ref, bf16[80,1024]{1,0:T(8,128)(2,1)S(1)} %shard_map.96.refs_0_, bf16[80,1024]{1,0:T(8,128)(2,1)S(1)} %collective-permute-done.4.refs_1_, ...), custom_call_target="tpu_custom_call" | custom-call | flops 3000000000 | tf_op jit(solution)/shard_map/pallas_call | solution.py:438
  33.3 2.7 %collective-permute-done.9.top_ref = bf16[160,1024]{1,0:T(8,128)(2,1)S(1)} collective-permute-done((bf16[160,1024]{1,0:T(8,128)(2,1)S(1)}, bf16[160,1024]{1,0:T(8,128)(2,1)S(1)}, u32[]{:S(2)}, u32[]{:S(2)}) %collective-permute-start.9) | collective-permute-done | bytes 327712 | tf_op jit(solution)/shard_map/ppermute | solution.py:23
  36.0 1.7 %shard_map.99 = (bf16[3,160,512]{2,1,0:T(8,128)(2,1)S(1)}, bf16[3,160,512]{2,1,0:T(8,128)(2,1)S(1)}, bf16[160,512]{1,0:T(8,128)(2,1)S(1)}, bf16[160,512]{1,0:T(8,128)(2,1)S(1)}, bf16[160,512]{1,0:T(8,128)(2,1)S(1)}) custom-call(s32[1]{0:T(128)} %bitcast.5.me_ref, bf16[160,1024]{1,0:T(8,128)(2,1)S(1)} %collective-permute-done.9.top_ref, ...), custom_call_target="tpu_custom_call" | custom-call | tf_op jit(solution)/shard_map/pallas_call | solution.py:517
  37.7 0.6 collective-permute-start.10
  38.3 0.5 collective-permute-start.11
  38.8 0.0 collective-permute-done.12.bottom_ref
  38.8 2.3 %shard_map.100 = (bf16[224,512]{1,0:T(8,128)(2,1)S(1)}, bf16[224,512]{1,0:T(8,128)(2,1)S(1)}, bf16[224,512]{1,0:T(8,128)(2,1)S(1)}) custom-call(s32[1]{0:T(128)} %bitcast.5.me_ref, bf16[160,1024]{1,0:T(8,128)(2,1)S(1)} %collective-permute-done.12.bottom_ref, f32[4,1,1024]{2,1,0:T(1,128)S(1)} %get-tuple-element.83.gain_ref.refs_4_.refs_2_, ...), custom_call_target="tpu_custom_call" | custom-call | flops 10000000000 | tf_op jit(solution)/shard_map/pallas_call | solution.py:556
  41.1 1.6 %collective-permute-start.17 = (bf16[224,512]{1,0:T(8,128)(2,1)S(1)}, bf16[224,512]{1,0:T(8,128)(2,1)S(1)}, u32[]{:S(2)}, u32[]{:S(2)}) collective-permute-start(bf16[224,512]{1,0:T(8,128)(2,1)S(1)} %get-tuple-element.122), channel_id=1, source_target_pairs={{0,2},{1,3},{2,0},{3,1},{4,6},{5,7},{6,4},{7,5},{8,10},{9,11},{10,... | collective-permute-start | bytes 688136 | tf_op jit(solution)/shard_map/ppermute | solution.py:23
  42.7 1.5 %collective-permute-start.15 = (bf16[224,512]{1,0:T(8,128)(2,1)S(1)}, bf16[224,512]{1,0:T(8,128)(2,1)S(1)}, u32[]{:S(2)}, u32[]{:S(2)}) collective-permute-start(bf16[224,512]{1,0:T(8,128)(2,1)S(1)} %get-tuple-element.119), channel_id=1, source_target_pairs={{0,1},{1,0},{2,3},{3,2},{4,5},{5,4},{6,7},{7,6},{8,9},{9,8},{10,11... | collective-permute-start | bytes 688136 | tf_op jit(solution)/shard_map/ppermute | solution.py:23
  44.2 0.0 collective-permute-done.10
  44.2 0.9 %collective-permute-done.11 = bf16[160,512]{1,0:T(8,128)(2,1)S(1)} collective-permute-done((bf16[160,512]{1,0:T(8,128)(2,1)S(1)}, bf16[160,512]{1,0:T(8,128)(2,1)S(1)}, u32[]{:S(2)}, u32[]{:S(2)}) %collective-permute-start.11) | collective-permute-done | bytes 163872 | tf_op jit(solution)/shard_map/ppermute | solution.py:23
  45.1 0.6 shard_map.103
  45.7 0.1 collective-permute-start.14
  45.8 0.6 shard_map.102
  46.4 0.0 copy-start
  46.4 1.9 %collective-permute-start.13 = (bf16[384,512]{1,0:T(8,128)(2,1)S(1)}, bf16[384,512]{1,0:T(8,128)(2,1)S(1)}, u32[]{:S(2)}, u32[]{:S(2)}) collective-permute-start(bf16[384,512]{1,0:T(8,128)(2,1)S(1)} %get-tuple-element.114), channel_id=1, source_target_pairs={{0,1},{1,0},{2,3},{3,2},{4,5},{5,4},{6,7},{7,6},{8,9},{9,8},{10,11... | collective-permute-start | bytes 1179656 | tf_op jit(solution)/shard_map/ppermute | solution.py:23
  48.2 1.8 %collective-permute-done.17 = bf16[224,512]{1,0:T(8,128)(2,1)S(1)} collective-permute-done((bf16[224,512]{1,0:T(8,128)(2,1)S(1)}, bf16[224,512]{1,0:T(8,128)(2,1)S(1)}, u32[]{:S(2)}, u32[]{:S(2)}) %collective-permute-start.17) | collective-permute-done | bytes 229408 | tf_op jit(solution)/shard_map/ppermute | solution.py:23
  50.0 0.1 add_convert_fusion.1
  50.1 1.8 %collective-permute-start.18 = (bf16[384,512]{1,0:T(8,128)(2,1)S(1)}, bf16[384,512]{1,0:T(8,128)(2,1)S(1)}, u32[]{:S(2)}, u32[]{:S(2)}) collective-permute-start(bf16[384,512]{1,0:T(8,128)(2,1)S(1)} %add_convert_fusion.1), channel_id=1, source_target_pairs={{0,1},{1,0},{2,3},{3,2},{4,5},{5,4},{6,7},{7,6},{8,9},{9,8},{10,11... | collective-permute-start | bytes 1179656 | tf_op jit(solution)/shard_map/ppermute | solution.py:23
  52.0 0.0 collective-permute-done.15
  52.0 0.1 add_convert_fusion.2
  52.1 1.0 %collective-permute-start.16 = (bf16[384,512]{1,0:T(8,128)(2,1)S(1)}, bf16[384,512]{1,0:T(8,128)(2,1)S(1)}, u32[]{:S(2)}, u32[]{:S(2)}) collective-permute-start(bf16[384,512]{1,0:T(8,128)(2,1)S(1)} %add_convert_fusion.2), channel_id=1, source_target_pairs={{0,2},{1,3},{2,0},{3,1},{4,6},{5,7},{6,4},{7,5},{8,10},{9,11},{10,... | collective-permute-start | bytes 1179656 | tf_op jit(solution)/shard_map/ppermute | solution.py:23
  53.0 0.1 slice_reduce_fusion
  53.2 0.0 copy-done
  53.2 0.4 add_convert_fusion.base_ref
  53.6 0.6 shard_map.101
  54.2 4.3 %collective-permute-done.14.refs_3_ = bf16[384,512]{1,0:T(8,128)(2,1)S(1)} collective-permute-done((bf16[384,512]{1,0:T(8,128)(2,1)S(1)}, bf16[384,512]{1,0:T(8,128)(2,1)S(1)}, u32[]{:S(2)}, u32[]{:S(2)}) %collective-permute-start.14) | collective-permute-done | bytes 393248 | tf_op jit(solution)/shard_map/ppermute | solution.py:23
  58.4 1.2 %collective-permute-done.13.refs_1_ = bf16[384,512]{1,0:T(8,128)(2,1)S(1)} collective-permute-done((bf16[384,512]{1,0:T(8,128)(2,1)S(1)}, bf16[384,512]{1,0:T(8,128)(2,1)S(1)}, u32[]{:S(2)}, u32[]{:S(2)}) %collective-permute-start.13) | collective-permute-done | bytes 393248 | tf_op jit(solution)/shard_map/ppermute | solution.py:23
  59.6 0.3 shard_map.104.base_ref
  59.9 5.2 %collective-permute-done.18.refs_1_ = bf16[384,512]{1,0:T(8,128)(2,1)S(1)} collective-permute-done((bf16[384,512]{1,0:T(8,128)(2,1)S(1)}, bf16[384,512]{1,0:T(8,128)(2,1)S(1)}, u32[]{:S(2)}, u32[]{:S(2)}) %collective-permute-start.18) | collective-permute-done | bytes 393248 | tf_op jit(solution)/shard_map/ppermute | solution.py:23
  65.1 0.2 collective-permute-done.16.refs_0_
  65.4 1.0 %shard_map.105 = bf16[384,1024]{1,0:T(8,128)(2,1)} custom-call(f32[384,1024]{1,0:T(8,128)S(1)} %shard_map.104.base_ref, bf16[384,512]{1,0:T(8,128)(2,1)S(1)} %collective-permute-done.16.refs_0_, bf16[384,512]{1,0:T(8,128)(2,1)S(1)} %collective-permute-done.18.refs_1_), custom_call_target="tpu_custom_call" | custom-call | tf_op jit(solution)/shard_map/pallas_call | solution.py:629
  (2 shorter events, 0.0 us)
Async XLA Ops:
  1.7 21.8 %collective-permute-start.7 = (bf16[320,1024]{1,0:T(8,128)(2,1)S(1)}, bf16[320,1024]{1,0:T(8,128)(2,1)S(1)}, u32[]{:S(2)}, u32[]{:S(2)}) collective-permute-start(bf16[320,1024]{1,0:T(8,128)(2,1)S(1)} %get-tuple-element.82.x_ref), channel_id=1, source_target_pairs={{0,1},{1,0},{2,3},{3,2},{4,5},{5,4},{6,7},{7,6},{8,9},{9,8},{10,11... | collective-permute-start | bytes 1966088 | tf_op jit(solution)/shard_map/ppermute | solution.py:23
  4.7 18.8 %collective-permute-start.8 = (bf16[320,1024]{1,0:T(8,128)(2,1)S(1)}, bf16[320,1024]{1,0:T(8,128)(2,1)S(1)}, u32[]{:S(2)}, u32[]{:S(2)}) collective-permute-start(bf16[320,1024]{1,0:T(8,128)(2,1)S(1)} %get-tuple-element.82.x_ref), channel_id=1, source_target_pairs={{0,2},{1,3},{2,0},{3,1},{4,6},{5,7},{6,4},{7,5},{8,10},{9,11},{10,... | collective-permute-start | bytes 1966088 | tf_op jit(solution)/shard_map/ppermute | solution.py:23
  8.2 1.4 %collective-permute-start = (bf16[4,16,1024]{2,1,0:T(8,128)(2,1)S(1)}, bf16[4,16,1024]{2,1,0:T(8,128)(2,1)S(1)}, u32[]{:S(2)}, u32[]{:S(2)}) collective-permute-start(bf16[4,16,1024]{2,1,0:T(8,128)(2,1)S(1)} %get-tuple-element.71), channel_id=1, source_target_pairs={{0,4},{4,0},{8,12},{12,8},{16,20},{20,16},{24,28},{28,24},{1,5},{5... | collective-permute-start | bytes 393224 | tf_op jit(solution)/shard_map/ppermute | solution.py:23
  9.7 10.0 %collective-permute-start.1 = (bf16[24,1024]{1,0:T(8,128)(2,1)S(1)}, bf16[24,1024]{1,0:T(8,128)(2,1)S(1)}, u32[]{:S(2)}, u32[]{:S(2)}) collective-permute-start(bf16[24,1024]{1,0:T(8,128)(2,1)S(1)} %get-tuple-element.73), channel_id=1, source_target_pairs={{0,8},{4,12},{8,0},{12,4},{16,24},{20,28},{24,16},{28,20},{1,9},{5... | collective-permute-start | bytes 147464 | tf_op jit(solution)/shard_map/ppermute | solution.py:23
  11.3 8.4 %collective-permute-start.2 = (bf16[24,1024]{1,0:T(8,128)(2,1)S(1)}, bf16[24,1024]{1,0:T(8,128)(2,1)S(1)}, u32[]{:S(2)}, u32[]{:S(2)}) collective-permute-start(bf16[24,1024]{1,0:T(8,128)(2,1)S(1)} %get-tuple-element.74), channel_id=1, source_target_pairs={{0,16},{4,20},{8,24},{12,28},{16,0},{20,4},{24,8},{28,12},{1,17},{... | collective-permute-start | bytes 147464 | tf_op jit(solution)/shard_map/ppermute | solution.py:23
  13.9 5.9 %collective-permute-start.3 = (bf16[24,1024]{1,0:T(8,128)(2,1)S(1)}, bf16[24,1024]{1,0:T(8,128)(2,1)S(1)}, u32[]{:S(2)}, u32[]{:S(2)}) collective-permute-start(bf16[24,1024]{1,0:T(8,128)(2,1)S(1)} %get-tuple-element.75), channel_id=1, source_target_pairs={{0,24},{4,28},{8,16},{12,20},{16,8},{20,12},{24,0},{28,4},{1,25},{... | collective-permute-start | bytes 147464 | tf_op jit(solution)/shard_map/ppermute | solution.py:23
  20.0 7.2 %collective-permute-start.4 = (bf16[80,1024]{1,0:T(8,128)(2,1)S(1)}, bf16[80,1024]{1,0:T(8,128)(2,1)S(1)}, u32[]{:S(2)}, u32[]{:S(2)}) collective-permute-start(bf16[80,1024]{1,0:T(8,128)(2,1)S(1)} %shard_map.96.refs_0_), channel_id=1, source_target_pairs={{0,1},{1,0},{2,3},{3,2},{4,5},{5,4},{6,7},{7,6},{8,9},{9,8},{10,11... | collective-permute-start | bytes 491528 | tf_op jit(solution)/shard_map/ppermute | solution.py:23
  20.6 7.5 %collective-permute-start.5 = (bf16[80,1024]{1,0:T(8,128)(2,1)S(1)}, bf16[80,1024]{1,0:T(8,128)(2,1)S(1)}, u32[]{:S(2)}, u32[]{:S(2)}) collective-permute-start(bf16[80,1024]{1,0:T(8,128)(2,1)S(1)} %shard_map.96.refs_0_), channel_id=1, source_target_pairs={{0,2},{1,3},{2,0},{3,1},{4,6},{5,7},{6,4},{7,5},{8,10},{9,11},{10,... | collective-permute-start | bytes 491528 | tf_op jit(solution)/shard_map/ppermute | solution.py:23
  21.1 9.6 %collective-permute-start.6 = (bf16[80,1024]{1,0:T(8,128)(2,1)S(1)}, bf16[80,1024]{1,0:T(8,128)(2,1)S(1)}, u32[]{:S(2)}, u32[]{:S(2)}) collective-permute-start(bf16[80,1024]{1,0:T(8,128)(2,1)S(1)} %shard_map.96.refs_0_), channel_id=1, source_target_pairs={{0,3},{1,2},{2,1},{3,0},{4,7},{5,6},{6,5},{7,4},{8,11},{9,10},{10,... | collective-permute-start | bytes 491528 | tf_op jit(solution)/shard_map/ppermute | solution.py:23
  25.9 10.2 %collective-permute-start.9 = (bf16[160,1024]{1,0:T(8,128)(2,1)S(1)}, bf16[160,1024]{1,0:T(8,128)(2,1)S(1)}, u32[]{:S(2)}, u32[]{:S(2)}) collective-permute-start(bf16[160,1024]{1,0:T(8,128)(2,1)S(1)} %slice.10), channel_id=1, source_target_pairs={{0,1},{1,0},{2,3},{3,2},{4,5},{5,4},{6,7},{7,6},{8,9},{9,8},{10,11... | collective-permute-start | bytes 983048 | tf_op jit(solution)/shard_map/ppermute | solution.py:23
  26.5 12.3 %collective-permute-start.12 = (bf16[160,1024]{1,0:T(8,128)(2,1)S(1)}, bf16[160,1024]{1,0:T(8,128)(2,1)S(1)}, u32[]{:S(2)}, u32[]{:S(2)}) collective-permute-start(bf16[160,1024]{1,0:T(8,128)(2,1)S(1)} %slice.11), channel_id=1, source_target_pairs={{0,2},{1,3},{2,0},{3,1},{4,6},{5,7},{6,4},{7,5},{8,10},{9,11},{10,... | collective-permute-start | bytes 983048 | tf_op jit(solution)/shard_map/ppermute | solution.py:23
  37.7 6.5 %collective-permute-start.10 = (bf16[160,512]{1,0:T(8,128)(2,1)S(1)}, bf16[160,512]{1,0:T(8,128)(2,1)S(1)}, u32[]{:S(2)}, u32[]{:S(2)}) collective-permute-start(bf16[160,512]{1,0:T(8,128)(2,1)S(1)} %get-tuple-element.104), channel_id=1, source_target_pairs={{0,1},{1,0},{2,3},{3,2},{4,5},{5,4},{6,7},{7,6},{8,9},{9,8},{10,11... | collective-permute-start | bytes 491528 | tf_op jit(solution)/shard_map/ppermute | solution.py:23
  38.3 6.8 %collective-permute-start.11 = (bf16[160,512]{1,0:T(8,128)(2,1)S(1)}, bf16[160,512]{1,0:T(8,128)(2,1)S(1)}, u32[]{:S(2)}, u32[]{:S(2)}) collective-permute-start(bf16[160,512]{1,0:T(8,128)(2,1)S(1)} %get-tuple-element.105), channel_id=1, source_target_pairs={{0,2},{1,3},{2,0},{3,1},{4,6},{5,7},{6,4},{7,5},{8,10},{9,11},{10,... | collective-permute-start | bytes 491528 | tf_op jit(solution)/shard_map/ppermute | solution.py:23
  41.1 8.9 %collective-permute-start.17 = (bf16[224,512]{1,0:T(8,128)(2,1)S(1)}, bf16[224,512]{1,0:T(8,128)(2,1)S(1)}, u32[]{:S(2)}, u32[]{:S(2)}) collective-permute-start(bf16[224,512]{1,0:T(8,128)(2,1)S(1)} %get-tuple-element.122), channel_id=1, source_target_pairs={{0,2},{1,3},{2,0},{3,1},{4,6},{5,7},{6,4},{7,5},{8,10},{9,11},{10,... | collective-permute-start | bytes 688136 | tf_op jit(solution)/shard_map/ppermute | solution.py:23
  42.7 9.3 %collective-permute-start.15 = (bf16[224,512]{1,0:T(8,128)(2,1)S(1)}, bf16[224,512]{1,0:T(8,128)(2,1)S(1)}, u32[]{:S(2)}, u32[]{:S(2)}) collective-permute-start(bf16[224,512]{1,0:T(8,128)(2,1)S(1)} %get-tuple-element.119), channel_id=1, source_target_pairs={{0,1},{1,0},{2,3},{3,2},{4,5},{5,4},{6,7},{7,6},{8,9},{9,8},{10,11... | collective-permute-start | bytes 688136 | tf_op jit(solution)/shard_map/ppermute | solution.py:23
  45.7 12.7 %collective-permute-start.14 = (bf16[384,512]{1,0:T(8,128)(2,1)S(1)}, bf16[384,512]{1,0:T(8,128)(2,1)S(1)}, u32[]{:S(2)}, u32[]{:S(2)}) collective-permute-start(bf16[384,512]{1,0:T(8,128)(2,1)S(1)} %get-tuple-element.116), channel_id=1, source_target_pairs={{0,2},{1,3},{2,0},{3,1},{4,6},{5,7},{6,4},{7,5},{8,10},{9,11},{10,... | collective-permute-start | bytes 1179656 | tf_op jit(solution)/shard_map/ppermute | solution.py:23
  46.4 6.8 %copy-start = (bf16[384,1024]{1,0:T(8,128)(2,1)S(1)}, bf16[384,1024]{1,0:T(8,128)(2,1)}, u32[]{:S(2)}) copy-start(bf16[384,1024]{1,0:T(8,128)(2,1)} %text_hbm.1) | copy-start | bytes 2359300
  46.4 13.3 %collective-permute-start.13 = (bf16[384,512]{1,0:T(8,128)(2,1)S(1)}, bf16[384,512]{1,0:T(8,128)(2,1)S(1)}, u32[]{:S(2)}, u32[]{:S(2)}) collective-permute-start(bf16[384,512]{1,0:T(8,128)(2,1)S(1)} %get-tuple-element.114), channel_id=1, source_target_pairs={{0,1},{1,0},{2,3},{3,2},{4,5},{5,4},{6,7},{7,6},{8,9},{9,8},{10,11... | collective-permute-start | bytes 1179656 | tf_op jit(solution)/shard_map/ppermute | solution.py:23
  50.1 15.0 %collective-permute-start.18 = (bf16[384,512]{1,0:T(8,128)(2,1)S(1)}, bf16[384,512]{1,0:T(8,128)(2,1)S(1)}, u32[]{:S(2)}, u32[]{:S(2)}) collective-permute-start(bf16[384,512]{1,0:T(8,128)(2,1)S(1)} %add_convert_fusion.1), channel_id=1, source_target_pairs={{0,1},{1,0},{2,3},{3,2},{4,5},{5,4},{6,7},{7,6},{8,9},{9,8},{10,11... | collective-permute-start | bytes 1179656 | tf_op jit(solution)/shard_map/ppermute | solution.py:23
  52.1 13.3 %collective-permute-start.16 = (bf16[384,512]{1,0:T(8,128)(2,1)S(1)}, bf16[384,512]{1,0:T(8,128)(2,1)S(1)}, u32[]{:S(2)}, u32[]{:S(2)}) collective-permute-start(bf16[384,512]{1,0:T(8,128)(2,1)S(1)} %add_convert_fusion.2), channel_id=1, source_target_pairs={{0,2},{1,3},{2,0},{3,1},{4,6},{5,7},{6,4},{7,5},{8,10},{9,11},{10,... | collective-permute-start | bytes 1179656 | tf_op jit(solution)/shard_map/ppermute | solution.py:23

commit v10 on v4

--- a/solution.py
+++ b/solution.py
@@ -39,11 +39,15 @@
     return sorted(range(1, n), key=lambda s: (bin(s).count("1"), s), reverse=reverse)
 
 
+def sides(n):
+    half = round_up(n // 2, 16)
+    return (0, half), (half, n - half)
+
+
 def halves(block):
     if isinstance(block, tuple):
         return block
-    half = block.shape[0] // 2
-    return block[:half], block[half:]
+    return tuple(block[first : first + rows] for first, rows in sides(block.shape[0]))
 
 
 def near_blocks(x, n):
@@ -300,7 +304,6 @@
 
 def own_kernel(me_ref, x_ref, gain_ref, w_ref, acc_ref, ss_ref, held_ref, sem_ref):
     n_ten, _, width, _ = held_ref.shape
-    half = x_ref.shape[0] // 2
     copies = []
     for s in range(n_ten):
         rows = pl.ds(pl.multiple_of((me_ref[0] ^ s) * width, width), width)
@@ -308,15 +311,15 @@
     for copy in copies:
         copy.start()
     scaled = []
-    for side in range(2):
-        rows = pl.ds(side * half, half)
+    for first, count in sides(x_ref.shape[0]):
+        rows = pl.ds(first, count)
         x, total = scale_rows(x_ref[rows], gain_ref[me_ref[0]])
         scaled.append(x)
-        ss_ref[rows] = jnp.broadcast_to(total, (half, 128))
+        ss_ref[rows] = jnp.broadcast_to(total, (count, 128))
     for j in range(3):
         copies[j].wait()
-        for side in range(2):
-            acc_ref[j, pl.ds(side * half, half)] = jnp.dot(
+        for side, (first, count) in enumerate(sides(x_ref.shape[0])):
+            acc_ref[j, pl.ds(first, count)] = jnp.dot(
                 scaled[side], held_ref[0, j], preferred_element_type=jnp.float32
             )
     for copy in copies[3:]:
@@ -345,14 +348,14 @@
     n_x = sum(pieces)
     x_refs, refs = list(refs[:n_x]), refs[n_x:]
     gain_ref, held_ref, acc_in, ss_in, acc_ref, ss_ref = refs
-    half = acc_ref.shape[1] // 2
+    parts = [pl.ds(first, count) for first, count in sides(acc_ref.shape[1])]
     views = []
     for n in pieces:
         mine, x_refs = x_refs[:n], x_refs[n:]
-        views.append([mine[0].at[pl.ds(side * half, half)] if n == 1 else mine[side] for side in range(2)])
+        views.append([mine[0].at[parts[side]] if n == 1 else mine[side] for side in range(2)])
     scaled = {}
     for side in range(2):
-        rows = pl.ds(side * half, half)
+        rows = parts[side]
         total = ss_in[rows]
         for b, s in enumerate(near):
             scaled[side, b], part = scale_rows(views[b][side][...], gain_ref[me_ref[0] ^ s])
@@ -360,7 +363,7 @@
         ss_ref[rows] = total
     for j in range(3):
         for side in range(2):
-            rows = pl.ds(side * half, half)
+            rows = parts[side]
             acc = acc_in[j, rows]
             for b, s in enumerate(near):
                 acc += jnp.dot(scaled[side, b], held_ref[s, j], preferred_element_type=jnp.float32)
@@ -434,8 +437,8 @@
 
 
 def project_side(side, far, me_ref, x_ref, gain_ref, held_ref, acc_ref, ss_ref, out_ref):
-    half = x_ref.shape[0]
-    part = pl.ds(side * half, half)
+    first, count = sides(acc_ref.shape[1])[side]
+    part = pl.ds(first, count)
     x, total = scale_rows(x_ref[...], gain_ref[me_ref[0] ^ far])
     scale = lax.rsqrt((ss_ref[part] + total) / D + EPS)[:, :1]
     for j in range(3):
@@ -652,7 +655,7 @@
 
     n_rows = n_req * region
     n_img = round_up(n_rows + 1, 16)
-    n_text = round_up(length - (n_rows if img_dev == n_req else 0), 32)
+    n_text = length - (n_rows if img_dev == n_req else 0)
     even, odd, ctext, rtext, sel, table, key_ok, gains, vis_row = prepare(
         req_at, image_request, slot_start, grids, text, jnp.transpose(patches, (1, 2, 0, 3)), dec_gain, vis_gain, n_req,
         n_text, n_img

time: 66.2 us -> 66.1 us (level)
  transfers between devices with their start and end apart: 19 -> 19, of which waited for: 10 -> 10; matrix products, arithmetic and copies ran while one was open for 1% -> 1% of each run, Pallas kernels for 25% -> 26%
where the time goes in v10:
time: 66.1 us; the launch traced here: 66 us
  starting transfers between devices  22.4 us (34%)
  waiting for transfers between devices  22.2 us (34%)
  Pallas kernels  20.5 us (31%)
    ppermute x19, starting transfers between devices, swap(): return lax.ppermute(x, axis, [(i, i ^ s) for i in range(n)])  22.4 us
    ppermute x19, waiting for transfers between devices, swap(): return lax.ppermute(x, axis, [(i, i ^ s) for i in range(n)])  22.2 us
    pallas_call x1, Pallas kernels, own_part(): pl.pallas_call(own_kernel, out_shape=(jax.ShapeDtypeStruct((3, rows, cols...  4.75 us
    pallas_call x1, Pallas kernels, prepare(): pl.pallas_call(functools.partial(prep_kernel, n_req), out_shape=tuple((ja...  2.72 us
    pallas_call x1, Pallas kernels, image_part(): pl.pallas_call(functools.partial(image_kernel, n_rows, len(blocks)), out_...  2.69 us
    pallas_call x1, Pallas kernels, near_part(): pl.pallas_call(functools.partial(near_kernel, near, pieces), out_shape=(j...  2.41 us
    pallas_call x1, Pallas kernels, tail_part(): pl.pallas_call(functools.partial(tail_kernel, far), out_shape=(jax.ShapeD...  2.3 us
    pallas_call x3, Pallas kernels, out_part(): pl.pallas_call(functools.partial(out_kernel, away), out_shape=(jax.ShapeD...  1.8 us
  transfers between devices with their start and end apart: 19, of which 10 were waited for; matrix products, arithmetic and copies ran while one was open for 1% of the time, Pallas kernels for 26%

profile of v10, /device:TPU:0, one launch (start us, length us, event | category | flops | bytes accessed | tf_op | source)
XLA Modules:
  0.0 66.0 jit_solution(4743832726708725277)
XLA Ops:
  0.0 2.7 %shard_map.91 = (bf16[4,16,1024]{2,1,0:T(8,128)(2,1)S(1)}, bf16[4,16,1024]{2,1,0:T(8,128)(2,1)S(1)}, bf16[312,1024]{1,0:T(8,128)(2,1)S(1)}, bf16[80,1024]{1,0:T(...) custom-call(s32[1]{0:T(128)} %bitcast.me_ref, ...), custom_call_target="tpu_custom_call" | custom-call | tf_op jit(solution)/shard_map/pallas_call | solution.py:203
  2.7 3.0 %collective-permute-start = (bf16[312,1024]{1,0:T(8,128)(2,1)S(1)}, bf16[312,1024]{1,0:T(8,128)(2,1)S(1)}, u32[]{:S(2)}, u32[]{:S(2)}) collective-permute-start(bf16[312,1024]{1,0:T(8,128)(2,1)S(1)} %get-tuple-element.69.x_ref), channel_id=1, source_target_pairs={{0,1},{1,0},{2,3},{3,2},{4,5},{5,4},{6,7},{7,6},{8,9},{9,8},{10,11... | collective-permute-start | bytes 1916936 | tf_op jit(solution)/shard_map/ppermute | solution.py:23
  5.7 1.5 %collective-permute-start.1 = (bf16[312,1024]{1,0:T(8,128)(2,1)S(1)}, bf16[312,1024]{1,0:T(8,128)(2,1)S(1)}, u32[]{:S(2)}, u32[]{:S(2)}) collective-permute-start(bf16[312,1024]{1,0:T(8,128)(2,1)S(1)} %get-tuple-element.69.x_ref), channel_id=1, source_target_pairs={{0,2},{1,3},{2,0},{3,1},{4,6},{5,7},{6,4},{7,5},{8,10},{9,11},{10,... | collective-permute-start | bytes 1916936 | tf_op jit(solution)/shard_map/ppermute | solution.py:23
  7.2 0.0 collective-permute-start.2
  7.3 1.3 %collective-permute-done.2.odd_ref = bf16[4,16,1024]{2,1,0:T(8,128)(2,1)S(1)} collective-permute-done((bf16[4,16,1024]{2,1,0:T(8,128)(2,1)S(1)}, bf16[4,16,1024]{2,1,0:T(8,128)(2,1)S(1)}, u32[]{:S(2)}, u32[]{:S(2)}) %collective-permute-start.2) | collective-permute-done | bytes 131104 | tf_op jit(solution)/shard_map/ppermute | solution.py:23
  8.6 1.6 %collective-permute-start.3 = (bf16[32,1024]{1,0:T(8,128)(2,1)S(1)}, bf16[32,1024]{1,0:T(8,128)(2,1)S(1)}, u32[]{:S(2)}, u32[]{:S(2)}) collective-permute-start(bf16[32,1024]{1,0:T(8,128)(2,1)S(1)} %get-tuple-element.66), channel_id=1, source_target_pairs={{0,8},{4,12},{8,0},{12,4},{16,24},{20,28},{24,16},{28,20},{1,9},{5... | collective-permute-start | bytes 196616 | tf_op jit(solution)/shard_map/ppermute | solution.py:23
  10.3 2.6 %collective-permute-start.4 = (bf16[32,1024]{1,0:T(8,128)(2,1)S(1)}, bf16[32,1024]{1,0:T(8,128)(2,1)S(1)}, u32[]{:S(2)}, u32[]{:S(2)}) collective-permute-start(bf16[32,1024]{1,0:T(8,128)(2,1)S(1)} %get-tuple-element.67), channel_id=1, source_target_pairs={{0,16},{4,20},{8,24},{12,28},{16,0},{20,4},{24,8},{28,12},{1,17},{... | collective-permute-start | bytes 196616 | tf_op jit(solution)/shard_map/ppermute | solution.py:23
  12.9 0.2 collective-permute-start.5
  13.1 0.0 collective-permute-done.3.refs_1_
  13.1 4.7 %collective-permute-done.4.refs_2_ = bf16[32,1024]{1,0:T(8,128)(2,1)S(1)} collective-permute-done((bf16[32,1024]{1,0:T(8,128)(2,1)S(1)}, bf16[32,1024]{1,0:T(8,128)(2,1)S(1)}, u32[]{:S(2)}, u32[]{:S(2)}) %collective-permute-start.4) | collective-permute-done | bytes 65568 | tf_op jit(solution)/shard_map/ppermute | solution.py:23
  17.8 1.2 %collective-permute-done.5.refs_3_ = bf16[32,1024]{1,0:T(8,128)(2,1)S(1)} collective-permute-done((bf16[32,1024]{1,0:T(8,128)(2,1)S(1)}, bf16[32,1024]{1,0:T(8,128)(2,1)S(1)}, u32[]{:S(2)}, u32[]{:S(2)}) %collective-permute-start.5) | collective-permute-done | bytes 65568 | tf_op jit(solution)/shard_map/ppermute | solution.py:23
  19.0 0.2 shard_map.93.refs_0_
  19.2 0.6 collective-permute-start.6
  19.8 0.5 collective-permute-start.7
  20.4 2.4 %collective-permute-start.8 = (bf16[80,1024]{1,0:T(8,128)(2,1)S(1)}, bf16[80,1024]{1,0:T(8,128)(2,1)S(1)}, u32[]{:S(2)}, u32[]{:S(2)}) collective-permute-start(bf16[80,1024]{1,0:T(8,128)(2,1)S(1)} %shard_map.93.refs_0_), channel_id=1, source_target_pairs={{0,3},{1,2},{2,1},{3,0},{4,7},{5,6},{6,5},{7,4},{8,11},{9,10},{10,... | collective-permute-start | bytes 491528 | tf_op jit(solution)/shard_map/ppermute | solution.py:23
  22.8 4.7 %shard_map.94 = (f32[3,312,512]{2,1,0:T(8,128)S(1)}, f32[312,128]{1,0:T(8,128)S(1)}, bf16[4,3,1024,512]{3,2,1,0:T(8,128)(2,1)S(1)}) custom-call(s32[1]{0:T(128)} %bitcast.5.me_ref, bf16[312,1024]{1,0:T(8,128)(2,1)S(1)} %get-tuple-element.69.x_ref, f32[4,1,1024]{2,1,0:T(1,128)S(1)} %get-tuple-element.59.gain_ref.refs_2_.refs_4_, bf16[3,4096,512]{2,1,0:T(8,128)(2,1)} %bitcast.9), custom_call_target="tpu_custom_call" | custom-call | tf_op jit(solution)/shard_map/pallas_call | solution.py:332
  27.5 0.0 collective-permute-done.refs_0_
  27.6 0.0 collective-permute-done.1.refs_1_
  27.6 0.6 collective-permute-start.9
  28.2 0.6 collective-permute-start.12
  28.8 2.4 %shard_map.95 = (f32[3,312,512]{2,1,0:T(8,128)S(1)}, f32[312,128]{1,0:T(8,128)S(1)}) custom-call(s32[1]{0:T(128)} %bitcast.5.me_ref, bf16[312,1024]{1,0:T(8,128)(2,1)S(1)} %collective-permute-done.refs_0_, bf16[312,1024]{1,0:T(8,128)(2,1)S(1)} %collective-permute-done.1.refs_1_, f32[4,1,1024]{2,1,0:T(1,128)S(1)} %get-tuple-element.59.gain_ref.refs_2_.refs_4_, ...), custom_call_target="tpu_custom_call" | custom-call | flops 99999997952 | tf_op jit(solution)/shard_map/pallas_call | solution.py:376
  31.2 0.7 %shard_map.96 = (bf16[384,312]{1,0:T(8,128)(2,1)S(1)}, bf16[384,80]{1,0:T(8,128)(2,1)S(1)}, f32[384,128]{1,0:T(8,128)S(1)}) custom-call(s32[8,128]{1,0:T(8,128)S(1)} %get-tuple-element.74.table_ref), custom_call_target="tpu_custom_call" | custom-call | tf_op jit(solution)/shard_map/pallas_call | solution.py:282
  31.9 0.0 collective-permute-done.6.refs_1_
  31.9 0.0 collective-permute-done.7.refs_2_
  32.0 0.0 collective-permute-done.8.refs_3_
  32.0 2.7 %shard_map.97 = (bf16[3,80,512]{2,1,0:T(8,128)(2,1)S(1)}, bf16[80,1024]{1,0:T(8,128)(2,1)S(1)}, bf16[512,4096]{1,0:T(8,128)(2,1)S(1)}) custom-call(s32[1]{0:T(128)} %bitcast.5.me_ref, bf16[80,1024]{1,0:T(8,128)(2,1)S(1)} %shard_map.93.refs_0_, bf16[80,1024]{1,0:T(8,128)(2,1)S(1)} %collective-permute-done.6.refs_1_, ...), custom_call_target="tpu_custom_call" | custom-call | tf_op jit(solution)/shard_map/pallas_call | solution.py:422
  34.7 0.2 collective-permute-done.9.top_ref
  34.9 1.7 %shard_map.98 = (bf16[3,160,512]{2,1,0:T(8,128)(2,1)S(1)}, bf16[3,160,512]{2,1,0:T(8,128)(2,1)S(1)}, bf16[160,512]{1,0:T(8,128)(2,1)S(1)}, bf16[160,512]{1,0:T(8,128)(2,1)S(1)}, bf16[160,512]{1,0:T(8,128)(2,1)S(1)}) custom-call(s32[1]{0:T(128)} %bitcast.5.me_ref, bf16[160,1024]{1,0:T(8,128)(2,1)S(1)} %collective-permute-done.9.top_ref, ...), custom_call_target="tpu_custom_call" | custom-call | tf_op jit(solution)/shard_map/pallas_call | solution.py:501
  36.6 1.4 %collective-permute-start.10 = (bf16[160,512]{1,0:T(8,128)(2,1)S(1)}, bf16[160,512]{1,0:T(8,128)(2,1)S(1)}, u32[]{:S(2)}, u32[]{:S(2)}) collective-permute-start(bf16[160,512]{1,0:T(8,128)(2,1)S(1)} %get-tuple-element.90), channel_id=1, source_target_pairs={{0,1},{1,0},{2,3},{3,2},{4,5},{5,4},{6,7},{7,6},{8,9},{9,8},{10,11... | collective-permute-start | bytes 491528 | tf_op jit(solution)/shard_map/ppermute | solution.py:23
  37.9 1.5 %collective-permute-start.11 = (bf16[160,512]{1,0:T(8,128)(2,1)S(1)}, bf16[160,512]{1,0:T(8,128)(2,1)S(1)}, u32[]{:S(2)}, u32[]{:S(2)}) collective-permute-start(bf16[160,512]{1,0:T(8,128)(2,1)S(1)} %get-tuple-element.91), channel_id=1, source_target_pairs={{0,2},{1,3},{2,0},{3,1},{4,6},{5,7},{6,4},{7,5},{8,10},{9,11},{10,... | collective-permute-start | bytes 491528 | tf_op jit(solution)/shard_map/ppermute | solution.py:23
  39.5 0.0 collective-permute-done.12.bottom_ref
  39.5 2.3 %shard_map.99 = (bf16[224,512]{1,0:T(8,128)(2,1)S(1)}, bf16[224,512]{1,0:T(8,128)(2,1)S(1)}, bf16[224,512]{1,0:T(8,128)(2,1)S(1)}) custom-call(s32[1]{0:T(128)} %bitcast.5.me_ref, bf16[152,1024]{1,0:T(8,128)(2,1)S(1)} %collective-permute-done.12.bottom_ref, f32[4,1,1024]{2,1,0:T(1,128)S(1)} %get-tuple-element.59.gain_ref.refs_2_.refs_4_, ...), custom_call_target="tpu_custom_call" | custom-call | flops 10000000000 | tf_op jit(solution)/shard_map/pallas_call | solution.py:540
  41.8 0.6 collective-permute-start.17
  42.4 0.8 %collective-permute-start.15 = (bf16[224,512]{1,0:T(8,128)(2,1)S(1)}, bf16[224,512]{1,0:T(8,128)(2,1)S(1)}, u32[]{:S(2)}, u32[]{:S(2)}) collective-permute-start(bf16[224,512]{1,0:T(8,128)(2,1)S(1)} %get-tuple-element.105), channel_id=1, source_target_pairs={{0,1},{1,0},{2,3},{3,2},{4,5},{5,4},{6,7},{7,6},{8,9},{9,8},{10,11... | collective-permute-start | bytes 688136 | tf_op jit(solution)/shard_map/ppermute | solution.py:23
  43.1 0.0 collective-permute-done.10
  43.1 1.6 %collective-permute-done.11 = bf16[160,512]{1,0:T(8,128)(2,1)S(1)} collective-permute-done((bf16[160,512]{1,0:T(8,128)(2,1)S(1)}, bf16[160,512]{1,0:T(8,128)(2,1)S(1)}, u32[]{:S(2)}, u32[]{:S(2)}) %collective-permute-start.11) | collective-permute-done | bytes 163872 | tf_op jit(solution)/shard_map/ppermute | solution.py:23
  44.7 0.6 shard_map.102
  45.4 1.8 %collective-permute-start.14 = (bf16[384,512]{1,0:T(8,128)(2,1)S(1)}, bf16[384,512]{1,0:T(8,128)(2,1)S(1)}, u32[]{:S(2)}, u32[]{:S(2)}) collective-permute-start(bf16[384,512]{1,0:T(8,128)(2,1)S(1)} %get-tuple-element.102), channel_id=1, source_target_pairs={{0,2},{1,3},{2,0},{3,1},{4,6},{5,7},{6,4},{7,5},{8,10},{9,11},{10,... | collective-permute-start | bytes 1179656 | tf_op jit(solution)/shard_map/ppermute | solution.py:23
  47.2 0.6 shard_map.101
  47.8 0.0 copy-start
  47.8 0.6 collective-permute-start.13
  48.4 1.9 %collective-permute-done.17 = bf16[224,512]{1,0:T(8,128)(2,1)S(1)} collective-permute-done((bf16[224,512]{1,0:T(8,128)(2,1)S(1)}, bf16[224,512]{1,0:T(8,128)(2,1)S(1)}, u32[]{:S(2)}, u32[]{:S(2)}) %collective-permute-start.17) | collective-permute-done | bytes 229408 | tf_op jit(solution)/shard_map/ppermute | solution.py:23
  50.4 0.1 add_convert_fusion.1
  50.5 0.6 collective-permute-start.18
  51.1 0.0 collective-permute-done.15
  51.1 0.1 add_convert_fusion.2
  51.2 1.4 %collective-permute-start.16 = (bf16[384,512]{1,0:T(8,128)(2,1)S(1)}, bf16[384,512]{1,0:T(8,128)(2,1)S(1)}, u32[]{:S(2)}, u32[]{:S(2)}) collective-permute-start(bf16[384,512]{1,0:T(8,128)(2,1)S(1)} %add_convert_fusion.2), channel_id=1, source_target_pairs={{0,2},{1,3},{2,0},{3,1},{4,6},{5,7},{6,4},{7,5},{8,10},{9,11},{10,... | collective-permute-start | bytes 1179656 | tf_op jit(solution)/shard_map/ppermute | solution.py:23
  52.6 0.1 slice_reduce_fusion
  52.7 0.0 copy-done
  52.7 0.4 add_convert_fusion.base_ref
  53.1 0.6 shard_map.100
  53.7 5.1 %collective-permute-done.14.refs_3_ = bf16[384,512]{1,0:T(8,128)(2,1)S(1)} collective-permute-done((bf16[384,512]{1,0:T(8,128)(2,1)S(1)}, bf16[384,512]{1,0:T(8,128)(2,1)S(1)}, u32[]{:S(2)}, u32[]{:S(2)}) %collective-permute-start.14) | collective-permute-done | bytes 393248 | tf_op jit(solution)/shard_map/ppermute | solution.py:23
  58.8 1.1 %collective-permute-done.13.refs_1_ = bf16[384,512]{1,0:T(8,128)(2,1)S(1)} collective-permute-done((bf16[384,512]{1,0:T(8,128)(2,1)S(1)}, bf16[384,512]{1,0:T(8,128)(2,1)S(1)}, u32[]{:S(2)}, u32[]{:S(2)}) %collective-permute-start.13) | collective-permute-done | bytes 393248 | tf_op jit(solution)/shard_map/ppermute | solution.py:23
  59.9 0.3 shard_map.103.base_ref
  60.2 4.1 %collective-permute-done.18.refs_1_ = bf16[384,512]{1,0:T(8,128)(2,1)S(1)} collective-permute-done((bf16[384,512]{1,0:T(8,128)(2,1)S(1)}, bf16[384,512]{1,0:T(8,128)(2,1)S(1)}, u32[]{:S(2)}, u32[]{:S(2)}) %collective-permute-start.18) | collective-permute-done | bytes 393248 | tf_op jit(solution)/shard_map/ppermute | solution.py:23
  64.3 0.7 %collective-permute-done.16.refs_0_ = bf16[384,512]{1,0:T(8,128)(2,1)S(1)} collective-permute-done((bf16[384,512]{1,0:T(8,128)(2,1)S(1)}, bf16[384,512]{1,0:T(8,128)(2,1)S(1)}, u32[]{:S(2)}, u32[]{:S(2)}) %collective-permute-start.16) | collective-permute-done | bytes 393248 | tf_op jit(solution)/shard_map/ppermute | solution.py:23
  65.0 1.0 %shard_map.104 = bf16[384,1024]{1,0:T(8,128)(2,1)} custom-call(f32[384,1024]{1,0:T(8,128)S(1)} %shard_map.103.base_ref, bf16[384,512]{1,0:T(8,128)(2,1)S(1)} %collective-permute-done.16.refs_0_, bf16[384,512]{1,0:T(8,128)(2,1)S(1)} %collective-permute-done.18.refs_1_), custom_call_target="tpu_custom_call" | custom-call | tf_op jit(solution)/shard_map/pallas_call | solution.py:613
  (3 shorter events, 0.1 us)
Async XLA Ops:
  2.7 24.8 %collective-permute-start = (bf16[312,1024]{1,0:T(8,128)(2,1)S(1)}, bf16[312,1024]{1,0:T(8,128)(2,1)S(1)}, u32[]{:S(2)}, u32[]{:S(2)}) collective-permute-start(bf16[312,1024]{1,0:T(8,128)(2,1)S(1)} %get-tuple-element.69.x_ref), channel_id=1, source_target_pairs={{0,1},{1,0},{2,3},{3,2},{4,5},{5,4},{6,7},{7,6},{8,9},{9,8},{10,11... | collective-permute-start | bytes 1916936 | tf_op jit(solution)/shard_map/ppermute | solution.py:23
  5.7 21.8 %collective-permute-start.1 = (bf16[312,1024]{1,0:T(8,128)(2,1)S(1)}, bf16[312,1024]{1,0:T(8,128)(2,1)S(1)}, u32[]{:S(2)}, u32[]{:S(2)}) collective-permute-start(bf16[312,1024]{1,0:T(8,128)(2,1)S(1)} %get-tuple-element.69.x_ref), channel_id=1, source_target_pairs={{0,2},{1,3},{2,0},{3,1},{4,6},{5,7},{6,4},{7,5},{8,10},{9,11},{10,... | collective-permute-start | bytes 1916936 | tf_op jit(solution)/shard_map/ppermute | solution.py:23
  7.2 1.3 %collective-permute-start.2 = (bf16[4,16,1024]{2,1,0:T(8,128)(2,1)S(1)}, bf16[4,16,1024]{2,1,0:T(8,128)(2,1)S(1)}, u32[]{:S(2)}, u32[]{:S(2)}) collective-permute-start(bf16[4,16,1024]{2,1,0:T(8,128)(2,1)S(1)} %get-tuple-element.64), channel_id=1, source_target_pairs={{0,4},{4,0},{8,12},{12,8},{16,20},{20,16},{24,28},{28,24},{1,5},{5... | collective-permute-start | bytes 393224 | tf_op jit(solution)/shard_map/ppermute | solution.py:23
  8.6 4.5 %collective-permute-start.3 = (bf16[32,1024]{1,0:T(8,128)(2,1)S(1)}, bf16[32,1024]{1,0:T(8,128)(2,1)S(1)}, u32[]{:S(2)}, u32[]{:S(2)}) collective-permute-start(bf16[32,1024]{1,0:T(8,128)(2,1)S(1)} %get-tuple-element.66), channel_id=1, source_target_pairs={{0,8},{4,12},{8,0},{12,4},{16,24},{20,28},{24,16},{28,20},{1,9},{5... | collective-permute-start | bytes 196616 | tf_op jit(solution)/shard_map/ppermute | solution.py:23
  10.3 7.5 %collective-permute-start.4 = (bf16[32,1024]{1,0:T(8,128)(2,1)S(1)}, bf16[32,1024]{1,0:T(8,128)(2,1)S(1)}, u32[]{:S(2)}, u32[]{:S(2)}) collective-permute-start(bf16[32,1024]{1,0:T(8,128)(2,1)S(1)} %get-tuple-element.67), channel_id=1, source_target_pairs={{0,16},{4,20},{8,24},{12,28},{16,0},{20,4},{24,8},{28,12},{1,17},{... | collective-permute-start | bytes 196616 | tf_op jit(solution)/shard_map/ppermute | solution.py:23
  12.9 6.2 %collective-permute-start.5 = (bf16[32,1024]{1,0:T(8,128)(2,1)S(1)}, bf16[32,1024]{1,0:T(8,128)(2,1)S(1)}, u32[]{:S(2)}, u32[]{:S(2)}) collective-permute-start(bf16[32,1024]{1,0:T(8,128)(2,1)S(1)} %get-tuple-element.68), channel_id=1, source_target_pairs={{0,24},{4,28},{8,16},{12,20},{16,8},{20,12},{24,0},{28,4},{1,25},{... | collective-permute-start | bytes 196616 | tf_op jit(solution)/shard_map/ppermute | solution.py:23
  19.2 12.7 %collective-permute-start.6 = (bf16[80,1024]{1,0:T(8,128)(2,1)S(1)}, bf16[80,1024]{1,0:T(8,128)(2,1)S(1)}, u32[]{:S(2)}, u32[]{:S(2)}) collective-permute-start(bf16[80,1024]{1,0:T(8,128)(2,1)S(1)} %shard_map.93.refs_0_), channel_id=1, source_target_pairs={{0,1},{1,0},{2,3},{3,2},{4,5},{5,4},{6,7},{7,6},{8,9},{9,8},{10,11... | collective-permute-start | bytes 491528 | tf_op jit(solution)/shard_map/ppermute | solution.py:23
  19.8 12.1 %collective-permute-start.7 = (bf16[80,1024]{1,0:T(8,128)(2,1)S(1)}, bf16[80,1024]{1,0:T(8,128)(2,1)S(1)}, u32[]{:S(2)}, u32[]{:S(2)}) collective-permute-start(bf16[80,1024]{1,0:T(8,128)(2,1)S(1)} %shard_map.93.refs_0_), channel_id=1, source_target_pairs={{0,2},{1,3},{2,0},{3,1},{4,6},{5,7},{6,4},{7,5},{8,10},{9,11},{10,... | collective-permute-start | bytes 491528 | tf_op jit(solution)/shard_map/ppermute | solution.py:23
  20.4 11.6 %collective-permute-start.8 = (bf16[80,1024]{1,0:T(8,128)(2,1)S(1)}, bf16[80,1024]{1,0:T(8,128)(2,1)S(1)}, u32[]{:S(2)}, u32[]{:S(2)}) collective-permute-start(bf16[80,1024]{1,0:T(8,128)(2,1)S(1)} %shard_map.93.refs_0_), channel_id=1, source_target_pairs={{0,3},{1,2},{2,1},{3,0},{4,7},{5,6},{6,5},{7,4},{8,11},{9,10},{10,... | collective-permute-start | bytes 491528 | tf_op jit(solution)/shard_map/ppermute | solution.py:23
  27.6 7.3 %collective-permute-start.9 = (bf16[160,1024]{1,0:T(8,128)(2,1)S(1)}, bf16[160,1024]{1,0:T(8,128)(2,1)S(1)}, u32[]{:S(2)}, u32[]{:S(2)}) collective-permute-start(bf16[160,1024]{1,0:T(8,128)(2,1)S(1)} %slice.10), channel_id=1, source_target_pairs={{0,1},{1,0},{2,3},{3,2},{4,5},{5,4},{6,7},{7,6},{8,9},{9,8},{10,11... | collective-permute-start | bytes 983048 | tf_op jit(solution)/shard_map/ppermute | solution.py:23
  28.2 11.2 %collective-permute-start.12 = (bf16[152,1024]{1,0:T(8,128)(2,1)S(1)}, bf16[152,1024]{1,0:T(8,128)(2,1)S(1)}, u32[]{:S(2)}, u32[]{:S(2)}) collective-permute-start(bf16[152,1024]{1,0:T(8,128)(2,1)S(1)} %slice.11), channel_id=1, source_target_pairs={{0,2},{1,3},{2,0},{3,1},{4,6},{5,7},{6,4},{7,5},{8,10},{9,11},{10,... | collective-permute-start | bytes 933896 | tf_op jit(solution)/shard_map/ppermute | solution.py:23
  36.6 6.5 %collective-permute-start.10 = (bf16[160,512]{1,0:T(8,128)(2,1)S(1)}, bf16[160,512]{1,0:T(8,128)(2,1)S(1)}, u32[]{:S(2)}, u32[]{:S(2)}) collective-permute-start(bf16[160,512]{1,0:T(8,128)(2,1)S(1)} %get-tuple-element.90), channel_id=1, source_target_pairs={{0,1},{1,0},{2,3},{3,2},{4,5},{5,4},{6,7},{7,6},{8,9},{9,8},{10,11... | collective-permute-start | bytes 491528 | tf_op jit(solution)/shard_map/ppermute | solution.py:23
  37.9 6.8 %collective-permute-start.11 = (bf16[160,512]{1,0:T(8,128)(2,1)S(1)}, bf16[160,512]{1,0:T(8,128)(2,1)S(1)}, u32[]{:S(2)}, u32[]{:S(2)}) collective-permute-start(bf16[160,512]{1,0:T(8,128)(2,1)S(1)} %get-tuple-element.91), channel_id=1, source_target_pairs={{0,2},{1,3},{2,0},{3,1},{4,6},{5,7},{6,4},{7,5},{8,10},{9,11},{10,... | collective-permute-start | bytes 491528 | tf_op jit(solution)/shard_map/ppermute | solution.py:23
  41.8 8.6 %collective-permute-start.17 = (bf16[224,512]{1,0:T(8,128)(2,1)S(1)}, bf16[224,512]{1,0:T(8,128)(2,1)S(1)}, u32[]{:S(2)}, u32[]{:S(2)}) collective-permute-start(bf16[224,512]{1,0:T(8,128)(2,1)S(1)} %get-tuple-element.108), channel_id=1, source_target_pairs={{0,2},{1,3},{2,0},{3,1},{4,6},{5,7},{6,4},{7,5},{8,10},{9,11},{10,... | collective-permute-start | bytes 688136 | tf_op jit(solution)/shard_map/ppermute | solution.py:23
  42.4 8.7 %collective-permute-start.15 = (bf16[224,512]{1,0:T(8,128)(2,1)S(1)}, bf16[224,512]{1,0:T(8,128)(2,1)S(1)}, u32[]{:S(2)}, u32[]{:S(2)}) collective-permute-start(bf16[224,512]{1,0:T(8,128)(2,1)S(1)} %get-tuple-element.105), channel_id=1, source_target_pairs={{0,1},{1,0},{2,3},{3,2},{4,5},{5,4},{6,7},{7,6},{8,9},{9,8},{10,11... | collective-permute-start | bytes 688136 | tf_op jit(solution)/shard_map/ppermute | solution.py:23
  45.4 13.5 %collective-permute-start.14 = (bf16[384,512]{1,0:T(8,128)(2,1)S(1)}, bf16[384,512]{1,0:T(8,128)(2,1)S(1)}, u32[]{:S(2)}, u32[]{:S(2)}) collective-permute-start(bf16[384,512]{1,0:T(8,128)(2,1)S(1)} %get-tuple-element.102), channel_id=1, source_target_pairs={{0,2},{1,3},{2,0},{3,1},{4,6},{5,7},{6,4},{7,5},{8,10},{9,11},{10,... | collective-permute-start | bytes 1179656 | tf_op jit(solution)/shard_map/ppermute | solution.py:23
  47.8 4.9 %copy-start = (bf16[384,1024]{1,0:T(8,128)(2,1)S(1)}, bf16[384,1024]{1,0:T(8,128)(2,1)}, u32[]{:S(2)}) copy-start(bf16[384,1024]{1,0:T(8,128)(2,1)} %text_hbm.1) | copy-start | bytes 2359300
  47.8 12.1 %collective-permute-start.13 = (bf16[384,512]{1,0:T(8,128)(2,1)S(1)}, bf16[384,512]{1,0:T(8,128)(2,1)S(1)}, u32[]{:S(2)}, u32[]{:S(2)}) collective-permute-start(bf16[384,512]{1,0:T(8,128)(2,1)S(1)} %get-tuple-element.100), channel_id=1, source_target_pairs={{0,1},{1,0},{2,3},{3,2},{4,5},{5,4},{6,7},{7,6},{8,9},{9,8},{10,11... | collective-permute-start | bytes 1179656 | tf_op jit(solution)/shard_map/ppermute | solution.py:23
  50.5 13.8 %collective-permute-start.18 = (bf16[384,512]{1,0:T(8,128)(2,1)S(1)}, bf16[384,512]{1,0:T(8,128)(2,1)S(1)}, u32[]{:S(2)}, u32[]{:S(2)}) collective-permute-start(bf16[384,512]{1,0:T(8,128)(2,1)S(1)} %add_convert_fusion.1), channel_id=1, source_target_pairs={{0,1},{1,0},{2,3},{3,2},{4,5},{5,4},{6,7},{7,6},{8,9},{9,8},{10,11... | collective-permute-start | bytes 1179656 | tf_op jit(solution)/shard_map/ppermute | solution.py:23
  51.2 13.8 %collective-permute-start.16 = (bf16[384,512]{1,0:T(8,128)(2,1)S(1)}, bf16[384,512]{1,0:T(8,128)(2,1)S(1)}, u32[]{:S(2)}, u32[]{:S(2)}) collective-permute-start(bf16[384,512]{1,0:T(8,128)(2,1)S(1)} %add_convert_fusion.2), channel_id=1, source_target_pairs={{0,2},{1,3},{2,0},{3,1},{4,6},{5,7},{6,4},{7,5},{8,10},{9,11},{10,... | collective-permute-start | bytes 1179656 | tf_op jit(solution)/shard_map/ppermute | solution.py:23

commit v11 on v10

--- a/solution.py
+++ b/solution.py
@@ -213,20 +213,24 @@
     )(me, *[in_hbm(x) for x in inputs])
 
 
-def mix_kernel(even_ref, odd_ref, *outs):
-    rows = even_ref.shape[1]
+def mix_kernel(region, even_ref, odd_ref, *refs):
+    outs, tmp_ref = refs[:-1], refs[-1]
     for i, out_ref in enumerate(outs):
-        out_ref[:rows] = even_ref[i]
-        out_ref[rows:] = odd_ref[i]
-
-
-def mix_pairs(even, odd):
-    n, rows, width = even.shape
-    return pl.pallas_call(
-        mix_kernel,
-        out_shape=(jax.ShapeDtypeStruct((2 * rows, width), jnp.bfloat16),) * n,
+        tmp_ref[:region] = even_ref[i].astype(jnp.float32)[:region]
+        tmp_ref[region : 2 * region] = odd_ref[i].astype(jnp.float32)[:region]
+        tmp_ref[2 * region :] = jnp.zeros((tmp_ref.shape[0] - 2 * region, tmp_ref.shape[1]), jnp.float32)
+        out_ref[...] = tmp_ref[...].astype(jnp.bfloat16)
+
+
+def mix_pairs(even, odd, region):
+    n, _, width = even.shape
+    rows = round_up(2 * region, 8)
+    return pl.pallas_call(
+        functools.partial(mix_kernel, region),
+        out_shape=(jax.ShapeDtypeStruct((rows, width), jnp.bfloat16),) * n,
         in_specs=vmem_specs(2),
         out_specs=tuple(vmem_specs(n)),
+        scratch_shapes=[pltpu.VMEM((rows, width), jnp.float32)],
         compiler_params=params(4),
         cost_estimate=TINY,
     )(even, odd)
@@ -236,11 +240,8 @@
     recs, (out_ref, tmp_ref) = refs[:-2], refs[-2:]
     done = 0
     for rec_ref in recs:
-        rows = rec_ref.shape[0] // 2
-        pair = rec_ref[...].astype(jnp.float32)
-        for first in (0, rows):
-            tmp_ref[done : done + region] = pair[first : first + region]
-            done += region
+        tmp_ref[done : done + 2 * region] = rec_ref[...].astype(jnp.float32)[: 2 * region]
+        done += 2 * region
     rest = tmp_ref.shape[0] - done
     tmp_ref[done:] = jnp.zeros((rest, tmp_ref.shape[1]), jnp.float32)
     picked = jnp.dot(sel_ref[...], tmp_ref[...].astype(jnp.bfloat16), preferred_element_type=jnp.float32)
@@ -662,8 +663,11 @@
     )
     blocks = near_blocks(ctext, n_ten)
 
-    pairs = mix_pairs(even, swap(odd, 1, "req"))
+    pairs = mix_pairs(even, swap(odd, 1, "req"), region)
     received = [pairs[0]] + [swap(pairs[i], 2 * i, "req") for i in range(1, n_req // 2)]
+    table, pairs = lax.optimization_barrier((table, pairs))
+    text_at, img_at, text_row = placement(table, region, length, n_text, n_img)
+    received, text_at = lax.optimization_barrier((received, text_at))
     img_own = pack_images(received, vis_row, rtext, sel, region)
     img_blocks = [img_own] + [swap(img_own, s) for s in range(1, n_ten)]
     own, img_own = lax.optimization_barrier((ctext, img_own))
@@ -673,9 +677,7 @@
 
     near = [blocks[s] for s in near_at]
     acc, ss = near_part(near_at, ten_at, near, gains, held, acc, ss)
-    table, acc = lax.optimization_barrier((table, acc))
-    text_at, img_at, text_row = placement(table, region, length, n_text, n_img)
-    img_blocks, text_at = lax.optimization_barrier((img_blocks, text_at))
+    img_blocks, acc = lax.optimization_barrier((img_blocks, acc))
     img_qkv, merged, w_out = image_part(ten_at, img_blocks, gains, sel, held, w_out, n_rows)
 
     shared = (gains, held, acc, ss, img_qkv, text_at, img_at, key_ok, w_out)

time: 66.1 us -> 65.9 us (level)
  waiting for transfers between devices: 22.2 us -> 21.5 us
    ppermute x19, waiting for transfers between devices: 22.2 us -> 21.5 us  [swap(): return lax.ppermute(x, axis, [(i, i ^ s) for i in range(n)])]
  transfers between devices with their start and end apart: 19 -> 19, of which waited for: 10 -> 9; matrix products, arithmetic and copies ran while one was open for 1% -> 1% of each run, Pallas kernels for 26% -> 26%
where the time goes in v11:
time: 65.9 us; the launch traced here: 65.8 us
  starting transfers between devices  22.8 us (35%)
  waiting for transfers between devices  21.5 us (33%)
  Pallas kernels  20.6 us (31%)
    ppermute x19, starting transfers between devices, swap(): return lax.ppermute(x, axis, [(i, i ^ s) for i in range(n)])  22.8 us
    ppermute x19, waiting for transfers between devices, swap(): return lax.ppermute(x, axis, [(i, i ^ s) for i in range(n)])  21.5 us
    pallas_call x1, Pallas kernels, own_part(): pl.pallas_call(own_kernel, out_shape=(jax.ShapeDtypeStruct((3, rows, cols...  4.75 us
    pallas_call x1, Pallas kernels, prepare(): pl.pallas_call(functools.partial(prep_kernel, n_req), out_shape=tuple((ja...  2.72 us
    pallas_call x1, Pallas kernels, image_part(): pl.pallas_call(functools.partial(image_kernel, n_rows, len(blocks)), out_...  2.69 us
    pallas_call x1, Pallas kernels, near_part(): pl.pallas_call(functools.partial(near_kernel, near, pieces), out_shape=(j...  2.41 us
    pallas_call x1, Pallas kernels, tail_part(): pl.pallas_call(functools.partial(tail_kernel, far), out_shape=(jax.ShapeD...  2.31 us
    pallas_call x3, Pallas kernels, out_part(): pl.pallas_call(functools.partial(out_kernel, away), out_shape=(jax.ShapeD...  1.8 us
  transfers between devices with their start and end apart: 19, of which 9 were waited for; matrix products, arithmetic and copies ran while one was open for 1% of the time, Pallas kernels for 26%

profile of v11, /device:TPU:0, one launch (start us, length us, event | category | flops | bytes accessed | tf_op | source)
XLA Modules:
  0.0 65.8 jit_solution(4047687882757938008)
XLA Ops:
  0.0 2.7 %shard_map.91 = (bf16[4,16,1024]{2,1,0:T(8,128)(2,1)S(1)}, bf16[4,16,1024]{2,1,0:T(8,128)(2,1)S(1)}, bf16[312,1024]{1,0:T(8,128)(2,1)S(1)}, bf16[80,1024]{1,0:T(...) custom-call(s32[1]{0:T(128)} %bitcast.me_ref, ...), custom_call_target="tpu_custom_call" | custom-call | tf_op jit(solution)/shard_map/pallas_call | solution.py:203
  2.7 3.0 %collective-permute-start.7 = (bf16[312,1024]{1,0:T(8,128)(2,1)S(1)}, bf16[312,1024]{1,0:T(8,128)(2,1)S(1)}, u32[]{:S(2)}, u32[]{:S(2)}) collective-permute-start(bf16[312,1024]{1,0:T(8,128)(2,1)S(1)} %get-tuple-element.81.x_ref), channel_id=1, source_target_pairs={{0,1},{1,0},{2,3},{3,2},{4,5},{5,4},{6,7},{7,6},{8,9},{9,8},{10,11... | collective-permute-start | bytes 1916936 | tf_op jit(solution)/shard_map/ppermute | solution.py:23
  5.7 1.5 %collective-permute-start.8 = (bf16[312,1024]{1,0:T(8,128)(2,1)S(1)}, bf16[312,1024]{1,0:T(8,128)(2,1)S(1)}, u32[]{:S(2)}, u32[]{:S(2)}) collective-permute-start(bf16[312,1024]{1,0:T(8,128)(2,1)S(1)} %get-tuple-element.81.x_ref), channel_id=1, source_target_pairs={{0,2},{1,3},{2,0},{3,1},{4,6},{5,7},{6,4},{7,5},{8,10},{9,11},{10,... | collective-permute-start | bytes 1916936 | tf_op jit(solution)/shard_map/ppermute | solution.py:23
  7.2 0.0 collective-permute-start
  7.3 1.3 %collective-permute-done.odd_ref = bf16[4,16,1024]{2,1,0:T(8,128)(2,1)S(1)} collective-permute-done((bf16[4,16,1024]{2,1,0:T(8,128)(2,1)S(1)}, bf16[4,16,1024]{2,1,0:T(8,128)(2,1)S(1)}, u32[]{:S(2)}, u32[]{:S(2)}) %collective-permute-start) | collective-permute-done | bytes 131104 | tf_op jit(solution)/shard_map/ppermute | solution.py:23
  8.6 0.1 shard_map.92
  8.7 1.6 %collective-permute-start.1 = (bf16[24,1024]{1,0:T(8,128)(2,1)S(1)}, bf16[24,1024]{1,0:T(8,128)(2,1)S(1)}, u32[]{:S(2)}, u32[]{:S(2)}) collective-permute-start(bf16[24,1024]{1,0:T(8,128)(2,1)S(1)} %get-tuple-element.65), channel_id=1, source_target_pairs={{0,8},{4,12},{8,0},{12,4},{16,24},{20,28},{24,16},{28,20},{1,9},{5... | collective-permute-start | bytes 147464 | tf_op jit(solution)/shard_map/ppermute | solution.py:23
  10.3 2.6 %collective-permute-start.2 = (bf16[24,1024]{1,0:T(8,128)(2,1)S(1)}, bf16[24,1024]{1,0:T(8,128)(2,1)S(1)}, u32[]{:S(2)}, u32[]{:S(2)}) collective-permute-start(bf16[24,1024]{1,0:T(8,128)(2,1)S(1)} %get-tuple-element.66), channel_id=1, source_target_pairs={{0,16},{4,20},{8,24},{12,28},{16,0},{20,4},{24,8},{28,12},{1,17},{... | collective-permute-start | bytes 147464 | tf_op jit(solution)/shard_map/ppermute | solution.py:23
  12.9 0.2 collective-permute-start.3
  13.1 0.7 %shard_map.93 = (bf16[384,312]{1,0:T(8,128)(2,1)S(1)}, bf16[384,80]{1,0:T(8,128)(2,1)S(1)}, f32[384,128]{1,0:T(8,128)S(1)}) custom-call(s32[8,128]{1,0:T(8,128)S(1)} %get-tuple-element.68.table_ref), custom_call_target="tpu_custom_call" | custom-call | tf_op jit(solution)/shard_map/pallas_call | solution.py:283
  13.8 0.0 collective-permute-done.1.refs_1_
  13.8 2.4 %collective-permute-done.2.refs_2_ = bf16[24,1024]{1,0:T(8,128)(2,1)S(1)} collective-permute-done((bf16[24,1024]{1,0:T(8,128)(2,1)S(1)}, bf16[24,1024]{1,0:T(8,128)(2,1)S(1)}, u32[]{:S(2)}, u32[]{:S(2)}) %collective-permute-start.2) | collective-permute-done | bytes 49184 | tf_op jit(solution)/shard_map/ppermute | solution.py:23
  16.2 2.6 %collective-permute-done.3.refs_3_ = bf16[24,1024]{1,0:T(8,128)(2,1)S(1)} collective-permute-done((bf16[24,1024]{1,0:T(8,128)(2,1)S(1)}, bf16[24,1024]{1,0:T(8,128)(2,1)S(1)}, u32[]{:S(2)}, u32[]{:S(2)}) %collective-permute-start.3) | collective-permute-done | bytes 49184 | tf_op jit(solution)/shard_map/ppermute | solution.py:23
  18.8 0.2 shard_map.94.refs_0_
  19.0 0.6 collective-permute-start.4
  19.6 0.5 collective-permute-start.5
  20.1 2.4 %collective-permute-start.6 = (bf16[80,1024]{1,0:T(8,128)(2,1)S(1)}, bf16[80,1024]{1,0:T(8,128)(2,1)S(1)}, u32[]{:S(2)}, u32[]{:S(2)}) collective-permute-start(bf16[80,1024]{1,0:T(8,128)(2,1)S(1)} %shard_map.94.refs_0_), channel_id=1, source_target_pairs={{0,3},{1,2},{2,1},{3,0},{4,7},{5,6},{6,5},{7,4},{8,11},{9,10},{10,... | collective-permute-start | bytes 491528 | tf_op jit(solution)/shard_map/ppermute | solution.py:23
  22.5 4.7 %shard_map.95 = (f32[3,312,512]{2,1,0:T(8,128)S(1)}, f32[312,128]{1,0:T(8,128)S(1)}, bf16[4,3,1024,512]{3,2,1,0:T(8,128)(2,1)S(1)}) custom-call(s32[1]{0:T(128)} %bitcast.5.me_ref, bf16[312,1024]{1,0:T(8,128)(2,1)S(1)} %get-tuple-element.81.x_ref, f32[4,1,1024]{2,1,0:T(1,128)S(1)} %get-tuple-element.80.gain_ref.refs_2_.refs_4_, bf16[3,4096,512]{2,1,0:T(8,128)(2,1)} %bitcast.9), custom_call_target="tpu_custom_call" | custom-call | tf_op jit(solution)/shard_map/pallas_call | solution.py:333
  27.3 0.0 collective-permute-done.7.refs_0_
  27.3 0.0 collective-permute-done.8.refs_1_
  27.3 0.6 collective-permute-start.9
  28.0 0.6 collective-permute-start.12
  28.5 2.4 %shard_map.96 = (f32[3,312,512]{2,1,0:T(8,128)S(1)}, f32[312,128]{1,0:T(8,128)S(1)}) custom-call(s32[1]{0:T(128)} %bitcast.5.me_ref, bf16[312,1024]{1,0:T(8,128)(2,1)S(1)} %collective-permute-done.7.refs_0_, bf16[312,1024]{1,0:T(8,128)(2,1)S(1)} %collective-permute-done.8.refs_1_, f32[4,1,1024]{2,1,0:T(1,128)S(1)} %get-tuple-element.80.gain_ref.refs_2_.refs_4_, ...), custom_call_target="tpu_custom_call" | custom-call | flops 99999997952 | tf_op jit(solution)/shard_map/pallas_call | solution.py:377
  31.0 0.0 collective-permute-done.4.refs_1_
  31.0 0.0 collective-permute-done.5.refs_2_
  31.0 0.0 collective-permute-done.6.refs_3_
  31.0 2.7 %shard_map.97 = (bf16[3,80,512]{2,1,0:T(8,128)(2,1)S(1)}, bf16[80,1024]{1,0:T(8,128)(2,1)S(1)}, bf16[512,4096]{1,0:T(8,128)(2,1)S(1)}) custom-call(s32[1]{0:T(128)} %bitcast.5.me_ref, bf16[80,1024]{1,0:T(8,128)(2,1)S(1)} %shard_map.94.refs_0_, bf16[80,1024]{1,0:T(8,128)(2,1)S(1)} %collective-permute-done.4.refs_1_, ...), custom_call_target="tpu_custom_call" | custom-call | tf_op jit(solution)/shard_map/pallas_call | solution.py:423
  33.7 1.0 %collective-permute-done.9.top_ref = bf16[160,1024]{1,0:T(8,128)(2,1)S(1)} collective-permute-done((bf16[160,1024]{1,0:T(8,128)(2,1)S(1)}, bf16[160,1024]{1,0:T(8,128)(2,1)S(1)}, u32[]{:S(2)}, u32[]{:S(2)}) %collective-permute-start.9) | collective-permute-done | bytes 327712 | tf_op jit(solution)/shard_map/ppermute | solution.py:23
  34.6 1.7 %shard_map.98 = (bf16[3,160,512]{2,1,0:T(8,128)(2,1)S(1)}, bf16[3,160,512]{2,1,0:T(8,128)(2,1)S(1)}, bf16[160,512]{1,0:T(8,128)(2,1)S(1)}, bf16[160,512]{1,0:T(8,128)(2,1)S(1)}, bf16[160,512]{1,0:T(8,128)(2,1)S(1)}) custom-call(s32[1]{0:T(128)} %bitcast.5.me_ref, bf16[160,1024]{1,0:T(8,128)(2,1)S(1)} %collective-permute-done.9.top_ref, ...), custom_call_target="tpu_custom_call" | custom-call | tf_op jit(solution)/shard_map/pallas_call | solution.py:502
  36.4 1.4 %collective-permute-start.10 = (bf16[160,512]{1,0:T(8,128)(2,1)S(1)}, bf16[160,512]{1,0:T(8,128)(2,1)S(1)}, u32[]{:S(2)}, u32[]{:S(2)}) collective-permute-start(bf16[160,512]{1,0:T(8,128)(2,1)S(1)} %get-tuple-element.98), channel_id=1, source_target_pairs={{0,1},{1,0},{2,3},{3,2},{4,5},{5,4},{6,7},{7,6},{8,9},{9,8},{10,11... | collective-permute-start | bytes 491528 | tf_op jit(solution)/shard_map/ppermute | solution.py:23
  37.7 1.5 %collective-permute-start.11 = (bf16[160,512]{1,0:T(8,128)(2,1)S(1)}, bf16[160,512]{1,0:T(8,128)(2,1)S(1)}, u32[]{:S(2)}, u32[]{:S(2)}) collective-permute-start(bf16[160,512]{1,0:T(8,128)(2,1)S(1)} %get-tuple-element.99), channel_id=1, source_target_pairs={{0,2},{1,3},{2,0},{3,1},{4,6},{5,7},{6,4},{7,5},{8,10},{9,11},{10,... | collective-permute-start | bytes 491528 | tf_op jit(solution)/shard_map/ppermute | solution.py:23
  39.2 0.0 collective-permute-done.12.bottom_ref
  39.2 2.3 %shard_map.99 = (bf16[224,512]{1,0:T(8,128)(2,1)S(1)}, bf16[224,512]{1,0:T(8,128)(2,1)S(1)}, bf16[224,512]{1,0:T(8,128)(2,1)S(1)}) custom-call(s32[1]{0:T(128)} %bitcast.5.me_ref, bf16[152,1024]{1,0:T(8,128)(2,1)S(1)} %collective-permute-done.12.bottom_ref, f32[4,1,1024]{2,1,0:T(1,128)S(1)} %get-tuple-element.80.gain_ref.refs_2_.refs_4_, ...), custom_call_target="tpu_custom_call" | custom-call | flops 10000000000 | tf_op jit(solution)/shard_map/pallas_call | solution.py:541
  41.5 0.6 collective-permute-start.17
  42.1 0.7 %collective-permute-start.15 = (bf16[224,512]{1,0:T(8,128)(2,1)S(1)}, bf16[224,512]{1,0:T(8,128)(2,1)S(1)}, u32[]{:S(2)}, u32[]{:S(2)}) collective-permute-start(bf16[224,512]{1,0:T(8,128)(2,1)S(1)} %get-tuple-element.113), channel_id=1, source_target_pairs={{0,1},{1,0},{2,3},{3,2},{4,5},{5,4},{6,7},{7,6},{8,9},{9,8},{10,11... | collective-permute-start | bytes 688136 | tf_op jit(solution)/shard_map/ppermute | solution.py:23
  42.9 0.0 collective-permute-done.10
  42.9 1.2 %collective-permute-done.11 = bf16[160,512]{1,0:T(8,128)(2,1)S(1)} collective-permute-done((bf16[160,512]{1,0:T(8,128)(2,1)S(1)}, bf16[160,512]{1,0:T(8,128)(2,1)S(1)}, u32[]{:S(2)}, u32[]{:S(2)}) %collective-permute-start.11) | collective-permute-done | bytes 163872 | tf_op jit(solution)/shard_map/ppermute | solution.py:23
  44.0 0.6 shard_map.102
  44.6 2.2 %collective-permute-start.14 = (bf16[384,512]{1,0:T(8,128)(2,1)S(1)}, bf16[384,512]{1,0:T(8,128)(2,1)S(1)}, u32[]{:S(2)}, u32[]{:S(2)}) collective-permute-start(bf16[384,512]{1,0:T(8,128)(2,1)S(1)} %get-tuple-element.110), channel_id=1, source_target_pairs={{0,2},{1,3},{2,0},{3,1},{4,6},{5,7},{6,4},{7,5},{8,10},{9,11},{10,... | collective-permute-start | bytes 1179656 | tf_op jit(solution)/shard_map/ppermute | solution.py:23
  46.9 0.6 shard_map.101
  47.5 0.0 copy-start
  47.5 0.7 %collective-permute-start.13 = (bf16[384,512]{1,0:T(8,128)(2,1)S(1)}, bf16[384,512]{1,0:T(8,128)(2,1)S(1)}, u32[]{:S(2)}, u32[]{:S(2)}) collective-permute-start(bf16[384,512]{1,0:T(8,128)(2,1)S(1)} %get-tuple-element.108), channel_id=1, source_target_pairs={{0,1},{1,0},{2,3},{3,2},{4,5},{5,4},{6,7},{7,6},{8,9},{9,8},{10,11... | collective-permute-start | bytes 1179656 | tf_op jit(solution)/shard_map/ppermute | solution.py:23
  48.2 2.0 %collective-permute-done.17 = bf16[224,512]{1,0:T(8,128)(2,1)S(1)} collective-permute-done((bf16[224,512]{1,0:T(8,128)(2,1)S(1)}, bf16[224,512]{1,0:T(8,128)(2,1)S(1)}, u32[]{:S(2)}, u32[]{:S(2)}) %collective-permute-start.17) | collective-permute-done | bytes 229408 | tf_op jit(solution)/shard_map/ppermute | solution.py:23
  50.1 0.1 add_convert_fusion.1
  50.2 0.6 collective-permute-start.18
  50.9 0.0 collective-permute-done.15
  50.9 0.1 add_convert_fusion.2
  51.0 1.4 %collective-permute-start.16 = (bf16[384,512]{1,0:T(8,128)(2,1)S(1)}, bf16[384,512]{1,0:T(8,128)(2,1)S(1)}, u32[]{:S(2)}, u32[]{:S(2)}) collective-permute-start(bf16[384,512]{1,0:T(8,128)(2,1)S(1)} %add_convert_fusion.2), channel_id=1, source_target_pairs={{0,2},{1,3},{2,0},{3,1},{4,6},{5,7},{6,4},{7,5},{8,10},{9,11},{10,... | collective-permute-start | bytes 1179656 | tf_op jit(solution)/shard_map/ppermute | solution.py:23
  52.3 0.1 slice_reduce_fusion
  52.5 0.0 copy-done
  52.5 0.4 add_convert_fusion.base_ref
  52.9 0.6 shard_map.100
  53.5 5.1 %collective-permute-done.14.refs_3_ = bf16[384,512]{1,0:T(8,128)(2,1)S(1)} collective-permute-done((bf16[384,512]{1,0:T(8,128)(2,1)S(1)}, bf16[384,512]{1,0:T(8,128)(2,1)S(1)}, u32[]{:S(2)}, u32[]{:S(2)}) %collective-permute-start.14) | collective-permute-done | bytes 393248 | tf_op jit(solution)/shard_map/ppermute | solution.py:23
  58.6 1.0 %collective-permute-done.13.refs_1_ = bf16[384,512]{1,0:T(8,128)(2,1)S(1)} collective-permute-done((bf16[384,512]{1,0:T(8,128)(2,1)S(1)}, bf16[384,512]{1,0:T(8,128)(2,1)S(1)}, u32[]{:S(2)}, u32[]{:S(2)}) %collective-permute-start.13) | collective-permute-done | bytes 393248 | tf_op jit(solution)/shard_map/ppermute | solution.py:23
  59.6 0.3 shard_map.103.base_ref
  59.9 4.9 %collective-permute-done.18.refs_1_ = bf16[384,512]{1,0:T(8,128)(2,1)S(1)} collective-permute-done((bf16[384,512]{1,0:T(8,128)(2,1)S(1)}, bf16[384,512]{1,0:T(8,128)(2,1)S(1)}, u32[]{:S(2)}, u32[]{:S(2)}) %collective-permute-start.18) | collective-permute-done | bytes 393248 | tf_op jit(solution)/shard_map/ppermute | solution.py:23
  64.8 0.0 collective-permute-done.16.refs_0_
  64.8 1.0 %shard_map.104 = bf16[384,1024]{1,0:T(8,128)(2,1)} custom-call(f32[384,1024]{1,0:T(8,128)S(1)} %shard_map.103.base_ref, bf16[384,512]{1,0:T(8,128)(2,1)S(1)} %collective-permute-done.16.refs_0_, bf16[384,512]{1,0:T(8,128)(2,1)S(1)} %collective-permute-done.18.refs_1_), custom_call_target="tpu_custom_call" | custom-call | tf_op jit(solution)/shard_map/pallas_call | solution.py:614
  (2 shorter events, 0.0 us)
Async XLA Ops:
  2.7 24.6 %collective-permute-start.7 = (bf16[312,1024]{1,0:T(8,128)(2,1)S(1)}, bf16[312,1024]{1,0:T(8,128)(2,1)S(1)}, u32[]{:S(2)}, u32[]{:S(2)}) collective-permute-start(bf16[312,1024]{1,0:T(8,128)(2,1)S(1)} %get-tuple-element.81.x_ref), channel_id=1, source_target_pairs={{0,1},{1,0},{2,3},{3,2},{4,5},{5,4},{6,7},{7,6},{8,9},{9,8},{10,11... | collective-permute-start | bytes 1916936 | tf_op jit(solution)/shard_map/ppermute | solution.py:23
  5.7 21.6 %collective-permute-start.8 = (bf16[312,1024]{1,0:T(8,128)(2,1)S(1)}, bf16[312,1024]{1,0:T(8,128)(2,1)S(1)}, u32[]{:S(2)}, u32[]{:S(2)}) collective-permute-start(bf16[312,1024]{1,0:T(8,128)(2,1)S(1)} %get-tuple-element.81.x_ref), channel_id=1, source_target_pairs={{0,2},{1,3},{2,0},{3,1},{4,6},{5,7},{6,4},{7,5},{8,10},{9,11},{10,... | collective-permute-start | bytes 1916936 | tf_op jit(solution)/shard_map/ppermute | solution.py:23
  7.2 1.3 %collective-permute-start = (bf16[4,16,1024]{2,1,0:T(8,128)(2,1)S(1)}, bf16[4,16,1024]{2,1,0:T(8,128)(2,1)S(1)}, u32[]{:S(2)}, u32[]{:S(2)}) collective-permute-start(bf16[4,16,1024]{2,1,0:T(8,128)(2,1)S(1)} %get-tuple-element.63), channel_id=1, source_target_pairs={{0,4},{4,0},{8,12},{12,8},{16,20},{20,16},{24,28},{28,24},{1,5},{5... | collective-permute-start | bytes 393224 | tf_op jit(solution)/shard_map/ppermute | solution.py:23
  8.7 5.2 %collective-permute-start.1 = (bf16[24,1024]{1,0:T(8,128)(2,1)S(1)}, bf16[24,1024]{1,0:T(8,128)(2,1)S(1)}, u32[]{:S(2)}, u32[]{:S(2)}) collective-permute-start(bf16[24,1024]{1,0:T(8,128)(2,1)S(1)} %get-tuple-element.65), channel_id=1, source_target_pairs={{0,8},{4,12},{8,0},{12,4},{16,24},{20,28},{24,16},{28,20},{1,9},{5... | collective-permute-start | bytes 147464 | tf_op jit(solution)/shard_map/ppermute | solution.py:23
  10.3 5.9 %collective-permute-start.2 = (bf16[24,1024]{1,0:T(8,128)(2,1)S(1)}, bf16[24,1024]{1,0:T(8,128)(2,1)S(1)}, u32[]{:S(2)}, u32[]{:S(2)}) collective-permute-start(bf16[24,1024]{1,0:T(8,128)(2,1)S(1)} %get-tuple-element.66), channel_id=1, source_target_pairs={{0,16},{4,20},{8,24},{12,28},{16,0},{20,4},{24,8},{28,12},{1,17},{... | collective-permute-start | bytes 147464 | tf_op jit(solution)/shard_map/ppermute | solution.py:23
  12.9 5.9 %collective-permute-start.3 = (bf16[24,1024]{1,0:T(8,128)(2,1)S(1)}, bf16[24,1024]{1,0:T(8,128)(2,1)S(1)}, u32[]{:S(2)}, u32[]{:S(2)}) collective-permute-start(bf16[24,1024]{1,0:T(8,128)(2,1)S(1)} %get-tuple-element.67), channel_id=1, source_target_pairs={{0,24},{4,28},{8,16},{12,20},{16,8},{20,12},{24,0},{28,4},{1,25},{... | collective-permute-start | bytes 147464 | tf_op jit(solution)/shard_map/ppermute | solution.py:23
  19.0 12.0 %collective-permute-start.4 = (bf16[80,1024]{1,0:T(8,128)(2,1)S(1)}, bf16[80,1024]{1,0:T(8,128)(2,1)S(1)}, u32[]{:S(2)}, u32[]{:S(2)}) collective-permute-start(bf16[80,1024]{1,0:T(8,128)(2,1)S(1)} %shard_map.94.refs_0_), channel_id=1, source_target_pairs={{0,1},{1,0},{2,3},{3,2},{4,5},{5,4},{6,7},{7,6},{8,9},{9,8},{10,11... | collective-permute-start | bytes 491528 | tf_op jit(solution)/shard_map/ppermute | solution.py:23
  19.6 11.4 %collective-permute-start.5 = (bf16[80,1024]{1,0:T(8,128)(2,1)S(1)}, bf16[80,1024]{1,0:T(8,128)(2,1)S(1)}, u32[]{:S(2)}, u32[]{:S(2)}) collective-permute-start(bf16[80,1024]{1,0:T(8,128)(2,1)S(1)} %shard_map.94.refs_0_), channel_id=1, source_target_pairs={{0,2},{1,3},{2,0},{3,1},{4,6},{5,7},{6,4},{7,5},{8,10},{9,11},{10,... | collective-permute-start | bytes 491528 | tf_op jit(solution)/shard_map/ppermute | solution.py:23
  20.1 10.9 %collective-permute-start.6 = (bf16[80,1024]{1,0:T(8,128)(2,1)S(1)}, bf16[80,1024]{1,0:T(8,128)(2,1)S(1)}, u32[]{:S(2)}, u32[]{:S(2)}) collective-permute-start(bf16[80,1024]{1,0:T(8,128)(2,1)S(1)} %shard_map.94.refs_0_), channel_id=1, source_target_pairs={{0,3},{1,2},{2,1},{3,0},{4,7},{5,6},{6,5},{7,4},{8,11},{9,10},{10,... | collective-permute-start | bytes 491528 | tf_op jit(solution)/shard_map/ppermute | solution.py:23
  27.3 7.3 %collective-permute-start.9 = (bf16[160,1024]{1,0:T(8,128)(2,1)S(1)}, bf16[160,1024]{1,0:T(8,128)(2,1)S(1)}, u32[]{:S(2)}, u32[]{:S(2)}) collective-permute-start(bf16[160,1024]{1,0:T(8,128)(2,1)S(1)} %slice.10), channel_id=1, source_target_pairs={{0,1},{1,0},{2,3},{3,2},{4,5},{5,4},{6,7},{7,6},{8,9},{9,8},{10,11... | collective-permute-start | bytes 983048 | tf_op jit(solution)/shard_map/ppermute | solution.py:23
  28.0 11.3 %collective-permute-start.12 = (bf16[152,1024]{1,0:T(8,128)(2,1)S(1)}, bf16[152,1024]{1,0:T(8,128)(2,1)S(1)}, u32[]{:S(2)}, u32[]{:S(2)}) collective-permute-start(bf16[152,1024]{1,0:T(8,128)(2,1)S(1)} %slice.11), channel_id=1, source_target_pairs={{0,2},{1,3},{2,0},{3,1},{4,6},{5,7},{6,4},{7,5},{8,10},{9,11},{10,... | collective-permute-start | bytes 933896 | tf_op jit(solution)/shard_map/ppermute | solution.py:23
  36.4 6.5 %collective-permute-start.10 = (bf16[160,512]{1,0:T(8,128)(2,1)S(1)}, bf16[160,512]{1,0:T(8,128)(2,1)S(1)}, u32[]{:S(2)}, u32[]{:S(2)}) collective-permute-start(bf16[160,512]{1,0:T(8,128)(2,1)S(1)} %get-tuple-element.98), channel_id=1, source_target_pairs={{0,1},{1,0},{2,3},{3,2},{4,5},{5,4},{6,7},{7,6},{8,9},{9,8},{10,11... | collective-permute-start | bytes 491528 | tf_op jit(solution)/shard_map/ppermute | solution.py:23
  37.7 6.3 %collective-permute-start.11 = (bf16[160,512]{1,0:T(8,128)(2,1)S(1)}, bf16[160,512]{1,0:T(8,128)(2,1)S(1)}, u32[]{:S(2)}, u32[]{:S(2)}) collective-permute-start(bf16[160,512]{1,0:T(8,128)(2,1)S(1)} %get-tuple-element.99), channel_id=1, source_target_pairs={{0,2},{1,3},{2,0},{3,1},{4,6},{5,7},{6,4},{7,5},{8,10},{9,11},{10,... | collective-permute-start | bytes 491528 | tf_op jit(solution)/shard_map/ppermute | solution.py:23
  41.5 8.6 %collective-permute-start.17 = (bf16[224,512]{1,0:T(8,128)(2,1)S(1)}, bf16[224,512]{1,0:T(8,128)(2,1)S(1)}, u32[]{:S(2)}, u32[]{:S(2)}) collective-permute-start(bf16[224,512]{1,0:T(8,128)(2,1)S(1)} %get-tuple-element.116), channel_id=1, source_target_pairs={{0,2},{1,3},{2,0},{3,1},{4,6},{5,7},{6,4},{7,5},{8,10},{9,11},{10,... | collective-permute-start | bytes 688136 | tf_op jit(solution)/shard_map/ppermute | solution.py:23
  42.1 8.7 %collective-permute-start.15 = (bf16[224,512]{1,0:T(8,128)(2,1)S(1)}, bf16[224,512]{1,0:T(8,128)(2,1)S(1)}, u32[]{:S(2)}, u32[]{:S(2)}) collective-permute-start(bf16[224,512]{1,0:T(8,128)(2,1)S(1)} %get-tuple-element.113), channel_id=1, source_target_pairs={{0,1},{1,0},{2,3},{3,2},{4,5},{5,4},{6,7},{7,6},{8,9},{9,8},{10,11... | collective-permute-start | bytes 688136 | tf_op jit(solution)/shard_map/ppermute | solution.py:23
  44.6 13.9 %collective-permute-start.14 = (bf16[384,512]{1,0:T(8,128)(2,1)S(1)}, bf16[384,512]{1,0:T(8,128)(2,1)S(1)}, u32[]{:S(2)}, u32[]{:S(2)}) collective-permute-start(bf16[384,512]{1,0:T(8,128)(2,1)S(1)} %get-tuple-element.110), channel_id=1, source_target_pairs={{0,2},{1,3},{2,0},{3,1},{4,6},{5,7},{6,4},{7,5},{8,10},{9,11},{10,... | collective-permute-start | bytes 1179656 | tf_op jit(solution)/shard_map/ppermute | solution.py:23
  47.5 5.0 %copy-start = (bf16[384,1024]{1,0:T(8,128)(2,1)S(1)}, bf16[384,1024]{1,0:T(8,128)(2,1)}, u32[]{:S(2)}) copy-start(bf16[384,1024]{1,0:T(8,128)(2,1)} %text_hbm.1) | copy-start | bytes 2359300
  47.5 12.1 %collective-permute-start.13 = (bf16[384,512]{1,0:T(8,128)(2,1)S(1)}, bf16[384,512]{1,0:T(8,128)(2,1)S(1)}, u32[]{:S(2)}, u32[]{:S(2)}) collective-permute-start(bf16[384,512]{1,0:T(8,128)(2,1)S(1)} %get-tuple-element.108), channel_id=1, source_target_pairs={{0,1},{1,0},{2,3},{3,2},{4,5},{5,4},{6,7},{7,6},{8,9},{9,8},{10,11... | collective-permute-start | bytes 1179656 | tf_op jit(solution)/shard_map/ppermute | solution.py:23
  50.2 14.6 %collective-permute-start.18 = (bf16[384,512]{1,0:T(8,128)(2,1)S(1)}, bf16[384,512]{1,0:T(8,128)(2,1)S(1)}, u32[]{:S(2)}, u32[]{:S(2)}) collective-permute-start(bf16[384,512]{1,0:T(8,128)(2,1)S(1)} %add_convert_fusion.1), channel_id=1, source_target_pairs={{0,1},{1,0},{2,3},{3,2},{4,5},{5,4},{6,7},{7,6},{8,9},{9,8},{10,11... | collective-permute-start | bytes 1179656 | tf_op jit(solution)/shard_map/ppermute | solution.py:23
  51.0 13.8 %collective-permute-start.16 = (bf16[384,512]{1,0:T(8,128)(2,1)S(1)}, bf16[384,512]{1,0:T(8,128)(2,1)S(1)}, u32[]{:S(2)}, u32[]{:S(2)}) collective-permute-start(bf16[384,512]{1,0:T(8,128)(2,1)S(1)} %add_convert_fusion.2), channel_id=1, source_target_pairs={{0,2},{1,3},{2,0},{3,1},{4,6},{5,7},{6,4},{7,5},{8,10},{9,11},{10,... | collective-permute-start | bytes 1179656 | tf_op jit(solution)/shard_map/ppermute | solution.py:23

commit v12 on v9

--- a/solution.py
+++ b/solution.py
@@ -404,7 +404,7 @@
 
 
 def image_kernel(n_rows, n_blk, me_ref, *refs):
-    x_refs, refs = refs[:n_blk], refs[n_blk:]
+    x_refs, refs = refs[:n_blk][::-1], refs[n_blk:]
     gain_ref, sel_ref, held_ref, w_out_ref, qkv_ref, own_ref, w_out_held, sem_ref = refs
     copy = pltpu.make_async_copy(w_out_ref, w_out_held, sem_ref)
     copy.start()
@@ -688,7 +688,8 @@
     text_at, img_at, text_row = placement(table, region, length, n_text, n_img)
     received, acc, text_at = lax.optimization_barrier((received, acc, text_at))
     img_own = pack_images(received, vis_row, rtext, sel, region)
-    img_blocks = [img_own] + [swap(img_own, s) for s in range(1, n_ten)]
+    img_far_first = {s: swap(img_own, s) for s in reversed(order)}
+    img_blocks = [img_own] + [img_far_first[s] for s in range(1, n_ten)]
 
     one_bit = sorted(blocks)
     between = [s for s in near_at if s not in one_bit]
@@ -698,7 +699,7 @@
     blocks = far_blocks(blocks, n_ten)
     if between:
         acc, ss = near_part(between, ten_at, [blocks[s] for s in between], gains, held, acc, ss)
-    img_qkv, merged, w_out = image_part(ten_at, img_blocks, gains, sel, held, w_out, n_rows)
+    img_qkv, merged, w_out = image_part(ten_at, img_blocks[::-1], gains, sel, held, w_out, n_rows)
 
     shared = (gains, held, acc, ss, img_qkv, text_at, img_at, key_ok, w_out)
     top_qkv, head_qkv, head_ctx, *head_far = head_part(far, ten_at, blocks[far][0], *shared)

time: 66.5 us -> 66.6 us (level)
  starting transfers between devices: 22.7 us -> 24.6 us
  waiting for transfers between devices: 21.4 us -> 19.6 us
    ppermute x19, starting transfers between devices: 22.7 us -> 24.6 us  [swap(): return lax.ppermute(x, axis, [(i, i ^ s) for i in range(n)])]
    ppermute x19, waiting for transfers between devices: 21.4 us -> 19.6 us  [swap(): return lax.ppermute(x, axis, [(i, i ^ s) for i in range(n)])]
  transfers between devices with their start and end apart: 19 -> 19, of which waited for: 12 -> 11; matrix products, arithmetic and copies ran while one was open for 1% -> 1% of each run, Pallas kernels for 28% -> 28%
where the time goes in v12:
time: 66.6 us; the launch traced here: 66.5 us
  starting transfers between devices  24.6 us (37%)
  Pallas kernels  21.4 us (32%)
  waiting for transfers between devices  19.6 us (29%)
    ppermute x19, starting transfers between devices, swap(): return lax.ppermute(x, axis, [(i, i ^ s) for i in range(n)])  24.6 us
    ppermute x19, waiting for transfers between devices, swap(): return lax.ppermute(x, axis, [(i, i ^ s) for i in range(n)])  19.6 us
    pallas_call x1, Pallas kernels, own_part(): pl.pallas_call(own_kernel, out_shape=(jax.ShapeDtypeStruct((3, rows, cols...  4.86 us
    pallas_call x1, Pallas kernels, image_part(): pl.pallas_call(functools.partial(image_kernel, n_rows, len(blocks)), out_...  2.64 us
    pallas_call x1, Pallas kernels, near_part(): pl.pallas_call(functools.partial(near_kernel, near, pieces), out_shape=(j...  2.28 us
    pallas_call x1, Pallas kernels, tail_part(): pl.pallas_call(functools.partial(tail_kernel, far), out_shape=(jax.ShapeD...  2.27 us
    pallas_call x1, Pallas kernels, prepare(): pl.pallas_call(functools.partial(prep_kernel, n_req), out_shape=tuple((ja...  1.94 us
    pallas_call x3, Pallas kernels, out_part(): pl.pallas_call(functools.partial(out_kernel, away), out_shape=(jax.ShapeD...  1.79 us
  transfers between devices with their start and end apart: 19, of which 11 were waited for; matrix products, arithmetic and copies ran while one was open for 1% of the time, Pallas kernels for 28%

profile of v12, /device:TPU:0, one launch (start us, length us, event | category | flops | bytes accessed | tf_op | source)
XLA Modules:
  0.0 66.5 jit_solution(10125601770634611203)
XLA Ops:
  0.0 1.7 %shard_map.91 = (bf16[320,1024]{1,0:T(8,128)(2,1)S(1)}, bf16[384,1024]{1,0:T(8,128)(2,1)S(1)}, bf16[6,6,8,1024]{3,2,1,0:T(8,128)(2,1)S(1)}, bf16[32,128]{1,0:T(8,128)(2,1)S(1)}, bf16[8,128]{1,0:T(8,128)(2,1)S(1)}) custom-call(s32[1]{0:T(128)} %bitcast.me_ref, s32[64]{0:T(128)} %req_hbm.3, s32[64]{0:T(128)} %start_hbm.3, bf16[384,1024]{1,0:T(8,128)(2,1)} %text_hbm.1, ...), custom_call_target="tpu_custom_call" | custom-call | tf_op jit(solution)/shard_map/pallas_call | solution.py:121
  1.7 3.0 %collective-permute-start.7 = (bf16[320,1024]{1,0:T(8,128)(2,1)S(1)}, bf16[320,1024]{1,0:T(8,128)(2,1)S(1)}, u32[]{:S(2)}, u32[]{:S(2)}) collective-permute-start(bf16[320,1024]{1,0:T(8,128)(2,1)S(1)} %get-tuple-element.82.x_ref), channel_id=1, source_target_pairs={{0,1},{1,0},{2,3},{3,2},{4,5},{5,4},{6,7},{7,6},{8,9},{9,8},{10,11... | collective-permute-start | bytes 1966088 | tf_op jit(solution)/shard_map/ppermute | solution.py:23
  4.7 1.5 %collective-permute-start.8 = (bf16[320,1024]{1,0:T(8,128)(2,1)S(1)}, bf16[320,1024]{1,0:T(8,128)(2,1)S(1)}, u32[]{:S(2)}, u32[]{:S(2)}) collective-permute-start(bf16[320,1024]{1,0:T(8,128)(2,1)S(1)} %get-tuple-element.82.x_ref), channel_id=1, source_target_pairs={{0,2},{1,3},{2,0},{3,1},{4,6},{5,7},{6,4},{7,5},{8,10},{9,11},{10,... | collective-permute-start | bytes 1966088 | tf_op jit(solution)/shard_map/ppermute | solution.py:23
  6.2 1.9 %shard_map.92 = (bf16[4,16,1024]{2,1,0:T(8,128)(2,1)S(1)}, bf16[4,16,1024]{2,1,0:T(8,128)(2,1)S(1)}, bf16[80,1024]{1,0:T(8,128)(2,1)S(1)}, bf16[80,80]{1,0:T(8,1...) custom-call(s32[1]{0:T(128)} %bitcast.me_ref, ...), custom_call_target="tpu_custom_call" | custom-call | tf_op jit(solution)/shard_map/pallas_call | solution.py:212
  8.2 0.1 collective-permute-start
  8.3 1.3 %collective-permute-done.odd_ref = bf16[4,16,1024]{2,1,0:T(8,128)(2,1)S(1)} collective-permute-done((bf16[4,16,1024]{2,1,0:T(8,128)(2,1)S(1)}, bf16[4,16,1024]{2,1,0:T(8,128)(2,1)S(1)}, u32[]{:S(2)}, u32[]{:S(2)}) %collective-permute-start) | collective-permute-done | bytes 131104 | tf_op jit(solution)/shard_map/ppermute | solution.py:23
  9.6 0.1 shard_map.93
  9.7 1.6 %collective-permute-start.1 = (bf16[24,1024]{1,0:T(8,128)(2,1)S(1)}, bf16[24,1024]{1,0:T(8,128)(2,1)S(1)}, u32[]{:S(2)}, u32[]{:S(2)}) collective-permute-start(bf16[24,1024]{1,0:T(8,128)(2,1)S(1)} %get-tuple-element.73), channel_id=1, source_target_pairs={{0,8},{4,12},{8,0},{12,4},{16,24},{20,28},{24,16},{28,20},{1,9},{5... | collective-permute-start | bytes 147464 | tf_op jit(solution)/shard_map/ppermute | solution.py:23
  11.3 2.6 %collective-permute-start.2 = (bf16[24,1024]{1,0:T(8,128)(2,1)S(1)}, bf16[24,1024]{1,0:T(8,128)(2,1)S(1)}, u32[]{:S(2)}, u32[]{:S(2)}) collective-permute-start(bf16[24,1024]{1,0:T(8,128)(2,1)S(1)} %get-tuple-element.74), channel_id=1, source_target_pairs={{0,16},{4,20},{8,24},{12,28},{16,0},{20,4},{24,8},{28,12},{1,17},{... | collective-permute-start | bytes 147464 | tf_op jit(solution)/shard_map/ppermute | solution.py:23
  13.9 0.2 collective-permute-start.3
  14.1 0.7 %shard_map.94 = (bf16[384,320]{1,0:T(8,128)(2,1)S(1)}, bf16[384,80]{1,0:T(8,128)(2,1)S(1)}, f32[384,128]{1,0:T(8,128)S(1)}) custom-call(s32[8,128]{1,0:T(8,128)S(1)} %get-tuple-element.76.table_ref), custom_call_target="tpu_custom_call" | custom-call | tf_op jit(solution)/shard_map/pallas_call | solution.py:297
  14.8 4.9 %shard_map.95 = (f32[3,320,512]{2,1,0:T(8,128)S(1)}, f32[320,128]{1,0:T(8,128)S(1)}, bf16[4,3,1024,512]{3,2,1,0:T(8,128)(2,1)S(1)}) custom-call(s32[1]{0:T(128)} %bitcast.5.me_ref, bf16[320,1024]{1,0:T(8,128)(2,1)S(1)} %get-tuple-element.82.x_ref, f32[4,1,1024]{2,1,0:T(1,128)S(1)} %get-tuple-element.83.gain_ref.refs_4_.refs_2_, bf16[3,4096,512]{2,1,0:T(8,128)(2,1)} %bitcast.9), custom_call_target="tpu_custom_call" | custom-call | tf_op jit(solution)/shard_map/pallas_call | solution.py:348
  19.7 0.0 collective-permute-done.1.refs_1_
  19.7 0.0 collective-permute-done.2.refs_2_
  19.7 0.1 collective-permute-done.3.refs_3_
  19.8 0.2 shard_map.96.refs_3_
  20.0 0.5 collective-permute-start.4
  20.5 1.5 %collective-permute-start.5 = (bf16[80,1024]{1,0:T(8,128)(2,1)S(1)}, bf16[80,1024]{1,0:T(8,128)(2,1)S(1)}, u32[]{:S(2)}, u32[]{:S(2)}) collective-permute-start(bf16[80,1024]{1,0:T(8,128)(2,1)S(1)} %shard_map.96.refs_3_), channel_id=1, source_target_pairs={{0,2},{1,3},{2,0},{3,1},{4,6},{5,7},{6,4},{7,5},{8,10},{9,11},{10,... | collective-permute-start | bytes 491528 | tf_op jit(solution)/shard_map/ppermute | solution.py:23
  22.0 1.5 %collective-permute-start.6 = (bf16[80,1024]{1,0:T(8,128)(2,1)S(1)}, bf16[80,1024]{1,0:T(8,128)(2,1)S(1)}, u32[]{:S(2)}, u32[]{:S(2)}) collective-permute-start(bf16[80,1024]{1,0:T(8,128)(2,1)S(1)} %shard_map.96.refs_3_), channel_id=1, source_target_pairs={{0,1},{1,0},{2,3},{3,2},{4,5},{5,4},{6,7},{7,6},{8,9},{9,8},{10,11... | collective-permute-start | bytes 491528 | tf_op jit(solution)/shard_map/ppermute | solution.py:23
  23.5 0.0 collective-permute-done.7.refs_0_
  23.5 0.0 collective-permute-done.8.refs_1_
  23.5 2.3 %shard_map.98 = (f32[3,320,512]{2,1,0:T(8,128)S(1)}, f32[320,128]{1,0:T(8,128)S(1)}) custom-call(s32[1]{0:T(128)} %bitcast.5.me_ref, bf16[320,1024]{1,0:T(8,128)(2,1)S(1)} %collective-permute-done.7.refs_0_, bf16[320,1024]{1,0:T(8,128)(2,1)S(1)} %collective-permute-done.8.refs_1_, f32[4,1,1024]{2,1,0:T(1,128)S(1)} %get-tuple-element.83.gain_ref.refs_4_.refs_2_, ...), custom_call_target="tpu_custom_call" | custom-call | flops 99999997952 | tf_op jit(solution)/shard_map/pallas_call | solution.py:392
  25.9 0.6 collective-permute-start.9
  26.5 0.6 collective-permute-start.12
  27.0 1.0 %collective-permute-done.4.refs_0_ = bf16[80,1024]{1,0:T(8,128)(2,1)S(1)} collective-permute-done((bf16[80,1024]{1,0:T(8,128)(2,1)S(1)}, bf16[80,1024]{1,0:T(8,128)(2,1)S(1)}, u32[]{:S(2)}, u32[]{:S(2)}) %collective-permute-start.4) | collective-permute-done | bytes 163872 | tf_op jit(solution)/shard_map/ppermute | solution.py:23
  28.1 2.0 %collective-permute-done.5.refs_1_ = bf16[80,1024]{1,0:T(8,128)(2,1)S(1)} collective-permute-done((bf16[80,1024]{1,0:T(8,128)(2,1)S(1)}, bf16[80,1024]{1,0:T(8,128)(2,1)S(1)}, u32[]{:S(2)}, u32[]{:S(2)}) %collective-permute-start.5) | collective-permute-done | bytes 163872 | tf_op jit(solution)/shard_map/ppermute | solution.py:23
  30.0 0.6 collective-permute-done.6.refs_2_
  30.6 2.6 %shard_map.97 = (bf16[3,80,512]{2,1,0:T(8,128)(2,1)S(1)}, bf16[80,1024]{1,0:T(8,128)(2,1)S(1)}, bf16[512,4096]{1,0:T(8,128)(2,1)S(1)}) custom-call(s32[1]{0:T(128)} %bitcast.5.me_ref, bf16[80,1024]{1,0:T(8,128)(2,1)S(1)} %collective-permute-done.4.refs_0_, bf16[80,1024]{1,0:T(8,128)(2,1)S(1)} %collective-permute-done.5.refs_1_, ...), custom_call_target="tpu_custom_call" | custom-call | flops 3000000000 | tf_op jit(solution)/shard_map/pallas_call | solution.py:438
  33.3 2.7 %collective-permute-done.9.top_ref = bf16[160,1024]{1,0:T(8,128)(2,1)S(1)} collective-permute-done((bf16[160,1024]{1,0:T(8,128)(2,1)S(1)}, bf16[160,1024]{1,0:T(8,128)(2,1)S(1)}, u32[]{:S(2)}, u32[]{:S(2)}) %collective-permute-start.9) | collective-permute-done | bytes 327712 | tf_op jit(solution)/shard_map/ppermute | solution.py:23
  35.9 1.7 %shard_map.99 = (bf16[3,160,512]{2,1,0:T(8,128)(2,1)S(1)}, bf16[3,160,512]{2,1,0:T(8,128)(2,1)S(1)}, bf16[160,512]{1,0:T(8,128)(2,1)S(1)}, bf16[160,512]{1,0:T(8,128)(2,1)S(1)}, bf16[160,512]{1,0:T(8,128)(2,1)S(1)}) custom-call(s32[1]{0:T(128)} %bitcast.5.me_ref, bf16[160,1024]{1,0:T(8,128)(2,1)S(1)} %collective-permute-done.9.top_ref, ...), custom_call_target="tpu_custom_call" | custom-call | tf_op jit(solution)/shard_map/pallas_call | solution.py:517
  37.6 0.6 collective-permute-start.10
  38.2 1.5 %collective-permute-start.11 = (bf16[160,512]{1,0:T(8,128)(2,1)S(1)}, bf16[160,512]{1,0:T(8,128)(2,1)S(1)}, u32[]{:S(2)}, u32[]{:S(2)}) collective-permute-start(bf16[160,512]{1,0:T(8,128)(2,1)S(1)} %get-tuple-element.105), channel_id=1, source_target_pairs={{0,2},{1,3},{2,0},{3,1},{4,6},{5,7},{6,4},{7,5},{8,10},{9,11},{10,... | collective-permute-start | bytes 491528 | tf_op jit(solution)/shard_map/ppermute | solution.py:23
  39.8 0.0 collective-permute-done.12.bottom_ref
  39.8 2.3 %shard_map.100 = (bf16[224,512]{1,0:T(8,128)(2,1)S(1)}, bf16[224,512]{1,0:T(8,128)(2,1)S(1)}, bf16[224,512]{1,0:T(8,128)(2,1)S(1)}) custom-call(s32[1]{0:T(128)} %bitcast.5.me_ref, bf16[160,1024]{1,0:T(8,128)(2,1)S(1)} %collective-permute-done.12.bottom_ref, f32[4,1,1024]{2,1,0:T(1,128)S(1)} %get-tuple-element.83.gain_ref.refs_4_.refs_2_, ...), custom_call_target="tpu_custom_call" | custom-call | flops 10000000000 | tf_op jit(solution)/shard_map/pallas_call | solution.py:556
  42.0 0.6 collective-permute-start.17
  42.6 1.5 %collective-permute-start.15 = (bf16[224,512]{1,0:T(8,128)(2,1)S(1)}, bf16[224,512]{1,0:T(8,128)(2,1)S(1)}, u32[]{:S(2)}, u32[]{:S(2)}) collective-permute-start(bf16[224,512]{1,0:T(8,128)(2,1)S(1)} %get-tuple-element.119), channel_id=1, source_target_pairs={{0,1},{1,0},{2,3},{3,2},{4,5},{5,4},{6,7},{7,6},{8,9},{9,8},{10,11... | collective-permute-start | bytes 688136 | tf_op jit(solution)/shard_map/ppermute | solution.py:23
  44.1 0.0 collective-permute-done.10
  44.1 0.5 collective-permute-done.11
  44.6 0.6 shard_map.103
  45.2 2.1 %collective-permute-start.14 = (bf16[384,512]{1,0:T(8,128)(2,1)S(1)}, bf16[384,512]{1,0:T(8,128)(2,1)S(1)}, u32[]{:S(2)}, u32[]{:S(2)}) collective-permute-start(bf16[384,512]{1,0:T(8,128)(2,1)S(1)} %get-tuple-element.116), channel_id=1, source_target_pairs={{0,2},{1,3},{2,0},{3,1},{4,6},{5,7},{6,4},{7,5},{8,10},{9,11},{10,... | collective-permute-start | bytes 1179656 | tf_op jit(solution)/shard_map/ppermute | solution.py:23
  47.3 0.6 shard_map.102
  47.9 0.0 copy-start
  47.9 1.8 %collective-permute-start.13 = (bf16[384,512]{1,0:T(8,128)(2,1)S(1)}, bf16[384,512]{1,0:T(8,128)(2,1)S(1)}, u32[]{:S(2)}, u32[]{:S(2)}) collective-permute-start(bf16[384,512]{1,0:T(8,128)(2,1)S(1)} %get-tuple-element.114), channel_id=1, source_target_pairs={{0,1},{1,0},{2,3},{3,2},{4,5},{5,4},{6,7},{7,6},{8,9},{9,8},{10,11... | collective-permute-start | bytes 1179656 | tf_op jit(solution)/shard_map/ppermute | solution.py:23
  49.7 0.9 %collective-permute-done.17 = bf16[224,512]{1,0:T(8,128)(2,1)S(1)} collective-permute-done((bf16[224,512]{1,0:T(8,128)(2,1)S(1)}, bf16[224,512]{1,0:T(8,128)(2,1)S(1)}, u32[]{:S(2)}, u32[]{:S(2)}) %collective-permute-start.17) | collective-permute-done | bytes 229408 | tf_op jit(solution)/shard_map/ppermute | solution.py:23
  50.7 0.1 add_convert_fusion.1
  50.8 1.6 %collective-permute-start.18 = (bf16[384,512]{1,0:T(8,128)(2,1)S(1)}, bf16[384,512]{1,0:T(8,128)(2,1)S(1)}, u32[]{:S(2)}, u32[]{:S(2)}) collective-permute-start(bf16[384,512]{1,0:T(8,128)(2,1)S(1)} %add_convert_fusion.1), channel_id=1, source_target_pairs={{0,1},{1,0},{2,3},{3,2},{4,5},{5,4},{6,7},{7,6},{8,9},{9,8},{10,11... | collective-permute-start | bytes 1179656 | tf_op jit(solution)/shard_map/ppermute | solution.py:23
  52.4 0.0 collective-permute-done.15
  52.4 0.1 add_convert_fusion.2
  52.5 1.2 %collective-permute-start.16 = (bf16[384,512]{1,0:T(8,128)(2,1)S(1)}, bf16[384,512]{1,0:T(8,128)(2,1)S(1)}, u32[]{:S(2)}, u32[]{:S(2)}) collective-permute-start(bf16[384,512]{1,0:T(8,128)(2,1)S(1)} %add_convert_fusion.2), channel_id=1, source_target_pairs={{0,2},{1,3},{2,0},{3,1},{4,6},{5,7},{6,4},{7,5},{8,10},{9,11},{10,... | collective-permute-start | bytes 1179656 | tf_op jit(solution)/shard_map/ppermute | solution.py:23
  53.6 0.1 slice_reduce_fusion
  53.8 0.0 copy-done
  53.8 0.4 add_convert_fusion.base_ref
  54.2 0.6 shard_map.101
  54.8 4.3 %collective-permute-done.14.refs_3_ = bf16[384,512]{1,0:T(8,128)(2,1)S(1)} collective-permute-done((bf16[384,512]{1,0:T(8,128)(2,1)S(1)}, bf16[384,512]{1,0:T(8,128)(2,1)S(1)}, u32[]{:S(2)}, u32[]{:S(2)}) %collective-permute-start.14) | collective-permute-done | bytes 393248 | tf_op jit(solution)/shard_map/ppermute | solution.py:23
  59.1 1.0 %collective-permute-done.13.refs_1_ = bf16[384,512]{1,0:T(8,128)(2,1)S(1)} collective-permute-done((bf16[384,512]{1,0:T(8,128)(2,1)S(1)}, bf16[384,512]{1,0:T(8,128)(2,1)S(1)}, u32[]{:S(2)}, u32[]{:S(2)}) %collective-permute-start.13) | collective-permute-done | bytes 393248 | tf_op jit(solution)/shard_map/ppermute | solution.py:23
  60.1 0.3 shard_map.104.base_ref
  60.3 5.2 %collective-permute-done.18.refs_1_ = bf16[384,512]{1,0:T(8,128)(2,1)S(1)} collective-permute-done((bf16[384,512]{1,0:T(8,128)(2,1)S(1)}, bf16[384,512]{1,0:T(8,128)(2,1)S(1)}, u32[]{:S(2)}, u32[]{:S(2)}) %collective-permute-start.18) | collective-permute-done | bytes 393248 | tf_op jit(solution)/shard_map/ppermute | solution.py:23
  65.5 0.0 collective-permute-done.16.refs_0_
  65.5 1.0 %shard_map.105 = bf16[384,1024]{1,0:T(8,128)(2,1)} custom-call(f32[384,1024]{1,0:T(8,128)S(1)} %shard_map.104.base_ref, bf16[384,512]{1,0:T(8,128)(2,1)S(1)} %collective-permute-done.16.refs_0_, bf16[384,512]{1,0:T(8,128)(2,1)S(1)} %collective-permute-done.18.refs_1_), custom_call_target="tpu_custom_call" | custom-call | tf_op jit(solution)/shard_map/pallas_call | solution.py:629
  (2 shorter events, 0.0 us)
Async XLA Ops:
  1.7 21.8 %collective-permute-start.7 = (bf16[320,1024]{1,0:T(8,128)(2,1)S(1)}, bf16[320,1024]{1,0:T(8,128)(2,1)S(1)}, u32[]{:S(2)}, u32[]{:S(2)}) collective-permute-start(bf16[320,1024]{1,0:T(8,128)(2,1)S(1)} %get-tuple-element.82.x_ref), channel_id=1, source_target_pairs={{0,1},{1,0},{2,3},{3,2},{4,5},{5,4},{6,7},{7,6},{8,9},{9,8},{10,11... | collective-permute-start | bytes 1966088 | tf_op jit(solution)/shard_map/ppermute | solution.py:23
  4.7 18.8 %collective-permute-start.8 = (bf16[320,1024]{1,0:T(8,128)(2,1)S(1)}, bf16[320,1024]{1,0:T(8,128)(2,1)S(1)}, u32[]{:S(2)}, u32[]{:S(2)}) collective-permute-start(bf16[320,1024]{1,0:T(8,128)(2,1)S(1)} %get-tuple-element.82.x_ref), channel_id=1, source_target_pairs={{0,2},{1,3},{2,0},{3,1},{4,6},{5,7},{6,4},{7,5},{8,10},{9,11},{10,... | collective-permute-start | bytes 1966088 | tf_op jit(solution)/shard_map/ppermute | solution.py:23
  8.2 1.4 %collective-permute-start = (bf16[4,16,1024]{2,1,0:T(8,128)(2,1)S(1)}, bf16[4,16,1024]{2,1,0:T(8,128)(2,1)S(1)}, u32[]{:S(2)}, u32[]{:S(2)}) collective-permute-start(bf16[4,16,1024]{2,1,0:T(8,128)(2,1)S(1)} %get-tuple-element.71), channel_id=1, source_target_pairs={{0,4},{4,0},{8,12},{12,8},{16,20},{20,16},{24,28},{28,24},{1,5},{5... | collective-permute-start | bytes 393224 | tf_op jit(solution)/shard_map/ppermute | solution.py:23
  9.7 10.0 %collective-permute-start.1 = (bf16[24,1024]{1,0:T(8,128)(2,1)S(1)}, bf16[24,1024]{1,0:T(8,128)(2,1)S(1)}, u32[]{:S(2)}, u32[]{:S(2)}) collective-permute-start(bf16[24,1024]{1,0:T(8,128)(2,1)S(1)} %get-tuple-element.73), channel_id=1, source_target_pairs={{0,8},{4,12},{8,0},{12,4},{16,24},{20,28},{24,16},{28,20},{1,9},{5... | collective-permute-start | bytes 147464 | tf_op jit(solution)/shard_map/ppermute | solution.py:23
  11.3 8.4 %collective-permute-start.2 = (bf16[24,1024]{1,0:T(8,128)(2,1)S(1)}, bf16[24,1024]{1,0:T(8,128)(2,1)S(1)}, u32[]{:S(2)}, u32[]{:S(2)}) collective-permute-start(bf16[24,1024]{1,0:T(8,128)(2,1)S(1)} %get-tuple-element.74), channel_id=1, source_target_pairs={{0,16},{4,20},{8,24},{12,28},{16,0},{20,4},{24,8},{28,12},{1,17},{... | collective-permute-start | bytes 147464 | tf_op jit(solution)/shard_map/ppermute | solution.py:23
  13.9 5.9 %collective-permute-start.3 = (bf16[24,1024]{1,0:T(8,128)(2,1)S(1)}, bf16[24,1024]{1,0:T(8,128)(2,1)S(1)}, u32[]{:S(2)}, u32[]{:S(2)}) collective-permute-start(bf16[24,1024]{1,0:T(8,128)(2,1)S(1)} %get-tuple-element.75), channel_id=1, source_target_pairs={{0,24},{4,28},{8,16},{12,20},{16,8},{20,12},{24,0},{28,4},{1,25},{... | collective-permute-start | bytes 147464 | tf_op jit(solution)/shard_map/ppermute | solution.py:23
  20.0 8.1 %collective-permute-start.4 = (bf16[80,1024]{1,0:T(8,128)(2,1)S(1)}, bf16[80,1024]{1,0:T(8,128)(2,1)S(1)}, u32[]{:S(2)}, u32[]{:S(2)}) collective-permute-start(bf16[80,1024]{1,0:T(8,128)(2,1)S(1)} %shard_map.96.refs_3_), channel_id=1, source_target_pairs={{0,3},{1,2},{2,1},{3,0},{4,7},{5,6},{6,5},{7,4},{8,11},{9,10},{10,... | collective-permute-start | bytes 491528 | tf_op jit(solution)/shard_map/ppermute | solution.py:23
  20.5 9.5 %collective-permute-start.5 = (bf16[80,1024]{1,0:T(8,128)(2,1)S(1)}, bf16[80,1024]{1,0:T(8,128)(2,1)S(1)}, u32[]{:S(2)}, u32[]{:S(2)}) collective-permute-start(bf16[80,1024]{1,0:T(8,128)(2,1)S(1)} %shard_map.96.refs_3_), channel_id=1, source_target_pairs={{0,2},{1,3},{2,0},{3,1},{4,6},{5,7},{6,4},{7,5},{8,10},{9,11},{10,... | collective-permute-start | bytes 491528 | tf_op jit(solution)/shard_map/ppermute | solution.py:23
  22.0 8.6 %collective-permute-start.6 = (bf16[80,1024]{1,0:T(8,128)(2,1)S(1)}, bf16[80,1024]{1,0:T(8,128)(2,1)S(1)}, u32[]{:S(2)}, u32[]{:S(2)}) collective-permute-start(bf16[80,1024]{1,0:T(8,128)(2,1)S(1)} %shard_map.96.refs_3_), channel_id=1, source_target_pairs={{0,1},{1,0},{2,3},{3,2},{4,5},{5,4},{6,7},{7,6},{8,9},{9,8},{10,11... | collective-permute-start | bytes 491528 | tf_op jit(solution)/shard_map/ppermute | solution.py:23
  25.9 10.1 %collective-permute-start.9 = (bf16[160,1024]{1,0:T(8,128)(2,1)S(1)}, bf16[160,1024]{1,0:T(8,128)(2,1)S(1)}, u32[]{:S(2)}, u32[]{:S(2)}) collective-permute-start(bf16[160,1024]{1,0:T(8,128)(2,1)S(1)} %slice.10), channel_id=1, source_target_pairs={{0,1},{1,0},{2,3},{3,2},{4,5},{5,4},{6,7},{7,6},{8,9},{9,8},{10,11... | collective-permute-start | bytes 983048 | tf_op jit(solution)/shard_map/ppermute | solution.py:23
  26.5 13.3 %collective-permute-start.12 = (bf16[160,1024]{1,0:T(8,128)(2,1)S(1)}, bf16[160,1024]{1,0:T(8,128)(2,1)S(1)}, u32[]{:S(2)}, u32[]{:S(2)}) collective-permute-start(bf16[160,1024]{1,0:T(8,128)(2,1)S(1)} %slice.11), channel_id=1, source_target_pairs={{0,2},{1,3},{2,0},{3,1},{4,6},{5,7},{6,4},{7,5},{8,10},{9,11},{10,... | collective-permute-start | bytes 983048 | tf_op jit(solution)/shard_map/ppermute | solution.py:23
  37.6 6.5 %collective-permute-start.10 = (bf16[160,512]{1,0:T(8,128)(2,1)S(1)}, bf16[160,512]{1,0:T(8,128)(2,1)S(1)}, u32[]{:S(2)}, u32[]{:S(2)}) collective-permute-start(bf16[160,512]{1,0:T(8,128)(2,1)S(1)} %get-tuple-element.104), channel_id=1, source_target_pairs={{0,1},{1,0},{2,3},{3,2},{4,5},{5,4},{6,7},{7,6},{8,9},{9,8},{10,11... | collective-permute-start | bytes 491528 | tf_op jit(solution)/shard_map/ppermute | solution.py:23
  38.2 6.4 %collective-permute-start.11 = (bf16[160,512]{1,0:T(8,128)(2,1)S(1)}, bf16[160,512]{1,0:T(8,128)(2,1)S(1)}, u32[]{:S(2)}, u32[]{:S(2)}) collective-permute-start(bf16[160,512]{1,0:T(8,128)(2,1)S(1)} %get-tuple-element.105), channel_id=1, source_target_pairs={{0,2},{1,3},{2,0},{3,1},{4,6},{5,7},{6,4},{7,5},{8,10},{9,11},{10,... | collective-permute-start | bytes 491528 | tf_op jit(solution)/shard_map/ppermute | solution.py:23
  42.0 8.6 %collective-permute-start.17 = (bf16[224,512]{1,0:T(8,128)(2,1)S(1)}, bf16[224,512]{1,0:T(8,128)(2,1)S(1)}, u32[]{:S(2)}, u32[]{:S(2)}) collective-permute-start(bf16[224,512]{1,0:T(8,128)(2,1)S(1)} %get-tuple-element.122), channel_id=1, source_target_pairs={{0,2},{1,3},{2,0},{3,1},{4,6},{5,7},{6,4},{7,5},{8,10},{9,11},{10,... | collective-permute-start | bytes 688136 | tf_op jit(solution)/shard_map/ppermute | solution.py:23
  42.6 9.8 %collective-permute-start.15 = (bf16[224,512]{1,0:T(8,128)(2,1)S(1)}, bf16[224,512]{1,0:T(8,128)(2,1)S(1)}, u32[]{:S(2)}, u32[]{:S(2)}) collective-permute-start(bf16[224,512]{1,0:T(8,128)(2,1)S(1)} %get-tuple-element.119), channel_id=1, source_target_pairs={{0,1},{1,0},{2,3},{3,2},{4,5},{5,4},{6,7},{7,6},{8,9},{9,8},{10,11... | collective-permute-start | bytes 688136 | tf_op jit(solution)/shard_map/ppermute | solution.py:23
  45.2 13.8 %collective-permute-start.14 = (bf16[384,512]{1,0:T(8,128)(2,1)S(1)}, bf16[384,512]{1,0:T(8,128)(2,1)S(1)}, u32[]{:S(2)}, u32[]{:S(2)}) collective-permute-start(bf16[384,512]{1,0:T(8,128)(2,1)S(1)} %get-tuple-element.116), channel_id=1, source_target_pairs={{0,2},{1,3},{2,0},{3,1},{4,6},{5,7},{6,4},{7,5},{8,10},{9,11},{10,... | collective-permute-start | bytes 1179656 | tf_op jit(solution)/shard_map/ppermute | solution.py:23
  47.9 5.9 %copy-start = (bf16[384,1024]{1,0:T(8,128)(2,1)S(1)}, bf16[384,1024]{1,0:T(8,128)(2,1)}, u32[]{:S(2)}) copy-start(bf16[384,1024]{1,0:T(8,128)(2,1)} %text_hbm.1) | copy-start | bytes 2359300
  47.9 12.1 %collective-permute-start.13 = (bf16[384,512]{1,0:T(8,128)(2,1)S(1)}, bf16[384,512]{1,0:T(8,128)(2,1)S(1)}, u32[]{:S(2)}, u32[]{:S(2)}) collective-permute-start(bf16[384,512]{1,0:T(8,128)(2,1)S(1)} %get-tuple-element.114), channel_id=1, source_target_pairs={{0,1},{1,0},{2,3},{3,2},{4,5},{5,4},{6,7},{7,6},{8,9},{9,8},{10,11... | collective-permute-start | bytes 1179656 | tf_op jit(solution)/shard_map/ppermute | solution.py:23
  50.8 14.7 %collective-permute-start.18 = (bf16[384,512]{1,0:T(8,128)(2,1)S(1)}, bf16[384,512]{1,0:T(8,128)(2,1)S(1)}, u32[]{:S(2)}, u32[]{:S(2)}) collective-permute-start(bf16[384,512]{1,0:T(8,128)(2,1)S(1)} %add_convert_fusion.1), channel_id=1, source_target_pairs={{0,1},{1,0},{2,3},{3,2},{4,5},{5,4},{6,7},{7,6},{8,9},{9,8},{10,11... | collective-permute-start | bytes 1179656 | tf_op jit(solution)/shard_map/ppermute | solution.py:23
  52.5 13.0 %collective-permute-start.16 = (bf16[384,512]{1,0:T(8,128)(2,1)S(1)}, bf16[384,512]{1,0:T(8,128)(2,1)S(1)}, u32[]{:S(2)}, u32[]{:S(2)}) collective-permute-start(bf16[384,512]{1,0:T(8,128)(2,1)S(1)} %add_convert_fusion.2), channel_id=1, source_target_pairs={{0,2},{1,3},{2,0},{3,1},{4,6},{5,7},{6,4},{7,5},{8,10},{9,11},{10,... | collective-permute-start | bytes 1179656 | tf_op jit(solution)/shard_map/ppermute | solution.py:23
